TPU v7x, 128 devices: a whole 4x4x4 slice. The times are simulated.
128 devices in a mesh: mem: 4 (over y), lat: 4 (over z_lo, core), lon: 8 (over x, z_hi).
Axes of the slice: x: 4, y: 4, z: 4 (z_hi: 2, z_lo: 2; z = z_hi * 2 + z_lo), core: 2. Of those that a mesh axis runs over, the one named last changes fastest.
Arguments:
- control: bfloat16 [4, 64, 768, 1536], P('mem', None, 'lon', 'lat'), may hold values from -6 to 6
- perturbation: bfloat16 [4, 64, 768, 1536], P('mem', None, 'lon', 'lat'), may hold values from -6 to 6
- slab_levels: int32 [32], replicated, may hold values from 1 to 3, 64 in all
- member_group: int32 [4], P('mem'), may hold values from 0 to 3
- band_width: int32 [4], replicated, may hold values from 1 to 8
- zonal_rate: float32 [32, 768], replicated, may hold values from 0.0003 to 0.4
- meridional_rate: float32 [32, 768], replicated, may hold values from 0.0003 to 0.03
Outputs:
- increment: float32 [64, 768, 1536], P('mem', 'lon', 'lat')
Inputs may be any that keep to these rules, and one draw needn't show every extreme that they name: `slab_levels`: the counts sum to 64 and the largest is exactly 3.
All inputs are finite; a program needn't handle non-finite values.
Results may differ from a plain program's by a relative error of at most 0.0046.
Values may be sent and summed in bfloat16 or wider, within the bound.
No kernel may reach another device: no remote copies, remote signals or barrier semaphores. Data moves between devices by JAX's collectives and lax.ppermute only.
A program may use at most 192 MiB of HBM per device.

v0:
```python
import math

import jax
import jax.numpy as jnp
from jax import lax
from jax.sharding import PartitionSpec as P

SLAB_MOST = 3


HIGHEST_PRECISION = lax.Precision.HIGHEST


def coefficients(rate):
    remain = 1.0 - rate
    gain = (rate * (2.0 - rate)) ** 0.75 * (1.0 + remain * remain) ** (-0.25)
    return (jnp.log1p(-rate), gain)


def along_block(values, triangle, trailing):
    if trailing:
        return jnp.einsum("ij,...ix->...jx", triangle, values, precision=HIGHEST_PRECISION)
    return jnp.matmul(values, triangle, precision=HIGHEST_PRECISION)


def block_edge(values, trailing, backward):
    position = 0 if backward else -1
    if trailing:
        return values[..., position, :]
    return values[..., position]


def blocked_recursion(values, log_decay, backward, trailing):
    block_width = values.shape[-2] if trailing else values.shape[-1]
    offsets = jnp.arange(block_width)
    if backward:
        triangle = (offsets[:, None] >= offsets[None, :]).astype(jnp.float32)
    else:
        triangle = (offsets[:, None] <= offsets[None, :]).astype(jnp.float32)
    if trailing:
        spread = log_decay
    else:
        spread = jnp.broadcast_to(log_decay, log_decay.shape[:-1] + (block_width,))
    cumulative = along_block(spread, triangle, trailing)
    growth = jnp.exp(cumulative)
    within = growth * along_block(values * jnp.exp(-cumulative), triangle, trailing)
    block_ends = block_edge(within, trailing, backward)
    block_decay = jnp.broadcast_to(block_edge(growth, trailing, backward), block_ends.shape)
    block_axis = -2 if trailing else -1
    moved_ends = jnp.moveaxis(block_ends, block_axis, 0)
    moved_decay = jnp.moveaxis(block_decay, block_axis, 0)

    def advance(incoming, element):
        return (element[1] * incoming + element[0], incoming)

    final_value, entering = lax.scan(
        advance,
        jnp.zeros(moved_ends.shape[1:], jnp.float32),
        (moved_ends, moved_decay),
        reverse=backward,
    )
    entering = jnp.moveaxis(entering, 0, block_axis)
    if trailing:
        entering = entering[..., None, :]
    else:
        entering = entering[..., None]
    return (within + growth * entering, final_value)


def one_pass(values, log_decay, gains, backward, trailing):
    length = values.shape[-2] if trailing else values.shape[-1]
    block_width = math.gcd(length, 128)
    block_count = length // block_width
    if trailing:
        blocked_values = (values * gains).reshape(
            values.shape[:-2] + (block_count, block_width, values.shape[-1])
        )
        blocked_decay = log_decay.reshape(log_decay.shape[:-2] + (block_count, block_width, 1))
    else:
        blocked_values = (values * gains).reshape(values.shape[:-1] + (block_count, block_width))
        blocked_decay = log_decay[..., None]
    result, final_value = blocked_recursion(blocked_values, blocked_decay, backward, trailing)
    result = result.reshape(values.shape)
    return result


def smooth(field, zonal_rows, meridional_rows):
    zonal_log, zonal_gain = coefficients(zonal_rows)
    meridional_log, meridional_gain = coefficients(meridional_rows)
    zonal_log = zonal_log[..., None]
    zonal_gain = zonal_gain[..., None]
    field = one_pass(field, zonal_log, zonal_gain, False, False)
    field = one_pass(field, zonal_log, zonal_gain, True, False)
    meridional_log = meridional_log[:, :, None]
    meridional_gain = meridional_gain[:, :, None]
    field = one_pass(field, meridional_log, meridional_gain, False, True)
    return one_pass(field, meridional_log, meridional_gain, True, True)


def through_slabs(outgoing, own_zonal, own_meridional):
    lat_count = lax.axis_size("lat")
    lon_count = lax.axis_size("lon")
    arrived = lax.all_to_all(outgoing, ("lat", "lon"), split_axis=1, concat_axis=1, tiled=True)
    members_here, source_count, slot_total, tile_rows, tile_cols = arrived.shape
    gathered_field = arrived.reshape(
        members_here, lat_count, lon_count, slot_total, tile_rows, tile_cols
    )
    gathered_field = gathered_field.transpose(0, 3, 2, 4, 1, 5).reshape(
        members_here, slot_total, lon_count * tile_rows, lat_count * tile_cols
    )

    def one_member(member_field):
        return smooth(member_field[None].astype(jnp.float32), own_zonal, own_meridional)[0].astype(
            jnp.bfloat16
        )

    smoothed = lax.map(one_member, gathered_field)
    returning = smoothed.reshape(
        members_here, slot_total, lon_count, tile_rows, lat_count, tile_cols
    )
    returning = returning.transpose(0, 4, 2, 1, 3, 5).reshape(
        members_here, source_count, slot_total, tile_rows, tile_cols
    )
    return lax.all_to_all(returning, ("lat", "lon"), split_axis=1, concat_axis=1, tiled=True)


def per_device(
    control, perturbation, slab_levels, member_group, band_width, zonal_rate, meridional_rate
):
    member_count, level_count, tile_rows, tile_cols = control.shape
    slab_count = slab_levels.shape[0]
    group_count = band_width.shape[0]
    level_index = jnp.arange(level_count, dtype=jnp.int32)
    spacing = (level_index[:, None] - level_index[None, :]).astype(jnp.float32)
    chosen = member_group[:, None] == jnp.arange(group_count)[None, :]
    member_band = jnp.sum(jnp.where(chosen, band_width[None, :], 0), axis=1).astype(jnp.float32)
    band_reach = member_band[:, None, None]
    kernel = jnp.where(
        jnp.abs(spacing)[None] <= band_reach, jnp.exp(-2.0 * (spacing[None] / band_reach) ** 2), 0.0
    ).astype(jnp.bfloat16)
    column = jnp.einsum(
        "mkl,mlyx->mkyx", kernel, control, preferred_element_type=jnp.float32
    ).astype(jnp.bfloat16)
    slab_ends = jnp.cumsum(slab_levels)
    slab_starts = slab_ends - slab_levels
    level_slab = jnp.sum((level_index[:, None] >= slab_ends[None, :]).astype(jnp.int32), axis=1)
    owner_index = lax.axis_index(("lat", "lon"))
    full_rows = zonal_rate.shape[1]
    slot_count = SLAB_MOST
    slot_index = jnp.arange(slot_count, dtype=jnp.int32)
    level_pick = jnp.minimum(slab_starts[:, None] + slot_index[None, :], level_count - 1)
    occupied = slot_index[None, :] < slab_levels[:, None]
    outgoing = jnp.take(column, level_pick.reshape(-1), axis=1).reshape(
        member_count, slab_count, slot_count, tile_rows, tile_cols
    )
    outgoing = jnp.where(occupied[None, :, :, None, None], outgoing, jnp.zeros_like(outgoing))
    own_zonal = jnp.broadcast_to(
        lax.dynamic_slice_in_dim(zonal_rate, owner_index, 1, 0), (slot_count, full_rows)
    )
    own_meridional = jnp.broadcast_to(
        lax.dynamic_slice_in_dim(meridional_rate, owner_index, 1, 0), (slot_count, full_rows)
    )
    returned = through_slabs(outgoing, own_zonal, own_meridional)
    flattened = returned.reshape(member_count, slab_count * slot_count, tile_rows, tile_cols)
    source = level_slab * slot_count + level_index - slab_starts[level_slab]
    filtered = jnp.take(flattened, source, axis=1)
    weight = 1.0 / math.sqrt(member_count * lax.axis_size("mem") - 1)
    local_sum = (
        jnp.einsum("mlyx,mlyx->lyx", perturbation, filtered, preferred_element_type=jnp.float32)
        * weight
    )
    return lax.psum_scatter(local_sum, "mem", scatter_dimension=0, tiled=True)


def solution(mesh):
    return jax.shard_map(
        per_device,
        mesh=mesh,
        in_specs=(
            P("mem", None, "lon", "lat"),
            P("mem", None, "lon", "lat"),
            P(),
            P("mem"),
            P(),
            P(),
            P(),
        ),
        out_specs=P("mem", "lon", "lat"),
        check_vma=False,
    )
```

profile of v0, /device:TPU:0, one launch (start us, length us, event | category | flops | bytes accessed | tf_op | source)
XLA Modules:
  0.0 618.7 jit_solution(15192709524241699606)
XLA Ops:
  11.5 4.4 fusion.43
  15.9 5.0 copy.96
  21.1 9.2 %gather_fusion.1 = bf16[96,96,384]{2,1,0:T(8,128)(2,1)} fusion(bf16[64,96,384]{2,1,0:T(8,128)(2,1)} %copy.96, s32[1024]{0:T(1024)S(1)} %pad_clamp_fusion.1), kind=kCustom, calls=%fused_computation.1 | custom fusion | bytes 14156160 | tf_op jit(solution)/shard_map/jit(_take)/gather | solution.py:153
  30.3 7.0 %select_bitcast_fusion = bf16[1,32,3,96,384]{4,3,2,0,1:T(8,128)(2,1)} fusion(bf16[1,32,3,96,384]{4,3,2,1,0:T(8,128)(2,1)} %bitcast.231, pred[32,3]{1,0:T(8,128)(4,1)S(1)} %copy.93, pred[32,3]{1,0:T(8,128)(4,1)S(1)} %iota_compare_fusion.2), kind=kLoop, calls=%fused_computation.62 | loop fusion | flops 7077888 | bytes 14155968 | tf_op jit(solution)/shard_map/jit(_where)/select_n | solution.py:156
  37.4 8.8 %all-to-all-start = ((bf16[1,32,3,96,384]{4,3,2,0,1:T(8,128)(2,1)}), bf16[1,32,3,96,384]{4,3,2,0,1:T(8,128)(2,1)}, u32[]{:S(2)}, u32[]{:S(2)}) async-start(bf16[1,32,3,96,384]{4,3,2,0,1:T(8,128)(2,1)} %select_bitcast_fusion), calls=%async_computation | async-start | bytes 14155776 | tf_op jit(solution)/shard_map/all_to_all | solution.py:103
  47.6 1.9 fusion.87
  54.3 1.4 copy.123
  55.7 1.5 exponential_bitcast_fusion.1
  57.2 1.4 copy.124
  58.6 1.4 broadcast_bitcast_fusion.1
  60.0 1.4 broadcast_bitcast_fusion
  61.4 79.9 %all-to-all-done = bf16[1,32,3,96,384]{4,3,2,0,1:T(8,128)(2,1)} async-done(((bf16[1,32,3,96,384]{4,3,2,0,1:T(8,128)(2,1)}), bf16[1,32,3,96,384]{4,3,2,0,1:T(8,128)(2,1)}, u32[]{:S(2)}, u32[]{:S(2)}) %all-to-all-start) | async-done | bytes 7077920 | tf_op jit(solution)/shard_map/all_to_all | solution.py:103
  141.4 13.5 %copy.98 = f32[1,4,8,3,96,384]{4,2,5,1,3,0:T(8,128)} copy(bf16[1,4,8,3,96,384]{5,4,3,2,1,0:T(8,128)(2,1)} %bitcast.71) | data formatting | bytes 21233664 | tf_op jit(solution)/shard_map/while/body/eval_jaxpr/convert_element_type | solution.py:113
  154.8 19.3 %reshape.489 = f32[3,768,12,128]{1,3,2,0:T(8,128)} reshape(f32[1,3,8,96,4,384]{3,2,5,4,1,0:T(8,128)} %bitcast.229) | data formatting | bytes 28311552 | tf_op jit(solution)/shard_map/while/body/eval_jaxpr/convert_element_type | solution.py:113
  174.1 15.0 %fusion.20 = f32[3,768,12,128]{1,3,2,0:T(8,128)} fusion(f32[3,768,12,128]{1,3,2,0:T(8,128)} %reshape.489, f32[3,768,128]{1,2,0:T(8,128)} %get-tuple-element.501, f32[768]{0:T(1024)} %get-tuple-element.510), kind=kOutput, calls=%fused_computation.43 | convolution fusion | flops 5442912256 | bytes 29494272 | tf_op jit(solution)/shard_map/while/body/eval_jaxpr/dot_general | solution.py:23
  189.1 11.8 %multiply_bitcast_fusion.1 = f32[1,3,768,12,128]{2,4,3,1,0:T(8,128)} fusion(f32[3,768,12,128]{1,3,2,0:T(8,128)} %fusion.20, f32[3,768,128]{1,2,0:T(8,128)S(1)} %get-tuple-element.499), kind=kLoop, calls=%fused_computation.48 | loop fusion | flops 3538944 | bytes 29491200 | tf_op jit(solution)/shard_map/while/body/eval_jaxpr/mul | solution.py:46
  200.9 1.9 slice_bitcast_fusion.3
  202.9 1.4 transpose.101
  204.9 39.4 %while.76 = (s32[]{:T(128)}, f32[1,3,768]{2,1,0:T(4,128)}, f32[12,1,3,768]{3,2,1,0:T(4,128)}, f32[12,1,3,768]{3,2,1,0:T(4,128)}, f32[12,1,3,768]{3,1,0,2:T(1,128)}, /*index=5*/s32[]{:T(128)}, s32[]{:T(128)}) while((s32[]{:T(128)}, f32[1,3,768]{2,1,0:T(4,128)}, f32[12,1,3,768]{3,2,1,0:T(4,128)}, f32[12,1,3,768]{3,2,1,0:T(4,128)}, ...), condition=%wide.region_4.5_spmd.clone, body=%wide.region_3.4_spmd.clone.sunk | while | flops 9219 | bytes 79980 | solution.py:56
  209.6 1.3 fusion.108
  212.9 1.3 fusion.108
  216.2 1.3 fusion.108
  219.6 1.3 fusion.108
  222.9 1.3 fusion.108
  226.3 1.4 fusion.108
  229.6 1.3 fusion.108
  233.0 1.3 fusion.108
  236.3 1.3 fusion.108
  239.7 1.3 fusion.108
  245.3 16.4 %fusion.15 = f32[3,768,12,128]{1,3,2,0:T(8,128)} fusion(f32[3,768,12,128]{1,3,2,0:T(8,128)} %fusion.20, f32[3,768,128]{1,2,0:T(8,128)S(1)} %get-tuple-element.498, f32[3,768,12]{1,2,0:T(8,128)S(1)} %copy.101, f32[768]{0:T(1024)} %get-tuple-element.510, f32[3,768,128]{1,2,0:T(8,128)S(1)} %get-tuple-element.499), kind=kOutput, calls=%fused_computation.38 | convolution fusion | flops 5453529088 | bytes 30784512 | tf_op jit(solution)/shard_map/while/body/eval_jaxpr/dot_general | solution.py:23
  261.6 11.7 %multiply_bitcast_fusion = f32[1,3,768,12,128]{2,4,3,1,0:T(8,128)} fusion(f32[3,768,12,128]{1,3,2,0:T(8,128)} %fusion.15, f32[3,768,128]{1,2,0:T(8,128)S(1)} %get-tuple-element.496), kind=kLoop, calls=%fused_computation.46 | loop fusion | flops 3538944 | bytes 29491200 | tf_op jit(solution)/shard_map/while/body/eval_jaxpr/mul | solution.py:46
  275.7 12.6 %multiply_add_fusion = f32[3,768,12,128]{1,3,2,0:T(8,128)} fusion(f32[3,768,12,128]{1,3,2,0:T(8,128)} %fusion.15, f32[3,768,12]{1,2,0:T(8,128)S(1)} %copy.104, f32[3,768,128]{1,2,0:T(8,128)S(1)} %get-tuple-element.496), kind=kLoop, calls=%fused_computation.37 | loop fusion | flops 10616832 | bytes 29601792 | tf_op jit(solution)/shard_map/while/body/eval_jaxpr/add | solution.py:67
  288.3 17.2 %reshape.531 = f32[3,6,128,1536]{2,1,3,0:T(8,128)} reshape(f32[3,768,12,128]{1,3,2,0:T(8,128)} %multiply_add_fusion) | data formatting | bytes 28311552 | tf_op jit(solution)/shard_map/while/body/eval_jaxpr/reshape | solution.py:83
  305.5 16.7 %copy.122 = f32[3,6,128,1536]{3,2,1,0:T(8,128)} copy(f32[3,6,128,1536]{2,1,3,0:T(8,128)} %reshape.531) | data formatting | bytes 28311552 | tf_op jit(solution)/shard_map/while/body/eval_jaxpr/reshape | solution.py:83
  322.2 13.4 %fusion.7 = f32[1,3,6,128,1536]{4,3,2,1,0:T(8,128)S(1)} fusion(f32[3,6,128,1536]{3,2,1,0:T(8,128)} %copy.122, f32[3,6,128]{2,1,0:T(8,128)S(1)} %copy-done.8, f32[6,128]{1,0:T(8,128)S(1)} %copy-done.4, f32[3,6,128]{2,1,0:T(8,128)S(1)} %copy-done.6), kind=kOutput, calls=%fused_computation.28 | convolution fusion | flops 5446451200 | bytes 28333056 | tf_op jit(solution)/shard_map/while/body/eval_jaxpr/ij,...ix->...jx/dot_general | solution.py:22
  335.6 5.0 copy-done.1
  340.8 5.0 while.78
  345.8 14.6 %fusion.4 = f32[1,3,6,128,1536]{4,3,2,1,0:T(8,128)S(1)} fusion(f32[1,3,6,128,1536]{4,3,2,1,0:T(8,128)} %copy-done.1, f32[3,6,128]{2,1,0:T(8,128)S(1)} %copy-done.7, f32[6,128]{1,0:T(8,128)S(1)} %copy-done.4, f32[3,6,1536]{2,1,0:T(8,128)S(1)} %copy.108, f32[3,6,128]{2,1,0:T(8,128)S(1)} %copy-done.6, f32[3,6,128]{2,1,0:T(8,128)S(1)} %copy-done.5), kind=kOutput, calls=%fused_computation.24 | convolution fusion | flops 5453529088 | bytes 28452864 | tf_op jit(solution)/shard_map/while/body/eval_jaxpr/ij,...ix->...jx/dot_general | solution.py:22
  360.5 5.0 copy-done
  365.6 5.0 while.79
  370.6 9.6 %add_convert_fusion = bf16[1,3,6,128,1536]{4,3,2,1,0:T(8,128)(2,1)} fusion(f32[1,3,6,128,1536]{4,3,2,1,0:T(8,128)} %copy-done, f32[3,6,1536]{2,1,0:T(8,128)S(1)} %copy.111, f32[3,6,128]{2,1,0:T(8,128)S(1)} %copy-done.5), kind=kLoop, calls=%fused_computation.29 | loop fusion | flops 10616832 | bytes 21353472 | tf_op jit(solution)/shard_map/while/body/eval_jaxpr/convert_element_type | solution.py:113
  380.2 12.8 %convert_element_type.104 = bf16[1,3,8,96,4,384]{5,4,3,2,1,0:T(4,128)(2,1)} reshape(bf16[1,3,6,128,1536]{4,3,2,1,0:T(8,128)(2,1)} %add_convert_fusion) | data formatting | bytes 14155776 | tf_op jit(solution)/shard_map/while/body/eval_jaxpr/convert_element_type | solution.py:113
  392.9 7.0 %copy.112 = bf16[1,3,8,96,4,384]{5,3,1,2,4,0:T(8,128)(2,1)} copy(bf16[1,3,8,96,4,384]{5,4,3,2,1,0:T(4,128)(2,1)} %convert_element_type.104) | data formatting | bytes 14155776 | tf_op jit(solution)/shard_map/while/body/eval_jaxpr/convert_element_type | solution.py:113
  399.9 8.5 %all-to-all-start.1 = ((bf16[1,32,3,96,384]{4,3,2,0,1:T(8,128)(2,1)}), bf16[1,32,3,96,384]{4,3,2,0,1:T(8,128)(2,1)}, u32[]{:S(2)}, u32[]{:S(2)}) async-start(bf16[1,32,3,96,384]{4,3,2,0,1:T(8,128)(2,1)} %bitcast.230), calls=%async_computation.1 | async-start | bytes 14155776 | tf_op jit(solution)/shard_map/all_to_all | solution.py:124
  409.4 94.5 %all-to-all-done.1 = bf16[1,32,3,96,384]{4,3,2,0,1:T(8,128)(2,1)} async-done(((bf16[1,32,3,96,384]{4,3,2,0,1:T(8,128)(2,1)}), bf16[1,32,3,96,384]{4,3,2,0,1:T(8,128)(2,1)}, u32[]{:S(2)}, u32[]{:S(2)}) %all-to-all-start.1) | async-done | bytes 7077920 | tf_op jit(solution)/shard_map/all_to_all | solution.py:124
  504.0 6.4 %gather_fusion.2 = bf16[64,96,384]{2,1,0:T(8,128)(2,1)} fusion(bf16[96,96,384]{2,1,0:T(8,128)(2,1)} %bitcast.54, s32[1024]{0:T(1024)S(1)} %pad_clamp_fusion), kind=kCustom, calls=%fused_computation.2 | custom fusion | bytes 9437440 | tf_op jit(solution)/shard_map/jit(_take)/gather | solution.py:166
  510.4 9.5 %fusion.24 = f32[64,96,384]{2,1,0:T(8,128)} fusion(bf16[1,64,96,384]{3,2,1,0:T(8,128)(2,1)} %param.16, bf16[64,96,384]{2,1,0:T(8,128)(2,1)} %gather_fusion.2, pred[64]{0:T(512)(128)(4,1)S(1)} %compare_and_fusion.1), kind=kLoop, calls=%fused_computation.50 | loop fusion | flops 11796480 | bytes 18874432 | tf_op jit(solution)/shard_map/mul | solution.py:169
  519.9 91.8 %reduce-scatter.2.cloned.1.call-done = f32[16,96,384]{2,1,0:T(8,128)} async-done(((f32[64,96,384]{2,1,0:T(8,128)}), f32[16,96,384]{2,1,0:T(8,128)}) %reduce-scatter.2.cloned.1.call-update) | async-done | bytes 2359312 | tf_op jit(solution)/shard_map/reduce_scatter | solution.py:172
  (171 shorter events, 51.4 us)
Async XLA Ops:
  7.4 0.7 copy-start.11
  37.4 104.0 %all-to-all-start = ((bf16[1,32,3,96,384]{4,3,2,0,1:T(8,128)(2,1)}), bf16[1,32,3,96,384]{4,3,2,0,1:T(8,128)(2,1)}, u32[]{:S(2)}, u32[]{:S(2)}) async-start(bf16[1,32,3,96,384]{4,3,2,0,1:T(8,128)(2,1)} %select_bitcast_fusion), calls=%async_computation | async-start | bytes 14155776 | tf_op jit(solution)/shard_map/all_to_all | solution.py:103
  52.2 0.6 copy-start.10
  261.6 13.0 %copy-start.9 = (f32[3,768,1,1]{1,0,3,2:T(4,128)S(1)}, f32[3,768,1,1]{1,0,3,2:T(4,128)}, u32[]{:S(2)}) copy-start(f32[3,768,1,1]{1,0,3,2:T(4,128)} %copy.149) | copy-start | bytes 27652
  305.5 16.7 %copy-start.4 = (f32[6,128]{1,0:T(8,128)S(1)}, f32[6,128]{1,0:T(8,128)}, u32[]{:S(2)}) copy-start(f32[6,128]{1,0:T(8,128)} %get-tuple-element.508) | copy-start | bytes 9220
  305.5 16.7 %copy-start.6 = (f32[3,6,128]{2,1,0:T(8,128)S(1)}, f32[3,6,128]{2,1,0:T(8,128)}, u32[]{:S(2)}) copy-start(f32[3,6,128]{2,1,0:T(8,128)} %get-tuple-element.507) | copy-start | bytes 27652
  305.5 16.7 %copy-start.8 = (f32[3,6,128]{2,1,0:T(8,128)S(1)}, f32[3,6,128]{2,1,0:T(8,128)}, u32[]{:S(2)}) copy-start(f32[3,6,128]{2,1,0:T(8,128)} %get-tuple-element.506) | copy-start | bytes 27652
  322.2 18.6 %copy-start.3 = (f32[1,3,1536]{2,1,0:T(4,128)S(1)}, f32[1,3,1536]{2,1,0:T(4,128)}, u32[]{:S(2)}) copy-start(f32[1,3,1536]{2,1,0:T(4,128)} %custom-call.2) | copy-start | bytes 55300
  322.2 23.6 %copy-start.5 = (f32[3,6,128]{2,1,0:T(8,128)S(1)}, f32[3,6,128]{2,1,0:T(8,128)}, u32[]{:S(2)}) copy-start(f32[3,6,128]{2,1,0:T(8,128)} %get-tuple-element.504) | copy-start | bytes 27652
  322.2 23.6 %copy-start.7 = (f32[3,6,128]{2,1,0:T(8,128)S(1)}, f32[3,6,128]{2,1,0:T(8,128)}, u32[]{:S(2)}) copy-start(f32[3,6,128]{2,1,0:T(8,128)} %get-tuple-element.503) | copy-start | bytes 27652
  335.6 5.0 copy-start.1
  345.8 19.8 %copy-start.2 = (f32[1,3,1536]{2,1,0:T(4,128)S(1)}, f32[1,3,1536]{2,1,0:T(4,128)}, u32[]{:S(2)}) copy-start(f32[1,3,1536]{2,1,0:T(4,128)} %custom-call.3) | copy-start | bytes 55300
  360.5 5.0 copy-start
  392.9 15.5 %copy-start.12 = (s32[32]{0:T(128)S(1)}, s32[32]{0:T(128)}, u32[]{:S(2)}) copy-start(s32[32]{0:T(128)} %copy-done.11) | copy-start | bytes 388
  399.9 104.0 %all-to-all-start.1 = ((bf16[1,32,3,96,384]{4,3,2,0,1:T(8,128)(2,1)}), bf16[1,32,3,96,384]{4,3,2,0,1:T(8,128)(2,1)}, u32[]{:S(2)}, u32[]{:S(2)}) async-start(bf16[1,32,3,96,384]{4,3,2,0,1:T(8,128)(2,1)} %bitcast.230), calls=%async_computation.1 | async-start | bytes 14155776 | tf_op jit(solution)/shard_map/all_to_all | solution.py:124
  408.4 203.2 %reduce-scatter.2.cloned.1.call-start = ((), (), s32[]{:S(2)}) async-start(), calls=%async_computation.3 | async-start | bytes 11796480 | tf_op jit(solution)/shard_map/reduce_scatter | solution.py:172
Sparse Core Ops, SparseCore 0:
  520.0 91.6 reduce-scatter.1
where the time goes:
time: 631 us; the launch traced here: 619 us
  waiting for transfers between devices  266 us (42%)
  local copies, waits for them, and re-layouts  143 us (23%)
  other arithmetic  107 us (17%)
  matrix products  68.8 us (11%)
  starting transfers between devices  17.4 us (3%)
  between operations  15.3 us (2%)
    all_to_all x1, waiting for transfers between devices, through_slabs(): lax.all_to_all(returning, ('lat', 'lon'), split_axis=1, concat_axis=1, ti...  94.5 us
    reduce_scatter x1, waiting for transfers between devices, per_device(): return lax.psum_scatter(local_sum, 'mem', scatter_dimension=0, tiled=True)  91.8 us
    all_to_all x1, waiting for transfers between devices, through_slabs(): lax.all_to_all(outgoing, ('lat', 'lon'), split_axis=1, concat_axis=1, til...  79.9 us
    dot_general x4, matrix products, along_block(): return jnp.matmul(values, triangle, precision=HIGHEST_PRECISION)  34.1 us
    reshape x2, local copies, waits for them, and re-layouts, one_pass(): result = result.reshape(values.shape)  33.9 us
    convert_element_type x2, local copies, waits for them, and re-layouts, one_member(): member_field[None].astype(jnp.float32)  32.7 us
    dot_general x4, matrix products, along_block(): jnp.einsum('ij,...ix->...jx', triangle, values, precision=HIGHEST_PRECISION)  30.3 us
    add x36, other arithmetic, advance(): return (element[1] * incoming + element[0], incoming)  25.5 us
  transfers between devices with their start and end apart: 3, of which 3 were waited for; matrix products, arithmetic and copies ran while one was open for 3% of the time, Pallas kernels for 0%

commit v1 on v0

v1 whole, which is shorter than its diff:
```python
import functools
import math

import jax
import jax.numpy as jnp
import numpy as np
from jax import lax
from jax.experimental import pallas as pl
from jax.experimental.pallas import tpu as pltpu
from jax.sharding import PartitionSpec as P

CHUNKS = 4
LANES = 128
ROW_GROUP = 16
VMEM_LIMIT = 48 * 1024 * 1024

F32 = jnp.float32
BF16 = jnp.bfloat16


def iota(shape, axis):
    return lax.broadcasted_iota(jnp.int32, shape, axis)


def log_decay(rate):
    t = rate / (2.0 - rate)
    s = t * t
    series = 1.0 + s * (1 / 3 + s * (1 / 5 + s * (1 / 7 + s * (1 / 9 + s * (1 / 11 + s / 13)))))
    return -2.0 * t * series


def split3(x):
    hi = x.astype(BF16)
    rest = x - hi.astype(F32)
    mid = rest.astype(BF16)
    return hi, mid, (rest - mid.astype(F32)).astype(BF16)


def split2(x):
    hi = x.astype(BF16)
    return hi, (x - hi.astype(F32)).astype(BF16)


def dot_nn(a, b):
    return lax.dot_general(a, b, (((1,), (0,)), ((), ())), preferred_element_type=F32)


def dot_nt(a, b):
    return lax.dot_general(a, b, (((1,), (1,)), ((), ())), preferred_element_type=F32)


def times_exact(x, zero_one):
    rows = x.shape[0]
    product = dot_nn(jnp.concatenate(split3(x), axis=0), zero_one)
    return product[:rows] + product[rows : 2 * rows] + product[2 * rows :]


def exact_times_t(zero_one, x):
    return sum(dot_nt(zero_one, part) for part in split3(x))


def level_of_place(place, levels, chunks, quarters):
    steps = levels // (chunks * quarters)
    in_chunk = steps * quarters
    chunk, rest = place // in_chunk, place % in_chunk
    return (rest // steps) * (levels // quarters) + chunk * steps + rest % steps


def traced_level(place, levels, chunks, quarters):
    steps = levels // (chunks * quarters)
    in_chunk = steps * quarters
    log_steps, log_chunk = int(math.log2(steps)), int(math.log2(in_chunk))
    chunk = jnp.right_shift(place, log_chunk)
    rest = jnp.bitwise_and(place, in_chunk - 1)
    return (
        jnp.right_shift(rest, log_steps) * (levels // quarters)
        + chunk * steps
        + jnp.bitwise_and(rest, steps - 1)
    )


def rates_by_place(slab_levels, rates, levels, quarters):
    slabs = rates.shape[0]
    level = traced_level(iota((levels, slabs), 0), levels, CHUNKS, quarters)
    index = jnp.zeros((levels, slabs), jnp.int32)
    end = jnp.int32(0)
    for s in range(slabs):
        end = end + slab_levels[s]
        index = index + (level >= end).astype(jnp.int32)
    chosen = (index == iota((levels, slabs), 1)).astype(F32).astype(BF16)
    return sum(dot_nn(chosen, part) for part in split3(rates))


def lane_of(table, lane):
    return jnp.take_along_axis(table, jnp.full(table.shape, lane, jnp.int32), axis=1)


def column_kernel(
    sizes, where_ref, slab_ref, group_ref, band_ref, control_ref, rate_ref,
    column_ref, decay_ref, gain_ref, end_ref, send1_ref, send2_ref, send3_ref,
    kron, decay_all,
):
    levels, rows, cols, quarters, lat_count = sizes
    step = pl.program_id(0)
    lat, lon = where_ref[1], where_ref[2]
    full = levels * 8

    @pl.when(step == 0)
    def _():
        band = band_ref[group_ref[0]].astype(F32)
        out_level = traced_level(jnp.right_shift(iota((full, full), 0), 3), levels, CHUNKS, quarters)
        spacing = out_level - jnp.right_shift(iota((full, full), 1), 3)
        same = jnp.bitwise_and(iota((full, full), 0), 7) == jnp.bitwise_and(iota((full, full), 1), 7)
        ratio = spacing.astype(F32) / band
        weight = jnp.exp(-2.0 * (ratio * ratio))
        keep = jnp.logical_and(same, jnp.abs(spacing).astype(F32) <= band)
        kron[...] = jnp.where(keep, weight, 0.0).astype(BF16)
        level_rates = rates_by_place(slab_ref, rate_ref[...], levels, quarters)
        own = iota((rows, rate_ref.shape[1]), 1) == lon * rows + iota((rows, rate_ref.shape[1]), 0)
        rate = exact_times_t(own.astype(F32).astype(BF16), level_rates)
        remain = 1.0 - rate
        decay_all[...] = log_decay(rate)
        decay_ref[...] = decay_all[...]
        gain_ref[...] = jnp.sqrt(rate * (2.0 - rate) / (1.0 + remain * remain))

    block = control_ref[0].astype(F32)
    halves = []
    for half in range(2):
        part = block[:, 8 * half : 8 * half + 8, :].reshape(full, cols).astype(BF16)
        halves.append(dot_nn(kron[...], part).reshape(levels, 8, cols))
    column = jnp.concatenate(halves, axis=1).astype(BF16)
    column_ref[...] = column

    log_a = decay_all[pl.ds(step * ROW_GROUP, ROW_GROUP), :]
    lane = iota((ROW_GROUP, LANES), 1).astype(F32)
    place_lane = iota((ROW_GROUP, levels), 1)
    forward = jnp.zeros((ROW_GROUP, levels), F32)
    backward = jnp.zeros((ROW_GROUP, levels), F32)
    blocks = cols // LANES
    for place in range(levels):
        log_b = jnp.broadcast_to(log_a[:, place : place + 1], (ROW_GROUP, LANES))
        over = jnp.exp(log_b * float(LANES))
        x = column_ref[place].astype(F32)
        parts = [x[:, LANES * b : LANES * (b + 1)] for b in range(blocks)]
        along, against = parts[0], parts[-1]
        for b in range(1, blocks):
            along = parts[b] + over * along
            against = parts[-1 - b] + over * against
        along = jnp.sum(along * jnp.exp(log_b * (LANES - 1.0 - lane)), axis=1, keepdims=True)
        against = jnp.sum(against * jnp.exp(log_b * lane), axis=1, keepdims=True)
        forward = jnp.where(place_lane == place, along, forward)
        backward = jnp.where(place_lane == place, against, backward)
    power = (1 + cols * (2 * (lat_count - 1 - lat) + 1)).astype(F32)
    returning = backward - jnp.exp(log_a * power) * forward
    end_ref[...] = forward
    for shift, ref in ((1, send1_ref), (2, send2_ref), (3, send3_ref)):
        ref[...] = jnp.where(lat + shift < lat_count, forward, returning)


def row_kernel(
    sizes, where_ref, slab_ref, rate_ref,
    left_ref, left_sum_ref, right_ref, right_sum_ref, chain_ref,
):
    levels, rows, quarters, lon_count = sizes
    lon = where_ref[2]
    total = rate_ref.shape[1]
    rate = rates_by_place(slab_ref, rate_ref[...], levels, quarters)
    remain = 1.0 - rate
    root = jnp.sqrt(rate * (2.0 - rate))
    gain = root * jnp.sqrt(root) / jnp.sqrt(jnp.sqrt(1.0 + remain * remain))
    log_c = log_decay(rate)
    owner = lambda at: jnp.right_shift(at * ((1 << 16) // rows + 1), 16)
    first, second = iota((total, total), 0), iota((total, total), 1)
    same = owner(first) == owner(second)
    upper = jnp.logical_and(same, first <= second).astype(F32).astype(BF16)
    lower = jnp.logical_and(same, first >= second).astype(F32).astype(BF16)
    running = times_exact(log_c, upper)
    before = running - log_c
    weight = gain * jnp.exp(running + before)
    sums = times_exact(weight, lower)
    left = jnp.exp(-before)
    right = gain * jnp.exp(-running)
    own = (iota((rows, total), 1) == lon * rows + iota((rows, total), 0)).astype(F32).astype(BF16)
    own_t = (iota((total, rows), 0) == lon * rows + iota((total, rows), 1)).astype(F32).astype(BF16)
    left_ref[...] = exact_times_t(own, left)
    left_sum_ref[...] = exact_times_t(own, left * sums)
    right_ref[...] = times_exact(right, own_t)
    right_sum_ref[...] = times_exact(right * sums, own_t)

    inside = (owner(iota((total, LANES), 0)) == iota((total, LANES), 1)).astype(F32).astype(BF16)
    log_over = times_exact(log_c, inside)
    bounce = times_exact(weight, inside)
    source, target = iota((LANES, LANES), 0), iota((LANES, LANES), 1)
    between = jnp.logical_and(source > lon, source < target).astype(F32).astype(BF16)
    device = iota((levels, LANES), 1)
    beyond = jnp.logical_and(device > lon, device < lon_count)
    echo = jnp.sum(
        jnp.where(beyond, bounce * jnp.exp(2.0 * times_exact(log_over, between)), 0.0),
        axis=1,
        keepdims=True,
    )
    over = jnp.sum(jnp.where(device == lon, jnp.exp(log_over), 0.0), axis=1, keepdims=True)
    origin = jnp.where(lon >= target, lon - target, lon - target + lon_count)
    low, high = jnp.minimum(origin, lon), jnp.maximum(origin, lon)
    path = jnp.logical_and(source > low, source < high).astype(F32).astype(BF16)
    reach = jnp.exp(times_exact(log_over, path))
    shift = device
    along = jnp.where(jnp.logical_and(shift >= 1, shift <= lon), reach, 0.0)
    against = jnp.where(jnp.logical_and(shift > lon, shift < lon_count), reach, 0.0)
    lane = device
    chain = jnp.where(lane < lon_count, along, 0.0)
    chain = chain + jnp.concatenate(
        [jnp.zeros((levels, 64), F32), against[:, :64]], axis=1
    )
    chain = jnp.where(lane == 32, over, chain)
    chain_ref[...] = jnp.where(lane == 33, echo, chain)


def field_kernel(
    sizes, where_ref, column_ref, decay_ref, gain_ref, end_ref, got1_ref, got2_ref, got3_ref,
    left_ref, left_sum_ref, right_ref, right_sum_ref, chain_ref, triangle_ref,
    field_ref, out_end_ref, *rest,
):
    rows, cols, chunk, in_chunk, per_step, lat_count, lon_count = sizes
    send_refs = rest[: lon_count - 1]
    tables, rights, edges = rest[lon_count - 1 :]
    step = pl.program_id(0)
    lat, lon = where_ref[1], where_ref[2]
    blocks = cols // LANES

    @pl.when(step == 0)
    def _():
        log_a, gain = decay_ref[...], gain_ref[...]
        enter_left = jnp.zeros(log_a.shape, F32)
        enter_right = jnp.zeros(log_a.shape, F32)
        for shift, ref in ((1, got1_ref), (2, got2_ref), (3, got3_ref)):
            got = ref[...]
            is_left = lat >= shift
            power = jnp.where(is_left, shift - 1, lat_count - 1 - shift) * cols
            scaled = jnp.exp(log_a * power.astype(F32)) * got
            enter_left = enter_left + jnp.where(is_left, scaled, 0.0)
            enter_right = enter_right + jnp.where(is_left, 0.0, scaled)
        leaving = end_ref[...] + jnp.exp(log_a * float(cols)) * enter_left
        power = (1 + 2 * cols * (lat_count - 1 - lat)).astype(F32)
        enter_right = enter_right - jnp.exp(log_a * power) * leaving
        enter_left = gain * jnp.exp(log_a) * enter_left
        enter_right = gain * jnp.exp(log_a * float(LANES)) * enter_right
        tables[0] = jnp.concatenate([log_a, gain], axis=1)
        tables[1] = jnp.concatenate([enter_left, enter_right], axis=1)
        tables[2] = jnp.concatenate([left_ref[...], left_sum_ref[...]], axis=1)

    half = tables.shape[2] // 2
    lane = iota((rows, LANES), 1).astype(F32)
    triangle = triangle_ref[...]
    below = iota((rows, rows), 0) >= iota((rows, rows), 1)
    row_number = iota((8, rows), 0)
    for u in range(per_step):
        row = step * per_step + u
        place = chunk * in_chunk + row
        log_a = lane_of(tables[0], place)
        gain = lane_of(tables[0], place + half)
        from_left = lane_of(tables[1], place)
        from_right = lane_of(tables[1], place + half)
        left = lane_of(tables[2], place)[:, :rows]
        left_sum = lane_of(tables[2], place + half)[:, :rows]
        grow = jnp.exp(log_a * lane)
        shrink = jnp.exp(log_a * (-lane))
        over = jnp.exp(log_a * float(LANES))
        decay = jnp.exp(log_a)
        gain_grow, gain_shrink = gain * grow, gain * shrink
        x = column_ref[u].astype(F32)
        parts = [x[:, LANES * b : LANES * (b + 1)] for b in range(blocks)]
        scaled = jnp.concatenate(
            [jnp.concatenate([p * gain_shrink, p * gain_grow], axis=1) for p in parts], axis=0
        )
        high, low = split2(scaled)
        sums = dot_nn(high, triangle) + dot_nn(low, triangle)
        ahead = [grow * sums[rows * b : rows * (b + 1), :LANES] for b in range(blocks)]
        behind = [sums[rows * b : rows * (b + 1), LANES:] for b in range(blocks)]
        lefts, rights_in = [from_left], [from_right]
        for b in range(blocks - 1):
            end = jnp.broadcast_to(ahead[b][:, LANES - 1 :], (rows, LANES))
            lefts.append(over * lefts[-1] + decay * end)
        for b in range(blocks - 1, 0, -1):
            whole = behind[b] + scaled[rows * b : rows * (b + 1), LANES:]
            end = jnp.broadcast_to(whole[:, :1], (rows, LANES))
            rights_in.append(over * (rights_in[-1] + end))
        rights_in = rights_in[::-1]
        field = jnp.concatenate(
            [
                ahead[b] + grow * lefts[b] + shrink * (behind[b] + rights_in[b])
                for b in range(blocks)
            ],
            axis=1,
        )
        right = right_ref[pl.ds(row, 1), :]
        right_sum = right_sum_ref[pl.ds(row, 1), :]
        matrix = jnp.where(below, left_sum * right, left * right_sum)
        extra = jnp.where(row_number == 0, right, jnp.where(row_number == 1, right_sum, 0.0))
        matrix_high, matrix_low = split2(jnp.concatenate([matrix, extra], axis=0))
        field_high, field_low = split2(field)
        result = (
            dot_nn(matrix_high, field_high)
            + dot_nn(matrix_high, field_low)
            + dot_nn(matrix_low, field_high)
        )
        field_ref[u] = result[:rows]
        chain = chain_ref[pl.ds(row, 1), :]
        over_rows, echo = chain[:, 32:33], chain[:, 33:34]
        end = over_rows * result[rows : rows + 1]
        edges[0, pl.ds(row, 1), :] = end
        edges[1, pl.ds(row, 1), :] = result[rows + 1 : rows + 2] + over_rows * echo * end

    @pl.when(step == pl.num_programs(0) - 1)
    def _():
        end, returning = edges[0], edges[1]
        out_end_ref[...] = end
        for shift, ref in enumerate(send_refs, 1):
            ref[...] = jnp.where(lon + shift < lon_count, end, returning)


def product(field, left, left_sum, enter, leave, spread):
    filtered = field + left_sum * enter + left * leave
    return spread.astype(F32) * filtered.astype(BF16).astype(F32)


def wide_lane(table_ref, lane, cols):
    one = lane_of(table_ref[...], lane)
    return jnp.concatenate([one] * (cols // LANES), axis=1)


def one_product(field_ref, spread_ref, table_ref, enter_ref, leave_ref, chunk, in_chunk, row, u):
    cols = field_ref.shape[-1]
    place = chunk * in_chunk + row
    half = table_ref.shape[1] // 2
    left = wide_lane(table_ref, place, cols)
    left_sum = wide_lane(table_ref, place + half, cols)
    enter, leave = enter_ref[pl.ds(row, 1), :], leave_ref[pl.ds(row, 1), :]
    return product(field_ref[u], left, left_sum, enter, leave, spread_ref[0, u])


def first_kernel(sizes, where_ref, *refs):
    chunk, in_chunk, steps, quarters, lon_count = sizes
    got_refs = refs[: lon_count - 1]
    end_ref, chain_ref, left_ref, left_sum_ref, field_ref, spread_ref = refs[lon_count - 1 : lon_count + 5]
    enter_ref, leave_ref, table_ref, up_ref, down_ref = refs[lon_count + 5 :]
    chain = chain_ref[...]
    enter = jnp.zeros(end_ref.shape, F32)
    leave = jnp.zeros(end_ref.shape, F32)
    for shift, ref in enumerate(got_refs, 1):
        got = ref[...]
        enter = enter + chain[:, shift : shift + 1] * got
        leave = leave + chain[:, 64 + shift : 65 + shift] * got
    over, echo = chain[:, 32:33], chain[:, 33:34]
    enter_ref[...] = enter
    leave_ref[...] = over * (leave + echo * (end_ref[...] + over * enter))
    table_ref[...] = jnp.concatenate([left_ref[...], left_sum_ref[...]], axis=1)
    quarter = lax.rem(where_ref[0] + 2, quarters)
    for u in range(steps):
        value = one_product(
            field_ref, spread_ref, table_ref, enter_ref, leave_ref, chunk, in_chunk, quarter * steps + u, u
        ).astype(BF16)
        if u < steps // 2:
            up_ref[u] = value
        else:
            down_ref[u - steps // 2] = value


def second_kernel(
    sizes, where_ref, field1_ref, spread1_ref, field3_ref, spread3_ref, enter_ref, leave_ref, table_ref,
    up_ref, down_ref, out1_ref, out3_ref,
):
    chunk, in_chunk, steps, quarters = sizes
    for u in range(steps):
        for turn, field_ref, spread_ref, out_ref in (
            (1, field1_ref, spread1_ref, out1_ref),
            (3, field3_ref, spread3_ref, out3_ref),
        ):
            quarter = lax.rem(where_ref[0] + turn, quarters)
            value = one_product(
                field_ref, spread_ref, table_ref, enter_ref, leave_ref, chunk, in_chunk, quarter * steps + u, u
            )
            if turn == 1 and u < steps // 2:
                value = value + up_ref[u].astype(F32)
            if turn == 3 and u >= steps // 2:
                value = value + down_ref[u - steps // 2].astype(F32)
            out_ref[u] = value.astype(BF16)


def third_kernel(
    sizes, where_ref, field_ref, spread_ref, enter_ref, leave_ref, table_ref, got1_ref, got3_ref, *rest
):
    chunk, in_chunk, steps, scale = sizes
    out_ref = rest[-1]
    for u in range(steps):
        value = one_product(
            field_ref, spread_ref, table_ref, enter_ref, leave_ref, chunk, in_chunk, where_ref[0] * steps + u, u
        )
        out_ref[u] = (value + got1_ref[u].astype(F32) + got3_ref[u].astype(F32)) * scale


def whole(shape):
    return pl.BlockSpec(shape, lambda *_: (0,) * len(shape))


def smem():
    return pl.BlockSpec(memory_space=pltpu.SMEM)


def call(kernel, name, inputs, in_specs, outputs, out_specs, scratch=(), grid=(1,), aliases=None, cost=None):
    return pl.pallas_call(
        kernel,
        out_shape=outputs,
        grid_spec=pltpu.PrefetchScalarGridSpec(
            num_scalar_prefetch=1,
            grid=grid,
            in_specs=in_specs,
            out_specs=out_specs,
            scratch_shapes=list(scratch),
        ),
        input_output_aliases=aliases or {},
        compiler_params=pltpu.CompilerParams(vmem_limit_bytes=VMEM_LIMIT),
        cost_estimate=cost,
        name=name,
    )(*inputs)


def cost(flops, data):
    return pl.CostEstimate(flops=flops, bytes_accessed=data, transcendentals=0)


def triangle_table():
    at = np.arange(LANES)
    table = np.zeros((2 * LANES, 2 * LANES), np.float32)
    table[:LANES, :LANES] = at[:, None] <= at[None, :]
    table[LANES:, LANES:] = at[:, None] > at[None, :]
    return jnp.asarray(table, BF16)


def ring(axis, shift):
    count = lax.axis_size(axis)
    return [(i, (i + shift) % count) for i in range(count)]


def per_device(control, perturbation, slab_levels, member_group, band_width, zonal_rate, meridional_rate):
    _, levels, rows, cols = control.shape
    quarters, lat_count, lon_count = (lax.axis_size(a) for a in ("mem", "lat", "lon"))
    steps = levels // (CHUNKS * quarters)
    in_chunk = steps * quarters
    total_rows = zonal_rate.shape[1]
    where = jnp.stack([lax.axis_index(a) for a in ("mem", "lat", "lon")]).astype(jnp.int32)
    sds = jax.ShapeDtypeStruct
    table = sds((rows, levels), F32)
    table_spec = pl.BlockSpec((ROW_GROUP, levels), lambda g, _: (g, 0))

    column, decay, gain, end, *sends = call(
        functools.partial(column_kernel, (levels, rows, cols, quarters, lat_count)),
        "vertical_columns",
        (where, slab_levels, member_group, band_width, control, zonal_rate),
        [
            smem(), smem(), smem(),
            pl.BlockSpec((1, levels, ROW_GROUP, cols), lambda g, _: (0, 0, g, 0)),
            whole(zonal_rate.shape),
        ],
        (sds((levels, rows, cols), BF16), table, table, table, table, table, table),
        (
            pl.BlockSpec((levels, ROW_GROUP, cols), lambda g, _: (0, g, 0)),
            whole((rows, levels)), whole((rows, levels)),
            table_spec, table_spec, table_spec, table_spec,
        ),
        scratch=[pltpu.VMEM((levels * 8, levels * 8), BF16), pltpu.VMEM((rows, levels), F32)],
        grid=(rows // ROW_GROUP,),
        cost=cost(2 * 512 * 512 * 384 * 12, 2 * levels * rows * cols * 2),
    )
    got = [lax.ppermute(s, "lat", ring("lat", i + 1)) for i, s in enumerate(sends)]
    left, left_sum, right, right_sum, chain = call(
        functools.partial(row_kernel, (levels, rows, quarters, lon_count)),
        "row_terms",
        (where, slab_levels, meridional_rate),
        [smem(), whole(meridional_rate.shape)],
        (table, table, sds((levels, rows), F32), sds((levels, rows), F32), sds((levels, LANES), F32)),
        (
            whole((rows, levels)), whole((rows, levels)),
            whole((levels, rows)), whole((levels, rows)), whole((levels, LANES)),
        ),
        cost=cost(2 * 3 * 64 * 768 * 768 * 2, 1 << 20),
    )

    triangle = triangle_table()
    scale = 1.0 / math.sqrt(control.shape[0] * quarters - 1)
    plane = rows * cols
    row_spec = pl.BlockSpec((in_chunk, cols), lambda *_: (0, 0))
    fields, ends, far = [], [], []
    for c in range(CHUNKS):
        by_place = lambda width: pl.BlockSpec((in_chunk, width), lambda g, _, c=c: (c, 0))
        field, out_end, *out_sends = call(
            functools.partial(field_kernel, (rows, cols, c, in_chunk, steps, lat_count, lon_count)),
            "zonal_rows",
            (where, column, decay, gain, end, *got, left, left_sum, right, right_sum, chain, triangle),
            [pl.BlockSpec((steps, rows, cols), lambda g, _, c=c: (c * quarters + g, 0, 0))]
            + [whole((rows, levels))] * 8
            + [by_place(rows), by_place(rows), by_place(LANES), whole(triangle.shape)],
            (sds((in_chunk, rows, cols), F32),) + (sds((in_chunk, cols), F32),) * lon_count,
            (pl.BlockSpec((steps, rows, cols), lambda g, _: (g, 0, 0)),) + (row_spec,) * lon_count,
            scratch=[
                pltpu.VMEM((3, rows, 2 * levels), F32),
                pltpu.VMEM((8, LANES), F32),
                pltpu.VMEM((2, in_chunk, cols), F32),
            ],
            grid=(quarters,),
            cost=cost(in_chunk * plane * 2 * 1024, in_chunk * plane * 6),
        )
        fields.append(field)
        ends.append(out_end)
        far.append([lax.ppermute(s, "lon", ring("lon", i + 1)) for i, s in enumerate(out_sends)])

    quarter_field = lambda turn: pl.BlockSpec(
        (steps, rows, cols), lambda g, w: (lax.rem(w[0] + turn, quarters), 0, 0)
    )
    quarter_spread = lambda turn, c: pl.BlockSpec(
        (1, steps, rows, cols), lambda g, w: (0, lax.rem(w[0] + turn, quarters) * CHUNKS + c, 0, 0)
    )
    piece = sds((steps, rows, cols), BF16)
    half_piece = sds((steps // 2, rows, cols), BF16)
    table_wide = sds((rows, 2 * levels), F32)
    row_pair = (row_spec, row_spec, whole((rows, 2 * levels)))
    arrived = []
    for c in range(CHUNKS):
        enter, leave, lanes, up, down = call(
            functools.partial(first_kernel, (c, in_chunk, steps, quarters, lon_count)),
            "first_products",
            (where, *far[c], ends[c], chain, left, left_sum, fields[c], perturbation),
            [row_spec] * lon_count
            + [
                pl.BlockSpec((in_chunk, LANES), lambda g, _, c=c: (c, 0)),
                whole((rows, levels)), whole((rows, levels)),
                quarter_field(2), quarter_spread(2, c),
            ],
            (sds((in_chunk, cols), F32), sds((in_chunk, cols), F32), table_wide, half_piece, half_piece),
            row_pair + (whole(half_piece.shape), whole(half_piece.shape)),
            cost=cost(steps * plane * 8, steps * plane * 8),
        )
        up = lax.ppermute(up, "mem", ring("mem", 1))
        down = lax.ppermute(down, "mem", ring("mem", -1))
        arrived.append((enter, leave, lanes, up, down))
    result = None
    gathered = []
    for c in range(CHUNKS):
        enter, leave, lanes, up, down = arrived[c]
        out1, out3 = call(
            functools.partial(second_kernel, (c, in_chunk, steps, quarters)),
            "second_products",
            (where, fields[c], perturbation, fields[c], perturbation, enter, leave, lanes, up, down),
            [quarter_field(1), quarter_spread(1, c), quarter_field(3), quarter_spread(3, c)]
            + list(row_pair)
            + [whole(half_piece.shape), whole(half_piece.shape)],
            (piece, piece),
            (whole(piece.shape), whole(piece.shape)),
            cost=cost(2 * steps * plane * 8, 2 * steps * plane * 8),
        )
        gathered.append(
            (lax.ppermute(out1, "mem", ring("mem", 1)), lax.ppermute(out3, "mem", ring("mem", -1)))
        )
    for c in range(CHUNKS):
        enter, leave, lanes, _, _ = arrived[c]
        extra = () if result is None else (result,)
        result = call(
            functools.partial(third_kernel, (c, in_chunk, steps, scale)),
            "third_products",
            (where, fields[c], perturbation, enter, leave, lanes, *gathered[c], *extra),
            [quarter_field(0), quarter_spread(0, c), *row_pair, whole(piece.shape), whole(piece.shape)]
            + [pl.BlockSpec(memory_space=pl.ANY)] * len(extra),
            sds((levels // quarters, rows, cols), F32),
            pl.BlockSpec((steps, rows, cols), lambda g, _, c=c: (c, 0, 0)),
            aliases={8: 0} if extra else None,
            cost=cost(steps * plane * 8, steps * plane * 14),
        )
    return result


def solution(mesh):
    return jax.shard_map(
        per_device,
        mesh=mesh,
        in_specs=(
            P("mem", None, "lon", "lat"),
            P("mem", None, "lon", "lat"),
            P(),
            P("mem"),
            P(),
            P(),
            P(),
        ),
        out_specs=P("mem", "lon", "lat"),
        check_vma=False,
    )
```

time: 631 us -> 210 us (0.33); the launches traced: 619 us -> 209 us
  waiting for transfers between devices: 266 us -> 29.1 us
  local copies, waits for them, and re-layouts: 143 us -> 4.39 us
  other arithmetic: 107 us -> 0.08 us
  Pallas kernels: 0 us -> 97.3 us
  matrix products: 68.8 us -> 0 us
  starting transfers between devices: 17.4 us -> 77.3 us
  between operations: 15.3 us -> 0.96 us
    all_to_all x2 -> x0, waiting for transfers between devices: 174 us -> none  [the longest x1 94.5 us: through_slabs(): lax.all_to_all(returning, ('lat', 'lon'), split_axis=1, concat_axis=1, ti...]
    pallas_call x0 -> x18, Pallas kernels: none -> 97.3 us  [call(): pl.pallas_call(kernel, out_shape=outputs, grid_spec=pltpu.PrefetchScalarG...]
    reduce_scatter x1 -> x0, waiting for transfers between devices: 91.8 us -> none  [per_device(): return lax.psum_scatter(local_sum, 'mem', scatter_dimension=0, tiled=True)]
    ppermute x0 -> x47, starting transfers between devices: none -> 77.3 us  [the longest x28 50.8 us: per_device(): lax.ppermute(s, 'lon', ring('lon', i + 1))]
    dot_general x9 -> x0, matrix products: 68.8 us -> none  [the longest x4 34.1 us: along_block(): return jnp.matmul(values, triangle, precision=HIGHEST_PRECISION)]
    convert_element_type x5 -> x0, local copies, waits for them, and re-layouts: 57.5 us -> none  [the longest x2 32.7 us: one_member(): member_field[None].astype(jnp.float32)]
    add x37 -> x0, other arithmetic: 38.1 us -> none  [the longest x36 25.5 us: advance(): return (element[1] * incoming + element[0], incoming)]
    mul x5 -> x0, other arithmetic: 34.2 us -> none  [the longest x2 23.5 us: blocked_recursion(): growth * along_block(values * jnp.exp(-cumulative), triangle, trailing)]
  transfers between devices with their start and end apart: 3 -> 47, of which waited for: 3 -> 5; matrix products, arithmetic and copies ran while one was open for 3% -> 0% of each run, Pallas kernels for 0% -> 25%
where the time goes in v1:
time: 210 us; the launch traced here: 209 us
  Pallas kernels  97.3 us (46%)
  starting transfers between devices  77.3 us (37%)
  waiting for transfers between devices  29.1 us (14%)
  local copies, waits for them, and re-layouts  4.39 us (2%)
    pallas_call x18, Pallas kernels, call(): pl.pallas_call(kernel, out_shape=outputs, grid_spec=pltpu.PrefetchScalarG...  97.3 us
    ppermute x28, starting transfers between devices, per_device(): lax.ppermute(s, 'lon', ring('lon', i + 1))  50.8 us
    ppermute x28, waiting for transfers between devices, per_device(): lax.ppermute(s, 'lon', ring('lon', i + 1))  22.3 us
    ppermute x4, starting transfers between devices, per_device(): down = lax.ppermute(down, 'mem', ring('mem', -1))  11.1 us
    ppermute x4, starting transfers between devices, per_device(): lax.ppermute(out3, 'mem', ring('mem', -1))  6.92 us
    ppermute x4, waiting for transfers between devices, per_device(): up = lax.ppermute(up, 'mem', ring('mem', 1))  6.76 us
    unnamed x12, local copies, waits for them, and re-layouts  4.39 us
  transfers between devices with their start and end apart: 47, of which 5 were waited for; matrix products, arithmetic and copies ran while one was open for 0% of the time, Pallas kernels for 25%

profile of v1, /device:TPU:0, one launch (start us, length us, event | category | flops | bytes accessed | tf_op | source)
XLA Modules:
  0.0 209.1 jit_solution(18178434207106661660)
XLA Ops:
  2.9 34.1 %vertical_columns.1 = (bf16[64,96,384]{2,1,0:T(8,128)(2,1)S(1)}, f32[96,64]{1,0:T(8,128)S(1)}, f32[96,64]{1,0:T(8,128)S(1)}, f32[96,64]{1,0:T(8,128)S(1)}, f32[9...) custom-call(s32[3]{0:T(128)S(1)} %pad_add_fusion.where_ref, s32[32]{0:T(128)S(1)} %copy-done.5, ...), custom_call_target="tpu_custom_call" | custom-call | flops 2415919104 | bytes 9437184 | tf_op jit(solution)/shard_map/vertical_columns/pallas_call | solution.py:411
  37.0 2.2 %copy-done = bf16[64,96,384]{2,1,0:T(8,128)(2,1)} copy-done((bf16[64,96,384]{2,1,0:T(8,128)(2,1)}, bf16[64,96,384]{2,1,0:T(8,128)(2,1)S(1)}, u32[]{:S(2)}) %copy-start) | copy-done | bytes 4718616
  39.2 2.0 collective-permute-start.1
  42.7 3.3 %row_terms.1 = (f32[96,64]{1,0:T(8,128)S(1)}, f32[96,64]{1,0:T(8,128)S(1)}, f32[64,96]{1,0:T(8,128)S(1)}, f32[64,96]{1,0:T(8,128)S(1)}, f32[64,128]{1,0:T(8,128)S(1)}) custom-call(s32[3]{0:T(128)S(1)} %pad_add_fusion.where_ref, s32[32]{0:T(128)S(1)} %copy-done.5, f32[32,768]{1,0:T(8,128)S(1)} %copy-done.3), custom_call_target="tpu_custom_call" | custom-call | flops 452984832 | bytes 1048576 | tf_op jit(solution)/shard_map/row_terms/pallas_call | solution.py:411
  46.0 8.4 %zonal_rows.7 = (f32[16,96,384]{2,1,0:T(8,128)S(1)}, f32[16,384]{1,0:T(8,128)S(1)}, f32[16,384]{1,0:T(8,128)S(1)}, f32[16,384]{1,0:T(8,128)S(1)}, f32[16,384]{1,...) custom-call(s32[3]{0:T(128)S(1)} %pad_add_fusion.where_ref, ...), custom_call_target="tpu_custom_call" | custom-call | flops 1207959552 | bytes 3538944 | tf_op jit(solution)/shard_map/zonal_rows/pallas_call | solution.py:411
  54.4 3.7 %collective-permute-start.36 = (f32[16,384]{1,0:T(8,128)S(1)}, f32[16,384]{1,0:T(8,128)S(1)}, u32[]{:S(2)}, u32[]{:S(2)}) collective-permute-start(f32[16,384]{1,0:T(8,128)S(1)} %get-tuple-element.142), channel_id=1, source_target_pairs={{0,1},{1,2},{2,3},{3,4},{4,5},{5,6},{6,7},{7,0},{8,9},{9,10},{10,1... | collective-permute-start | bytes 73736 | tf_op jit(solution)/shard_map/ppermute | solution.py:515
  59.5 1.5 collective-permute-start.38
  61.0 2.0 collective-permute-start.39
  63.0 5.2 %collective-permute-start.40 = (f32[16,384]{1,0:T(8,128)S(1)}, f32[16,384]{1,0:T(8,128)S(1)}, u32[]{:S(2)}, u32[]{:S(2)}) collective-permute-start(f32[16,384]{1,0:T(8,128)S(1)} %get-tuple-element.146), channel_id=1, source_target_pairs={{0,5},{1,6},{2,7},{3,0},{4,1},{5,2},{6,3},{7,4},{8,13},{9,14},{10,... | collective-permute-start | bytes 73736 | tf_op jit(solution)/shard_map/ppermute | solution.py:515
  68.2 8.4 %zonal_rows.6 = (f32[16,96,384]{2,1,0:T(8,128)S(1)}, f32[16,384]{1,0:T(8,128)S(1)}, f32[16,384]{1,0:T(8,128)S(1)}, f32[16,384]{1,0:T(8,128)S(1)}, f32[16,384]{1,...) custom-call(s32[3]{0:T(128)S(1)} %pad_add_fusion.where_ref, ...), custom_call_target="tpu_custom_call" | custom-call | flops 1207959552 | bytes 3538944 | tf_op jit(solution)/shard_map/zonal_rows/pallas_call | solution.py:411
  78.1 3.5 %collective-permute-start.25 = (f32[16,384]{1,0:T(8,128)S(1)}, f32[16,384]{1,0:T(8,128)S(1)}, u32[]{:S(2)}, u32[]{:S(2)}) collective-permute-start(f32[16,384]{1,0:T(8,128)S(1)} %get-tuple-element.126), channel_id=1, source_target_pairs={{0,1},{1,2},{2,3},{3,4},{4,5},{5,6},{6,7},{7,0},{8,9},{9,10},{10,1... | collective-permute-start | bytes 73736 | tf_op jit(solution)/shard_map/ppermute | solution.py:515
  82.4 8.4 %zonal_rows.5 = (f32[16,96,384]{2,1,0:T(8,128)S(1)}, f32[16,384]{1,0:T(8,128)S(1)}, f32[16,384]{1,0:T(8,128)S(1)}, f32[16,384]{1,0:T(8,128)S(1)}, f32[16,384]{1,...) custom-call(s32[3]{0:T(128)S(1)} %pad_add_fusion.where_ref, ...), custom_call_target="tpu_custom_call" | custom-call | flops 1207959552 | bytes 3538944 | tf_op jit(solution)/shard_map/zonal_rows/pallas_call | solution.py:411
  90.8 3.7 %collective-permute-start.28 = (f32[16,384]{1,0:T(8,128)S(1)}, f32[16,384]{1,0:T(8,128)S(1)}, u32[]{:S(2)}, u32[]{:S(2)}) collective-permute-start(f32[16,384]{1,0:T(8,128)S(1)} %get-tuple-element.129), channel_id=1, source_target_pairs={{0,4},{1,5},{2,6},{3,7},{4,0},{5,1},{6,2},{7,3},{8,12},{9,13},{10,... | collective-permute-start | bytes 73736 | tf_op jit(solution)/shard_map/ppermute | solution.py:515
  94.5 3.1 %collective-permute-start.29 = (f32[16,384]{1,0:T(8,128)S(1)}, f32[16,384]{1,0:T(8,128)S(1)}, u32[]{:S(2)}, u32[]{:S(2)}) collective-permute-start(f32[16,384]{1,0:T(8,128)S(1)} %get-tuple-element.130), channel_id=1, source_target_pairs={{0,5},{1,6},{2,7},{3,0},{4,1},{5,2},{6,3},{7,4},{8,13},{9,14},{10,... | collective-permute-start | bytes 73736 | tf_op jit(solution)/shard_map/ppermute | solution.py:515
  97.6 1.8 collective-permute-start.30
  99.5 3.5 %collective-permute-start.14 = (f32[16,384]{1,0:T(8,128)S(1)}, f32[16,384]{1,0:T(8,128)S(1)}, u32[]{:S(2)}, u32[]{:S(2)}) collective-permute-start(f32[16,384]{1,0:T(8,128)S(1)} %get-tuple-element.110), channel_id=1, source_target_pairs={{0,1},{1,2},{2,3},{3,4},{4,5},{5,6},{6,7},{7,0},{8,9},{9,10},{10,1... | collective-permute-start | bytes 73736 | tf_op jit(solution)/shard_map/ppermute | solution.py:515
  103.8 1.8 collective-permute-start.16
  105.5 3.2 %collective-permute-start.17 = (f32[16,384]{1,0:T(8,128)S(1)}, f32[16,384]{1,0:T(8,128)S(1)}, u32[]{:S(2)}, u32[]{:S(2)}) collective-permute-start(f32[16,384]{1,0:T(8,128)S(1)} %get-tuple-element.113), channel_id=1, source_target_pairs={{0,4},{1,5},{2,6},{3,7},{4,0},{5,1},{6,2},{7,3},{8,12},{9,13},{10,... | collective-permute-start | bytes 73736 | tf_op jit(solution)/shard_map/ppermute | solution.py:515
  108.7 3.1 %collective-permute-start.18 = (f32[16,384]{1,0:T(8,128)S(1)}, f32[16,384]{1,0:T(8,128)S(1)}, u32[]{:S(2)}, u32[]{:S(2)}) collective-permute-start(f32[16,384]{1,0:T(8,128)S(1)} %get-tuple-element.114), channel_id=1, source_target_pairs={{0,5},{1,6},{2,7},{3,0},{4,1},{5,2},{6,3},{7,4},{8,13},{9,14},{10,... | collective-permute-start | bytes 73736 | tf_op jit(solution)/shard_map/ppermute | solution.py:515
  111.8 2.6 %collective-permute-start.19 = (f32[16,384]{1,0:T(8,128)S(1)}, f32[16,384]{1,0:T(8,128)S(1)}, u32[]{:S(2)}, u32[]{:S(2)}) collective-permute-start(f32[16,384]{1,0:T(8,128)S(1)} %get-tuple-element.115), channel_id=1, source_target_pairs={{0,6},{1,7},{2,0},{3,1},{4,2},{5,3},{6,4},{7,5},{8,14},{9,15},{10,... | collective-permute-start | bytes 73736 | tf_op jit(solution)/shard_map/ppermute | solution.py:515
  114.3 1.9 first_products.7
  116.2 1.9 first_products.6
  118.4 1.6 collective-permute-start.43
  120.0 1.7 collective-permute-start.44
  122.1 2.9 %collective-permute-start.33 = (bf16[2,96,384]{2,1,0:T(8,128)(2,1)S(1)}, bf16[2,96,384]{2,1,0:T(8,128)(2,1)S(1)}, u32[]{:S(2)}, u32[]{:S(2)}) collective-permute-start(bf16[2,96,384]{2,1,0:T(8,128)(2,1)S(1)} %get-tuple-element.138), channel_id=1, source_target_pairs={{0,96},{32,0},{64,32},{96,64},{1,97},{33,1},{65,33},{97,65},{2,98}... | collective-permute-start | bytes 442376 | tf_op jit(solution)/shard_map/ppermute | solution.py:544
  124.9 8.4 %zonal_rows.4 = (f32[16,96,384]{2,1,0:T(8,128)S(1)}, f32[16,384]{1,0:T(8,128)S(1)}, f32[16,384]{1,0:T(8,128)S(1)}, f32[16,384]{1,0:T(8,128)S(1)}, f32[16,384]{1,...) custom-call(s32[3]{0:T(128)S(1)} %pad_add_fusion.where_ref, ...), custom_call_target="tpu_custom_call" | custom-call | flops 1207959552 | bytes 3538944 | tf_op jit(solution)/shard_map/zonal_rows/pallas_call | solution.py:411
  133.3 3.3 %collective-permute-start.3 = (f32[16,384]{1,0:T(8,128)S(1)}, f32[16,384]{1,0:T(8,128)S(1)}, u32[]{:S(2)}, u32[]{:S(2)}) collective-permute-start(f32[16,384]{1,0:T(8,128)S(1)} %get-tuple-element.94), channel_id=1, source_target_pairs={{0,1},{1,2},{2,3},{3,4},{4,5},{5,6},{6,7},{7,0},{8,9},{9,10},{10,1... | collective-permute-start | bytes 73736 | tf_op jit(solution)/shard_map/ppermute | solution.py:515
  136.7 4.2 %collective-permute-done.3.refs_0_ = f32[16,384]{1,0:T(8,128)S(1)} collective-permute-done((f32[16,384]{1,0:T(8,128)S(1)}, f32[16,384]{1,0:T(8,128)S(1)}, u32[]{:S(2)}, u32[]{:S(2)}) %collective-permute-start.3) | collective-permute-done | bytes 24608 | tf_op jit(solution)/shard_map/ppermute | solution.py:515
  140.8 5.0 %collective-permute-done.4.refs_1_ = f32[16,384]{1,0:T(8,128)S(1)} collective-permute-done((f32[16,384]{1,0:T(8,128)S(1)}, f32[16,384]{1,0:T(8,128)S(1)}, u32[]{:S(2)}, u32[]{:S(2)}) %collective-permute-start.4) | collective-permute-done | bytes 24608 | tf_op jit(solution)/shard_map/ppermute | solution.py:515
  145.9 7.7 %collective-permute-done.5.refs_2_ = f32[16,384]{1,0:T(8,128)S(1)} collective-permute-done((f32[16,384]{1,0:T(8,128)S(1)}, f32[16,384]{1,0:T(8,128)S(1)}, u32[]{:S(2)}, u32[]{:S(2)}) %collective-permute-start.5) | collective-permute-done | bytes 24608 | tf_op jit(solution)/shard_map/ppermute | solution.py:515
  153.6 5.3 %collective-permute-done.6.refs_3_ = f32[16,384]{1,0:T(8,128)S(1)} collective-permute-done((f32[16,384]{1,0:T(8,128)S(1)}, f32[16,384]{1,0:T(8,128)S(1)}, u32[]{:S(2)}, u32[]{:S(2)}) %collective-permute-start.6) | collective-permute-done | bytes 24608 | tf_op jit(solution)/shard_map/ppermute | solution.py:515
  160.1 2.9 %collective-permute-start.9 = (f32[16,384]{1,0:T(8,128)S(1)}, f32[16,384]{1,0:T(8,128)S(1)}, u32[]{:S(2)}, u32[]{:S(2)}) collective-permute-start(f32[16,384]{1,0:T(8,128)S(1)} %get-tuple-element.100), channel_id=1, source_target_pairs={{0,7},{1,0},{2,1},{3,2},{4,3},{5,4},{6,5},{7,6},{8,15},{9,8},{10,9... | collective-permute-start | bytes 73736 | tf_op jit(solution)/shard_map/ppermute | solution.py:515
  163.0 1.9 first_products.5
  165.0 3.2 %collective-permute-start.22 = (bf16[2,96,384]{2,1,0:T(8,128)(2,1)S(1)}, bf16[2,96,384]{2,1,0:T(8,128)(2,1)S(1)}, u32[]{:S(2)}, u32[]{:S(2)}) collective-permute-start(bf16[2,96,384]{2,1,0:T(8,128)(2,1)S(1)} %get-tuple-element.122), channel_id=1, source_target_pairs={{0,96},{32,0},{64,32},{96,64},{1,97},{33,1},{65,33},{97,65},{2,98}... | collective-permute-start | bytes 442376 | tf_op jit(solution)/shard_map/ppermute | solution.py:544
  168.2 2.1 second_products.7
  170.3 2.1 second_products.6
  172.5 3.2 %collective-permute-start.46 = (bf16[4,96,384]{2,1,0:T(8,128)(2,1)S(1)}, bf16[4,96,384]{2,1,0:T(8,128)(2,1)S(1)}, u32[]{:S(2)}, u32[]{:S(2)}) collective-permute-start(bf16[4,96,384]{2,1,0:T(8,128)(2,1)S(1)} %get-tuple-element.156), channel_id=1, source_target_pairs={{0,96},{32,0},{64,32},{96,64},{1,97},{33,1},{65,33},{97,65},{2,98}... | collective-permute-start | bytes 884744 | tf_op jit(solution)/shard_map/ppermute | solution.py:562
  175.7 1.9 first_products.4
  177.7 3.3 %collective-permute-start.11 = (bf16[2,96,384]{2,1,0:T(8,128)(2,1)S(1)}, bf16[2,96,384]{2,1,0:T(8,128)(2,1)S(1)}, u32[]{:S(2)}, u32[]{:S(2)}) collective-permute-start(bf16[2,96,384]{2,1,0:T(8,128)(2,1)S(1)} %get-tuple-element.106), channel_id=1, source_target_pairs={{0,96},{32,0},{64,32},{96,64},{1,97},{33,1},{65,33},{97,65},{2,98}... | collective-permute-start | bytes 442376 | tf_op jit(solution)/shard_map/ppermute | solution.py:544
  181.0 2.1 second_products.5
  183.0 6.8 %collective-permute-done.10.up_ref = bf16[2,96,384]{2,1,0:T(8,128)(2,1)S(1)} collective-permute-done((bf16[2,96,384]{2,1,0:T(8,128)(2,1)S(1)}, bf16[2,96,384]{2,1,0:T(8,128)(2,1)S(1)}, u32[]{:S(2)}, u32[]{:S(2)}) %collective-permute-start.10) | collective-permute-done | bytes 147488 | tf_op jit(solution)/shard_map/ppermute | solution.py:543
  189.8 2.0 collective-permute-start.23
  191.8 2.1 second_products.4
  196.0 2.4 %collective-permute-start.13 = (bf16[4,96,384]{2,1,0:T(8,128)(2,1)S(1)}, bf16[4,96,384]{2,1,0:T(8,128)(2,1)S(1)}, u32[]{:S(2)}, u32[]{:S(2)}) collective-permute-start(bf16[4,96,384]{2,1,0:T(8,128)(2,1)S(1)} %get-tuple-element.108), channel_id=1, source_target_pairs={{0,96},{32,0},{64,32},{96,64},{1,97},{33,1},{65,33},{97,65},{2,98}... | collective-permute-start | bytes 884744 | tf_op jit(solution)/shard_map/ppermute | solution.py:562
  198.4 2.7 %third_products.4.rest_0_ = f32[16,96,384]{2,1,0:T(8,128)} custom-call(s32[3]{0:T(128)S(1)} %pad_add_fusion.where_ref, f32[16,96,384]{2,1,0:T(8,128)S(1)} %get-tuple-element.141.refs_11_.field1_ref.field3_ref.field_ref, bf16[1,64,96,384]{3,2,1,0:T(8,128)(2,1)} %spread_ref.7, f32[16,384]{1,0:T(8,128)S(1)} %get-tuple-element.150.enter_ref, ...), custom_call_target="tpu_custom_call" | custom-call | flops 1179648 | bytes 2064384 | tf_op jit(solution)/shard_map/third_products/pallas_call | solution.py:411
  201.1 2.7 %third_products.5.rest_0_ = f32[16,96,384]{2,1,0:T(8,128)} custom-call(s32[3]{0:T(128)S(1)} %pad_add_fusion.where_ref, f32[16,96,384]{2,1,0:T(8,128)S(1)} %get-tuple-element.125.refs_11_.field1_ref.field3_ref.field_ref, bf16[1,64,96,384]{3,2,1,0:T(8,128)(2,1)} %spread_ref.7, ...), custom_call_target="tpu_custom_call", output_to_operand_aliasing={{}: (8, {})} | custom-call | flops 1179648 | bytes 2064384 | tf_op jit(solution)/shard_map/third_products/pallas_call | solution.py:411
  203.8 2.7 %third_products.6.rest_0_ = f32[16,96,384]{2,1,0:T(8,128)} custom-call(s32[3]{0:T(128)S(1)} %pad_add_fusion.where_ref, f32[16,96,384]{2,1,0:T(8,128)S(1)} %get-tuple-element.109.refs_11_.field1_ref.field3_ref.field_ref, bf16[1,64,96,384]{3,2,1,0:T(8,128)(2,1)} %spread_ref.7, ...), custom_call_target="tpu_custom_call", output_to_operand_aliasing={{}: (8, {})} | custom-call | flops 1179648 | bytes 2064384 | tf_op jit(solution)/shard_map/third_products/pallas_call | solution.py:411
  206.5 2.7 %third_products.7 = f32[16,96,384]{2,1,0:T(8,128)} custom-call(s32[3]{0:T(128)S(1)} %pad_add_fusion.where_ref, f32[16,96,384]{2,1,0:T(8,128)S(1)} %get-tuple-element.93.refs_11_.field1_ref.field3_ref.field_ref, bf16[1,64,96,384]{3,2,1,0:T(8,128)(2,1)} %spread_ref.7, f32[16,384]{1,0:T(8,128)S(1)} %get-tuple-element.102.enter_ref, ...), custom_call_target="tpu_custom_call", output_to_operand_aliasing={{}: (8, {})} | custom-call | flops 1179648 | bytes 2064384 | tf_op jit(solution)/shard_map/third_products/pallas_call | solution.py:411
  (77 shorter events, 12.7 us)
Async XLA Ops:
  2.9 43.0 %copy-start.1 = (bf16[256,256]{1,0:T(8,128)(2,1)S(1)}, bf16[256,256]{1,0:T(8,128)(2,1)}, u32[]{:S(2)}) copy-start(bf16[256,256]{1,0:T(8,128)(2,1)} %constant.14.clone.triangle_ref) | copy-start | bytes 393220
  39.2 6.7 %collective-permute-start = (f32[96,64]{1,0:T(8,128)S(1)}, f32[96,64]{1,0:T(8,128)S(1)}, u32[]{:S(2)}, u32[]{:S(2)}) collective-permute-start(f32[96,64]{1,0:T(8,128)S(1)} %get-tuple-element.85), channel_id=1, source_target_pairs={{0,8},{8,16},{16,24},{24,0},{1,9},{9,17},{17,25},{25,1},{2,10},{10... | collective-permute-start | bytes 73736 | tf_op jit(solution)/shard_map/ppermute | solution.py:475
  39.2 6.8 %collective-permute-start.1 = (f32[96,64]{1,0:T(8,128)S(1)}, f32[96,64]{1,0:T(8,128)S(1)}, u32[]{:S(2)}, u32[]{:S(2)}) collective-permute-start(f32[96,64]{1,0:T(8,128)S(1)} %get-tuple-element.86), channel_id=1, source_target_pairs={{0,16},{8,24},{16,0},{24,8},{1,17},{9,25},{17,1},{25,9},{2,18},{10... | collective-permute-start | bytes 73736 | tf_op jit(solution)/shard_map/ppermute | solution.py:475
  41.2 4.7 %collective-permute-start.2 = (f32[96,64]{1,0:T(8,128)S(1)}, f32[96,64]{1,0:T(8,128)S(1)}, u32[]{:S(2)}, u32[]{:S(2)}) collective-permute-start(f32[96,64]{1,0:T(8,128)S(1)} %get-tuple-element.87), channel_id=1, source_target_pairs={{0,24},{8,0},{16,8},{24,16},{1,25},{9,1},{17,9},{25,17},{2,26},{10... | collective-permute-start | bytes 73736 | tf_op jit(solution)/shard_map/ppermute | solution.py:475
  54.4 22.2 %collective-permute-start.36 = (f32[16,384]{1,0:T(8,128)S(1)}, f32[16,384]{1,0:T(8,128)S(1)}, u32[]{:S(2)}, u32[]{:S(2)}) collective-permute-start(f32[16,384]{1,0:T(8,128)S(1)} %get-tuple-element.142), channel_id=1, source_target_pairs={{0,1},{1,2},{2,3},{3,4},{4,5},{5,6},{6,7},{7,0},{8,9},{9,10},{10,1... | collective-permute-start | bytes 73736 | tf_op jit(solution)/shard_map/ppermute | solution.py:515
  58.0 20.1 %collective-permute-start.37 = (f32[16,384]{1,0:T(8,128)S(1)}, f32[16,384]{1,0:T(8,128)S(1)}, u32[]{:S(2)}, u32[]{:S(2)}) collective-permute-start(f32[16,384]{1,0:T(8,128)S(1)} %get-tuple-element.143), channel_id=1, source_target_pairs={{0,2},{1,3},{2,4},{3,5},{4,6},{5,7},{6,0},{7,1},{8,10},{9,11},{10,... | collective-permute-start | bytes 73736 | tf_op jit(solution)/shard_map/ppermute | solution.py:515
  59.5 18.6 %collective-permute-start.38 = (f32[16,384]{1,0:T(8,128)S(1)}, f32[16,384]{1,0:T(8,128)S(1)}, u32[]{:S(2)}, u32[]{:S(2)}) collective-permute-start(f32[16,384]{1,0:T(8,128)S(1)} %get-tuple-element.144), channel_id=1, source_target_pairs={{0,3},{1,4},{2,5},{3,6},{4,7},{5,0},{6,1},{7,2},{8,11},{9,12},{10,... | collective-permute-start | bytes 73736 | tf_op jit(solution)/shard_map/ppermute | solution.py:515
  61.0 20.6 %collective-permute-start.39 = (f32[16,384]{1,0:T(8,128)S(1)}, f32[16,384]{1,0:T(8,128)S(1)}, u32[]{:S(2)}, u32[]{:S(2)}) collective-permute-start(f32[16,384]{1,0:T(8,128)S(1)} %get-tuple-element.145), channel_id=1, source_target_pairs={{0,4},{1,5},{2,6},{3,7},{4,0},{5,1},{6,2},{7,3},{8,12},{9,13},{10,... | collective-permute-start | bytes 73736 | tf_op jit(solution)/shard_map/ppermute | solution.py:515
  63.0 19.2 %collective-permute-start.40 = (f32[16,384]{1,0:T(8,128)S(1)}, f32[16,384]{1,0:T(8,128)S(1)}, u32[]{:S(2)}, u32[]{:S(2)}) collective-permute-start(f32[16,384]{1,0:T(8,128)S(1)} %get-tuple-element.146), channel_id=1, source_target_pairs={{0,5},{1,6},{2,7},{3,0},{4,1},{5,2},{6,3},{7,4},{8,13},{9,14},{10,... | collective-permute-start | bytes 73736 | tf_op jit(solution)/shard_map/ppermute | solution.py:515
  76.6 14.2 %collective-permute-start.41 = (f32[16,384]{1,0:T(8,128)S(1)}, f32[16,384]{1,0:T(8,128)S(1)}, u32[]{:S(2)}, u32[]{:S(2)}) collective-permute-start(f32[16,384]{1,0:T(8,128)S(1)} %get-tuple-element.147), channel_id=1, source_target_pairs={{0,6},{1,7},{2,0},{3,1},{4,2},{5,3},{6,4},{7,5},{8,14},{9,15},{10,... | collective-permute-start | bytes 73736 | tf_op jit(solution)/shard_map/ppermute | solution.py:515
  78.1 16.5 %collective-permute-start.42 = (f32[16,384]{1,0:T(8,128)S(1)}, f32[16,384]{1,0:T(8,128)S(1)}, u32[]{:S(2)}, u32[]{:S(2)}) collective-permute-start(f32[16,384]{1,0:T(8,128)S(1)} %get-tuple-element.148), channel_id=1, source_target_pairs={{0,7},{1,0},{2,1},{3,2},{4,3},{5,4},{6,5},{7,6},{8,15},{9,8},{10,9... | collective-permute-start | bytes 73736 | tf_op jit(solution)/shard_map/ppermute | solution.py:515
  78.1 19.5 %collective-permute-start.25 = (f32[16,384]{1,0:T(8,128)S(1)}, f32[16,384]{1,0:T(8,128)S(1)}, u32[]{:S(2)}, u32[]{:S(2)}) collective-permute-start(f32[16,384]{1,0:T(8,128)S(1)} %get-tuple-element.126), channel_id=1, source_target_pairs={{0,1},{1,2},{2,3},{3,4},{4,5},{5,6},{6,7},{7,0},{8,9},{9,10},{10,1... | collective-permute-start | bytes 73736 | tf_op jit(solution)/shard_map/ppermute | solution.py:515
  81.6 17.8 %collective-permute-start.26 = (f32[16,384]{1,0:T(8,128)S(1)}, f32[16,384]{1,0:T(8,128)S(1)}, u32[]{:S(2)}, u32[]{:S(2)}) collective-permute-start(f32[16,384]{1,0:T(8,128)S(1)} %get-tuple-element.127), channel_id=1, source_target_pairs={{0,2},{1,3},{2,4},{3,5},{4,6},{5,7},{6,0},{7,1},{8,10},{9,11},{10,... | collective-permute-start | bytes 73736 | tf_op jit(solution)/shard_map/ppermute | solution.py:515
  82.2 17.2 %collective-permute-start.27 = (f32[16,384]{1,0:T(8,128)S(1)}, f32[16,384]{1,0:T(8,128)S(1)}, u32[]{:S(2)}, u32[]{:S(2)}) collective-permute-start(f32[16,384]{1,0:T(8,128)S(1)} %get-tuple-element.128), channel_id=1, source_target_pairs={{0,3},{1,4},{2,5},{3,6},{4,7},{5,0},{6,1},{7,2},{8,11},{9,12},{10,... | collective-permute-start | bytes 73736 | tf_op jit(solution)/shard_map/ppermute | solution.py:515
  90.8 12.1 %collective-permute-start.28 = (f32[16,384]{1,0:T(8,128)S(1)}, f32[16,384]{1,0:T(8,128)S(1)}, u32[]{:S(2)}, u32[]{:S(2)}) collective-permute-start(f32[16,384]{1,0:T(8,128)S(1)} %get-tuple-element.129), channel_id=1, source_target_pairs={{0,4},{1,5},{2,6},{3,7},{4,0},{5,1},{6,2},{7,3},{8,12},{9,13},{10,... | collective-permute-start | bytes 73736 | tf_op jit(solution)/shard_map/ppermute | solution.py:515
  94.5 9.2 %collective-permute-start.29 = (f32[16,384]{1,0:T(8,128)S(1)}, f32[16,384]{1,0:T(8,128)S(1)}, u32[]{:S(2)}, u32[]{:S(2)}) collective-permute-start(f32[16,384]{1,0:T(8,128)S(1)} %get-tuple-element.130), channel_id=1, source_target_pairs={{0,5},{1,6},{2,7},{3,0},{4,1},{5,2},{6,3},{7,4},{8,13},{9,14},{10,... | collective-permute-start | bytes 73736 | tf_op jit(solution)/shard_map/ppermute | solution.py:515
  97.6 7.9 %collective-permute-start.30 = (f32[16,384]{1,0:T(8,128)S(1)}, f32[16,384]{1,0:T(8,128)S(1)}, u32[]{:S(2)}, u32[]{:S(2)}) collective-permute-start(f32[16,384]{1,0:T(8,128)S(1)} %get-tuple-element.131), channel_id=1, source_target_pairs={{0,6},{1,7},{2,0},{3,1},{4,2},{5,3},{6,4},{7,5},{8,14},{9,15},{10,... | collective-permute-start | bytes 73736 | tf_op jit(solution)/shard_map/ppermute | solution.py:515
  99.4 9.3 %collective-permute-start.31 = (f32[16,384]{1,0:T(8,128)S(1)}, f32[16,384]{1,0:T(8,128)S(1)}, u32[]{:S(2)}, u32[]{:S(2)}) collective-permute-start(f32[16,384]{1,0:T(8,128)S(1)} %get-tuple-element.132), channel_id=1, source_target_pairs={{0,7},{1,0},{2,1},{3,2},{4,3},{5,4},{6,5},{7,6},{8,15},{9,8},{10,9... | collective-permute-start | bytes 73736 | tf_op jit(solution)/shard_map/ppermute | solution.py:515
  99.5 12.3 %collective-permute-start.14 = (f32[16,384]{1,0:T(8,128)S(1)}, f32[16,384]{1,0:T(8,128)S(1)}, u32[]{:S(2)}, u32[]{:S(2)}) collective-permute-start(f32[16,384]{1,0:T(8,128)S(1)} %get-tuple-element.110), channel_id=1, source_target_pairs={{0,1},{1,2},{2,3},{3,4},{4,5},{5,6},{6,7},{7,0},{8,9},{9,10},{10,1... | collective-permute-start | bytes 73736 | tf_op jit(solution)/shard_map/ppermute | solution.py:515
  102.9 15.2 %collective-permute-start.15 = (f32[16,384]{1,0:T(8,128)S(1)}, f32[16,384]{1,0:T(8,128)S(1)}, u32[]{:S(2)}, u32[]{:S(2)}) collective-permute-start(f32[16,384]{1,0:T(8,128)S(1)} %get-tuple-element.111), channel_id=1, source_target_pairs={{0,2},{1,3},{2,4},{3,5},{4,6},{5,7},{6,0},{7,1},{8,10},{9,11},{10,... | collective-permute-start | bytes 73736 | tf_op jit(solution)/shard_map/ppermute | solution.py:515
  103.8 14.7 %collective-permute-start.16 = (f32[16,384]{1,0:T(8,128)S(1)}, f32[16,384]{1,0:T(8,128)S(1)}, u32[]{:S(2)}, u32[]{:S(2)}) collective-permute-start(f32[16,384]{1,0:T(8,128)S(1)} %get-tuple-element.112), channel_id=1, source_target_pairs={{0,3},{1,4},{2,5},{3,6},{4,7},{5,0},{6,1},{7,2},{8,11},{9,12},{10,... | collective-permute-start | bytes 73736 | tf_op jit(solution)/shard_map/ppermute | solution.py:515
  105.5 14.5 %collective-permute-start.17 = (f32[16,384]{1,0:T(8,128)S(1)}, f32[16,384]{1,0:T(8,128)S(1)}, u32[]{:S(2)}, u32[]{:S(2)}) collective-permute-start(f32[16,384]{1,0:T(8,128)S(1)} %get-tuple-element.113), channel_id=1, source_target_pairs={{0,4},{1,5},{2,6},{3,7},{4,0},{5,1},{6,2},{7,3},{8,12},{9,13},{10,... | collective-permute-start | bytes 73736 | tf_op jit(solution)/shard_map/ppermute | solution.py:515
  108.7 13.0 %collective-permute-start.18 = (f32[16,384]{1,0:T(8,128)S(1)}, f32[16,384]{1,0:T(8,128)S(1)}, u32[]{:S(2)}, u32[]{:S(2)}) collective-permute-start(f32[16,384]{1,0:T(8,128)S(1)} %get-tuple-element.114), channel_id=1, source_target_pairs={{0,5},{1,6},{2,7},{3,0},{4,1},{5,2},{6,3},{7,4},{8,13},{9,14},{10,... | collective-permute-start | bytes 73736 | tf_op jit(solution)/shard_map/ppermute | solution.py:515
  111.8 10.3 %collective-permute-start.19 = (f32[16,384]{1,0:T(8,128)S(1)}, f32[16,384]{1,0:T(8,128)S(1)}, u32[]{:S(2)}, u32[]{:S(2)}) collective-permute-start(f32[16,384]{1,0:T(8,128)S(1)} %get-tuple-element.115), channel_id=1, source_target_pairs={{0,6},{1,7},{2,0},{3,1},{4,2},{5,3},{6,4},{7,5},{8,14},{9,15},{10,... | collective-permute-start | bytes 73736 | tf_op jit(solution)/shard_map/ppermute | solution.py:515
  118.1 15.2 %collective-permute-start.20 = (f32[16,384]{1,0:T(8,128)S(1)}, f32[16,384]{1,0:T(8,128)S(1)}, u32[]{:S(2)}, u32[]{:S(2)}) collective-permute-start(f32[16,384]{1,0:T(8,128)S(1)} %get-tuple-element.116), channel_id=1, source_target_pairs={{0,7},{1,0},{2,1},{3,2},{4,3},{5,4},{6,5},{7,6},{8,15},{9,8},{10,9... | collective-permute-start | bytes 73736 | tf_op jit(solution)/shard_map/ppermute | solution.py:515
  118.4 40.8 %collective-permute-start.43 = (bf16[2,96,384]{2,1,0:T(8,128)(2,1)S(1)}, bf16[2,96,384]{2,1,0:T(8,128)(2,1)S(1)}, u32[]{:S(2)}, u32[]{:S(2)}) collective-permute-start(bf16[2,96,384]{2,1,0:T(8,128)(2,1)S(1)} %get-tuple-element.153), channel_id=1, source_target_pairs={{0,32},{32,64},{64,96},{96,0},{1,33},{33,65},{65,97},{97,1},{2,34}... | collective-permute-start | bytes 442376 | tf_op jit(solution)/shard_map/ppermute | solution.py:543
  120.0 40.1 %collective-permute-start.44 = (bf16[2,96,384]{2,1,0:T(8,128)(2,1)S(1)}, bf16[2,96,384]{2,1,0:T(8,128)(2,1)S(1)}, u32[]{:S(2)}, u32[]{:S(2)}) collective-permute-start(bf16[2,96,384]{2,1,0:T(8,128)(2,1)S(1)} %get-tuple-element.154), channel_id=1, source_target_pairs={{0,96},{32,0},{64,32},{96,64},{1,97},{33,1},{65,33},{97,65},{2,98}... | collective-permute-start | bytes 442376 | tf_op jit(solution)/shard_map/ppermute | solution.py:544
  121.7 43.2 %collective-permute-start.32 = (bf16[2,96,384]{2,1,0:T(8,128)(2,1)S(1)}, bf16[2,96,384]{2,1,0:T(8,128)(2,1)S(1)}, u32[]{:S(2)}, u32[]{:S(2)}) collective-permute-start(bf16[2,96,384]{2,1,0:T(8,128)(2,1)S(1)} %get-tuple-element.137), channel_id=1, source_target_pairs={{0,32},{32,64},{64,96},{96,0},{1,33},{33,65},{65,97},{97,1},{2,34}... | collective-permute-start | bytes 442376 | tf_op jit(solution)/shard_map/ppermute | solution.py:543
  122.1 42.9 %collective-permute-start.33 = (bf16[2,96,384]{2,1,0:T(8,128)(2,1)S(1)}, bf16[2,96,384]{2,1,0:T(8,128)(2,1)S(1)}, u32[]{:S(2)}, u32[]{:S(2)}) collective-permute-start(bf16[2,96,384]{2,1,0:T(8,128)(2,1)S(1)} %get-tuple-element.138), channel_id=1, source_target_pairs={{0,96},{32,0},{64,32},{96,64},{1,97},{33,1},{65,33},{97,65},{2,98}... | collective-permute-start | bytes 442376 | tf_op jit(solution)/shard_map/ppermute | solution.py:544
  133.3 7.5 %collective-permute-start.3 = (f32[16,384]{1,0:T(8,128)S(1)}, f32[16,384]{1,0:T(8,128)S(1)}, u32[]{:S(2)}, u32[]{:S(2)}) collective-permute-start(f32[16,384]{1,0:T(8,128)S(1)} %get-tuple-element.94), channel_id=1, source_target_pairs={{0,1},{1,2},{2,3},{3,4},{4,5},{5,6},{6,7},{7,0},{8,9},{9,10},{10,1... | collective-permute-start | bytes 73736 | tf_op jit(solution)/shard_map/ppermute | solution.py:515
  140.8 5.0 %collective-permute-start.4 = (f32[16,384]{1,0:T(8,128)S(1)}, f32[16,384]{1,0:T(8,128)S(1)}, u32[]{:S(2)}, u32[]{:S(2)}) collective-permute-start(f32[16,384]{1,0:T(8,128)S(1)} %get-tuple-element.95), channel_id=1, source_target_pairs={{0,2},{1,3},{2,4},{3,5},{4,6},{5,7},{6,0},{7,1},{8,10},{9,11},{10,... | collective-permute-start | bytes 73736 | tf_op jit(solution)/shard_map/ppermute | solution.py:515
  145.9 7.7 %collective-permute-start.5 = (f32[16,384]{1,0:T(8,128)S(1)}, f32[16,384]{1,0:T(8,128)S(1)}, u32[]{:S(2)}, u32[]{:S(2)}) collective-permute-start(f32[16,384]{1,0:T(8,128)S(1)} %get-tuple-element.96), channel_id=1, source_target_pairs={{0,3},{1,4},{2,5},{3,6},{4,7},{5,0},{6,1},{7,2},{8,11},{9,12},{10,... | collective-permute-start | bytes 73736 | tf_op jit(solution)/shard_map/ppermute | solution.py:515
  153.6 5.3 %collective-permute-start.6 = (f32[16,384]{1,0:T(8,128)S(1)}, f32[16,384]{1,0:T(8,128)S(1)}, u32[]{:S(2)}, u32[]{:S(2)}) collective-permute-start(f32[16,384]{1,0:T(8,128)S(1)} %get-tuple-element.97), channel_id=1, source_target_pairs={{0,4},{1,5},{2,6},{3,7},{4,0},{5,1},{6,2},{7,3},{8,12},{9,13},{10,... | collective-permute-start | bytes 73736 | tf_op jit(solution)/shard_map/ppermute | solution.py:515
  158.9 13.4 %collective-permute-start.7 = (f32[16,384]{1,0:T(8,128)S(1)}, f32[16,384]{1,0:T(8,128)S(1)}, u32[]{:S(2)}, u32[]{:S(2)}) collective-permute-start(f32[16,384]{1,0:T(8,128)S(1)} %get-tuple-element.98), channel_id=1, source_target_pairs={{0,5},{1,6},{2,7},{3,0},{4,1},{5,2},{6,3},{7,4},{8,13},{9,14},{10,... | collective-permute-start | bytes 73736 | tf_op jit(solution)/shard_map/ppermute | solution.py:515
  159.3 13.2 %collective-permute-start.8 = (f32[16,384]{1,0:T(8,128)S(1)}, f32[16,384]{1,0:T(8,128)S(1)}, u32[]{:S(2)}, u32[]{:S(2)}) collective-permute-start(f32[16,384]{1,0:T(8,128)S(1)} %get-tuple-element.99), channel_id=1, source_target_pairs={{0,6},{1,7},{2,0},{3,1},{4,2},{5,3},{6,4},{7,5},{8,14},{9,15},{10,... | collective-permute-start | bytes 73736 | tf_op jit(solution)/shard_map/ppermute | solution.py:515
  160.1 15.6 %collective-permute-start.9 = (f32[16,384]{1,0:T(8,128)S(1)}, f32[16,384]{1,0:T(8,128)S(1)}, u32[]{:S(2)}, u32[]{:S(2)}) collective-permute-start(f32[16,384]{1,0:T(8,128)S(1)} %get-tuple-element.100), channel_id=1, source_target_pairs={{0,7},{1,0},{2,1},{3,2},{4,3},{5,4},{6,5},{7,6},{8,15},{9,8},{10,9... | collective-permute-start | bytes 73736 | tf_op jit(solution)/shard_map/ppermute | solution.py:515
  164.9 12.7 %collective-permute-start.21 = (bf16[2,96,384]{2,1,0:T(8,128)(2,1)S(1)}, bf16[2,96,384]{2,1,0:T(8,128)(2,1)S(1)}, u32[]{:S(2)}, u32[]{:S(2)}) collective-permute-start(bf16[2,96,384]{2,1,0:T(8,128)(2,1)S(1)} %get-tuple-element.121), channel_id=1, source_target_pairs={{0,32},{32,64},{64,96},{96,0},{1,33},{33,65},{65,97},{97,1},{2,34}... | collective-permute-start | bytes 442376 | tf_op jit(solution)/shard_map/ppermute | solution.py:543
  165.0 12.7 %collective-permute-start.22 = (bf16[2,96,384]{2,1,0:T(8,128)(2,1)S(1)}, bf16[2,96,384]{2,1,0:T(8,128)(2,1)S(1)}, u32[]{:S(2)}, u32[]{:S(2)}) collective-permute-start(bf16[2,96,384]{2,1,0:T(8,128)(2,1)S(1)} %get-tuple-element.122), channel_id=1, source_target_pairs={{0,96},{32,0},{64,32},{96,64},{1,97},{33,1},{65,33},{97,65},{2,98}... | collective-permute-start | bytes 442376 | tf_op jit(solution)/shard_map/ppermute | solution.py:544
  172.4 21.5 %collective-permute-start.45 = (bf16[4,96,384]{2,1,0:T(8,128)(2,1)S(1)}, bf16[4,96,384]{2,1,0:T(8,128)(2,1)S(1)}, u32[]{:S(2)}, u32[]{:S(2)}) collective-permute-start(bf16[4,96,384]{2,1,0:T(8,128)(2,1)S(1)} %get-tuple-element.155), channel_id=1, source_target_pairs={{0,32},{32,64},{64,96},{96,0},{1,33},{33,65},{65,97},{97,1},{2,34}... | collective-permute-start | bytes 884744 | tf_op jit(solution)/shard_map/ppermute | solution.py:562
  172.5 22.7 %collective-permute-start.46 = (bf16[4,96,384]{2,1,0:T(8,128)(2,1)S(1)}, bf16[4,96,384]{2,1,0:T(8,128)(2,1)S(1)}, u32[]{:S(2)}, u32[]{:S(2)}) collective-permute-start(bf16[4,96,384]{2,1,0:T(8,128)(2,1)S(1)} %get-tuple-element.156), channel_id=1, source_target_pairs={{0,96},{32,0},{64,32},{96,64},{1,97},{33,1},{65,33},{97,65},{2,98}... | collective-permute-start | bytes 884744 | tf_op jit(solution)/shard_map/ppermute | solution.py:562
  175.7 20.3 %collective-permute-start.34 = (bf16[4,96,384]{2,1,0:T(8,128)(2,1)S(1)}, bf16[4,96,384]{2,1,0:T(8,128)(2,1)S(1)}, u32[]{:S(2)}, u32[]{:S(2)}) collective-permute-start(bf16[4,96,384]{2,1,0:T(8,128)(2,1)S(1)} %get-tuple-element.139), channel_id=1, source_target_pairs={{0,32},{32,64},{64,96},{96,0},{1,33},{33,65},{65,97},{97,1},{2,34}... | collective-permute-start | bytes 884744 | tf_op jit(solution)/shard_map/ppermute | solution.py:562
  177.6 12.2 %collective-permute-start.10 = (bf16[2,96,384]{2,1,0:T(8,128)(2,1)S(1)}, bf16[2,96,384]{2,1,0:T(8,128)(2,1)S(1)}, u32[]{:S(2)}, u32[]{:S(2)}) collective-permute-start(bf16[2,96,384]{2,1,0:T(8,128)(2,1)S(1)} %get-tuple-element.105), channel_id=1, source_target_pairs={{0,32},{32,64},{64,96},{96,0},{1,33},{33,65},{65,97},{97,1},{2,34}... | collective-permute-start | bytes 442376 | tf_op jit(solution)/shard_map/ppermute | solution.py:543
  177.7 12.1 %collective-permute-start.11 = (bf16[2,96,384]{2,1,0:T(8,128)(2,1)S(1)}, bf16[2,96,384]{2,1,0:T(8,128)(2,1)S(1)}, u32[]{:S(2)}, u32[]{:S(2)}) collective-permute-start(bf16[2,96,384]{2,1,0:T(8,128)(2,1)S(1)} %get-tuple-element.106), channel_id=1, source_target_pairs={{0,96},{32,0},{64,32},{96,64},{1,97},{33,1},{65,33},{97,65},{2,98}... | collective-permute-start | bytes 442376 | tf_op jit(solution)/shard_map/ppermute | solution.py:544
  189.8 11.3 %collective-permute-start.35 = (bf16[4,96,384]{2,1,0:T(8,128)(2,1)S(1)}, bf16[4,96,384]{2,1,0:T(8,128)(2,1)S(1)}, u32[]{:S(2)}, u32[]{:S(2)}) collective-permute-start(bf16[4,96,384]{2,1,0:T(8,128)(2,1)S(1)} %get-tuple-element.140), channel_id=1, source_target_pairs={{0,96},{32,0},{64,32},{96,64},{1,97},{33,1},{65,33},{97,65},{2,98}... | collective-permute-start | bytes 884744 | tf_op jit(solution)/shard_map/ppermute | solution.py:562
  189.8 14.0 %collective-permute-start.23 = (bf16[4,96,384]{2,1,0:T(8,128)(2,1)S(1)}, bf16[4,96,384]{2,1,0:T(8,128)(2,1)S(1)}, u32[]{:S(2)}, u32[]{:S(2)}) collective-permute-start(bf16[4,96,384]{2,1,0:T(8,128)(2,1)S(1)} %get-tuple-element.123), channel_id=1, source_target_pairs={{0,32},{32,64},{64,96},{96,0},{1,33},{33,65},{65,97},{97,1},{2,34}... | collective-permute-start | bytes 884744 | tf_op jit(solution)/shard_map/ppermute | solution.py:562
  193.9 9.9 %collective-permute-start.24 = (bf16[4,96,384]{2,1,0:T(8,128)(2,1)S(1)}, bf16[4,96,384]{2,1,0:T(8,128)(2,1)S(1)}, u32[]{:S(2)}, u32[]{:S(2)}) collective-permute-start(bf16[4,96,384]{2,1,0:T(8,128)(2,1)S(1)} %get-tuple-element.124), channel_id=1, source_target_pairs={{0,96},{32,0},{64,32},{96,64},{1,97},{33,1},{65,33},{97,65},{2,98}... | collective-permute-start | bytes 884744 | tf_op jit(solution)/shard_map/ppermute | solution.py:562
  195.2 11.3 %collective-permute-start.12 = (bf16[4,96,384]{2,1,0:T(8,128)(2,1)S(1)}, bf16[4,96,384]{2,1,0:T(8,128)(2,1)S(1)}, u32[]{:S(2)}, u32[]{:S(2)}) collective-permute-start(bf16[4,96,384]{2,1,0:T(8,128)(2,1)S(1)} %get-tuple-element.107), channel_id=1, source_target_pairs={{0,32},{32,64},{64,96},{96,0},{1,33},{33,65},{65,97},{97,1},{2,34}... | collective-permute-start | bytes 884744 | tf_op jit(solution)/shard_map/ppermute | solution.py:562
  196.0 10.4 %collective-permute-start.13 = (bf16[4,96,384]{2,1,0:T(8,128)(2,1)S(1)}, bf16[4,96,384]{2,1,0:T(8,128)(2,1)S(1)}, u32[]{:S(2)}, u32[]{:S(2)}) collective-permute-start(bf16[4,96,384]{2,1,0:T(8,128)(2,1)S(1)} %get-tuple-element.108), channel_id=1, source_target_pairs={{0,96},{32,0},{64,32},{96,64},{1,97},{33,1},{65,33},{97,65},{2,98}... | collective-permute-start | bytes 884744 | tf_op jit(solution)/shard_map/ppermute | solution.py:562
  (5 other events, 44.1 us)

commit v2 on v1

--- a/solution.py
+++ b/solution.py
@@ -9,9 +9,14 @@
 from jax.experimental.pallas import tpu as pltpu
 from jax.sharding import PartitionSpec as P
 
-CHUNKS = 4
+CHUNKS = 2
 LANES = 128
+GROUP_AT = 3
+BAND_AT = 4
+SLAB_AT = 8
 ROW_GROUP = 16
+FIELD_STEP = 4
+PRODUCT_STEP = 2
 VMEM_LIMIT = 48 * 1024 * 1024
 
 F32 = jnp.float32
@@ -85,7 +90,7 @@
     index = jnp.zeros((levels, slabs), jnp.int32)
     end = jnp.int32(0)
     for s in range(slabs):
-        end = end + slab_levels[s]
+        end = end + slab_levels[SLAB_AT + s]
         index = index + (level >= end).astype(jnp.int32)
     chosen = (index == iota((levels, slabs), 1)).astype(F32).astype(BF16)
     return sum(dot_nn(chosen, part) for part in split3(rates))
@@ -96,9 +101,9 @@
 
 
 def column_kernel(
-    sizes, where_ref, slab_ref, group_ref, band_ref, control_ref, rate_ref,
+    sizes, where_ref, control_ref, rate_ref,
     column_ref, decay_ref, gain_ref, end_ref, send1_ref, send2_ref, send3_ref,
-    kron, decay_all,
+    kron, decay_all, weighted,
 ):
     levels, rows, cols, quarters, lat_count = sizes
     step = pl.program_id(0)
@@ -107,7 +112,7 @@
 
     @pl.when(step == 0)
     def _():
-        band = band_ref[group_ref[0]].astype(F32)
+        band = where_ref[BAND_AT + where_ref[GROUP_AT]].astype(F32)
         out_level = traced_level(jnp.right_shift(iota((full, full), 0), 3), levels, CHUNKS, quarters)
         spacing = out_level - jnp.right_shift(iota((full, full), 1), 3)
         same = jnp.bitwise_and(iota((full, full), 0), 7) == jnp.bitwise_and(iota((full, full), 1), 7)
@@ -115,7 +120,7 @@
         weight = jnp.exp(-2.0 * (ratio * ratio))
         keep = jnp.logical_and(same, jnp.abs(spacing).astype(F32) <= band)
         kron[...] = jnp.where(keep, weight, 0.0).astype(BF16)
-        level_rates = rates_by_place(slab_ref, rate_ref[...], levels, quarters)
+        level_rates = rates_by_place(where_ref, rate_ref[...], levels, quarters)
         own = iota((rows, rate_ref.shape[1]), 1) == lon * rows + iota((rows, rate_ref.shape[1]), 0)
         rate = exact_times_t(own.astype(F32).astype(BF16), level_rates)
         remain = 1.0 - rate
@@ -133,9 +138,6 @@
 
     log_a = decay_all[pl.ds(step * ROW_GROUP, ROW_GROUP), :]
     lane = iota((ROW_GROUP, LANES), 1).astype(F32)
-    place_lane = iota((ROW_GROUP, levels), 1)
-    forward = jnp.zeros((ROW_GROUP, levels), F32)
-    backward = jnp.zeros((ROW_GROUP, levels), F32)
     blocks = cols // LANES
     for place in range(levels):
         log_b = jnp.broadcast_to(log_a[:, place : place + 1], (ROW_GROUP, LANES))
@@ -146,8 +148,14 @@
         for b in range(1, blocks):
             along = parts[b] + over * along
             against = parts[-1 - b] + over * against
-        along = jnp.sum(along * jnp.exp(log_b * (LANES - 1.0 - lane)), axis=1, keepdims=True)
-        against = jnp.sum(against * jnp.exp(log_b * lane), axis=1, keepdims=True)
+        weighted[0, place] = along * jnp.exp(log_b * (LANES - 1.0 - lane))
+        weighted[1, place] = against * jnp.exp(log_b * lane)
+    place_lane = iota((ROW_GROUP, levels), 1)
+    forward = jnp.zeros((ROW_GROUP, levels), F32)
+    backward = jnp.zeros((ROW_GROUP, levels), F32)
+    for place in range(levels):
+        along = jnp.sum(weighted[0, place], axis=1, keepdims=True)
+        against = jnp.sum(weighted[1, place], axis=1, keepdims=True)
         forward = jnp.where(place_lane == place, along, forward)
         backward = jnp.where(place_lane == place, against, backward)
     power = (1 + cols * (2 * (lat_count - 1 - lat) + 1)).astype(F32)
@@ -158,13 +166,13 @@
 
 
 def row_kernel(
-    sizes, where_ref, slab_ref, rate_ref,
+    sizes, where_ref, rate_ref,
     left_ref, left_sum_ref, right_ref, right_sum_ref, chain_ref,
 ):
     levels, rows, quarters, lon_count = sizes
     lon = where_ref[2]
     total = rate_ref.shape[1]
-    rate = rates_by_place(slab_ref, rate_ref[...], levels, quarters)
+    rate = rates_by_place(where_ref, rate_ref[...], levels, quarters)
     remain = 1.0 - rate
     root = jnp.sqrt(rate * (2.0 - rate))
     gain = root * jnp.sqrt(root) / jnp.sqrt(jnp.sqrt(1.0 + remain * remain))
@@ -199,33 +207,34 @@
         axis=1,
         keepdims=True,
     )
-    over = jnp.sum(jnp.where(device == lon, jnp.exp(log_over), 0.0), axis=1, keepdims=True)
-    origin = jnp.where(lon >= target, lon - target, lon - target + lon_count)
-    low, high = jnp.minimum(origin, lon), jnp.maximum(origin, lon)
+    every = jnp.exp(log_over)
+    over = jnp.sum(jnp.where(device == lon, every, 0.0), axis=1, keepdims=True)
+    partner = jnp.bitwise_xor(lon, 1)
+    partner_over = jnp.sum(jnp.where(device == partner, every, 0.0), axis=1, keepdims=True)
+    pair, pairs = jnp.right_shift(lon, 1), lon_count // 2
+    shift = jnp.bitwise_and(target, 63)
+    is_before = pair >= shift
+    low = jnp.where(is_before, 2 * (pair - shift) + 1, lon)
+    high = jnp.where(is_before, lon, 2 * (pair - shift + pairs))
     path = jnp.logical_and(source > low, source < high).astype(F32).astype(BF16)
     reach = jnp.exp(times_exact(log_over, path))
-    shift = device
-    along = jnp.where(jnp.logical_and(shift >= 1, shift <= lon), reach, 0.0)
-    against = jnp.where(jnp.logical_and(shift > lon, shift < lon_count), reach, 0.0)
-    lane = device
-    chain = jnp.where(lane < lon_count, along, 0.0)
-    chain = chain + jnp.concatenate(
-        [jnp.zeros((levels, 64), F32), against[:, :64]], axis=1
-    )
-    chain = jnp.where(lane == 32, over, chain)
-    chain_ref[...] = jnp.where(lane == 33, echo, chain)
+    shift = jnp.bitwise_and(device, 63)
+    counted = jnp.logical_and(shift >= 1, shift < pairs)
+    counted = jnp.logical_and(counted, (pair >= shift) == (device < 64))
+    chain = jnp.where(counted, reach, 0.0)
+    for at, value in ((32, over), (33, echo), (34, partner_over)):
+        chain = jnp.where(device == at, value, chain)
+    chain_ref[...] = chain
 
 
 def field_kernel(
     sizes, where_ref, column_ref, decay_ref, gain_ref, end_ref, got1_ref, got2_ref, got3_ref,
     left_ref, left_sum_ref, right_ref, right_sum_ref, chain_ref, triangle_ref,
-    field_ref, out_end_ref, *rest,
+    field_ref, edge_ref, tables,
 ):
-    rows, cols, chunk, in_chunk, per_step, lat_count, lon_count = sizes
-    send_refs = rest[: lon_count - 1]
-    tables, rights, edges = rest[lon_count - 1 :]
+    rows, cols, chunk, in_chunk, per_step, lat_count = sizes
     step = pl.program_id(0)
-    lat, lon = where_ref[1], where_ref[2]
+    lat = where_ref[1]
     blocks = cols // LANES
 
     @pl.when(step == 0)
@@ -308,103 +317,86 @@
         chain = chain_ref[pl.ds(row, 1), :]
         over_rows, echo = chain[:, 32:33], chain[:, 33:34]
         end = over_rows * result[rows : rows + 1]
-        edges[0, pl.ds(row, 1), :] = end
-        edges[1, pl.ds(row, 1), :] = result[rows + 1 : rows + 2] + over_rows * echo * end
-
-    @pl.when(step == pl.num_programs(0) - 1)
-    def _():
-        end, returning = edges[0], edges[1]
-        out_end_ref[...] = end
-        for shift, ref in enumerate(send_refs, 1):
-            ref[...] = jnp.where(lon + shift < lon_count, end, returning)
-
-
-def product(field, left, left_sum, enter, leave, spread):
-    filtered = field + left_sum * enter + left * leave
-    return spread.astype(F32) * filtered.astype(BF16).astype(F32)
-
-
-def wide_lane(table_ref, lane, cols):
-    one = lane_of(table_ref[...], lane)
-    return jnp.concatenate([one] * (cols // LANES), axis=1)
-
-
-def one_product(field_ref, spread_ref, table_ref, enter_ref, leave_ref, chunk, in_chunk, row, u):
+        edge_ref[0, pl.ds(row, 1), :] = end
+        edge_ref[1, pl.ds(row, 1), :] = result[rows + 1 : rows + 2] + over_rows * echo * end
+
+
+def pair_kernel(where_ref, own_ref, got_ref, chain_ref, send1_ref, send2_ref, send3_ref, *, pairs):
+    lon = where_ref[2]
+    second = jnp.bitwise_and(lon, 1) == 1
+    pair = jnp.right_shift(lon, 1)
+    chain = chain_ref[...]
+    over, partner_over = chain[:, 32:33], chain[:, 34:35]
+    end, returning = own_ref[0], own_ref[1]
+    got_end, got_returning = got_ref[0], got_ref[1]
+    pair_end = jnp.where(second, end + over * got_end, got_end + partner_over * end)
+    pair_returning = jnp.where(
+        second, got_returning + partner_over * returning, returning + over * got_returning
+    )
+    for shift, ref in ((1, send1_ref), (2, send2_ref), (3, send3_ref)):
+        ref[...] = jnp.where(pair + shift < pairs, pair_end, pair_returning)
+
+
+def enter_kernel(where_ref, own_ref, got_ref, got1_ref, got2_ref, got3_ref, chain_ref, left_ref, left_sum_ref,
+                 enter_ref, leave_ref, table_ref):
+    second = jnp.bitwise_and(where_ref[2], 1) == 1
+    chain = chain_ref[...]
+    over, echo = chain[:, 32:33], chain[:, 33:34]
+    enter = jnp.where(second, got_ref[0], 0.0)
+    leave = jnp.where(second, 0.0, got_ref[1])
+    for shift, ref in ((1, got1_ref), (2, got2_ref), (3, got3_ref)):
+        enter = enter + chain[:, shift : shift + 1] * ref[...]
+        leave = leave + chain[:, 64 + shift : 65 + shift] * ref[...]
+    enter_ref[...] = enter
+    leave_ref[...] = over * (leave + echo * (own_ref[0] + over * enter))
+    table_ref[...] = jnp.concatenate([left_ref[...], left_sum_ref[...]], axis=1)
+
+
+def one_product(where_ref, refs, sizes, turn, step, u):
+    field_ref, spread_ref, enter_ref, leave_ref, table_ref = refs
+    chunk, in_chunk, steps, quarters = sizes
     cols = field_ref.shape[-1]
+    row = lax.rem(where_ref[0] + turn, quarters) * steps + step
     place = chunk * in_chunk + row
     half = table_ref.shape[1] // 2
-    left = wide_lane(table_ref, place, cols)
-    left_sum = wide_lane(table_ref, place + half, cols)
+    wide = lambda lane: jnp.concatenate([lane_of(table_ref[...], lane)] * (cols // LANES), axis=1)
     enter, leave = enter_ref[pl.ds(row, 1), :], leave_ref[pl.ds(row, 1), :]
-    return product(field_ref[u], left, left_sum, enter, leave, spread_ref[0, u])
-
-
-def first_kernel(sizes, where_ref, *refs):
-    chunk, in_chunk, steps, quarters, lon_count = sizes
-    got_refs = refs[: lon_count - 1]
-    end_ref, chain_ref, left_ref, left_sum_ref, field_ref, spread_ref = refs[lon_count - 1 : lon_count + 5]
-    enter_ref, leave_ref, table_ref, up_ref, down_ref = refs[lon_count + 5 :]
-    chain = chain_ref[...]
-    enter = jnp.zeros(end_ref.shape, F32)
-    leave = jnp.zeros(end_ref.shape, F32)
-    for shift, ref in enumerate(got_refs, 1):
-        got = ref[...]
-        enter = enter + chain[:, shift : shift + 1] * got
-        leave = leave + chain[:, 64 + shift : 65 + shift] * got
-    over, echo = chain[:, 32:33], chain[:, 33:34]
-    enter_ref[...] = enter
-    leave_ref[...] = over * (leave + echo * (end_ref[...] + over * enter))
-    table_ref[...] = jnp.concatenate([left_ref[...], left_sum_ref[...]], axis=1)
-    quarter = lax.rem(where_ref[0] + 2, quarters)
-    for u in range(steps):
-        value = one_product(
-            field_ref, spread_ref, table_ref, enter_ref, leave_ref, chunk, in_chunk, quarter * steps + u, u
-        ).astype(BF16)
-        if u < steps // 2:
-            up_ref[u] = value
-        else:
-            down_ref[u - steps // 2] = value
-
-
-def second_kernel(
-    sizes, where_ref, field1_ref, spread1_ref, field3_ref, spread3_ref, enter_ref, leave_ref, table_ref,
-    up_ref, down_ref, out1_ref, out3_ref,
+    filtered = field_ref[u] + wide(place + half) * enter + wide(place) * leave
+    return spread_ref[0, u].astype(F32) * filtered.astype(BF16).astype(F32)
+
+
+def send_kernel(sizes, items, added, where_ref, enter_ref, leave_ref, table_ref, *refs):
+    steps = sizes[2]
+    count = len(items)
+    ins, adds, outs = refs[: 2 * count], refs[2 * count : -count], refs[-count:]
+    for at, (turn, half) in enumerate(items):
+        for u in range(PRODUCT_STEP):
+            step = half * (steps // 2) + pl.program_id(0) * PRODUCT_STEP + u
+            row_refs = (ins[2 * at], ins[2 * at + 1], enter_ref, leave_ref, table_ref)
+            value = one_product(where_ref, row_refs, sizes, turn, step, u)
+            if added:
+                value = value + adds[at][u].astype(F32)
+            outs[at][u] = value.astype(BF16)
+
+
+def last_kernel(
+    sizes, scale, where_ref, enter_ref, leave_ref, table_ref, field_ref, spread_ref,
+    a0_ref, a1_ref, b0_ref, b1_ref, *rest
 ):
-    chunk, in_chunk, steps, quarters = sizes
-    for u in range(steps):
-        for turn, field_ref, spread_ref, out_ref in (
-            (1, field1_ref, spread1_ref, out1_ref),
-            (3, field3_ref, spread3_ref, out3_ref),
-        ):
-            quarter = lax.rem(where_ref[0] + turn, quarters)
-            value = one_product(
-                field_ref, spread_ref, table_ref, enter_ref, leave_ref, chunk, in_chunk, quarter * steps + u, u
-            )
-            if turn == 1 and u < steps // 2:
-                value = value + up_ref[u].astype(F32)
-            if turn == 3 and u >= steps // 2:
-                value = value + down_ref[u - steps // 2].astype(F32)
-            out_ref[u] = value.astype(BF16)
-
-
-def third_kernel(
-    sizes, where_ref, field_ref, spread_ref, enter_ref, leave_ref, table_ref, got1_ref, got3_ref, *rest
-):
-    chunk, in_chunk, steps, scale = sizes
+    steps = sizes[2]
     out_ref = rest[-1]
-    for u in range(steps):
-        value = one_product(
-            field_ref, spread_ref, table_ref, enter_ref, leave_ref, chunk, in_chunk, where_ref[0] * steps + u, u
-        )
-        out_ref[u] = (value + got1_ref[u].astype(F32) + got3_ref[u].astype(F32)) * scale
+    in_first = pl.program_id(0) * PRODUCT_STEP < steps // 2
+    for u in range(PRODUCT_STEP):
+        step = pl.program_id(0) * PRODUCT_STEP + u
+        row_refs = (field_ref, spread_ref, enter_ref, leave_ref, table_ref)
+        value = one_product(where_ref, row_refs, sizes, 0, step, u)
+        got_a = jnp.where(in_first, a0_ref[u].astype(F32), a1_ref[u].astype(F32))
+        got_b = jnp.where(in_first, b0_ref[u].astype(F32), b1_ref[u].astype(F32))
+        out_ref[u] = (value + got_a + got_b) * scale
 
 
 def whole(shape):
     return pl.BlockSpec(shape, lambda *_: (0,) * len(shape))
-
-
-def smem():
-    return pl.BlockSpec(memory_space=pltpu.SMEM)
 
 
 def call(kernel, name, inputs, in_specs, outputs, out_specs, scratch=(), grid=(1,), aliases=None, cost=None):
@@ -448,7 +440,8 @@
     steps = levels // (CHUNKS * quarters)
     in_chunk = steps * quarters
     total_rows = zonal_rate.shape[1]
-    where = jnp.stack([lax.axis_index(a) for a in ("mem", "lat", "lon")]).astype(jnp.int32)
+    here = jnp.stack([lax.axis_index(a) for a in ("mem", "lat", "lon")]).astype(jnp.int32)
+    where = jnp.concatenate([here, member_group, band_width, slab_levels])
     sds = jax.ShapeDtypeStruct
     table = sds((rows, levels), F32)
     table_spec = pl.BlockSpec((ROW_GROUP, levels), lambda g, _: (g, 0))
@@ -456,9 +449,8 @@
     column, decay, gain, end, *sends = call(
         functools.partial(column_kernel, (levels, rows, cols, quarters, lat_count)),
         "vertical_columns",
-        (where, slab_levels, member_group, band_width, control, zonal_rate),
+        (where, control, zonal_rate),
         [
-            smem(), smem(), smem(),
             pl.BlockSpec((1, levels, ROW_GROUP, cols), lambda g, _: (0, 0, g, 0)),
             whole(zonal_rate.shape),
         ],
@@ -468,7 +460,11 @@
             whole((rows, levels)), whole((rows, levels)),
             table_spec, table_spec, table_spec, table_spec,
         ),
-        scratch=[pltpu.VMEM((levels * 8, levels * 8), BF16), pltpu.VMEM((rows, levels), F32)],
+        scratch=[
+            pltpu.VMEM((levels * 8, levels * 8), BF16),
+            pltpu.VMEM((rows, levels), F32),
+            pltpu.VMEM((2, levels, ROW_GROUP, LANES), F32),
+        ],
         grid=(rows // ROW_GROUP,),
         cost=cost(2 * 512 * 512 * 384 * 12, 2 * levels * rows * cols * 2),
     )
@@ -476,8 +472,8 @@
     left, left_sum, right, right_sum, chain = call(
         functools.partial(row_kernel, (levels, rows, quarters, lon_count)),
         "row_terms",
-        (where, slab_levels, meridional_rate),
-        [smem(), whole(meridional_rate.shape)],
+        (where, meridional_rate),
+        [whole(meridional_rate.shape)],
         (table, table, sds((levels, rows), F32), sds((levels, rows), F32), sds((levels, LANES), F32)),
         (
             whole((rows, levels)), whole((rows, levels)),
@@ -490,89 +486,109 @@
     scale = 1.0 / math.sqrt(control.shape[0] * quarters - 1)
     plane = rows * cols
     row_spec = pl.BlockSpec((in_chunk, cols), lambda *_: (0, 0))
-    fields, ends, far = [], [], []
+    row_spec = whole((in_chunk, cols))
+    edge_spec = whole((2, in_chunk, cols))
+    table_wide = sds((rows, 2 * levels), F32)
+    edge_row = sds((in_chunk, cols), F32)
+    sizes_of = lambda c: (c, in_chunk, steps, quarters)
+    half_steps = steps // 2
+    half_piece = sds((half_steps, rows, cols), BF16)
+    half_spec = pl.BlockSpec((PRODUCT_STEP, rows, cols), lambda g, _: (g, 0, 0))
+    to_partner = [(i, i ^ 1) for i in range(lon_count)]
+    to_pair = lambda s: [(i, (i + 2 * s) % lon_count) for i in range(lon_count)]
+    per_half = half_steps // PRODUCT_STEP
+    first_half = pl.BlockSpec((PRODUCT_STEP, rows, cols), lambda g, _: (jnp.minimum(g, per_half - 1), 0, 0))
+    last_half = pl.BlockSpec((PRODUCT_STEP, rows, cols), lambda g, _: (jnp.maximum(g - per_half, 0), 0, 0))
+
+    def quarter_specs(c, turn, half):
+        at = lambda g, w, wide: (lax.rem(w[0] + turn, quarters) * wide + half) * per_half + g
+        return [
+            pl.BlockSpec((PRODUCT_STEP, rows, cols), lambda g, w: (at(g, w, 2), 0, 0)),
+            pl.BlockSpec(
+                (1, PRODUCT_STEP, rows, cols),
+                lambda g, w: (0, at(g, w, 2 * CHUNKS) + c * 2 * per_half, 0, 0),
+            ),
+        ]
+
+    def send(c, name, state, items, adds=()):
+        field, enter, leave, lanes = state
+        return call(
+            functools.partial(send_kernel, sizes_of(c), items, bool(adds)),
+            name,
+            (where, enter, leave, lanes, *([field, perturbation] * len(items)), *adds),
+            [row_spec, row_spec, whole(table_wide.shape)]
+            + [spec for item in items for spec in quarter_specs(c, *item)]
+            + [half_spec] * len(adds),
+            (half_piece,) * len(items),
+            (half_spec,) * len(items),
+            grid=(per_half,),
+            cost=cost(steps * plane * 8, steps * plane * 8),
+        )
+
+    up, down = ring("mem", 1), ring("mem", -1)
+    states, fields = [], []
     for c in range(CHUNKS):
         by_place = lambda width: pl.BlockSpec((in_chunk, width), lambda g, _, c=c: (c, 0))
-        field, out_end, *out_sends = call(
-            functools.partial(field_kernel, (rows, cols, c, in_chunk, steps, lat_count, lon_count)),
+        field_steps = in_chunk // FIELD_STEP
+        field, edge = call(
+            functools.partial(field_kernel, (rows, cols, c, in_chunk, FIELD_STEP, lat_count)),
             "zonal_rows",
             (where, column, decay, gain, end, *got, left, left_sum, right, right_sum, chain, triangle),
-            [pl.BlockSpec((steps, rows, cols), lambda g, _, c=c: (c * quarters + g, 0, 0))]
+            [pl.BlockSpec((FIELD_STEP, rows, cols), lambda g, _, c=c: (c * field_steps + g, 0, 0))]
             + [whole((rows, levels))] * 8
             + [by_place(rows), by_place(rows), by_place(LANES), whole(triangle.shape)],
-            (sds((in_chunk, rows, cols), F32),) + (sds((in_chunk, cols), F32),) * lon_count,
-            (pl.BlockSpec((steps, rows, cols), lambda g, _: (g, 0, 0)),) + (row_spec,) * lon_count,
-            scratch=[
-                pltpu.VMEM((3, rows, 2 * levels), F32),
-                pltpu.VMEM((8, LANES), F32),
-                pltpu.VMEM((2, in_chunk, cols), F32),
-            ],
-            grid=(quarters,),
+            (sds((in_chunk, rows, cols), F32), sds((2, in_chunk, cols), F32)),
+            (pl.BlockSpec((FIELD_STEP, rows, cols), lambda g, _: (g, 0, 0)), edge_spec),
+            scratch=[pltpu.VMEM((3, rows, 2 * levels), F32)],
+            grid=(field_steps,),
             cost=cost(in_chunk * plane * 2 * 1024, in_chunk * plane * 6),
         )
         fields.append(field)
-        ends.append(out_end)
-        far.append([lax.ppermute(s, "lon", ring("lon", i + 1)) for i, s in enumerate(out_sends)])
-
-    quarter_field = lambda turn: pl.BlockSpec(
-        (steps, rows, cols), lambda g, w: (lax.rem(w[0] + turn, quarters), 0, 0)
-    )
-    quarter_spread = lambda turn, c: pl.BlockSpec(
-        (1, steps, rows, cols), lambda g, w: (0, lax.rem(w[0] + turn, quarters) * CHUNKS + c, 0, 0)
-    )
-    piece = sds((steps, rows, cols), BF16)
-    half_piece = sds((steps // 2, rows, cols), BF16)
-    table_wide = sds((rows, 2 * levels), F32)
-    row_pair = (row_spec, row_spec, whole((rows, 2 * levels)))
-    arrived = []
+        partner = lax.ppermute(edge, "lon", to_partner)
+        pair_sends = call(
+            functools.partial(pair_kernel, pairs=lon_count // 2),
+            "pair_ends",
+            (where, edge, partner, chain),
+            [edge_spec, edge_spec, by_place(LANES)],
+            (edge_row,) * 3,
+            (row_spec,) * 3,
+        )
+        pair_got = [lax.ppermute(s, "lon", to_pair(i + 1)) for i, s in enumerate(pair_sends)]
+        enter, leave, lanes = call(
+            enter_kernel,
+            "entering",
+            (where, edge, partner, *pair_got, chain, left, left_sum),
+            [edge_spec, edge_spec, row_spec, row_spec, row_spec, by_place(LANES)]
+            + [whole((rows, levels))] * 2,
+            (edge_row, edge_row, table_wide),
+            (row_spec, row_spec, whole(table_wide.shape)),
+        )
+        states.append((field, enter, leave, lanes))
+    result = None
+    moved = []
     for c in range(CHUNKS):
-        enter, leave, lanes, up, down = call(
-            functools.partial(first_kernel, (c, in_chunk, steps, quarters, lon_count)),
-            "first_products",
-            (where, *far[c], ends[c], chain, left, left_sum, fields[c], perturbation),
-            [row_spec] * lon_count
-            + [
-                pl.BlockSpec((in_chunk, LANES), lambda g, _, c=c: (c, 0)),
-                whole((rows, levels)), whole((rows, levels)),
-                quarter_field(2), quarter_spread(2, c),
-            ],
-            (sds((in_chunk, cols), F32), sds((in_chunk, cols), F32), table_wide, half_piece, half_piece),
-            row_pair + (whole(half_piece.shape), whole(half_piece.shape)),
-            cost=cost(steps * plane * 8, steps * plane * 8),
-        )
-        up = lax.ppermute(up, "mem", ring("mem", 1))
-        down = lax.ppermute(down, "mem", ring("mem", -1))
-        arrived.append((enter, leave, lanes, up, down))
-    result = None
-    gathered = []
+        two_up, two_down = send(c, "products_two_away", states[c], ((2, 0), (2, 1)))
+        two_up, two_down = lax.ppermute(two_up, "mem", up), lax.ppermute(two_down, "mem", down)
+        one_up, one_down = send(c, "products_one_away", states[c], ((1, 1), (3, 0)))
+        one_up, one_down = lax.ppermute(one_up, "mem", up), lax.ppermute(one_down, "mem", down)
+        sum_up, sum_down = send(c, "products_added", states[c], ((1, 0), (3, 1)), (two_up, two_down))
+        sum_up, sum_down = lax.ppermute(sum_up, "mem", up), lax.ppermute(sum_down, "mem", down)
+        moved.append((sum_up, one_up, one_down, sum_down))
     for c in range(CHUNKS):
-        enter, leave, lanes, up, down = arrived[c]
-        out1, out3 = call(
-            functools.partial(second_kernel, (c, in_chunk, steps, quarters)),
-            "second_products",
-            (where, fields[c], perturbation, fields[c], perturbation, enter, leave, lanes, up, down),
-            [quarter_field(1), quarter_spread(1, c), quarter_field(3), quarter_spread(3, c)]
-            + list(row_pair)
-            + [whole(half_piece.shape), whole(half_piece.shape)],
-            (piece, piece),
-            (whole(piece.shape), whole(piece.shape)),
-            cost=cost(2 * steps * plane * 8, 2 * steps * plane * 8),
-        )
-        gathered.append(
-            (lax.ppermute(out1, "mem", ring("mem", 1)), lax.ppermute(out3, "mem", ring("mem", -1)))
-        )
-    for c in range(CHUNKS):
-        enter, leave, lanes, _, _ = arrived[c]
+        field, enter, leave, lanes = states[c]
         extra = () if result is None else (result,)
+        full_specs = quarter_specs(c, 0, 0)
         result = call(
-            functools.partial(third_kernel, (c, in_chunk, steps, scale)),
-            "third_products",
-            (where, fields[c], perturbation, enter, leave, lanes, *gathered[c], *extra),
-            [quarter_field(0), quarter_spread(0, c), *row_pair, whole(piece.shape), whole(piece.shape)]
+            functools.partial(last_kernel, sizes_of(c), scale),
+            "products_here",
+            (where, enter, leave, lanes, field, perturbation, *moved[c], *extra),
+            [row_spec, row_spec, whole(table_wide.shape), *full_specs]
+            + [first_half, last_half, first_half, last_half]
             + [pl.BlockSpec(memory_space=pl.ANY)] * len(extra),
             sds((levels // quarters, rows, cols), F32),
-            pl.BlockSpec((steps, rows, cols), lambda g, _, c=c: (c, 0, 0)),
-            aliases={8: 0} if extra else None,
+            pl.BlockSpec((PRODUCT_STEP, rows, cols), lambda g, _, c=c: (c * 2 * per_half + g, 0, 0)),
+            grid=(2 * per_half,),
+            aliases={10: 0} if extra else None,
             cost=cost(steps * plane * 8, steps * plane * 14),
         )
     return result

time: 210 us -> 126 us (0.60)
  starting transfers between devices: 77.3 us -> 36.1 us
  Pallas kernels: 97.3 us -> 66.3 us
  waiting for transfers between devices: 29.1 us -> 17.9 us
    ppermute x44 -> x20, starting transfers between devices: 73.8 us -> 32.6 us  [the longest x6 9.93 us: per_device(): lax.ppermute(s, 'lon', to_pair(i + 1))]
    pallas_call x18 -> x16, Pallas kernels: 97.3 us -> 66.3 us  [call(): pl.pallas_call(kernel, out_shape=outputs, grid_spec=pltpu.PrefetchScalarG...]
    ppermute x44 -> x20, waiting for transfers between devices: 29.1 us -> 17.9 us  [the longest x6 6.71 us: per_device(): lax.ppermute(s, 'lon', to_pair(i + 1))]
    unnamed x12 -> x8, local copies, waits for them, and re-layouts: 4.39 us -> 3.04 us
  transfers between devices with their start and end apart: 47 -> 23, of which waited for: 5 -> 10; matrix products, arithmetic and copies ran while one was open for 0% -> 0% of each run, Pallas kernels for 25% -> 27%
where the time goes in v2:
time: 126 us; the launch traced here: 125 us
  Pallas kernels  66.3 us (53%)
  starting transfers between devices  36.1 us (29%)
  waiting for transfers between devices  17.9 us (14%)
  local copies, waits for them, and re-layouts  3.79 us (3%)
    pallas_call x16, Pallas kernels, call(): pl.pallas_call(kernel, out_shape=outputs, grid_spec=pltpu.PrefetchScalarG...  66.3 us
    ppermute x6, starting transfers between devices, per_device(): lax.ppermute(s, 'lon', to_pair(i + 1))  9.93 us
    ppermute x2, starting transfers between devices, per_device(): partner = lax.ppermute(edge, 'lon', to_partner)  7.27 us
    ppermute x6, waiting for transfers between devices, per_device(): lax.ppermute(s, 'lon', to_pair(i + 1))  6.71 us
    ppermute x2, starting transfers between devices, per_device(): lax.ppermute(one_down, 'mem', down)  5.22 us
    ppermute x2, waiting for transfers between devices, per_device(): partner = lax.ppermute(edge, 'lon', to_partner)  5.19 us
    ppermute x2, starting transfers between devices, per_device(): lax.ppermute(two_down, 'mem', down)  4.53 us
    ppermute x2, waiting for transfers between devices, per_device(): lax.ppermute(sum_down, 'mem', down)  3.79 us
  transfers between devices with their start and end apart: 23, of which 10 were waited for; matrix products, arithmetic and copies ran while one was open for 0% of the time, Pallas kernels for 27%

profile of v2, /device:TPU:0, one launch (start us, length us, event | category | flops | bytes accessed | tf_op | source)
XLA Modules:
  0.0 124.9 jit_solution(6804078583899220422)
XLA Ops:
  0.7 0.8 concatenate.3.where_ref
  1.4 0.9 copy-done
  2.3 9.7 %vertical_columns.1 = (bf16[64,96,384]{2,1,0:T(8,128)(2,1)S(1)}, f32[96,64]{1,0:T(8,128)S(1)}, f32[96,64]{1,0:T(8,128)S(1)}, f32[96,64]{1,0:T(8,128)S(1)}, f32[9...) custom-call(s32[40]{0:T(128)S(1)} %concatenate.3.where_ref, bf16[1,64,96,384]{3,2,1,0:T(8,128)(2,1)} %control_ref.1, ...), custom_call_target="tpu_custom_call" | custom-call | flops 2415919104 | bytes 9437184 | tf_op jit(solution)/shard_map/vertical_columns/pallas_call | solution.py:403
  12.0 2.1 %copy-done.3 = bf16[64,96,384]{2,1,0:T(8,128)(2,1)} copy-done((bf16[64,96,384]{2,1,0:T(8,128)(2,1)}, bf16[64,96,384]{2,1,0:T(8,128)(2,1)S(1)}, u32[]{:S(2)}) %copy-start.3) | copy-done | bytes 4718616
  14.2 2.0 %collective-permute-start.1 = (f32[96,64]{1,0:T(8,128)S(1)}, f32[96,64]{1,0:T(8,128)S(1)}, u32[]{:S(2)}, u32[]{:S(2)}) collective-permute-start(f32[96,64]{1,0:T(8,128)S(1)} %get-tuple-element.50), channel_id=1, source_target_pairs={{0,16},{8,24},{16,0},{24,8},{1,17},{9,25},{17,1},{25,9},{2,18},{10... | collective-permute-start | bytes 73736 | tf_op jit(solution)/shard_map/ppermute | solution.py:471
  16.2 1.4 %collective-permute-start.2 = (f32[96,64]{1,0:T(8,128)S(1)}, f32[96,64]{1,0:T(8,128)S(1)}, u32[]{:S(2)}, u32[]{:S(2)}) collective-permute-start(f32[96,64]{1,0:T(8,128)S(1)} %get-tuple-element.51), channel_id=1, source_target_pairs={{0,24},{8,0},{16,8},{24,16},{1,25},{9,1},{17,9},{25,17},{2,26},{10... | collective-permute-start | bytes 73736 | tf_op jit(solution)/shard_map/ppermute | solution.py:471
  17.6 2.7 %row_terms.1 = (f32[96,64]{1,0:T(8,128)S(1)}, f32[96,64]{1,0:T(8,128)S(1)}, f32[64,96]{1,0:T(8,128)S(1)}, f32[64,96]{1,0:T(8,128)S(1)}, f32[64,128]{1,0:T(8,128)S(1)}) custom-call(s32[40]{0:T(128)S(1)} %concatenate.3.where_ref, f32[32,768]{1,0:T(8,128)S(1)} %copy-done.1), custom_call_target="tpu_custom_call" | custom-call | flops 452984832 | bytes 1048576 | tf_op jit(solution)/shard_map/row_terms/pallas_call | solution.py:403
  20.4 15.0 %zonal_rows.3 = (f32[32,96,384]{2,1,0:T(8,128)S(1)}, f32[2,32,384]{2,1,0:T(8,128)S(1)}) custom-call(s32[40]{0:T(128)S(1)} %concatenate.3.where_ref, bf16[64,96,384]{2,1,0:T(8,128)(2,1)} %copy-done.3, f32[96,64]{1,0:T(8,128)S(1)} %get-tuple-element.46.decay_ref, f32[96,64]{1,0:T(8,128)S(1)} %get-tuple-element.47.gain_ref, ...), custom_call_target="tpu_custom_call" | custom-call | flops 2415919104 | bytes 7077888 | tf_op jit(solution)/shard_map/zonal_rows/pallas_call | solution.py:403
  35.4 3.7 %collective-permute-start.13 = (f32[2,32,384]{2,1,0:T(8,128)S(1)}, f32[2,32,384]{2,1,0:T(8,128)S(1)}, u32[]{:S(2)}, u32[]{:S(2)}) collective-permute-start(f32[2,32,384]{2,1,0:T(8,128)S(1)} %get-tuple-element.71.own_ref), channel_id=1, source_target_pairs={{0,1},{1,0},{2,3},{3,2},{4,5},{5,4},{6,7},{7,6},{8,9},{9,8},{10,11... | collective-permute-start | bytes 294920 | tf_op jit(solution)/shard_map/ppermute | solution.py:547
  39.1 2.6 %collective-permute-done.13.got_ref = f32[2,32,384]{2,1,0:T(8,128)S(1)} collective-permute-done((f32[2,32,384]{2,1,0:T(8,128)S(1)}, f32[2,32,384]{2,1,0:T(8,128)S(1)}, u32[]{:S(2)}, u32[]{:S(2)}) %collective-permute-start.13) | collective-permute-done | bytes 98336 | tf_op jit(solution)/shard_map/ppermute | solution.py:547
  41.7 0.6 pair_ends.3
  42.3 1.6 %collective-permute-start.14 = (f32[32,384]{1,0:T(8,128)S(1)}, f32[32,384]{1,0:T(8,128)S(1)}, u32[]{:S(2)}, u32[]{:S(2)}) collective-permute-start(f32[32,384]{1,0:T(8,128)S(1)} %get-tuple-element.72), channel_id=1, source_target_pairs={{0,2},{1,3},{2,4},{3,5},{4,6},{5,7},{6,0},{7,1},{8,10},{9,11},{10,... | collective-permute-start | bytes 147464 | tf_op jit(solution)/shard_map/ppermute | solution.py:556
  43.9 2.7 %collective-permute-start.15 = (f32[32,384]{1,0:T(8,128)S(1)}, f32[32,384]{1,0:T(8,128)S(1)}, u32[]{:S(2)}, u32[]{:S(2)}) collective-permute-start(f32[32,384]{1,0:T(8,128)S(1)} %get-tuple-element.73), channel_id=1, source_target_pairs={{0,4},{1,5},{2,6},{3,7},{4,0},{5,1},{6,2},{7,3},{8,12},{9,13},{10,... | collective-permute-start | bytes 147464 | tf_op jit(solution)/shard_map/ppermute | solution.py:556
  46.6 1.4 %collective-permute-start.16 = (f32[32,384]{1,0:T(8,128)S(1)}, f32[32,384]{1,0:T(8,128)S(1)}, u32[]{:S(2)}, u32[]{:S(2)}) collective-permute-start(f32[32,384]{1,0:T(8,128)S(1)} %get-tuple-element.74), channel_id=1, source_target_pairs={{0,6},{1,7},{2,0},{3,1},{4,2},{5,3},{6,4},{7,5},{8,14},{9,15},{10,... | collective-permute-start | bytes 147464 | tf_op jit(solution)/shard_map/ppermute | solution.py:556
  48.0 1.4 %collective-permute-done.15.got2_ref = f32[32,384]{1,0:T(8,128)S(1)} collective-permute-done((f32[32,384]{1,0:T(8,128)S(1)}, f32[32,384]{1,0:T(8,128)S(1)}, u32[]{:S(2)}, u32[]{:S(2)}) %collective-permute-start.15) | collective-permute-done | bytes 49184 | tf_op jit(solution)/shard_map/ppermute | solution.py:556
  49.5 1.2 collective-permute-done.16.got3_ref
  50.7 0.7 entering.3
  51.4 2.1 %products_two_away.3 = (bf16[4,96,384]{2,1,0:T(8,128)(2,1)S(1)}, bf16[4,96,384]{2,1,0:T(8,128)(2,1)S(1)}) custom-call(s32[40]{0:T(128)S(1)} %concatenate.3.where_ref, f32[32,384]{1,0:T(8,128)S(1)} %get-tuple-element.75.enter_ref, f32[32,384]{1,0:T(8,128)S(1)} %get-tuple-element.76.leave_ref, f32[96,128]{1,0:T(8,128)S(1)} %get-tuple-element.77.table_ref, ...), custom_call_target="tpu_custom_call" | custom-call | flops 2359296 | bytes 2359296 | tf_op jit(solution)/shard_map/products_two_away/pallas_call | solution.py:403
  53.5 1.6 %collective-permute-start.17 = (bf16[4,96,384]{2,1,0:T(8,128)(2,1)S(1)}, bf16[4,96,384]{2,1,0:T(8,128)(2,1)S(1)}, u32[]{:S(2)}, u32[]{:S(2)}) collective-permute-start(bf16[4,96,384]{2,1,0:T(8,128)(2,1)S(1)} %get-tuple-element.79), channel_id=1, source_target_pairs={{0,32},{32,64},{64,96},{96,0},{1,33},{33,65},{65,97},{97,1},{2,34}... | collective-permute-start | bytes 884744 | tf_op jit(solution)/shard_map/ppermute | solution.py:571
  55.1 1.7 %collective-permute-start.18 = (bf16[4,96,384]{2,1,0:T(8,128)(2,1)S(1)}, bf16[4,96,384]{2,1,0:T(8,128)(2,1)S(1)}, u32[]{:S(2)}, u32[]{:S(2)}) collective-permute-start(bf16[4,96,384]{2,1,0:T(8,128)(2,1)S(1)} %get-tuple-element.80), channel_id=1, source_target_pairs={{0,96},{32,0},{64,32},{96,64},{1,97},{33,1},{65,33},{97,65},{2,98}... | collective-permute-start | bytes 884744 | tf_op jit(solution)/shard_map/ppermute | solution.py:571
  56.8 15.0 %zonal_rows.2 = (f32[32,96,384]{2,1,0:T(8,128)S(1)}, f32[2,32,384]{2,1,0:T(8,128)S(1)}) custom-call(s32[40]{0:T(128)S(1)} %concatenate.3.where_ref, bf16[64,96,384]{2,1,0:T(8,128)(2,1)} %copy-done.3, f32[96,64]{1,0:T(8,128)S(1)} %get-tuple-element.46.decay_ref, f32[96,64]{1,0:T(8,128)S(1)} %get-tuple-element.47.gain_ref, ...), custom_call_target="tpu_custom_call" | custom-call | flops 2415919104 | bytes 7077888 | tf_op jit(solution)/shard_map/zonal_rows/pallas_call | solution.py:403
  71.8 3.6 %collective-permute-start.3 = (f32[2,32,384]{2,1,0:T(8,128)S(1)}, f32[2,32,384]{2,1,0:T(8,128)S(1)}, u32[]{:S(2)}, u32[]{:S(2)}) collective-permute-start(f32[2,32,384]{2,1,0:T(8,128)S(1)} %get-tuple-element.57.own_ref), channel_id=1, source_target_pairs={{0,1},{1,0},{2,3},{3,2},{4,5},{5,4},{6,7},{7,6},{8,9},{9,8},{10,11... | collective-permute-start | bytes 294920 | tf_op jit(solution)/shard_map/ppermute | solution.py:547
  75.4 2.6 %collective-permute-done.3.got_ref = f32[2,32,384]{2,1,0:T(8,128)S(1)} collective-permute-done((f32[2,32,384]{2,1,0:T(8,128)S(1)}, f32[2,32,384]{2,1,0:T(8,128)S(1)}, u32[]{:S(2)}, u32[]{:S(2)}) %collective-permute-start.3) | collective-permute-done | bytes 98336 | tf_op jit(solution)/shard_map/ppermute | solution.py:547
  78.0 0.6 pair_ends.2
  78.7 0.5 collective-permute-start.4
  79.1 3.7 %collective-permute-start.5 = (f32[32,384]{1,0:T(8,128)S(1)}, f32[32,384]{1,0:T(8,128)S(1)}, u32[]{:S(2)}, u32[]{:S(2)}) collective-permute-start(f32[32,384]{1,0:T(8,128)S(1)} %get-tuple-element.59), channel_id=1, source_target_pairs={{0,4},{1,5},{2,6},{3,7},{4,0},{5,1},{6,2},{7,3},{8,12},{9,13},{10,... | collective-permute-start | bytes 147464 | tf_op jit(solution)/shard_map/ppermute | solution.py:556
  82.9 1.2 collective-permute-done.4.got1_ref
  84.0 1.4 %collective-permute-done.5.got2_ref = f32[32,384]{1,0:T(8,128)S(1)} collective-permute-done((f32[32,384]{1,0:T(8,128)S(1)}, f32[32,384]{1,0:T(8,128)S(1)}, u32[]{:S(2)}, u32[]{:S(2)}) %collective-permute-start.5) | collective-permute-done | bytes 49184 | tf_op jit(solution)/shard_map/ppermute | solution.py:556
  85.4 1.5 %collective-permute-done.6.got3_ref = f32[32,384]{1,0:T(8,128)S(1)} collective-permute-done((f32[32,384]{1,0:T(8,128)S(1)}, f32[32,384]{1,0:T(8,128)S(1)}, u32[]{:S(2)}, u32[]{:S(2)}) %collective-permute-start.6) | collective-permute-done | bytes 49184 | tf_op jit(solution)/shard_map/ppermute | solution.py:556
  86.9 0.7 entering.2
  87.6 2.1 %products_two_away.2 = (bf16[4,96,384]{2,1,0:T(8,128)(2,1)S(1)}, bf16[4,96,384]{2,1,0:T(8,128)(2,1)S(1)}) custom-call(s32[40]{0:T(128)S(1)} %concatenate.3.where_ref, f32[32,384]{1,0:T(8,128)S(1)} %get-tuple-element.61.enter_ref, f32[32,384]{1,0:T(8,128)S(1)} %get-tuple-element.62.leave_ref, f32[96,128]{1,0:T(8,128)S(1)} %get-tuple-element.63.table_ref, ...), custom_call_target="tpu_custom_call" | custom-call | flops 2359296 | bytes 2359296 | tf_op jit(solution)/shard_map/products_two_away/pallas_call | solution.py:403
  89.7 0.4 collective-permute-start.7
  90.1 2.9 %collective-permute-start.8 = (bf16[4,96,384]{2,1,0:T(8,128)(2,1)S(1)}, bf16[4,96,384]{2,1,0:T(8,128)(2,1)S(1)}, u32[]{:S(2)}, u32[]{:S(2)}) collective-permute-start(bf16[4,96,384]{2,1,0:T(8,128)(2,1)S(1)} %get-tuple-element.66), channel_id=1, source_target_pairs={{0,96},{32,0},{64,32},{96,64},{1,97},{33,1},{65,33},{97,65},{2,98}... | collective-permute-start | bytes 884744 | tf_op jit(solution)/shard_map/ppermute | solution.py:571
  93.0 2.1 %products_one_away.3 = (bf16[4,96,384]{2,1,0:T(8,128)(2,1)S(1)}, bf16[4,96,384]{2,1,0:T(8,128)(2,1)S(1)}) custom-call(s32[40]{0:T(128)S(1)} %concatenate.3.where_ref, f32[32,384]{1,0:T(8,128)S(1)} %get-tuple-element.75.enter_ref, f32[32,384]{1,0:T(8,128)S(1)} %get-tuple-element.76.leave_ref, f32[96,128]{1,0:T(8,128)S(1)} %get-tuple-element.77.table_ref, ...), custom_call_target="tpu_custom_call" | custom-call | flops 2359296 | bytes 2359296 | tf_op jit(solution)/shard_map/products_one_away/pallas_call | solution.py:403
  95.1 0.1 collective-permute-start.20
  95.2 3.2 %collective-permute-start.21 = (bf16[4,96,384]{2,1,0:T(8,128)(2,1)S(1)}, bf16[4,96,384]{2,1,0:T(8,128)(2,1)S(1)}, u32[]{:S(2)}, u32[]{:S(2)}) collective-permute-start(bf16[4,96,384]{2,1,0:T(8,128)(2,1)S(1)} %get-tuple-element.83), channel_id=1, source_target_pairs={{0,96},{32,0},{64,32},{96,64},{1,97},{33,1},{65,33},{97,65},{2,98}... | collective-permute-start | bytes 884744 | tf_op jit(solution)/shard_map/ppermute | solution.py:573
  98.4 2.2 %products_added.3 = (bf16[4,96,384]{2,1,0:T(8,128)(2,1)S(1)}, bf16[4,96,384]{2,1,0:T(8,128)(2,1)S(1)}) custom-call(s32[40]{0:T(128)S(1)} %concatenate.3.where_ref, f32[32,384]{1,0:T(8,128)S(1)} %get-tuple-element.75.enter_ref, f32[32,384]{1,0:T(8,128)S(1)} %get-tuple-element.76.leave_ref, f32[96,128]{1,0:T(8,128)S(1)} %get-tuple-element.77.table_ref, ...), custom_call_target="tpu_custom_call" | custom-call | flops 2359296 | bytes 2359296 | tf_op jit(solution)/shard_map/products_added/pallas_call | solution.py:403
  100.6 0.1 collective-permute-start.19
  100.7 2.1 %products_one_away.2 = (bf16[4,96,384]{2,1,0:T(8,128)(2,1)S(1)}, bf16[4,96,384]{2,1,0:T(8,128)(2,1)S(1)}) custom-call(s32[40]{0:T(128)S(1)} %concatenate.3.where_ref, f32[32,384]{1,0:T(8,128)S(1)} %get-tuple-element.61.enter_ref, f32[32,384]{1,0:T(8,128)S(1)} %get-tuple-element.62.leave_ref, f32[96,128]{1,0:T(8,128)S(1)} %get-tuple-element.63.table_ref, ...), custom_call_target="tpu_custom_call" | custom-call | flops 2359296 | bytes 2359296 | tf_op jit(solution)/shard_map/products_one_away/pallas_call | solution.py:403
  102.9 3.3 %collective-permute-start.22 = (bf16[4,96,384]{2,1,0:T(8,128)(2,1)S(1)}, bf16[4,96,384]{2,1,0:T(8,128)(2,1)S(1)}, u32[]{:S(2)}, u32[]{:S(2)}) collective-permute-start(bf16[4,96,384]{2,1,0:T(8,128)(2,1)S(1)} %get-tuple-element.84), channel_id=1, source_target_pairs={{0,96},{32,0},{64,32},{96,64},{1,97},{33,1},{65,33},{97,65},{2,98}... | collective-permute-start | bytes 884744 | tf_op jit(solution)/shard_map/ppermute | solution.py:575
  106.2 2.2 %products_added.2 = (bf16[4,96,384]{2,1,0:T(8,128)(2,1)S(1)}, bf16[4,96,384]{2,1,0:T(8,128)(2,1)S(1)}) custom-call(s32[40]{0:T(128)S(1)} %concatenate.3.where_ref, f32[32,384]{1,0:T(8,128)S(1)} %get-tuple-element.61.enter_ref, f32[32,384]{1,0:T(8,128)S(1)} %get-tuple-element.62.leave_ref, f32[96,128]{1,0:T(8,128)S(1)} %get-tuple-element.63.table_ref, ...), custom_call_target="tpu_custom_call" | custom-call | flops 2359296 | bytes 2359296 | tf_op jit(solution)/shard_map/products_added/pallas_call | solution.py:403
  108.4 2.0 %collective-permute-start.11 = (bf16[4,96,384]{2,1,0:T(8,128)(2,1)S(1)}, bf16[4,96,384]{2,1,0:T(8,128)(2,1)S(1)}, u32[]{:S(2)}, u32[]{:S(2)}) collective-permute-start(bf16[4,96,384]{2,1,0:T(8,128)(2,1)S(1)} %get-tuple-element.69), channel_id=1, source_target_pairs={{0,96},{32,0},{64,32},{96,64},{1,97},{33,1},{65,33},{97,65},{2,98}... | collective-permute-start | bytes 884744 | tf_op jit(solution)/shard_map/ppermute | solution.py:573
  110.4 0.1 collective-permute-start.12
  110.5 2.2 %collective-permute-done.19.a0_ref = bf16[4,96,384]{2,1,0:T(8,128)(2,1)S(1)} collective-permute-done((bf16[4,96,384]{2,1,0:T(8,128)(2,1)S(1)}, bf16[4,96,384]{2,1,0:T(8,128)(2,1)S(1)}, u32[]{:S(2)}, u32[]{:S(2)}) %collective-permute-start.19) | collective-permute-done | bytes 294944 | tf_op jit(solution)/shard_map/ppermute | solution.py:575
  112.7 1.0 collective-permute-done.22.b1_ref
  113.7 4.2 %products_here.2.rest_0_ = f32[16,96,384]{2,1,0:T(8,128)} custom-call(s32[40]{0:T(128)S(1)} %concatenate.3.where_ref, f32[32,384]{1,0:T(8,128)S(1)} %get-tuple-element.75.enter_ref, f32[32,384]{1,0:T(8,128)S(1)} %get-tuple-element.76.leave_ref, f32[96,128]{1,0:T(8,128)S(1)} %get-tuple-element.77.table_ref, ...), custom_call_target="tpu_custom_call" | custom-call | flops 2359296 | bytes 4128768 | tf_op jit(solution)/shard_map/products_here/pallas_call | solution.py:403
  117.9 2.8 %collective-permute-done.12.b1_ref = bf16[4,96,384]{2,1,0:T(8,128)(2,1)S(1)} collective-permute-done((bf16[4,96,384]{2,1,0:T(8,128)(2,1)S(1)}, bf16[4,96,384]{2,1,0:T(8,128)(2,1)S(1)}, u32[]{:S(2)}, u32[]{:S(2)}) %collective-permute-start.12) | collective-permute-done | bytes 294944 | tf_op jit(solution)/shard_map/ppermute | solution.py:575
  120.7 4.2 %products_here.3 = f32[16,96,384]{2,1,0:T(8,128)} custom-call(s32[40]{0:T(128)S(1)} %concatenate.3.where_ref, f32[32,384]{1,0:T(8,128)S(1)} %get-tuple-element.61.enter_ref, f32[32,384]{1,0:T(8,128)S(1)} %get-tuple-element.62.leave_ref, f32[96,128]{1,0:T(8,128)S(1)} %get-tuple-element.63.table_ref, ...), custom_call_target="tpu_custom_call", output_to_operand_aliasing={{}: (10, {})} | custom-call | flops 2359296 | bytes 4128768 | tf_op jit(solution)/shard_map/products_here/pallas_call | solution.py:403
  (23 shorter events, 0.2 us)
Async XLA Ops:
  1.4 0.9 copy-start
  2.3 15.3 %copy-start.1 = (f32[32,768]{1,0:T(8,128)S(1)}, f32[32,768]{1,0:T(8,128)}, u32[]{:S(2)}) copy-start(f32[32,768]{1,0:T(8,128)} %rate_ref.3) | copy-start | bytes 294916
  2.3 18.1 %copy-start.2 = (bf16[256,256]{1,0:T(8,128)(2,1)S(1)}, bf16[256,256]{1,0:T(8,128)(2,1)}, u32[]{:S(2)}) copy-start(bf16[256,256]{1,0:T(8,128)(2,1)} %constant.14.clone.triangle_ref) | copy-start | bytes 393220
  12.0 2.1 %copy-start.3 = (bf16[64,96,384]{2,1,0:T(8,128)(2,1)}, bf16[64,96,384]{2,1,0:T(8,128)(2,1)S(1)}, u32[]{:S(2)}) copy-start(bf16[64,96,384]{2,1,0:T(8,128)(2,1)S(1)} %get-tuple-element.45.column_ref) | copy-start | bytes 14155780
  14.2 6.2 %collective-permute-start = (f32[96,64]{1,0:T(8,128)S(1)}, f32[96,64]{1,0:T(8,128)S(1)}, u32[]{:S(2)}, u32[]{:S(2)}) collective-permute-start(f32[96,64]{1,0:T(8,128)S(1)} %get-tuple-element.49), channel_id=1, source_target_pairs={{0,8},{8,16},{16,24},{24,0},{1,9},{9,17},{17,25},{25,1},{2,10},{10... | collective-permute-start | bytes 73736 | tf_op jit(solution)/shard_map/ppermute | solution.py:471
  14.2 6.2 %collective-permute-start.1 = (f32[96,64]{1,0:T(8,128)S(1)}, f32[96,64]{1,0:T(8,128)S(1)}, u32[]{:S(2)}, u32[]{:S(2)}) collective-permute-start(f32[96,64]{1,0:T(8,128)S(1)} %get-tuple-element.50), channel_id=1, source_target_pairs={{0,16},{8,24},{16,0},{24,8},{1,17},{9,25},{17,1},{25,9},{2,18},{10... | collective-permute-start | bytes 73736 | tf_op jit(solution)/shard_map/ppermute | solution.py:471
  16.2 4.2 %collective-permute-start.2 = (f32[96,64]{1,0:T(8,128)S(1)}, f32[96,64]{1,0:T(8,128)S(1)}, u32[]{:S(2)}, u32[]{:S(2)}) collective-permute-start(f32[96,64]{1,0:T(8,128)S(1)} %get-tuple-element.51), channel_id=1, source_target_pairs={{0,24},{8,0},{16,8},{24,16},{1,25},{9,1},{17,9},{25,17},{2,26},{10... | collective-permute-start | bytes 73736 | tf_op jit(solution)/shard_map/ppermute | solution.py:471
  35.4 6.3 %collective-permute-start.13 = (f32[2,32,384]{2,1,0:T(8,128)S(1)}, f32[2,32,384]{2,1,0:T(8,128)S(1)}, u32[]{:S(2)}, u32[]{:S(2)}) collective-permute-start(f32[2,32,384]{2,1,0:T(8,128)S(1)} %get-tuple-element.71.own_ref), channel_id=1, source_target_pairs={{0,1},{1,0},{2,3},{3,2},{4,5},{5,4},{6,7},{7,6},{8,9},{9,8},{10,11... | collective-permute-start | bytes 294920 | tf_op jit(solution)/shard_map/ppermute | solution.py:547
  42.3 5.7 %collective-permute-start.14 = (f32[32,384]{1,0:T(8,128)S(1)}, f32[32,384]{1,0:T(8,128)S(1)}, u32[]{:S(2)}, u32[]{:S(2)}) collective-permute-start(f32[32,384]{1,0:T(8,128)S(1)} %get-tuple-element.72), channel_id=1, source_target_pairs={{0,2},{1,3},{2,4},{3,5},{4,6},{5,7},{6,0},{7,1},{8,10},{9,11},{10,... | collective-permute-start | bytes 147464 | tf_op jit(solution)/shard_map/ppermute | solution.py:556
  43.9 5.6 %collective-permute-start.15 = (f32[32,384]{1,0:T(8,128)S(1)}, f32[32,384]{1,0:T(8,128)S(1)}, u32[]{:S(2)}, u32[]{:S(2)}) collective-permute-start(f32[32,384]{1,0:T(8,128)S(1)} %get-tuple-element.73), channel_id=1, source_target_pairs={{0,4},{1,5},{2,6},{3,7},{4,0},{5,1},{6,2},{7,3},{8,12},{9,13},{10,... | collective-permute-start | bytes 147464 | tf_op jit(solution)/shard_map/ppermute | solution.py:556
  46.6 4.1 %collective-permute-start.16 = (f32[32,384]{1,0:T(8,128)S(1)}, f32[32,384]{1,0:T(8,128)S(1)}, u32[]{:S(2)}, u32[]{:S(2)}) collective-permute-start(f32[32,384]{1,0:T(8,128)S(1)} %get-tuple-element.74), channel_id=1, source_target_pairs={{0,6},{1,7},{2,0},{3,1},{4,2},{5,3},{6,4},{7,5},{8,14},{9,15},{10,... | collective-permute-start | bytes 147464 | tf_op jit(solution)/shard_map/ppermute | solution.py:556
  53.5 41.7 %collective-permute-start.17 = (bf16[4,96,384]{2,1,0:T(8,128)(2,1)S(1)}, bf16[4,96,384]{2,1,0:T(8,128)(2,1)S(1)}, u32[]{:S(2)}, u32[]{:S(2)}) collective-permute-start(bf16[4,96,384]{2,1,0:T(8,128)(2,1)S(1)} %get-tuple-element.79), channel_id=1, source_target_pairs={{0,32},{32,64},{64,96},{96,0},{1,33},{33,65},{65,97},{97,1},{2,34}... | collective-permute-start | bytes 884744 | tf_op jit(solution)/shard_map/ppermute | solution.py:571
  55.1 43.3 %collective-permute-start.18 = (bf16[4,96,384]{2,1,0:T(8,128)(2,1)S(1)}, bf16[4,96,384]{2,1,0:T(8,128)(2,1)S(1)}, u32[]{:S(2)}, u32[]{:S(2)}) collective-permute-start(bf16[4,96,384]{2,1,0:T(8,128)(2,1)S(1)} %get-tuple-element.80), channel_id=1, source_target_pairs={{0,96},{32,0},{64,32},{96,64},{1,97},{33,1},{65,33},{97,65},{2,98}... | collective-permute-start | bytes 884744 | tf_op jit(solution)/shard_map/ppermute | solution.py:571
  71.8 6.2 %collective-permute-start.3 = (f32[2,32,384]{2,1,0:T(8,128)S(1)}, f32[2,32,384]{2,1,0:T(8,128)S(1)}, u32[]{:S(2)}, u32[]{:S(2)}) collective-permute-start(f32[2,32,384]{2,1,0:T(8,128)S(1)} %get-tuple-element.57.own_ref), channel_id=1, source_target_pairs={{0,1},{1,0},{2,3},{3,2},{4,5},{5,4},{6,7},{7,6},{8,9},{9,8},{10,11... | collective-permute-start | bytes 294920 | tf_op jit(solution)/shard_map/ppermute | solution.py:547
  78.7 5.4 %collective-permute-start.4 = (f32[32,384]{1,0:T(8,128)S(1)}, f32[32,384]{1,0:T(8,128)S(1)}, u32[]{:S(2)}, u32[]{:S(2)}) collective-permute-start(f32[32,384]{1,0:T(8,128)S(1)} %get-tuple-element.58), channel_id=1, source_target_pairs={{0,2},{1,3},{2,4},{3,5},{4,6},{5,7},{6,0},{7,1},{8,10},{9,11},{10,... | collective-permute-start | bytes 147464 | tf_op jit(solution)/shard_map/ppermute | solution.py:556
  79.1 6.3 %collective-permute-start.5 = (f32[32,384]{1,0:T(8,128)S(1)}, f32[32,384]{1,0:T(8,128)S(1)}, u32[]{:S(2)}, u32[]{:S(2)}) collective-permute-start(f32[32,384]{1,0:T(8,128)S(1)} %get-tuple-element.59), channel_id=1, source_target_pairs={{0,4},{1,5},{2,6},{3,7},{4,0},{5,1},{6,2},{7,3},{8,12},{9,13},{10,... | collective-permute-start | bytes 147464 | tf_op jit(solution)/shard_map/ppermute | solution.py:556
  82.8 4.1 %collective-permute-start.6 = (f32[32,384]{1,0:T(8,128)S(1)}, f32[32,384]{1,0:T(8,128)S(1)}, u32[]{:S(2)}, u32[]{:S(2)}) collective-permute-start(f32[32,384]{1,0:T(8,128)S(1)} %get-tuple-element.60), channel_id=1, source_target_pairs={{0,6},{1,7},{2,0},{3,1},{4,2},{5,3},{6,4},{7,5},{8,14},{9,15},{10,... | collective-permute-start | bytes 147464 | tf_op jit(solution)/shard_map/ppermute | solution.py:556
  89.7 13.1 %collective-permute-start.7 = (bf16[4,96,384]{2,1,0:T(8,128)(2,1)S(1)}, bf16[4,96,384]{2,1,0:T(8,128)(2,1)S(1)}, u32[]{:S(2)}, u32[]{:S(2)}) collective-permute-start(bf16[4,96,384]{2,1,0:T(8,128)(2,1)S(1)} %get-tuple-element.65), channel_id=1, source_target_pairs={{0,32},{32,64},{64,96},{96,0},{1,33},{33,65},{65,97},{97,1},{2,34}... | collective-permute-start | bytes 884744 | tf_op jit(solution)/shard_map/ppermute | solution.py:571
  90.1 12.8 %collective-permute-start.8 = (bf16[4,96,384]{2,1,0:T(8,128)(2,1)S(1)}, bf16[4,96,384]{2,1,0:T(8,128)(2,1)S(1)}, u32[]{:S(2)}, u32[]{:S(2)}) collective-permute-start(bf16[4,96,384]{2,1,0:T(8,128)(2,1)S(1)} %get-tuple-element.66), channel_id=1, source_target_pairs={{0,96},{32,0},{64,32},{96,64},{1,97},{33,1},{65,33},{97,65},{2,98}... | collective-permute-start | bytes 884744 | tf_op jit(solution)/shard_map/ppermute | solution.py:571
  95.1 13.3 %collective-permute-start.20 = (bf16[4,96,384]{2,1,0:T(8,128)(2,1)S(1)}, bf16[4,96,384]{2,1,0:T(8,128)(2,1)S(1)}, u32[]{:S(2)}, u32[]{:S(2)}) collective-permute-start(bf16[4,96,384]{2,1,0:T(8,128)(2,1)S(1)} %get-tuple-element.82), channel_id=1, source_target_pairs={{0,32},{32,64},{64,96},{96,0},{1,33},{33,65},{65,97},{97,1},{2,34}... | collective-permute-start | bytes 884744 | tf_op jit(solution)/shard_map/ppermute | solution.py:573
  95.2 15.2 %collective-permute-start.21 = (bf16[4,96,384]{2,1,0:T(8,128)(2,1)S(1)}, bf16[4,96,384]{2,1,0:T(8,128)(2,1)S(1)}, u32[]{:S(2)}, u32[]{:S(2)}) collective-permute-start(bf16[4,96,384]{2,1,0:T(8,128)(2,1)S(1)} %get-tuple-element.83), channel_id=1, source_target_pairs={{0,96},{32,0},{64,32},{96,64},{1,97},{33,1},{65,33},{97,65},{2,98}... | collective-permute-start | bytes 884744 | tf_op jit(solution)/shard_map/ppermute | solution.py:573
  100.6 12.0 %collective-permute-start.19 = (bf16[4,96,384]{2,1,0:T(8,128)(2,1)S(1)}, bf16[4,96,384]{2,1,0:T(8,128)(2,1)S(1)}, u32[]{:S(2)}, u32[]{:S(2)}) collective-permute-start(bf16[4,96,384]{2,1,0:T(8,128)(2,1)S(1)} %get-tuple-element.81), channel_id=1, source_target_pairs={{0,32},{32,64},{64,96},{96,0},{1,33},{33,65},{65,97},{97,1},{2,34}... | collective-permute-start | bytes 884744 | tf_op jit(solution)/shard_map/ppermute | solution.py:575
  102.8 15.1 %collective-permute-start.10 = (bf16[4,96,384]{2,1,0:T(8,128)(2,1)S(1)}, bf16[4,96,384]{2,1,0:T(8,128)(2,1)S(1)}, u32[]{:S(2)}, u32[]{:S(2)}) collective-permute-start(bf16[4,96,384]{2,1,0:T(8,128)(2,1)S(1)} %get-tuple-element.68), channel_id=1, source_target_pairs={{0,32},{32,64},{64,96},{96,0},{1,33},{33,65},{65,97},{97,1},{2,34}... | collective-permute-start | bytes 884744 | tf_op jit(solution)/shard_map/ppermute | solution.py:573
  102.9 10.7 %collective-permute-start.22 = (bf16[4,96,384]{2,1,0:T(8,128)(2,1)S(1)}, bf16[4,96,384]{2,1,0:T(8,128)(2,1)S(1)}, u32[]{:S(2)}, u32[]{:S(2)}) collective-permute-start(bf16[4,96,384]{2,1,0:T(8,128)(2,1)S(1)} %get-tuple-element.84), channel_id=1, source_target_pairs={{0,96},{32,0},{64,32},{96,64},{1,97},{33,1},{65,33},{97,65},{2,98}... | collective-permute-start | bytes 884744 | tf_op jit(solution)/shard_map/ppermute | solution.py:575
  108.4 9.5 %collective-permute-start.11 = (bf16[4,96,384]{2,1,0:T(8,128)(2,1)S(1)}, bf16[4,96,384]{2,1,0:T(8,128)(2,1)S(1)}, u32[]{:S(2)}, u32[]{:S(2)}) collective-permute-start(bf16[4,96,384]{2,1,0:T(8,128)(2,1)S(1)} %get-tuple-element.69), channel_id=1, source_target_pairs={{0,96},{32,0},{64,32},{96,64},{1,97},{33,1},{65,33},{97,65},{2,98}... | collective-permute-start | bytes 884744 | tf_op jit(solution)/shard_map/ppermute | solution.py:573
  110.4 10.3 %collective-permute-start.12 = (bf16[4,96,384]{2,1,0:T(8,128)(2,1)S(1)}, bf16[4,96,384]{2,1,0:T(8,128)(2,1)S(1)}, u32[]{:S(2)}, u32[]{:S(2)}) collective-permute-start(bf16[4,96,384]{2,1,0:T(8,128)(2,1)S(1)} %get-tuple-element.70), channel_id=1, source_target_pairs={{0,96},{32,0},{64,32},{96,64},{1,97},{33,1},{65,33},{97,65},{2,98}... | collective-permute-start | bytes 884744 | tf_op jit(solution)/shard_map/ppermute | solution.py:575
  112.7 8.0 %collective-permute-start.9 = (bf16[4,96,384]{2,1,0:T(8,128)(2,1)S(1)}, bf16[4,96,384]{2,1,0:T(8,128)(2,1)S(1)}, u32[]{:S(2)}, u32[]{:S(2)}) collective-permute-start(bf16[4,96,384]{2,1,0:T(8,128)(2,1)S(1)} %get-tuple-element.67), channel_id=1, source_target_pairs={{0,32},{32,64},{64,96},{96,0},{1,33},{33,65},{65,97},{97,1},{2,34}... | collective-permute-start | bytes 884744 | tf_op jit(solution)/shard_map/ppermute | solution.py:575

commit v3 on v2

v3 whole, which is shorter than its diff:
```python
import functools
import math

import jax
import jax.numpy as jnp
import numpy as np
from jax import lax
from jax.experimental import pallas as pl
from jax.experimental.pallas import tpu as pltpu
from jax.sharding import PartitionSpec as P

CHUNKS = ((8, 8),)
LANES = 128
GROUP_AT = 3
BAND_AT = 4
SLAB_AT = 8
ROW_GROUP = 16
FIELD_STEP = 8
PRODUCT_STEP = 4
VMEM_LIMIT = 8 * 1024 * 1024
COLUMN_VMEM_LIMIT = 14 * 1024 * 1024
FIELD_VMEM_LIMIT = 16 * 1024 * 1024

F32 = jnp.float32
BF16 = jnp.bfloat16


def iota(shape, axis):
    return lax.broadcasted_iota(jnp.int32, shape, axis)


def log_decay(rate):
    t = rate / (2.0 - rate)
    s = t * t
    series = 1.0 + s * (1 / 3 + s * (1 / 5 + s * (1 / 7 + s * (1 / 9 + s * (1 / 11 + s / 13)))))
    return -2.0 * t * series


def split3(x):
    hi = x.astype(BF16)
    rest = x - hi.astype(F32)
    mid = rest.astype(BF16)
    return hi, mid, (rest - mid.astype(F32)).astype(BF16)


def split2(x):
    hi = x.astype(BF16)
    return hi, (x - hi.astype(F32)).astype(BF16)


def dot_nn(a, b):
    return lax.dot_general(a, b, (((1,), (0,)), ((), ())), preferred_element_type=F32)


def dot_nt(a, b):
    return lax.dot_general(a, b, (((1,), (1,)), ((), ())), preferred_element_type=F32)


def times_exact(x, zero_one):
    rows = x.shape[0]
    product = dot_nn(jnp.concatenate(split3(x), axis=0), zero_one)
    return product[:rows] + product[rows : 2 * rows] + product[2 * rows :]


def exact_times_t(zero_one, x):
    return sum(dot_nt(zero_one, part) for part in split3(x))


def traced_level(place, levels, quarters):
    level = jnp.zeros_like(place)
    first, begin = 0, 0
    for parts in CHUNKS:
        steps = sum(parts)
        rest = place - first
        quarter = sum((rest >= k * steps).astype(jnp.int32) for k in range(1, quarters))
        here = quarter * (levels // quarters - steps) + rest + begin
        level = jnp.where(rest >= 0, here, level)
        first, begin = first + steps * quarters, begin + steps
    return level


def rates_by_place(slab_levels, rates, levels, quarters):
    slabs = rates.shape[0]
    level = traced_level(iota((levels, slabs), 0), levels, quarters)
    index = jnp.zeros((levels, slabs), jnp.int32)
    end = jnp.int32(0)
    for s in range(slabs):
        end = end + slab_levels[SLAB_AT + s]
        index = index + (level >= end).astype(jnp.int32)
    chosen = (index == iota((levels, slabs), 1)).astype(F32).astype(BF16)
    return sum(dot_nn(chosen, part) for part in split3(rates))


def lane_of(table, lane):
    return jnp.take_along_axis(table, jnp.full(table.shape, lane, jnp.int32), axis=1)


def column_kernel(
    sizes, where_ref, control_ref, rate_ref,
    column_ref, decay_ref, gain_ref, end_ref, send1_ref, send2_ref, send3_ref,
    kron, decay_all, weighted,
):
    levels, rows, cols, quarters, lat_count = sizes
    step = pl.program_id(0)
    lat, lon = where_ref[1], where_ref[2]
    full = levels * 8

    @pl.when(step == 0)
    def _():
        band = where_ref[BAND_AT + where_ref[GROUP_AT]].astype(F32)
        out_level = traced_level(jnp.right_shift(iota((full, full), 0), 3), levels, quarters)
        spacing = out_level - jnp.right_shift(iota((full, full), 1), 3)
        same = jnp.bitwise_and(iota((full, full), 0), 7) == jnp.bitwise_and(iota((full, full), 1), 7)
        ratio = spacing.astype(F32) / band
        weight = jnp.exp(-2.0 * (ratio * ratio))
        keep = jnp.logical_and(same, jnp.abs(spacing).astype(F32) <= band)
        kron[...] = jnp.where(keep, weight, 0.0).astype(BF16)
        level_rates = rates_by_place(where_ref, rate_ref[...], levels, quarters)
        own = iota((rows, rate_ref.shape[1]), 1) == lon * rows + iota((rows, rate_ref.shape[1]), 0)
        rate = exact_times_t(own.astype(F32).astype(BF16), level_rates)
        remain = 1.0 - rate
        decay_all[...] = log_decay(rate)
        decay_ref[...] = decay_all[...]
        gain_ref[...] = jnp.sqrt(rate * (2.0 - rate) / (1.0 + remain * remain))

    block = control_ref[0].astype(F32)
    halves = []
    for half in range(2):
        part = block[:, 8 * half : 8 * half + 8, :].reshape(full, cols).astype(BF16)
        halves.append(dot_nn(kron[...], part).reshape(levels, 8, cols))
    column = jnp.concatenate(halves, axis=1).astype(BF16)
    column_ref[...] = column

    log_a = decay_all[pl.ds(step * ROW_GROUP, ROW_GROUP), :]
    lane = iota((ROW_GROUP, LANES), 1).astype(F32)
    blocks = cols // LANES
    for place in range(levels):
        log_b = jnp.broadcast_to(log_a[:, place : place + 1], (ROW_GROUP, LANES))
        over = jnp.exp(log_b * float(LANES))
        x = column_ref[place].astype(F32)
        parts = [x[:, LANES * b : LANES * (b + 1)] for b in range(blocks)]
        along, against = parts[0], parts[-1]
        for b in range(1, blocks):
            along = parts[b] + over * along
            against = parts[-1 - b] + over * against
        weighted[0, place] = along * jnp.exp(log_b * (LANES - 1.0 - lane))
        weighted[1, place] = against * jnp.exp(log_b * lane)
    place_lane = iota((ROW_GROUP, levels), 1)
    forward = jnp.zeros((ROW_GROUP, levels), F32)
    backward = jnp.zeros((ROW_GROUP, levels), F32)
    for place in range(levels):
        along = jnp.sum(weighted[0, place], axis=1, keepdims=True)
        against = jnp.sum(weighted[1, place], axis=1, keepdims=True)
        forward = jnp.where(place_lane == place, along, forward)
        backward = jnp.where(place_lane == place, against, backward)
    power = (1 + cols * (2 * (lat_count - 1 - lat) + 1)).astype(F32)
    returning = backward - jnp.exp(log_a * power) * forward
    end_ref[...] = forward
    for shift, ref in ((1, send1_ref), (2, send2_ref), (3, send3_ref)):
        ref[...] = jnp.where(lat + shift < lat_count, forward, returning)


def row_kernel(
    sizes, where_ref, rate_ref,
    left_ref, left_sum_ref, right_ref, right_sum_ref, chain_ref,
):
    levels, rows, quarters, lon_count = sizes
    lon = where_ref[2]
    total = rate_ref.shape[1]
    rate = rates_by_place(where_ref, rate_ref[...], levels, quarters)
    remain = 1.0 - rate
    root = jnp.sqrt(rate * (2.0 - rate))
    gain = root * jnp.sqrt(root) / jnp.sqrt(jnp.sqrt(1.0 + remain * remain))
    log_c = log_decay(rate)
    owner = lambda at: jnp.right_shift(at * ((1 << 16) // rows + 1), 16)
    first, second = iota((total, total), 0), iota((total, total), 1)
    same = owner(first) == owner(second)
    upper = jnp.logical_and(same, first <= second).astype(F32).astype(BF16)
    lower = jnp.logical_and(same, first >= second).astype(F32).astype(BF16)
    running = times_exact(log_c, upper)
    before = running - log_c
    weight = gain * jnp.exp(running + before)
    sums = times_exact(weight, lower)
    left = jnp.exp(-before)
    right = gain * jnp.exp(-running)
    own = (iota((rows, total), 1) == lon * rows + iota((rows, total), 0)).astype(F32).astype(BF16)
    own_t = iota((total, LANES), 0) == lon * rows + iota((total, LANES), 1)
    own_t = jnp.logical_and(own_t, iota((total, LANES), 1) < rows).astype(F32).astype(BF16)
    left_ref[...] = exact_times_t(own, left)
    left_sum_ref[...] = exact_times_t(own, left * sums)
    right_ref[...] = times_exact(right, own_t)
    right_sum_ref[...] = times_exact(right * sums, own_t)

    inside = (owner(iota((total, LANES), 0)) == iota((total, LANES), 1)).astype(F32).astype(BF16)
    log_over = times_exact(log_c, inside)
    bounce = times_exact(weight, inside)
    source, target = iota((LANES, LANES), 0), iota((LANES, LANES), 1)
    between = jnp.logical_and(source > lon, source < target).astype(F32).astype(BF16)
    device = iota((levels, LANES), 1)
    beyond = jnp.logical_and(device > lon, device < lon_count)
    echo = jnp.sum(
        jnp.where(beyond, bounce * jnp.exp(2.0 * times_exact(log_over, between)), 0.0),
        axis=1,
        keepdims=True,
    )
    every = jnp.exp(log_over)
    over = jnp.sum(jnp.where(device == lon, every, 0.0), axis=1, keepdims=True)
    partner = jnp.bitwise_xor(lon, 1)
    partner_over = jnp.sum(jnp.where(device == partner, every, 0.0), axis=1, keepdims=True)
    pair, pairs = jnp.right_shift(lon, 1), lon_count // 2
    shift = jnp.bitwise_and(target, 63)
    is_before = pair >= shift
    low = jnp.where(is_before, 2 * (pair - shift) + 1, lon)
    high = jnp.where(is_before, lon, 2 * (pair - shift + pairs))
    path = jnp.logical_and(source > low, source < high).astype(F32).astype(BF16)
    reach = jnp.exp(times_exact(log_over, path))
    shift = jnp.bitwise_and(device, 63)
    counted = jnp.logical_and(shift >= 1, shift < pairs)
    counted = jnp.logical_and(counted, (pair >= shift) == (device < 64))
    chain = jnp.where(counted, reach, 0.0)
    for at, value in ((32, over), (33, echo), (34, partner_over)):
        chain = jnp.where(device == at, value, chain)
    chain_ref[...] = chain


def field_kernel(
    sizes, where_ref, column_ref, decay_ref, gain_ref, end_ref, got1_ref, got2_ref, got3_ref,
    right_ref, right_sum_ref, chain_ref, triangle_ref,
    fields, edge_ref, tables, powers, enters, scaled, sums,
):
    rows, cols, first_place, per_step, lat_count = sizes
    step = pl.program_id(0)
    lat = where_ref[1]
    blocks = cols // LANES

    @pl.when(step == 0)
    def _():
        log_a, gain = decay_ref[...], gain_ref[...]
        enter_left = jnp.zeros(log_a.shape, F32)
        enter_right = jnp.zeros(log_a.shape, F32)
        for shift, ref in ((1, got1_ref), (2, got2_ref), (3, got3_ref)):
            got = ref[...]
            is_left = lat >= shift
            power = jnp.where(is_left, shift - 1, lat_count - 1 - shift) * cols
            scaled = jnp.exp(log_a * power.astype(F32)) * got
            enter_left = enter_left + jnp.where(is_left, scaled, 0.0)
            enter_right = enter_right + jnp.where(is_left, 0.0, scaled)
        leaving = end_ref[...] + jnp.exp(log_a * float(cols)) * enter_left
        power = (1 + 2 * cols * (lat_count - 1 - lat)).astype(F32)
        enter_right = enter_right - jnp.exp(log_a * power) * leaving
        enter_left = gain * jnp.exp(log_a) * enter_left
        enter_right = gain * jnp.exp(log_a * float(LANES)) * enter_right
        tables[0] = jnp.concatenate([log_a, gain], axis=1)
        tables[1] = jnp.concatenate([enter_left, enter_right], axis=1)

    half = tables.shape[2] // 2
    lane = iota((rows, LANES), 1).astype(F32)
    row_number = iota((16, LANES), 0)
    tall = blocks * rows
    place_of = lambda u: first_place + step * per_step + u
    for u in range(per_step):
        log_a = lane_of(tables[0], place_of(u))
        gain = lane_of(tables[0], place_of(u) + half)
        enters[u, 0] = lane_of(tables[1], place_of(u))
        enters[u, 1] = lane_of(tables[1], place_of(u) + half)
        grow = jnp.exp(log_a * lane)
        shrink = jnp.exp(log_a * (-lane))
        powers[u, 0] = grow
        powers[u, 1] = shrink
        powers[u, 2] = jnp.exp(log_a * float(LANES))
        powers[u, 3] = jnp.exp(log_a)
        gain_grow, gain_shrink = gain * grow, gain * shrink
        x = column_ref[u].astype(F32)
        for b in range(blocks):
            part = x[:, LANES * b : LANES * (b + 1)]
            rows_at = slice(u * tall + b * rows, u * tall + (b + 1) * rows)
            for side, factor in enumerate((gain_shrink, gain_grow)):
                high, low = split2(part * factor)
                at = LANES * side
                scaled[rows_at, at : at + LANES] = high
                scaled[rows_at, 2 * LANES + at : 3 * LANES + at] = low
    for u in range(per_step):
        at = slice(u * tall, (u + 1) * tall)
        sums[at, :] = dot_nn(scaled[at, :], triangle_ref[...])
    for u in range(per_step):
        grow, shrink, over, decay = (powers[u, k] for k in range(4))
        at = lambda b: slice(u * tall + b * rows, u * tall + (b + 1) * rows)
        ahead = [grow * sums[at(b), :LANES] for b in range(blocks)]
        behind = [sums[at(b), LANES:] for b in range(blocks)]
        lefts, rights_in = [enters[u, 0]], [enters[u, 1]]
        for b in range(blocks - 1):
            end = jnp.broadcast_to(ahead[b][:, LANES - 1 :], (rows, LANES))
            lefts.append(over * lefts[-1] + decay * end)
        for b in range(blocks - 1, 0, -1):
            first = (
                scaled[at(b), LANES : 2 * LANES].astype(F32)
                + scaled[at(b), 3 * LANES :].astype(F32)
                + behind[b]
            )
            end = jnp.broadcast_to(first[:, :1], (rows, LANES))
            rights_in.append(over * (rights_in[-1] + end))
        rights_in = rights_in[::-1]
        for b in range(blocks):
            field = ahead[b] + grow * lefts[b] + shrink * (behind[b] + rights_in[b])
            high, low = split2(field)
            fields[u, :rows, LANES * b : LANES * (b + 1)] = high
            fields[u, LANES : LANES + rows, LANES * b : LANES * (b + 1)] = low
        nothing = jnp.zeros((LANES - rows, cols), BF16)
        fields[u, rows:LANES, :] = nothing
        fields[u, LANES + rows :, :] = nothing
    for u in range(per_step):
        ends = [split2(ref[u : u + 1, :]) for ref in (right_ref, right_sum_ref)]
        first = jnp.zeros((16, LANES), F32)
        for at, part in enumerate((ends[0][0], ends[1][0], ends[0][1], ends[1][1])):
            first = jnp.where(row_number == at, part.astype(F32), first)
        second = jnp.where(row_number < 2, first, 0.0)
        result = dot_nn(jnp.concatenate([first, second], axis=1).astype(BF16), fields[u])
        row = step * per_step + u
        chain_row = chain_ref[u : u + 1, :]
        over_rows, echo = chain_row[:, 32:33], chain_row[:, 33:34]
        end = over_rows * (result[0:1] + result[2:3])
        edge_ref[0, pl.ds(row, 1), :] = end
        edge_ref[1, pl.ds(row, 1), :] = result[1:2] + result[3:4] + over_rows * echo * end


def row_kernel_of(rows, first_place):
    def kernel(where_ref, fields_ref, left_ref, left_sum_ref, right_ref, right_sum_ref, *rest):
        field_ref, table, matrices = rest[-3:]
        step, per_step = pl.program_id(0), fields_ref.shape[0]
        half = table.shape[1] // 2
        below = iota((rows, LANES), 0) >= iota((rows, LANES), 1)

        @pl.when(step == 0)
        def _():
            table[...] = jnp.concatenate([left_ref[...], left_sum_ref[...]], axis=1)
            matrices[...] = jnp.zeros_like(matrices)

        for u in range(per_step):
            place = first_place + step * per_step + u
            left, left_sum = lane_of(table[...], place), lane_of(table[...], place + half)
            right, right_sum = right_ref[u : u + 1, :], right_sum_ref[u : u + 1, :]
            high, low = split2(jnp.where(below, left_sum * right, left * right_sum))
            matrices[u, :rows, :LANES] = high
            matrices[u, :rows, LANES:] = high
            matrices[u, rows:, :LANES] = low
        for u in range(per_step):
            result = dot_nn(matrices[u], fields_ref[u])
            field_ref[u] = result[:rows] + result[rows:]

    return kernel


def pair_kernel(where_ref, own_ref, got_ref, chain_ref, send1_ref, send2_ref, send3_ref, *, pairs, places):
    lon = where_ref[2]
    second = jnp.bitwise_and(lon, 1) == 1
    pair = jnp.right_shift(lon, 1)
    chain = chain_ref[places, :]
    over, partner_over = chain[:, 32:33], chain[:, 34:35]
    end, returning = own_ref[0], own_ref[1]
    got_end, got_returning = got_ref[0], got_ref[1]
    pair_end = jnp.where(second, end + over * got_end, got_end + partner_over * end)
    pair_returning = jnp.where(
        second, got_returning + partner_over * returning, returning + over * got_returning
    )
    for shift, ref in ((1, send1_ref), (2, send2_ref), (3, send3_ref)):
        ref[...] = jnp.where(pair + shift < pairs, pair_end, pair_returning)


def enter_kernel(where_ref, own_ref, got_ref, got1_ref, got2_ref, got3_ref, chain_ref, left_ref, left_sum_ref,
                 enter_ref, leave_ref, table_ref, *, places):
    second = jnp.bitwise_and(where_ref[2], 1) == 1
    chain = chain_ref[places, :]
    over, echo = chain[:, 32:33], chain[:, 33:34]
    enter = jnp.where(second, got_ref[0], 0.0)
    leave = jnp.where(second, 0.0, got_ref[1])
    for shift, ref in ((1, got1_ref), (2, got2_ref), (3, got3_ref)):
        enter = enter + chain[:, shift : shift + 1] * ref[...]
        leave = leave + chain[:, 64 + shift : 65 + shift] * ref[...]
    enter_ref[...] = enter
    leave_ref[...] = over * (leave + echo * (own_ref[0] + over * enter))
    table_ref[...] = jnp.concatenate([left_ref[...], left_sum_ref[...]], axis=1)


def one_product(where_ref, refs, sizes, turn, step, u):
    field_ref, spread_ref, enter_ref, leave_ref, table_ref = refs
    first_place, steps, quarters = sizes
    cols = field_ref.shape[-1]
    row = lax.rem(where_ref[0] + turn, quarters) * steps + step
    place = first_place + row
    half = table_ref.shape[1] // 2
    wide = lambda lane: jnp.concatenate([lane_of(table_ref[...], lane)] * (cols // LANES), axis=1)
    enter, leave = enter_ref[pl.ds(row, 1), :], leave_ref[pl.ds(row, 1), :]
    filtered = field_ref[u] + wide(place + half) * enter + wide(place) * leave
    return spread_ref[0, u].astype(F32) * filtered.astype(BF16).astype(F32)


def send_kernel(sizes, turn, start, where_ref, enter_ref, leave_ref, table_ref, field_ref, spread_ref, *refs):
    *adds, out_ref = refs
    row_refs = (field_ref, spread_ref, enter_ref, leave_ref, table_ref)
    for u in range(PRODUCT_STEP):
        step = start + pl.program_id(0) * PRODUCT_STEP + u
        value = one_product(where_ref, row_refs, sizes, turn, step, u)
        for ref in adds:
            value = value + ref[u].astype(F32)
        out_ref[u] = value.astype(BF16)


def here_kernel(sizes, first_part, where_ref, enter_ref, leave_ref, table_ref, field_ref, spread_ref, got0_ref, got1_ref, out_ref):
    in_first = pl.program_id(0) * PRODUCT_STEP < first_part
    row_refs = (field_ref, spread_ref, enter_ref, leave_ref, table_ref)
    for u in range(PRODUCT_STEP):
        step = pl.program_id(0) * PRODUCT_STEP + u
        value = one_product(where_ref, row_refs, sizes, 0, step, u)
        out_ref[u] = value + jnp.where(in_first, got0_ref[u], got1_ref[u]).astype(F32)


def last_kernel(scale, first_part, where_ref, sum_ref, got0_ref, got1_ref, out_ref):
    in_first = pl.program_id(0) * PRODUCT_STEP < first_part
    out_ref[...] = (sum_ref[...] + jnp.where(in_first, got0_ref[...], got1_ref[...]).astype(F32)) * scale


def whole(shape):
    return pl.BlockSpec(shape, lambda *_: (0,) * len(shape))


def call(
    kernel, name, inputs, in_specs, outputs, out_specs, scratch=(), grid=(1,), cost=None, after=(), vmem=VMEM_LIMIT, aliases=None
):
    count = len(inputs)

    def ordered(*refs):
        return kernel(*refs[:count], *refs[count + len(after) :])

    inputs = (*inputs, *after)
    in_specs = [*in_specs, *([pl.BlockSpec(memory_space=pl.ANY)] * len(after))]
    return pl.pallas_call(
        ordered,
        out_shape=outputs,
        grid_spec=pltpu.PrefetchScalarGridSpec(
            num_scalar_prefetch=1,
            grid=grid,
            in_specs=in_specs,
            out_specs=out_specs,
            scratch_shapes=list(scratch),
        ),
        input_output_aliases=aliases or {},
        compiler_params=pltpu.CompilerParams(vmem_limit_bytes=vmem),
        cost_estimate=cost,
        name=name,
    )(*inputs)


def cost(flops, data):
    return pl.CostEstimate(flops=flops, bytes_accessed=data, transcendentals=0)


def triangle_table():
    at = np.arange(LANES)
    table = np.zeros((2 * LANES, 2 * LANES), np.float32)
    table[:LANES, :LANES] = at[:, None] <= at[None, :]
    table[LANES:, LANES:] = at[:, None] > at[None, :]
    return jnp.asarray(np.concatenate([table, table]), BF16)


def ring(axis, shift):
    count = lax.axis_size(axis)
    return [(i, (i + shift) % count) for i in range(count)]


def per_device(control, perturbation, slab_levels, member_group, band_width, zonal_rate, meridional_rate):
    _, levels, rows, cols = control.shape
    quarters, lat_count, lon_count = (lax.axis_size(a) for a in ("mem", "lat", "lon"))
    per_quarter = levels // quarters
    here = jnp.stack([lax.axis_index(a) for a in ("mem", "lat", "lon")]).astype(jnp.int32)
    where = jnp.concatenate([here, member_group, band_width, slab_levels])
    sds = jax.ShapeDtypeStruct
    table = sds((rows, levels), F32)
    table_spec = pl.BlockSpec((ROW_GROUP, levels), lambda g, _: (g, 0))

    column, decay, gain, end, *sends = call(
        functools.partial(column_kernel, (levels, rows, cols, quarters, lat_count)),
        "vertical_columns",
        (where, control, zonal_rate),
        [
            pl.BlockSpec((1, levels, ROW_GROUP, cols), lambda g, _: (0, 0, g, 0)),
            whole(zonal_rate.shape),
        ],
        (sds((levels, rows, cols), BF16), table, table, table, table, table, table),
        (
            pl.BlockSpec((levels, ROW_GROUP, cols), lambda g, _: (0, g, 0)),
            whole((rows, levels)), whole((rows, levels)),
            table_spec, table_spec, table_spec, table_spec,
        ),
        scratch=[
            pltpu.VMEM((levels * 8, levels * 8), BF16),
            pltpu.VMEM((rows, levels), F32),
            pltpu.VMEM((2, levels, ROW_GROUP, LANES), F32),
        ],
        grid=(rows // ROW_GROUP,),
        cost=cost(2 * 512 * 512 * 384 * 12, 2 * levels * rows * cols * 2),
        vmem=COLUMN_VMEM_LIMIT,
    )
    got = [lax.ppermute(s, "lat", ring("lat", i + 1)) for i, s in enumerate(sends)]
    left, left_sum, right, right_sum, chain = call(
        functools.partial(row_kernel, (levels, rows, quarters, lon_count)),
        "row_terms",
        (where, meridional_rate),
        [whole(meridional_rate.shape)],
        (table, table, sds((levels, LANES), F32), sds((levels, LANES), F32), sds((levels, LANES), F32)),
        (
            whole((rows, levels)), whole((rows, levels)),
            whole((levels, LANES)), whole((levels, LANES)), whole((levels, LANES)),
        ),
        cost=cost(2 * 3 * 64 * 768 * 768 * 2, 1 << 20),
    )

    triangle = triangle_table()
    scale = 1.0 / math.sqrt(control.shape[0] * quarters - 1)
    plane = rows * cols
    table_wide = sds((rows, 2 * levels), F32)
    table_specs = [whole((rows, levels))] * 2
    to_partner = [(i, i ^ 1) for i in range(lon_count)]
    to_pair = lambda k: [(i, (i + 2 * k) % lon_count) for i in range(lon_count)]
    up, down = ring("mem", 1), ring("mem", -1)
    by_step = lambda offset, low=0, high=levels: pl.BlockSpec(
        (PRODUCT_STEP, rows, cols), lambda g, _: (jnp.clip(g - offset, low, high), 0, 0)
    )
    ends = np.cumsum([sum(parts) for parts in CHUNKS])

    def quarter_specs(c, turn, start):
        steps, begin = sum(CHUNKS[c]), int(ends[c]) - sum(CHUNKS[c])
        at = lambda g, w, wide, off: (
            lax.rem(w[0] + turn, quarters) * (wide // PRODUCT_STEP) + (off + start) // PRODUCT_STEP + g
        )
        return [
            pl.BlockSpec((PRODUCT_STEP, rows, cols), lambda g, w: (at(g, w, steps, 0), 0, 0)),
            pl.BlockSpec(
                (1, PRODUCT_STEP, rows, cols), lambda g, w: (0, at(g, w, per_quarter, begin), 0, 0)
            ),
        ]

    def edge_specs(steps):
        row = whole((steps * quarters, cols))
        return [row, row, whole(table_wide.shape)]

    def product_sizes(c):
        steps = sum(CHUNKS[c])
        return (int(ends[c]) - steps) * quarters, steps, quarters

    def send(c, turn, part, adds=(), after=()):
        field, enter, leave, lanes = states[c]
        start, count = part * CHUNKS[c][0], CHUNKS[c][part]
        (piece,) = call(
            functools.partial(send_kernel, product_sizes(c), turn, start),
            f"products_{turn}",
            (where, enter, leave, lanes, field, perturbation, *adds),
            edge_specs(sum(CHUNKS[c])) + quarter_specs(c, turn, start) + [by_step(0)] * len(adds),
            (sds((count, rows, cols), BF16),),
            (by_step(0),),
            grid=(count // PRODUCT_STEP,),
            cost=cost(count * plane * 8, count * plane * 8),
            after=after,
        )
        return piece

    def finish(c, two, one, after=()):
        sum_up = send(c, 1, 0, (two[0],), after)
        moved_up = lax.ppermute(sum_up, "mem", up)
        sum_down = send(c, 3, 1, (two[1],), (sum_up, *after))
        moved_down = lax.ppermute(sum_down, "mem", down)
        steps, first = sum(CHUNKS[c]), CHUNKS[c][0] // PRODUCT_STEP
        halves = [by_step(0, 0, first - 1), by_step(first, 0)]
        field, enter, leave, lanes = states[c]
        own = sds((steps, rows, cols), F32)
        here = call(
            functools.partial(here_kernel, product_sizes(c), CHUNKS[c][0]),
            "products_here",
            (where, enter, leave, lanes, field, perturbation, one[1], one[0]),
            edge_specs(steps) + quarter_specs(c, 0, 0) + halves,
            own,
            by_step(0),
            grid=(steps // PRODUCT_STEP,),
            cost=cost(steps * plane * 8, steps * plane * 14),
            after=(sum_down,),
        )
        return call(
            functools.partial(last_kernel, scale, CHUNKS[c][0]),
            "increment",
            (where, here, moved_up, moved_down),
            [by_step(0), *halves],
            own,
            by_step(0),
            grid=(steps // PRODUCT_STEP,),
            cost=cost(steps * plane * 2, steps * plane * 10),
        )

    states, increments = [], []
    for c, parts in enumerate(CHUNKS):
        steps = sum(parts)
        in_chunk, first_place = steps * quarters, (int(ends[c]) - steps) * quarters
        places = slice(first_place, first_place + in_chunk)
        edge_spec, row_spec = whole((2, in_chunk, cols)), whole((in_chunk, cols))
        edge_row = sds((in_chunk, cols), F32)
        block = first_place // FIELD_STEP
        by_place = pl.BlockSpec((FIELD_STEP, LANES), lambda g, _, block=block: (block + g, 0))
        fields, edge = call(
            functools.partial(field_kernel, (rows, cols, first_place, FIELD_STEP, lat_count)),
            "zonal_rows",
            (where, column, decay, gain, end, *got, right, right_sum, chain, triangle),
            [pl.BlockSpec((FIELD_STEP, rows, cols), lambda g, _, block=block: (block + g, 0, 0))]
            + [whole((rows, levels))] * 6
            + [by_place, by_place, by_place, whole(triangle.shape)],
            (sds((in_chunk, 2 * LANES, cols), BF16), sds((2, in_chunk, cols), F32)),
            (pl.BlockSpec((FIELD_STEP, 2 * LANES, cols), lambda g, _: (g, 0, 0)), edge_spec),
            scratch=[
                pltpu.VMEM((2, rows, 2 * levels), F32),
                pltpu.VMEM((FIELD_STEP, 4, rows, LANES), F32),
                pltpu.VMEM((FIELD_STEP, 2, rows, LANES), F32),
                pltpu.VMEM((FIELD_STEP * rows * cols // LANES, 4 * LANES), BF16),
                pltpu.VMEM((FIELD_STEP * rows * cols // LANES, 2 * LANES), F32),
            ],
            grid=(in_chunk // FIELD_STEP,),
            cost=cost(in_chunk * plane * 2 * 1024 * 3, in_chunk * plane * 6),
            vmem=FIELD_VMEM_LIMIT,
        )
        def filter_rows(part, before, after=()):
            half_steps = in_chunk // FIELD_STEP // 2
            here = block + part * half_steps
            level_rows = pl.BlockSpec((FIELD_STEP, LANES), lambda g, _: (here + g, 0))
            step_of = lambda height: pl.BlockSpec(
                (FIELD_STEP, height, cols), lambda g, _: (part * half_steps + g, 0, 0)
            )
            extra = () if before is None else (before,)
            return call(
                row_kernel_of(rows, first_place + part * half_steps * FIELD_STEP),
                "row_filter",
                (where, fields, left, left_sum, right, right_sum, *extra),
                [step_of(2 * LANES), *table_specs, level_rows, level_rows]
                + [pl.BlockSpec(memory_space=pl.ANY)] * len(extra),
                sds((in_chunk, rows, cols), F32),
                step_of(rows),
                scratch=[
                    pltpu.VMEM((rows, 2 * levels), F32),
                    pltpu.VMEM((FIELD_STEP, 2 * rows, 2 * LANES), BF16),
                ],
                grid=(half_steps,),
                cost=cost(in_chunk * plane * 512, in_chunk * plane * 4),
                after=after,
                aliases={6: 0} if extra else None,
            )

        partner = lax.ppermute(edge, "lon", to_partner)
        field = filter_rows(0, None)
        pair_sends = call(
            functools.partial(pair_kernel, pairs=lon_count // 2, places=places),
            "pair_ends",
            (where, edge, partner, chain),
            [edge_spec, edge_spec, whole((levels, LANES))],
            (edge_row,) * 3,
            (row_spec,) * 3,
            after=(field,),
        )
        field = filter_rows(1, field, after=(pair_sends[0],))
        pair_got = [lax.ppermute(p, "lon", to_pair(k + 1)) for k, p in enumerate(pair_sends)]
        enter, leave, lanes = call(
            functools.partial(enter_kernel, places=places),
            "entering",
            (where, edge, partner, *pair_got, chain, left, left_sum),
            [edge_spec, edge_spec, row_spec, row_spec, row_spec, whole((levels, LANES)), *table_specs],
            (edge_row, edge_row, table_wide),
            (row_spec, row_spec, whole(table_wide.shape)),
        )
        states.append((field, enter, leave, lanes))
        two_up = send(c, 2, 0)
        two_up_moved = lax.ppermute(two_up, "mem", up)
        two_down = send(c, 2, 1, after=(two_up,))
        two = two_up_moved, lax.ppermute(two_down, "mem", down)
        one_up = send(c, 1, 1, after=(two_down,))
        one_up_moved = lax.ppermute(one_up, "mem", up)
        one_down = send(c, 3, 0, after=(one_up,))
        one = one_up_moved, lax.ppermute(one_down, "mem", down)
        increments.append(finish(c, two, one))
    return increments[0] if len(increments) == 1 else jnp.concatenate(increments)


def solution(mesh):
    return jax.shard_map(
        per_device,
        mesh=mesh,
        in_specs=(
            P("mem", None, "lon", "lat"),
            P("mem", None, "lon", "lat"),
            P(),
            P("mem"),
            P(),
            P(),
            P(),
        ),
        out_specs=P("mem", "lon", "lat"),
        check_vma=False,
    )
```

time: 126 us -> 101 us (0.80)
  Pallas kernels: 66.3 us -> 48.8 us
  starting transfers between devices: 36.1 us -> 23 us
  waiting for transfers between devices: 17.9 us -> 24.3 us
    pallas_call x16 -> x15, Pallas kernels: 66.3 us -> 48.8 us  [call(): pl.pallas_call(ordered, out_shape=outputs, grid_spec=pltpu.PrefetchScalar...]
    ppermute x18 -> x9, waiting for transfers between devices: 12.7 us -> 23.8 us  [the longest x1 8.44 us: per_device(): one = (one_up_moved, lax.ppermute(one_down, 'mem', down))]
    ppermute x18 -> x9, starting transfers between devices: 25.4 us -> 15.8 us  [the longest x3 5.73 us: per_device(): lax.ppermute(p, 'lon', to_pair(k + 1))]
    ppermute x2 -> x1, waiting for transfers between devices: 5.19 us -> 0.55 us  [per_device(): partner = lax.ppermute(edge, 'lon', to_partner)]
    ppermute x2 -> x1, starting transfers between devices: 7.27 us -> 3.66 us  [per_device(): partner = lax.ppermute(edge, 'lon', to_partner)]
    unnamed x8 -> x12, local copies, waits for them, and re-layouts: 3.04 us -> 3.25 us
  transfers between devices with their start and end apart: 23 -> 13, of which waited for: 10 -> 5; matrix products, arithmetic and copies ran while one was open for 0% -> 0% of each run, Pallas kernels for 27% -> 18%
where the time goes in v3:
time: 101 us
  Pallas kernels  48.8 us (48%)
  waiting for transfers between devices  24.3 us (24%)
  starting transfers between devices  23 us (23%)
  local copies, waits for them, and re-layouts  4 us (4%)
    pallas_call x15, Pallas kernels, call(): pl.pallas_call(ordered, out_shape=outputs, grid_spec=pltpu.PrefetchScalar...  48.8 us
    ppermute x1, waiting for transfers between devices, per_device(): one = (one_up_moved, lax.ppermute(one_down, 'mem', down))  8.44 us
    ppermute x1, waiting for transfers between devices, per_device(): two_up_moved = lax.ppermute(two_up, 'mem', up)  7.59 us
    ppermute x1, waiting for transfers between devices, finish(): moved_up = lax.ppermute(sum_up, 'mem', up)  6.59 us
    ppermute x3, starting transfers between devices, per_device(): lax.ppermute(p, 'lon', to_pair(k + 1))  5.73 us
    ppermute x1, starting transfers between devices, per_device(): partner = lax.ppermute(edge, 'lon', to_partner)  3.66 us
    ppermute x3, starting transfers between devices, per_device(): lax.ppermute(s, 'lat', ring('lat', i + 1))  3.53 us
    unnamed x12, local copies, waits for them, and re-layouts  3.25 us
  transfers between devices with their start and end apart: 13, of which 5 were waited for; matrix products, arithmetic and copies ran while one was open for 0% of the time, Pallas kernels for 18%

profile of v3, /device:TPU:0, one launch (start us, length us, event | category | flops | bytes accessed | tf_op | source)
XLA Modules:
  0.0 101.0 jit_solution(10010233952029661855)
XLA Ops:
  0.7 0.8 concatenate.3.refs_0_
  1.4 2.3 %copy-done = bf16[1,64,96,384]{3,2,1,0:T(8,128)(2,1)S(1)} copy-done((bf16[1,64,96,384]{3,2,1,0:T(8,128)(2,1)S(1)}, bf16[1,64,96,384]{3,2,1,0:T(8,128)(2,1)}, u32[]{:S(2)}) %copy-start) | copy-done | bytes 4718616
  3.7 0.9 copy-done.1
  4.6 8.8 %vertical_columns.1 = (bf16[64,96,384]{2,1,0:T(8,128)(2,1)S(1)}, f32[96,64]{1,0:T(8,128)S(1)}, f32[96,64]{1,0:T(8,128)S(1)}, f32[96,64]{1,0:T(8,128)S(1)}, f32[9...) custom-call(s32[40]{0:T(128)S(1)} %concatenate.3.refs_0_, bf16[1,64,96,384]{3,2,1,0:T(8,128)(2,1)S(1)} %copy-done, ...), custom_call_target="tpu_custom_call" | custom-call | flops 2415919104 | bytes 9437184 | tf_op jit(solution)/shard_map/vertical_columns/pallas_call | solution.py:436
  13.4 0.1 collective-permute-start
  13.5 2.1 %collective-permute-start.1 = (f32[96,64]{1,0:T(8,128)S(1)}, f32[96,64]{1,0:T(8,128)S(1)}, u32[]{:S(2)}, u32[]{:S(2)}) collective-permute-start(f32[96,64]{1,0:T(8,128)S(1)} %get-tuple-element.30), channel_id=1, source_target_pairs={{0,16},{8,24},{16,0},{24,8},{1,17},{9,25},{17,1},{25,9},{2,18},{10... | collective-permute-start | bytes 73736 | tf_op jit(solution)/shard_map/ppermute | solution.py:503
  15.6 1.4 %collective-permute-start.2 = (f32[96,64]{1,0:T(8,128)S(1)}, f32[96,64]{1,0:T(8,128)S(1)}, u32[]{:S(2)}, u32[]{:S(2)}) collective-permute-start(f32[96,64]{1,0:T(8,128)S(1)} %get-tuple-element.31), channel_id=1, source_target_pairs={{0,24},{8,0},{16,8},{24,16},{1,25},{9,1},{17,9},{25,17},{2,26},{10... | collective-permute-start | bytes 73736 | tf_op jit(solution)/shard_map/ppermute | solution.py:503
  17.0 0.0 copy-done.2
  17.0 2.7 %row_terms.1 = (f32[96,64]{1,0:T(8,128)S(1)}, f32[96,64]{1,0:T(8,128)S(1)}, f32[64,128]{1,0:T(8,128)S(1)}, f32[64,128]{1,0:T(8,128)S(1)}, f32[64,128]{1,0:T(8,128)S(1)}) custom-call(s32[40]{0:T(128)S(1)} %concatenate.3.refs_0_, f32[32,768]{1,0:T(8,128)S(1)} %copy-done.2), custom_call_target="tpu_custom_call" | custom-call | flops 452984832 | bytes 1048576 | tf_op jit(solution)/shard_map/row_terms/pallas_call | solution.py:436
  19.7 0.0 collective-permute-done.refs_5_
  19.7 0.0 collective-permute-done.1.refs_6_
  19.7 0.0 collective-permute-done.2.refs_7_
  19.7 0.0 copy-done.3
  19.7 17.1 %zonal_rows.1 = (bf16[64,256,384]{2,1,0:T(8,128)(2,1)S(1)}, f32[2,64,384]{2,1,0:T(8,128)S(1)}) custom-call(s32[40]{0:T(128)S(1)} %concatenate.3.refs_0_, bf16[64,96,384]{2,1,0:T(8,128)(2,1)S(1)} %get-tuple-element.25.refs_1_, f32[96,64]{1,0:T(8,128)S(1)} %get-tuple-element.26.refs_2_, f32[96,64]{1,0:T(8,128)S(1)} %get-tuple-element.27.refs_3_, ...), custom_call_target="tpu_custom_call" | custom-call | flops 14495514624 | bytes 14155776 | tf_op jit(solution)/shard_map/zonal_rows/pallas_call | solution.py:436
  36.8 3.7 %collective-permute-start.3 = (f32[2,64,384]{2,1,0:T(8,128)S(1)}, f32[2,64,384]{2,1,0:T(8,128)S(1)}, u32[]{:S(2)}, u32[]{:S(2)}) collective-permute-start(f32[2,64,384]{2,1,0:T(8,128)S(1)} %get-tuple-element.35.refs_1_), channel_id=1, source_target_pairs={{0,1},{1,0},{2,3},{3,2},{4,5},{5,4},{6,7},{7,6},{8,9},{9,8},{10,11... | collective-permute-start | bytes 589832 | tf_op jit(solution)/shard_map/ppermute | solution.py:652
  40.5 4.0 %row_filter.2.refs_4_.refs_6_ = f32[64,96,384]{2,1,0:T(8,128)S(1)} custom-call(s32[40]{0:T(128)S(1)} %concatenate.3.refs_0_, bf16[64,256,384]{2,1,0:T(8,128)(2,1)S(1)} %get-tuple-element.36.refs_1_, f32[96,64]{1,0:T(8,128)S(1)} %get-tuple-element.37.refs_2_.refs_7_, f32[96,64]{1,0:T(8,128)S(1)} %get-tuple-element.38.refs_3_.refs_8_, ...), custom_call_target="tpu_custom_call" | custom-call | flops 1207959552 | bytes 9437184 | tf_op jit(solution)/shard_map/row_filter/pallas_call | solution.py:436
  44.5 0.6 collective-permute-done.3.refs_2_
  45.1 0.7 pair_ends.1
  45.7 1.6 %collective-permute-start.4 = (f32[64,384]{1,0:T(8,128)S(1)}, f32[64,384]{1,0:T(8,128)S(1)}, u32[]{:S(2)}, u32[]{:S(2)}) collective-permute-start(f32[64,384]{1,0:T(8,128)S(1)} %get-tuple-element.39.refs_7_), channel_id=1, source_target_pairs={{0,2},{1,3},{2,4},{3,5},{4,6},{5,7},{6,0},{7,1},{8,10},{9,11},{10,... | collective-permute-start | bytes 294920 | tf_op jit(solution)/shard_map/ppermute | solution.py:664
  47.3 2.7 %collective-permute-start.5 = (f32[64,384]{1,0:T(8,128)S(1)}, f32[64,384]{1,0:T(8,128)S(1)}, u32[]{:S(2)}, u32[]{:S(2)}) collective-permute-start(f32[64,384]{1,0:T(8,128)S(1)} %get-tuple-element.40), channel_id=1, source_target_pairs={{0,4},{1,5},{2,6},{3,7},{4,0},{5,1},{6,2},{7,3},{8,12},{9,13},{10,... | collective-permute-start | bytes 294920 | tf_op jit(solution)/shard_map/ppermute | solution.py:664
  50.0 1.4 %collective-permute-start.6 = (f32[64,384]{1,0:T(8,128)S(1)}, f32[64,384]{1,0:T(8,128)S(1)}, u32[]{:S(2)}, u32[]{:S(2)}) collective-permute-start(f32[64,384]{1,0:T(8,128)S(1)} %get-tuple-element.41), channel_id=1, source_target_pairs={{0,6},{1,7},{2,0},{3,1},{4,2},{5,3},{6,4},{7,5},{8,14},{9,15},{10,... | collective-permute-start | bytes 294920 | tf_op jit(solution)/shard_map/ppermute | solution.py:664
  51.5 4.0 %row_filter.3.refs_4_ = f32[64,96,384]{2,1,0:T(8,128)S(1)} custom-call(s32[40]{0:T(128)S(1)} %concatenate.3.refs_0_, bf16[64,256,384]{2,1,0:T(8,128)(2,1)S(1)} %get-tuple-element.36.refs_1_, f32[96,64]{1,0:T(8,128)S(1)} %get-tuple-element.37.refs_2_.refs_7_, f32[96,64]{1,0:T(8,128)S(1)} %get-tuple-element.38.refs_3_.refs_8_, ...), custom_call_target="tpu_custom_call", output_to_operand_aliasing={{}: (6, {})} | custom-call | flops 1207959552 | bytes 9437184 | tf_op jit(solution)/shard_map/row_filter/pallas_call | solution.py:436
  55.5 0.0 collective-permute-done.4.refs_3_
  55.5 0.0 collective-permute-done.5.refs_4_
  55.5 0.0 collective-permute-done.6.refs_5_
  55.5 0.7 entering.1
  56.2 0.0 slice-done
  56.2 0.0 slice-done.1
  56.2 1.1 %products_2.2.refs_6_ = bf16[8,96,384]{2,1,0:T(8,128)(2,1)S(1)} custom-call(s32[40]{0:T(128)S(1)} %concatenate.3.refs_0_, f32[64,384]{1,0:T(8,128)S(1)} %get-tuple-element.42.refs_1_, f32[64,384]{1,0:T(8,128)S(1)} %get-tuple-element.43.refs_2_, f32[96,128]{1,0:T(8,128)S(1)} %get-tuple-element.44.refs_3_, f32[64,96,384]{2,1,0:T(8,128)S(1)} %row_filter.3.refs_4_, ...), custom_call_target="tpu_custom_call" | custom-call | flops 2359296 | bytes 2359296 | tf_op jit(solution)/shard_map/products_2/pallas_call | solution.py:436
  57.3 1.6 %collective-permute-start.10 = (bf16[8,96,384]{2,1,0:T(8,128)(2,1)S(1)}, bf16[8,96,384]{2,1,0:T(8,128)(2,1)S(1)}, u32[]{:S(2)}, u32[]{:S(2)}) collective-permute-start(bf16[8,96,384]{2,1,0:T(8,128)(2,1)S(1)} %products_2.2.refs_6_), channel_id=1, source_target_pairs={{0,32},{32,64},{64,96},{96,0},{1,33},{33,65},{65,97},{97,1},{2,34}... | collective-permute-start | bytes 1769480 | tf_op jit(solution)/shard_map/ppermute | solution.py:675
  59.0 1.1 %products_2.3.refs_6_ = bf16[8,96,384]{2,1,0:T(8,128)(2,1)S(1)} custom-call(s32[40]{0:T(128)S(1)} %concatenate.3.refs_0_, f32[64,384]{1,0:T(8,128)S(1)} %get-tuple-element.42.refs_1_, f32[64,384]{1,0:T(8,128)S(1)} %get-tuple-element.43.refs_2_, f32[96,128]{1,0:T(8,128)S(1)} %get-tuple-element.44.refs_3_, f32[64,96,384]{2,1,0:T(8,128)S(1)} %row_filter.3.refs_4_, ...), custom_call_target="tpu_custom_call" | custom-call | flops 2359296 | bytes 2359296 | tf_op jit(solution)/shard_map/products_2/pallas_call | solution.py:436
  60.0 1.7 %collective-permute-start.9 = (bf16[8,96,384]{2,1,0:T(8,128)(2,1)S(1)}, bf16[8,96,384]{2,1,0:T(8,128)(2,1)S(1)}, u32[]{:S(2)}, u32[]{:S(2)}) collective-permute-start(bf16[8,96,384]{2,1,0:T(8,128)(2,1)S(1)} %products_2.3.refs_6_), channel_id=1, source_target_pairs={{0,96},{32,0},{64,32},{96,64},{1,97},{33,1},{65,33},{97,65},{2,98}... | collective-permute-start | bytes 1769480 | tf_op jit(solution)/shard_map/ppermute | solution.py:677
  61.8 1.1 %products_1.2.refs_6_ = bf16[8,96,384]{2,1,0:T(8,128)(2,1)S(1)} custom-call(s32[40]{0:T(128)S(1)} %concatenate.3.refs_0_, f32[64,384]{1,0:T(8,128)S(1)} %get-tuple-element.42.refs_1_, f32[64,384]{1,0:T(8,128)S(1)} %get-tuple-element.43.refs_2_, f32[96,128]{1,0:T(8,128)S(1)} %get-tuple-element.44.refs_3_, f32[64,96,384]{2,1,0:T(8,128)S(1)} %row_filter.3.refs_4_, ...), custom_call_target="tpu_custom_call" | custom-call | flops 2359296 | bytes 2359296 | tf_op jit(solution)/shard_map/products_1/pallas_call | solution.py:436
  62.8 0.4 collective-permute-start.8
  63.3 1.1 %products_3.2 = bf16[8,96,384]{2,1,0:T(8,128)(2,1)S(1)} custom-call(s32[40]{0:T(128)S(1)} %concatenate.3.refs_0_, f32[64,384]{1,0:T(8,128)S(1)} %get-tuple-element.42.refs_1_, f32[64,384]{1,0:T(8,128)S(1)} %get-tuple-element.43.refs_2_, f32[96,128]{1,0:T(8,128)S(1)} %get-tuple-element.44.refs_3_, f32[64,96,384]{2,1,0:T(8,128)S(1)} %row_filter.3.refs_4_, ...), custom_call_target="tpu_custom_call" | custom-call | flops 2359296 | bytes 2359296 | tf_op jit(solution)/shard_map/products_3/pallas_call | solution.py:436
  64.3 2.9 %collective-permute-start.7 = (bf16[8,96,384]{2,1,0:T(8,128)(2,1)S(1)}, bf16[8,96,384]{2,1,0:T(8,128)(2,1)S(1)}, u32[]{:S(2)}, u32[]{:S(2)}) collective-permute-start(bf16[8,96,384]{2,1,0:T(8,128)(2,1)S(1)} %products_3.2), channel_id=1, source_target_pairs={{0,96},{32,0},{64,32},{96,64},{1,97},{33,1},{65,33},{97,65},{2,98}... | collective-permute-start | bytes 1769480 | tf_op jit(solution)/shard_map/ppermute | solution.py:681
  67.3 7.6 %collective-permute-done.10.refs_6_ = bf16[8,96,384]{2,1,0:T(8,128)(2,1)S(1)} collective-permute-done((bf16[8,96,384]{2,1,0:T(8,128)(2,1)S(1)}, bf16[8,96,384]{2,1,0:T(8,128)(2,1)S(1)}, u32[]{:S(2)}, u32[]{:S(2)}) %collective-permute-start.10) | collective-permute-done | bytes 589856 | tf_op jit(solution)/shard_map/ppermute | solution.py:675
  74.9 1.2 %products_1.3.refs_7_ = bf16[8,96,384]{2,1,0:T(8,128)(2,1)S(1)} custom-call(s32[40]{0:T(128)S(1)} %concatenate.3.refs_0_, f32[64,384]{1,0:T(8,128)S(1)} %get-tuple-element.42.refs_1_, f32[64,384]{1,0:T(8,128)S(1)} %get-tuple-element.43.refs_2_, f32[96,128]{1,0:T(8,128)S(1)} %get-tuple-element.44.refs_3_, f32[64,96,384]{2,1,0:T(8,128)S(1)} %row_filter.3.refs_4_, ...), custom_call_target="tpu_custom_call" | custom-call | flops 2359296 | bytes 2359296 | tf_op jit(solution)/shard_map/products_1/pallas_call | solution.py:436
  76.0 0.4 collective-permute-start.11
  76.5 0.0 collective-permute-done.9.refs_6_
  76.5 1.2 %products_3.3.refs_8_ = bf16[8,96,384]{2,1,0:T(8,128)(2,1)S(1)} custom-call(s32[40]{0:T(128)S(1)} %concatenate.3.refs_0_, f32[64,384]{1,0:T(8,128)S(1)} %get-tuple-element.42.refs_1_, f32[64,384]{1,0:T(8,128)S(1)} %get-tuple-element.43.refs_2_, f32[96,128]{1,0:T(8,128)S(1)} %get-tuple-element.44.refs_3_, f32[64,96,384]{2,1,0:T(8,128)S(1)} %row_filter.3.refs_4_, ...), custom_call_target="tpu_custom_call" | custom-call | flops 2359296 | bytes 2359296 | tf_op jit(solution)/shard_map/products_3/pallas_call | solution.py:436
  77.6 2.9 %collective-permute-start.12 = (bf16[8,96,384]{2,1,0:T(8,128)(2,1)S(1)}, bf16[8,96,384]{2,1,0:T(8,128)(2,1)S(1)}, u32[]{:S(2)}, u32[]{:S(2)}) collective-permute-start(bf16[8,96,384]{2,1,0:T(8,128)(2,1)S(1)} %products_3.3.refs_8_), channel_id=1, source_target_pairs={{0,96},{32,0},{64,32},{96,64},{1,97},{33,1},{65,33},{97,65},{2,98}... | collective-permute-start | bytes 1769480 | tf_op jit(solution)/shard_map/ppermute | solution.py:570
  80.6 8.4 %collective-permute-done.7.refs_6_ = bf16[8,96,384]{2,1,0:T(8,128)(2,1)S(1)} collective-permute-done((bf16[8,96,384]{2,1,0:T(8,128)(2,1)S(1)}, bf16[8,96,384]{2,1,0:T(8,128)(2,1)S(1)}, u32[]{:S(2)}, u32[]{:S(2)}) %collective-permute-start.7) | collective-permute-done | bytes 589856 | tf_op jit(solution)/shard_map/ppermute | solution.py:681
  89.0 0.0 collective-permute-done.8.refs_7_
  89.0 1.7 %products_here.1.refs_1_ = f32[16,96,384]{2,1,0:T(8,128)S(1)} custom-call(s32[40]{0:T(128)S(1)} %concatenate.3.refs_0_, f32[64,384]{1,0:T(8,128)S(1)} %get-tuple-element.42.refs_1_, f32[64,384]{1,0:T(8,128)S(1)} %get-tuple-element.43.refs_2_, f32[96,128]{1,0:T(8,128)S(1)} %get-tuple-element.44.refs_3_, f32[64,96,384]{2,1,0:T(8,128)S(1)} %row_filter.3.refs_4_, ...), custom_call_target="tpu_custom_call" | custom-call | flops 4718592 | bytes 8257536 | tf_op jit(solution)/shard_map/products_here/pallas_call | solution.py:436
  90.7 6.6 %collective-permute-done.11.refs_2_ = bf16[8,96,384]{2,1,0:T(8,128)(2,1)S(1)} collective-permute-done((bf16[8,96,384]{2,1,0:T(8,128)(2,1)S(1)}, bf16[8,96,384]{2,1,0:T(8,128)(2,1)S(1)}, u32[]{:S(2)}, u32[]{:S(2)}) %collective-permute-start.11) | collective-permute-done | bytes 589856 | tf_op jit(solution)/shard_map/ppermute | solution.py:568
  97.3 1.1 %collective-permute-done.12.refs_3_ = bf16[8,96,384]{2,1,0:T(8,128)(2,1)S(1)} collective-permute-done((bf16[8,96,384]{2,1,0:T(8,128)(2,1)S(1)}, bf16[8,96,384]{2,1,0:T(8,128)(2,1)S(1)}, u32[]{:S(2)}, u32[]{:S(2)}) %collective-permute-start.12) | collective-permute-done | bytes 589856 | tf_op jit(solution)/shard_map/ppermute | solution.py:570
  98.4 2.6 %increment.1 = f32[16,96,384]{2,1,0:T(8,128)} custom-call(s32[40]{0:T(128)S(1)} %concatenate.3.refs_0_, f32[16,96,384]{2,1,0:T(8,128)S(1)} %products_here.1.refs_1_, bf16[8,96,384]{2,1,0:T(8,128)(2,1)S(1)} %collective-permute-done.11.refs_2_, bf16[8,96,384]{2,1,0:T(8,128)(2,1)S(1)} %collective-permute-done.12.refs_3_), custom_call_target="tpu_custom_call" | custom-call | flops 1179648 | bytes 5898240 | tf_op jit(solution)/shard_map/increment/pallas_call | solution.py:436
  (7 shorter events, 0.0 us)
Async XLA Ops:
  1.4 2.3 %copy-start = (bf16[1,64,96,384]{3,2,1,0:T(8,128)(2,1)S(1)}, bf16[1,64,96,384]{3,2,1,0:T(8,128)(2,1)}, u32[]{:S(2)}) copy-start(bf16[1,64,96,384]{3,2,1,0:T(8,128)(2,1)} %refs_1_.2) | copy-start | bytes 14155780
  3.7 0.9 copy-start.1
  4.6 12.3 %copy-start.2 = (f32[32,768]{1,0:T(8,128)S(1)}, f32[32,768]{1,0:T(8,128)}, u32[]{:S(2)}) copy-start(f32[32,768]{1,0:T(8,128)} %refs_1_.3) | copy-start | bytes 294916
  4.6 15.1 %copy-start.3 = (bf16[512,256]{1,0:T(8,128)(2,1)S(1)}, bf16[512,256]{1,0:T(8,128)(2,1)}, u32[]{:S(2)}) copy-start(bf16[512,256]{1,0:T(8,128)(2,1)} %constant.14.clone.refs_11_) | copy-start | bytes 786436
  13.4 6.3 %collective-permute-start = (f32[96,64]{1,0:T(8,128)S(1)}, f32[96,64]{1,0:T(8,128)S(1)}, u32[]{:S(2)}, u32[]{:S(2)}) collective-permute-start(f32[96,64]{1,0:T(8,128)S(1)} %get-tuple-element.29), channel_id=1, source_target_pairs={{0,8},{8,16},{16,24},{24,0},{1,9},{9,17},{17,25},{25,1},{2,10},{10... | collective-permute-start | bytes 73736 | tf_op jit(solution)/shard_map/ppermute | solution.py:503
  13.5 6.2 %collective-permute-start.1 = (f32[96,64]{1,0:T(8,128)S(1)}, f32[96,64]{1,0:T(8,128)S(1)}, u32[]{:S(2)}, u32[]{:S(2)}) collective-permute-start(f32[96,64]{1,0:T(8,128)S(1)} %get-tuple-element.30), channel_id=1, source_target_pairs={{0,16},{8,24},{16,0},{24,8},{1,17},{9,25},{17,1},{25,9},{2,18},{10... | collective-permute-start | bytes 73736 | tf_op jit(solution)/shard_map/ppermute | solution.py:503
  15.6 4.1 %collective-permute-start.2 = (f32[96,64]{1,0:T(8,128)S(1)}, f32[96,64]{1,0:T(8,128)S(1)}, u32[]{:S(2)}, u32[]{:S(2)}) collective-permute-start(f32[96,64]{1,0:T(8,128)S(1)} %get-tuple-element.31), channel_id=1, source_target_pairs={{0,24},{8,0},{16,8},{24,16},{1,25},{9,1},{17,9},{25,17},{2,26},{10... | collective-permute-start | bytes 73736 | tf_op jit(solution)/shard_map/ppermute | solution.py:503
  36.8 8.3 %collective-permute-start.3 = (f32[2,64,384]{2,1,0:T(8,128)S(1)}, f32[2,64,384]{2,1,0:T(8,128)S(1)}, u32[]{:S(2)}, u32[]{:S(2)}) collective-permute-start(f32[2,64,384]{2,1,0:T(8,128)S(1)} %get-tuple-element.35.refs_1_), channel_id=1, source_target_pairs={{0,1},{1,0},{2,3},{3,2},{4,5},{5,4},{6,7},{7,6},{8,9},{9,8},{10,11... | collective-permute-start | bytes 589832 | tf_op jit(solution)/shard_map/ppermute | solution.py:652
  45.7 9.8 %collective-permute-start.4 = (f32[64,384]{1,0:T(8,128)S(1)}, f32[64,384]{1,0:T(8,128)S(1)}, u32[]{:S(2)}, u32[]{:S(2)}) collective-permute-start(f32[64,384]{1,0:T(8,128)S(1)} %get-tuple-element.39.refs_7_), channel_id=1, source_target_pairs={{0,2},{1,3},{2,4},{3,5},{4,6},{5,7},{6,0},{7,1},{8,10},{9,11},{10,... | collective-permute-start | bytes 294920 | tf_op jit(solution)/shard_map/ppermute | solution.py:664
  47.3 8.2 %collective-permute-start.5 = (f32[64,384]{1,0:T(8,128)S(1)}, f32[64,384]{1,0:T(8,128)S(1)}, u32[]{:S(2)}, u32[]{:S(2)}) collective-permute-start(f32[64,384]{1,0:T(8,128)S(1)} %get-tuple-element.40), channel_id=1, source_target_pairs={{0,4},{1,5},{2,6},{3,7},{4,0},{5,1},{6,2},{7,3},{8,12},{9,13},{10,... | collective-permute-start | bytes 294920 | tf_op jit(solution)/shard_map/ppermute | solution.py:664
  50.0 6.2 %slice-start = ((s8[4718592]{0:T(1024)(128)(4,1)}), s8[4194304]{0:T(1024)(128)(4,1)S(1)}, s32[]{:S(2)}) async-start(s8[4718592]{0:T(1024)(128)(4,1)} %bitcast.3), calls=%async_computation | async-start | bytes 8388608
  50.0 6.2 %slice-start.1 = ((s8[4718592]{0:T(1024)(128)(4,1)}), s8[524288]{0:T(1024)(128)(4,1)S(1)}, s32[]{:S(2)}) async-start(s8[4718592]{0:T(1024)(128)(4,1)} %bitcast.3), calls=%async_computation.1 | async-start | bytes 1048576
  50.0 5.5 %collective-permute-start.6 = (f32[64,384]{1,0:T(8,128)S(1)}, f32[64,384]{1,0:T(8,128)S(1)}, u32[]{:S(2)}, u32[]{:S(2)}) collective-permute-start(f32[64,384]{1,0:T(8,128)S(1)} %get-tuple-element.41), channel_id=1, source_target_pairs={{0,6},{1,7},{2,0},{3,1},{4,2},{5,3},{6,4},{7,5},{8,14},{9,15},{10,... | collective-permute-start | bytes 294920 | tf_op jit(solution)/shard_map/ppermute | solution.py:664
  57.3 17.5 %collective-permute-start.10 = (bf16[8,96,384]{2,1,0:T(8,128)(2,1)S(1)}, bf16[8,96,384]{2,1,0:T(8,128)(2,1)S(1)}, u32[]{:S(2)}, u32[]{:S(2)}) collective-permute-start(bf16[8,96,384]{2,1,0:T(8,128)(2,1)S(1)} %products_2.2.refs_6_), channel_id=1, source_target_pairs={{0,32},{32,64},{64,96},{96,0},{1,33},{33,65},{65,97},{97,1},{2,34}... | collective-permute-start | bytes 1769480 | tf_op jit(solution)/shard_map/ppermute | solution.py:675
  60.0 16.4 %collective-permute-start.9 = (bf16[8,96,384]{2,1,0:T(8,128)(2,1)S(1)}, bf16[8,96,384]{2,1,0:T(8,128)(2,1)S(1)}, u32[]{:S(2)}, u32[]{:S(2)}) collective-permute-start(bf16[8,96,384]{2,1,0:T(8,128)(2,1)S(1)} %products_2.3.refs_6_), channel_id=1, source_target_pairs={{0,96},{32,0},{64,32},{96,64},{1,97},{33,1},{65,33},{97,65},{2,98}... | collective-permute-start | bytes 1769480 | tf_op jit(solution)/shard_map/ppermute | solution.py:677
  62.8 26.2 %collective-permute-start.8 = (bf16[8,96,384]{2,1,0:T(8,128)(2,1)S(1)}, bf16[8,96,384]{2,1,0:T(8,128)(2,1)S(1)}, u32[]{:S(2)}, u32[]{:S(2)}) collective-permute-start(bf16[8,96,384]{2,1,0:T(8,128)(2,1)S(1)} %products_1.2.refs_6_), channel_id=1, source_target_pairs={{0,32},{32,64},{64,96},{96,0},{1,33},{33,65},{65,97},{97,1},{2,34}... | collective-permute-start | bytes 1769480 | tf_op jit(solution)/shard_map/ppermute | solution.py:679
  64.3 24.7 %collective-permute-start.7 = (bf16[8,96,384]{2,1,0:T(8,128)(2,1)S(1)}, bf16[8,96,384]{2,1,0:T(8,128)(2,1)S(1)}, u32[]{:S(2)}, u32[]{:S(2)}) collective-permute-start(bf16[8,96,384]{2,1,0:T(8,128)(2,1)S(1)} %products_3.2), channel_id=1, source_target_pairs={{0,96},{32,0},{64,32},{96,64},{1,97},{33,1},{65,33},{97,65},{2,98}... | collective-permute-start | bytes 1769480 | tf_op jit(solution)/shard_map/ppermute | solution.py:681
  76.0 21.3 %collective-permute-start.11 = (bf16[8,96,384]{2,1,0:T(8,128)(2,1)S(1)}, bf16[8,96,384]{2,1,0:T(8,128)(2,1)S(1)}, u32[]{:S(2)}, u32[]{:S(2)}) collective-permute-start(bf16[8,96,384]{2,1,0:T(8,128)(2,1)S(1)} %products_1.3.refs_7_), channel_id=1, source_target_pairs={{0,32},{32,64},{64,96},{96,0},{1,33},{33,65},{65,97},{97,1},{2,34}... | collective-permute-start | bytes 1769480 | tf_op jit(solution)/shard_map/ppermute | solution.py:568
  77.6 20.8 %collective-permute-start.12 = (bf16[8,96,384]{2,1,0:T(8,128)(2,1)S(1)}, bf16[8,96,384]{2,1,0:T(8,128)(2,1)S(1)}, u32[]{:S(2)}, u32[]{:S(2)}) collective-permute-start(bf16[8,96,384]{2,1,0:T(8,128)(2,1)S(1)} %products_3.3.refs_8_), channel_id=1, source_target_pairs={{0,96},{32,0},{64,32},{96,64},{1,97},{33,1},{65,33},{97,65},{2,98}... | collective-permute-start | bytes 1769480 | tf_op jit(solution)/shard_map/ppermute | solution.py:570

commit v4 on v3

--- a/solution.py
+++ b/solution.py
@@ -14,11 +14,11 @@
 GROUP_AT = 3
 BAND_AT = 4
 SLAB_AT = 8
-ROW_GROUP = 16
+ROW_GROUP = 32
 FIELD_STEP = 8
 PRODUCT_STEP = 4
 VMEM_LIMIT = 8 * 1024 * 1024
-COLUMN_VMEM_LIMIT = 14 * 1024 * 1024
+COLUMN_VMEM_LIMIT = 48 * 1024 * 1024
 FIELD_VMEM_LIMIT = 16 * 1024 * 1024
 
 F32 = jnp.float32
@@ -96,9 +96,9 @@
 
 
 def column_kernel(
-    sizes, where_ref, control_ref, rate_ref,
+    sizes, where_ref, control_ref, rate_hbm,
     column_ref, decay_ref, gain_ref, end_ref, send1_ref, send2_ref, send3_ref,
-    kron, decay_all, weighted,
+    kron, decay_all, weighted, rate_ref, arrived,
 ):
     levels, rows, cols, quarters, lat_count = sizes
     step = pl.program_id(0)
@@ -107,6 +107,8 @@
 
     @pl.when(step == 0)
     def _():
+        fetch = pltpu.make_async_copy(rate_hbm, rate_ref, arrived)
+        fetch.start()
         band = where_ref[BAND_AT + where_ref[GROUP_AT]].astype(F32)
         out_level = traced_level(jnp.right_shift(iota((full, full), 0), 3), levels, quarters)
         spacing = out_level - jnp.right_shift(iota((full, full), 1), 3)
@@ -115,6 +117,7 @@
         weight = jnp.exp(-2.0 * (ratio * ratio))
         keep = jnp.logical_and(same, jnp.abs(spacing).astype(F32) <= band)
         kron[...] = jnp.where(keep, weight, 0.0).astype(BF16)
+        fetch.wait()
         level_rates = rates_by_place(where_ref, rate_ref[...], levels, quarters)
         own = iota((rows, rate_ref.shape[1]), 1) == lon * rows + iota((rows, rate_ref.shape[1]), 0)
         rate = exact_times_t(own.astype(F32).astype(BF16), level_rates)
@@ -125,7 +128,7 @@
 
     block = control_ref[0].astype(F32)
     halves = []
-    for half in range(2):
+    for half in range(ROW_GROUP // 8):
         part = block[:, 8 * half : 8 * half + 8, :].reshape(full, cols).astype(BF16)
         halves.append(dot_nn(kron[...], part).reshape(levels, 8, cols))
     column = jnp.concatenate(halves, axis=1).astype(BF16)
@@ -268,40 +271,32 @@
         powers[u, 0] = grow
         powers[u, 1] = shrink
         powers[u, 2] = jnp.exp(log_a * float(LANES))
-        powers[u, 3] = jnp.exp(log_a)
         gain_grow, gain_shrink = gain * grow, gain * shrink
         x = column_ref[u].astype(F32)
         for b in range(blocks):
             part = x[:, LANES * b : LANES * (b + 1)]
             rows_at = slice(u * tall + b * rows, u * tall + (b + 1) * rows)
             for side, factor in enumerate((gain_shrink, gain_grow)):
-                high, low = split2(part * factor)
-                at = LANES * side
-                scaled[rows_at, at : at + LANES] = high
-                scaled[rows_at, 2 * LANES + at : 3 * LANES + at] = low
+                scaled[rows_at, LANES * side : LANES * (side + 1)] = (part * factor).astype(BF16)
     for u in range(per_step):
         at = slice(u * tall, (u + 1) * tall)
         sums[at, :] = dot_nn(scaled[at, :], triangle_ref[...])
     for u in range(per_step):
-        grow, shrink, over, decay = (powers[u, k] for k in range(4))
+        grow, shrink, over = (powers[u, k] for k in range(3))
         at = lambda b: slice(u * tall + b * rows, u * tall + (b + 1) * rows)
-        ahead = [grow * sums[at(b), :LANES] for b in range(blocks)]
+        ahead = [sums[at(b), :LANES] for b in range(blocks)]
         behind = [sums[at(b), LANES:] for b in range(blocks)]
         lefts, rights_in = [enters[u, 0]], [enters[u, 1]]
         for b in range(blocks - 1):
             end = jnp.broadcast_to(ahead[b][:, LANES - 1 :], (rows, LANES))
-            lefts.append(over * lefts[-1] + decay * end)
+            lefts.append(over * (lefts[-1] + end))
         for b in range(blocks - 1, 0, -1):
-            first = (
-                scaled[at(b), LANES : 2 * LANES].astype(F32)
-                + scaled[at(b), 3 * LANES :].astype(F32)
-                + behind[b]
-            )
+            first = scaled[at(b), LANES:].astype(F32) + behind[b]
             end = jnp.broadcast_to(first[:, :1], (rows, LANES))
             rights_in.append(over * (rights_in[-1] + end))
         rights_in = rights_in[::-1]
         for b in range(blocks):
-            field = ahead[b] + grow * lefts[b] + shrink * (behind[b] + rights_in[b])
+            field = grow * (ahead[b] + lefts[b]) + shrink * (behind[b] + rights_in[b])
             high, low = split2(field)
             fields[u, :rows, LANES * b : LANES * (b + 1)] = high
             fields[u, LANES : LANES + rows, LANES * b : LANES * (b + 1)] = low
@@ -323,7 +318,13 @@
         edge_ref[1, pl.ds(row, 1), :] = result[1:2] + result[3:4] + over_rows * echo * end
 
 
-def row_kernel_of(rows, first_place):
+def turn_block(scalars, number, quarters, blocks):
+    turn = number // blocks
+    turn = jnp.where(turn == 0, 2, jnp.where(turn == 1, 1, jnp.where(turn == 2, 3, 0)))
+    return lax.rem(scalars[0] + turn, quarters) * blocks + lax.rem(number, blocks)
+
+
+def row_kernel_of(rows, first, quarters, blocks):
     def kernel(where_ref, fields_ref, left_ref, left_sum_ref, right_ref, right_sum_ref, *rest):
         field_ref, table, matrices = rest[-3:]
         step, per_step = pl.program_id(0), fields_ref.shape[0]
@@ -336,7 +337,7 @@
             matrices[...] = jnp.zeros_like(matrices)
 
         for u in range(per_step):
-            place = first_place + step * per_step + u
+            place = turn_block(where_ref, first + step, quarters, blocks) * per_step + u
             left, left_sum = lane_of(table[...], place), lane_of(table[...], place + half)
             right, right_sum = right_ref[u : u + 1, :], right_sum_ref[u : u + 1, :]
             high, low = split2(jnp.where(below, left_sum * right, left * right_sum))
@@ -366,19 +367,25 @@
         ref[...] = jnp.where(pair + shift < pairs, pair_end, pair_returning)
 
 
-def enter_kernel(where_ref, own_ref, got_ref, got1_ref, got2_ref, got3_ref, chain_ref, left_ref, left_sum_ref,
-                 enter_ref, leave_ref, table_ref, *, places):
-    second = jnp.bitwise_and(where_ref[2], 1) == 1
-    chain = chain_ref[places, :]
-    over, echo = chain[:, 32:33], chain[:, 33:34]
-    enter = jnp.where(second, got_ref[0], 0.0)
-    leave = jnp.where(second, 0.0, got_ref[1])
-    for shift, ref in ((1, got1_ref), (2, got2_ref), (3, got3_ref)):
-        enter = enter + chain[:, shift : shift + 1] * ref[...]
-        leave = leave + chain[:, 64 + shift : 65 + shift] * ref[...]
-    enter_ref[...] = enter
-    leave_ref[...] = over * (leave + echo * (own_ref[0] + over * enter))
-    table_ref[...] = jnp.concatenate([left_ref[...], left_sum_ref[...]], axis=1)
+def first_send_kernel(
+    sizes, turn, places, where_ref, own_ref, got_ref, got1_ref, got2_ref, got3_ref, chain_ref, left_ref, left_sum_ref,
+    field_ref, spread_ref, out_ref, enter_ref, leave_ref, table_ref,
+):
+    @pl.when(pl.program_id(0) == 0)
+    def _():
+        second = jnp.bitwise_and(where_ref[2], 1) == 1
+        chain = chain_ref[places, :]
+        over, echo = chain[:, 32:33], chain[:, 33:34]
+        enter = jnp.where(second, got_ref[0], 0.0)
+        leave = jnp.where(second, 0.0, got_ref[1])
+        for shift, ref in ((1, got1_ref), (2, got2_ref), (3, got3_ref)):
+            enter = enter + chain[:, shift : shift + 1] * ref[...]
+            leave = leave + chain[:, 64 + shift : 65 + shift] * ref[...]
+        enter_ref[...] = enter
+        leave_ref[...] = over * (leave + echo * (own_ref[0] + over * enter))
+        table_ref[...] = jnp.concatenate([left_ref[...], left_sum_ref[...]], axis=1)
+
+    send_kernel(sizes, turn, 0, where_ref, enter_ref, leave_ref, table_ref, field_ref, spread_ref, out_ref)
 
 
 def one_product(where_ref, refs, sizes, turn, step, u):
@@ -412,11 +419,6 @@
         step = pl.program_id(0) * PRODUCT_STEP + u
         value = one_product(where_ref, row_refs, sizes, 0, step, u)
         out_ref[u] = value + jnp.where(in_first, got0_ref[u], got1_ref[u]).astype(F32)
-
-
-def last_kernel(scale, first_part, where_ref, sum_ref, got0_ref, got1_ref, out_ref):
-    in_first = pl.program_id(0) * PRODUCT_STEP < first_part
-    out_ref[...] = (sum_ref[...] + jnp.where(in_first, got0_ref[...], got1_ref[...]).astype(F32)) * scale
 
 
 def whole(shape):
@@ -459,7 +461,7 @@
     table = np.zeros((2 * LANES, 2 * LANES), np.float32)
     table[:LANES, :LANES] = at[:, None] <= at[None, :]
     table[LANES:, LANES:] = at[:, None] > at[None, :]
-    return jnp.asarray(np.concatenate([table, table]), BF16)
+    return jnp.asarray(table, BF16)
 
 
 def ring(axis, shift):
@@ -483,7 +485,7 @@
         (where, control, zonal_rate),
         [
             pl.BlockSpec((1, levels, ROW_GROUP, cols), lambda g, _: (0, 0, g, 0)),
-            whole(zonal_rate.shape),
+            pl.BlockSpec(memory_space=pltpu.HBM),
         ],
         (sds((levels, rows, cols), BF16), table, table, table, table, table, table),
         (
@@ -495,6 +497,8 @@
             pltpu.VMEM((levels * 8, levels * 8), BF16),
             pltpu.VMEM((rows, levels), F32),
             pltpu.VMEM((2, levels, ROW_GROUP, LANES), F32),
+            pltpu.VMEM(zonal_rate.shape, F32),
+            pltpu.SemaphoreType.DMA,
         ],
         grid=(rows // ROW_GROUP,),
         cost=cost(2 * 512 * 512 * 384 * 12, 2 * levels * rows * cols * 2),
@@ -583,16 +587,8 @@
             cost=cost(steps * plane * 8, steps * plane * 14),
             after=(sum_down,),
         )
-        return call(
-            functools.partial(last_kernel, scale, CHUNKS[c][0]),
-            "increment",
-            (where, here, moved_up, moved_down),
-            [by_step(0), *halves],
-            own,
-            by_step(0),
-            grid=(steps // PRODUCT_STEP,),
-            cost=cost(steps * plane * 2, steps * plane * 10),
-        )
+        moved = jnp.concatenate([moved_up, moved_down]).astype(F32)
+        return (here + moved) * scale
 
     states, increments = [], []
     for c, parts in enumerate(CHUNKS):
@@ -614,25 +610,25 @@
             (pl.BlockSpec((FIELD_STEP, 2 * LANES, cols), lambda g, _: (g, 0, 0)), edge_spec),
             scratch=[
                 pltpu.VMEM((2, rows, 2 * levels), F32),
-                pltpu.VMEM((FIELD_STEP, 4, rows, LANES), F32),
+                pltpu.VMEM((FIELD_STEP, 3, rows, LANES), F32),
                 pltpu.VMEM((FIELD_STEP, 2, rows, LANES), F32),
-                pltpu.VMEM((FIELD_STEP * rows * cols // LANES, 4 * LANES), BF16),
+                pltpu.VMEM((FIELD_STEP * rows * cols // LANES, 2 * LANES), BF16),
                 pltpu.VMEM((FIELD_STEP * rows * cols // LANES, 2 * LANES), F32),
             ],
             grid=(in_chunk // FIELD_STEP,),
             cost=cost(in_chunk * plane * 2 * 1024 * 3, in_chunk * plane * 6),
             vmem=FIELD_VMEM_LIMIT,
         )
-        def filter_rows(part, before, after=()):
-            half_steps = in_chunk // FIELD_STEP // 2
-            here = block + part * half_steps
-            level_rows = pl.BlockSpec((FIELD_STEP, LANES), lambda g, _: (here + g, 0))
+        def filter_rows(first, count, before, after=()):
+            blocks = steps // FIELD_STEP
+            number = lambda g, w: turn_block(w, first + g, quarters, blocks)
+            level_rows = pl.BlockSpec((FIELD_STEP, LANES), lambda g, w: (number(g, w), 0))
             step_of = lambda height: pl.BlockSpec(
-                (FIELD_STEP, height, cols), lambda g, _: (part * half_steps + g, 0, 0)
+                (FIELD_STEP, height, cols), lambda g, w: (number(g, w), 0, 0)
             )
             extra = () if before is None else (before,)
             return call(
-                row_kernel_of(rows, first_place + part * half_steps * FIELD_STEP),
+                row_kernel_of(rows, first, quarters, blocks),
                 "row_filter",
                 (where, fields, left, left_sum, right, right_sum, *extra),
                 [step_of(2 * LANES), *table_specs, level_rows, level_rows]
@@ -643,14 +639,14 @@
                     pltpu.VMEM((rows, 2 * levels), F32),
                     pltpu.VMEM((FIELD_STEP, 2 * rows, 2 * LANES), BF16),
                 ],
-                grid=(half_steps,),
-                cost=cost(in_chunk * plane * 512, in_chunk * plane * 4),
+                grid=(count,),
+                cost=cost(count * FIELD_STEP * plane * 512, count * FIELD_STEP * plane * 8),
                 after=after,
                 aliases={6: 0} if extra else None,
             )
 
         partner = lax.ppermute(edge, "lon", to_partner)
-        field = filter_rows(0, None)
+        field = filter_rows(0, 4, None)
         pair_sends = call(
             functools.partial(pair_kernel, pairs=lon_count // 2, places=places),
             "pair_ends",
@@ -660,18 +656,21 @@
             (row_spec,) * 3,
             after=(field,),
         )
-        field = filter_rows(1, field, after=(pair_sends[0],))
+        field = filter_rows(4, 2, field, after=(pair_sends[0],))
         pair_got = [lax.ppermute(p, "lon", to_pair(k + 1)) for k, p in enumerate(pair_sends)]
-        enter, leave, lanes = call(
-            functools.partial(enter_kernel, places=places),
-            "entering",
-            (where, edge, partner, *pair_got, chain, left, left_sum),
-            [edge_spec, edge_spec, row_spec, row_spec, row_spec, whole((levels, LANES)), *table_specs],
-            (edge_row, edge_row, table_wide),
-            (row_spec, row_spec, whole(table_wide.shape)),
+        count = parts[0]
+        two_up, enter, leave, lanes = call(
+            functools.partial(first_send_kernel, product_sizes(c), 2, places),
+            "products_2",
+            (where, edge, partner, *pair_got, chain, left, left_sum, field, perturbation),
+            [edge_spec, edge_spec, row_spec, row_spec, row_spec, whole((levels, LANES)), *table_specs]
+            + quarter_specs(c, 2, 0),
+            (sds((count, rows, cols), BF16), edge_row, edge_row, table_wide),
+            (by_step(0), row_spec, row_spec, whole(table_wide.shape)),
+            grid=(count // PRODUCT_STEP,),
+            cost=cost(count * plane * 8, count * plane * 8),
         )
         states.append((field, enter, leave, lanes))
-        two_up = send(c, 2, 0)
         two_up_moved = lax.ppermute(two_up, "mem", up)
         two_down = send(c, 2, 1, after=(two_up,))
         two = two_up_moved, lax.ppermute(two_down, "mem", down)
@@ -679,6 +678,8 @@
         one_up_moved = lax.ppermute(one_up, "mem", up)
         one_down = send(c, 3, 0, after=(one_up,))
         one = one_up_moved, lax.ppermute(one_down, "mem", down)
+        field = filter_rows(6, 2, field, after=(one_down,))
+        states[c] = (field, enter, leave, lanes)
         increments.append(finish(c, two, one))
     return increments[0] if len(increments) == 1 else jnp.concatenate(increments)
 

time: 101 us -> 93.5 us (0.926)
  Pallas kernels: 48.8 us -> 42.7 us
  local copies, waits for them, and re-layouts: 4 us -> 1.66 us
  other arithmetic: 0.01 us -> 1.72 us
    ppermute x1, waiting for transfers between devices: 6.59 us -> 0.01 us  [finish(): moved_up = lax.ppermute(sum_up, 'mem', up)]
    ppermute x1, waiting for transfers between devices: 1.14 us -> 7.26 us  [finish(): moved_down = lax.ppermute(sum_down, 'mem', down)]
    pallas_call x15 -> x14, Pallas kernels: 48.8 us -> 42.7 us  [call(): pl.pallas_call(ordered, out_shape=outputs, grid_spec=pltpu.PrefetchScalar...]
    ppermute x3, waiting for transfers between devices: 0.01 us -> 2.57 us  [per_device(): lax.ppermute(p, 'lon', to_pair(k + 1))]
    ppermute x1, waiting for transfers between devices: 7.59 us -> 5.05 us  [per_device(): two_up_moved = lax.ppermute(two_up, 'mem', up)]
    unnamed x12 -> x10, local copies, waits for them, and re-layouts: 3.25 us -> 0.91 us
    mul x0 -> x1, other arithmetic: none -> 1.72 us  [finish(): return (here + moved) * scale]
  transfers between devices with their start and end apart: 13 -> 13, of which waited for: 5 -> 7; matrix products, arithmetic and copies ran while one was open for 0% -> 0% of each run, Pallas kernels for 18% -> 20%
where the time goes in v4:
time: 93.5 us; the launch traced here: 93.3 us
  Pallas kernels  42.7 us (46%)
  waiting for transfers between devices  24.3 us (26%)
  starting transfers between devices  22.2 us (24%)
  other arithmetic  1.72 us (2%)
  local copies, waits for them, and re-layouts  1.66 us (2%)
    pallas_call x14, Pallas kernels, call(): pl.pallas_call(ordered, out_shape=outputs, grid_spec=pltpu.PrefetchScalar...  42.7 us
    ppermute x1, waiting for transfers between devices, per_device(): one = (one_up_moved, lax.ppermute(one_down, 'mem', down))  8.54 us
    ppermute x1, waiting for transfers between devices, finish(): moved_down = lax.ppermute(sum_down, 'mem', down)  7.26 us
    ppermute x3, starting transfers between devices, per_device(): lax.ppermute(p, 'lon', to_pair(k + 1))  5.13 us
    ppermute x1, waiting for transfers between devices, per_device(): two_up_moved = lax.ppermute(two_up, 'mem', up)  5.05 us
    ppermute x1, starting transfers between devices, per_device(): partner = lax.ppermute(edge, 'lon', to_partner)  3.66 us
    ppermute x3, starting transfers between devices, per_device(): lax.ppermute(s, 'lat', ring('lat', i + 1))  3.53 us
    ppermute x1, starting transfers between devices, finish(): moved_down = lax.ppermute(sum_down, 'mem', down)  2.93 us
  transfers between devices with their start and end apart: 13, of which 7 were waited for; matrix products, arithmetic and copies ran while one was open for 0% of the time, Pallas kernels for 20%

profile of v4, /device:TPU:0, one launch (start us, length us, event | category | flops | bytes accessed | tf_op | source)
XLA Modules:
  0.0 93.3 jit_solution(4852879569031370252)
XLA Ops:
  0.7 0.8 concatenate.6.refs_0_
  1.4 0.0 copy-start
  1.4 0.9 copy-done
  2.3 8.4 %vertical_columns.1 = (bf16[64,96,384]{2,1,0:T(8,128)(2,1)S(1)}, f32[96,64]{1,0:T(8,128)S(1)}, f32[96,64]{1,0:T(8,128)S(1)}, f32[96,64]{1,0:T(8,128)S(1)}, f32[9...) custom-call(s32[40]{0:T(128)S(1)} %concatenate.6.refs_0_, bf16[1,64,96,384]{3,2,1,0:T(8,128)(2,1)} %refs_1_.2, ...), custom_call_target="tpu_custom_call" | custom-call | flops 2415919104 | bytes 9437184 | tf_op jit(solution)/shard_map/vertical_columns/pallas_call | solution.py:438
  10.7 0.1 collective-permute-start
  10.8 2.1 %collective-permute-start.1 = (f32[96,64]{1,0:T(8,128)S(1)}, f32[96,64]{1,0:T(8,128)S(1)}, u32[]{:S(2)}, u32[]{:S(2)}) collective-permute-start(f32[96,64]{1,0:T(8,128)S(1)} %get-tuple-element.31), channel_id=1, source_target_pairs={{0,16},{8,24},{16,0},{24,8},{1,17},{9,25},{17,1},{25,9},{2,18},{10... | collective-permute-start | bytes 73736 | tf_op jit(solution)/shard_map/ppermute | solution.py:507
  12.9 1.4 %collective-permute-start.2 = (f32[96,64]{1,0:T(8,128)S(1)}, f32[96,64]{1,0:T(8,128)S(1)}, u32[]{:S(2)}, u32[]{:S(2)}) collective-permute-start(f32[96,64]{1,0:T(8,128)S(1)} %get-tuple-element.32), channel_id=1, source_target_pairs={{0,24},{8,0},{16,8},{24,16},{1,25},{9,1},{17,9},{25,17},{2,26},{10... | collective-permute-start | bytes 73736 | tf_op jit(solution)/shard_map/ppermute | solution.py:507
  14.2 0.0 copy-done.1
  14.2 2.7 %row_terms.1 = (f32[96,64]{1,0:T(8,128)S(1)}, f32[96,64]{1,0:T(8,128)S(1)}, f32[64,128]{1,0:T(8,128)S(1)}, f32[64,128]{1,0:T(8,128)S(1)}, f32[64,128]{1,0:T(8,128)S(1)}) custom-call(s32[40]{0:T(128)S(1)} %concatenate.6.refs_0_, f32[32,768]{1,0:T(8,128)S(1)} %copy-done.1), custom_call_target="tpu_custom_call" | custom-call | flops 452984832 | bytes 1048576 | tf_op jit(solution)/shard_map/row_terms/pallas_call | solution.py:438
  17.0 0.0 collective-permute-done.refs_5_
  17.0 0.0 collective-permute-done.1.refs_6_
  17.0 0.0 collective-permute-done.2.refs_7_
  17.0 0.0 copy-done.2
  17.0 13.7 %zonal_rows.1 = (bf16[64,256,384]{2,1,0:T(8,128)(2,1)S(1)}, f32[2,64,384]{2,1,0:T(8,128)S(1)}) custom-call(s32[40]{0:T(128)S(1)} %concatenate.6.refs_0_, bf16[64,96,384]{2,1,0:T(8,128)(2,1)S(1)} %get-tuple-element.26.refs_1_, f32[96,64]{1,0:T(8,128)S(1)} %get-tuple-element.27.refs_2_, f32[96,64]{1,0:T(8,128)S(1)} %get-tuple-element.28.refs_3_, ...), custom_call_target="tpu_custom_call" | custom-call | flops 14495514624 | bytes 14155776 | tf_op jit(solution)/shard_map/zonal_rows/pallas_call | solution.py:438
  30.7 3.7 %collective-permute-start.3 = (f32[2,64,384]{2,1,0:T(8,128)S(1)}, f32[2,64,384]{2,1,0:T(8,128)S(1)}, u32[]{:S(2)}, u32[]{:S(2)}) collective-permute-start(f32[2,64,384]{2,1,0:T(8,128)S(1)} %get-tuple-element.36.refs_1_), channel_id=1, source_target_pairs={{0,1},{1,0},{2,3},{3,2},{4,5},{5,4},{6,7},{7,6},{8,9},{9,8},{10,11... | collective-permute-start | bytes 589832 | tf_op jit(solution)/shard_map/ppermute | solution.py:648
  34.3 4.1 %row_filter.3.refs_4_.refs_6_ = f32[64,96,384]{2,1,0:T(8,128)S(1)} custom-call(s32[40]{0:T(128)S(1)} %concatenate.6.refs_0_, bf16[64,256,384]{2,1,0:T(8,128)(2,1)S(1)} %get-tuple-element.37.refs_1_, f32[96,64]{1,0:T(8,128)S(1)} %get-tuple-element.38.refs_2_.refs_7_, f32[96,64]{1,0:T(8,128)S(1)} %get-tuple-element.39.refs_3_.refs_8_, ...), custom_call_target="tpu_custom_call" | custom-call | flops 603979776 | bytes 9437184 | tf_op jit(solution)/shard_map/row_filter/pallas_call | solution.py:438
  38.4 0.5 collective-permute-done.3.refs_2_
  38.9 0.7 pair_ends.1
  39.6 3.1 %collective-permute-start.5 = (f32[64,384]{1,0:T(8,128)S(1)}, f32[64,384]{1,0:T(8,128)S(1)}, u32[]{:S(2)}, u32[]{:S(2)}) collective-permute-start(f32[64,384]{1,0:T(8,128)S(1)} %get-tuple-element.41), channel_id=1, source_target_pairs={{0,4},{1,5},{2,6},{3,7},{4,0},{5,1},{6,2},{7,3},{8,12},{9,13},{10,... | collective-permute-start | bytes 294920 | tf_op jit(solution)/shard_map/ppermute | solution.py:660
  42.7 1.1 %collective-permute-start.6 = (f32[64,384]{1,0:T(8,128)S(1)}, f32[64,384]{1,0:T(8,128)S(1)}, u32[]{:S(2)}, u32[]{:S(2)}) collective-permute-start(f32[64,384]{1,0:T(8,128)S(1)} %get-tuple-element.42), channel_id=1, source_target_pairs={{0,6},{1,7},{2,0},{3,1},{4,2},{5,3},{6,4},{7,5},{8,14},{9,15},{10,... | collective-permute-start | bytes 294920 | tf_op jit(solution)/shard_map/ppermute | solution.py:660
  43.8 0.9 collective-permute-start.4
  44.7 2.4 %row_filter.4.refs_9_.refs_4_.refs_6_ = f32[64,96,384]{2,1,0:T(8,128)S(1)} custom-call(s32[40]{0:T(128)S(1)} %concatenate.6.refs_0_, bf16[64,256,384]{2,1,0:T(8,128)(2,1)S(1)} %get-tuple-element.37.refs_1_, f32[96,64]{1,0:T(8,128)S(1)} %get-tuple-element.38.refs_2_.refs_7_, ...), custom_call_target="tpu_custom_call", output_to_operand_aliasing={{}: (6, {})} | custom-call | flops 301989888 | bytes 4718592 | tf_op jit(solution)/shard_map/row_filter/pallas_call | solution.py:438
  47.1 0.0 collective-permute-done.5.refs_4_
  47.1 0.2 collective-permute-done.6.refs_5_
  47.3 2.4 %collective-permute-done.4.refs_3_ = f32[64,384]{1,0:T(8,128)S(1)} collective-permute-done((f32[64,384]{1,0:T(8,128)S(1)}, f32[64,384]{1,0:T(8,128)S(1)}, u32[]{:S(2)}, u32[]{:S(2)}) %collective-permute-start.4) | collective-permute-done | bytes 98336 | tf_op jit(solution)/shard_map/ppermute | solution.py:660
  49.7 0.0 slice-done
  49.7 0.0 slice-done.1
  49.7 1.3 %products_2.2 = (bf16[8,96,384]{2,1,0:T(8,128)(2,1)S(1)}, f32[64,384]{1,0:T(8,128)S(1)}, f32[64,384]{1,0:T(8,128)S(1)}, f32[96,128]{1,0:T(8,128)S(1)}) custom-call(s32[40]{0:T(128)S(1)} %concatenate.6.refs_0_, f32[2,64,384]{2,1,0:T(8,128)S(1)} %get-tuple-element.36.refs_1_, f32[2,64,384]{2,1,0:T(8,128)S(1)} %collective-permute-done.3.refs_2_, ...), custom_call_target="tpu_custom_call" | custom-call | flops 2359296 | bytes 2359296 | tf_op jit(solution)/shard_map/products_2/pallas_call | solution.py:438
  50.9 1.6 %collective-permute-start.10 = (bf16[8,96,384]{2,1,0:T(8,128)(2,1)S(1)}, bf16[8,96,384]{2,1,0:T(8,128)(2,1)S(1)}, u32[]{:S(2)}, u32[]{:S(2)}) collective-permute-start(bf16[8,96,384]{2,1,0:T(8,128)(2,1)S(1)} %get-tuple-element.46.refs_6_), channel_id=1, source_target_pairs={{0,32},{32,64},{64,96},{96,0},{1,33},{33,65},{65,97},{97,1},{2,34}... | collective-permute-start | bytes 1769480 | tf_op jit(solution)/shard_map/ppermute | solution.py:674
  52.6 1.1 %products_2.3.refs_6_ = bf16[8,96,384]{2,1,0:T(8,128)(2,1)S(1)} custom-call(s32[40]{0:T(128)S(1)} %concatenate.6.refs_0_, f32[64,384]{1,0:T(8,128)S(1)} %get-tuple-element.43.refs_1_, f32[64,384]{1,0:T(8,128)S(1)} %get-tuple-element.44.refs_2_, f32[96,128]{1,0:T(8,128)S(1)} %get-tuple-element.45.refs_3_, ...), custom_call_target="tpu_custom_call" | custom-call | flops 2359296 | bytes 2359296 | tf_op jit(solution)/shard_map/products_2/pallas_call | solution.py:438
  53.7 1.7 %collective-permute-start.9 = (bf16[8,96,384]{2,1,0:T(8,128)(2,1)S(1)}, bf16[8,96,384]{2,1,0:T(8,128)(2,1)S(1)}, u32[]{:S(2)}, u32[]{:S(2)}) collective-permute-start(bf16[8,96,384]{2,1,0:T(8,128)(2,1)S(1)} %products_2.3.refs_6_), channel_id=1, source_target_pairs={{0,96},{32,0},{64,32},{96,64},{1,97},{33,1},{65,33},{97,65},{2,98}... | collective-permute-start | bytes 1769480 | tf_op jit(solution)/shard_map/ppermute | solution.py:676
  55.4 1.1 %products_1.2.refs_6_ = bf16[8,96,384]{2,1,0:T(8,128)(2,1)S(1)} custom-call(s32[40]{0:T(128)S(1)} %concatenate.6.refs_0_, f32[64,384]{1,0:T(8,128)S(1)} %get-tuple-element.43.refs_1_, f32[64,384]{1,0:T(8,128)S(1)} %get-tuple-element.44.refs_2_, f32[96,128]{1,0:T(8,128)S(1)} %get-tuple-element.45.refs_3_, ...), custom_call_target="tpu_custom_call" | custom-call | flops 2359296 | bytes 2359296 | tf_op jit(solution)/shard_map/products_1/pallas_call | solution.py:438
  56.5 0.6 collective-permute-start.8
  57.1 1.1 %products_3.2.refs_7_ = bf16[8,96,384]{2,1,0:T(8,128)(2,1)S(1)} custom-call(s32[40]{0:T(128)S(1)} %concatenate.6.refs_0_, f32[64,384]{1,0:T(8,128)S(1)} %get-tuple-element.43.refs_1_, f32[64,384]{1,0:T(8,128)S(1)} %get-tuple-element.44.refs_2_, f32[96,128]{1,0:T(8,128)S(1)} %get-tuple-element.45.refs_3_, ...), custom_call_target="tpu_custom_call" | custom-call | flops 2359296 | bytes 2359296 | tf_op jit(solution)/shard_map/products_3/pallas_call | solution.py:438
  58.2 2.9 %collective-permute-start.7 = (bf16[8,96,384]{2,1,0:T(8,128)(2,1)S(1)}, bf16[8,96,384]{2,1,0:T(8,128)(2,1)S(1)}, u32[]{:S(2)}, u32[]{:S(2)}) collective-permute-start(bf16[8,96,384]{2,1,0:T(8,128)(2,1)S(1)} %products_3.2.refs_7_), channel_id=1, source_target_pairs={{0,96},{32,0},{64,32},{96,64},{1,97},{33,1},{65,33},{97,65},{2,98}... | collective-permute-start | bytes 1769480 | tf_op jit(solution)/shard_map/ppermute | solution.py:680
  61.1 2.4 %row_filter.5.refs_4_ = f32[64,96,384]{2,1,0:T(8,128)S(1)} custom-call(s32[40]{0:T(128)S(1)} %concatenate.6.refs_0_, bf16[64,256,384]{2,1,0:T(8,128)(2,1)S(1)} %get-tuple-element.37.refs_1_, f32[96,64]{1,0:T(8,128)S(1)} %get-tuple-element.38.refs_2_.refs_7_, f32[96,64]{1,0:T(8,128)S(1)} %get-tuple-element.39.refs_3_.refs_8_, ...), custom_call_target="tpu_custom_call", output_to_operand_aliasing={{}: (6, {})} | custom-call | flops 301989888 | bytes 4718592 | tf_op jit(solution)/shard_map/row_filter/pallas_call | solution.py:438
  63.4 5.0 %collective-permute-done.10.refs_6_ = bf16[8,96,384]{2,1,0:T(8,128)(2,1)S(1)} collective-permute-done((bf16[8,96,384]{2,1,0:T(8,128)(2,1)S(1)}, bf16[8,96,384]{2,1,0:T(8,128)(2,1)S(1)}, u32[]{:S(2)}, u32[]{:S(2)}) %collective-permute-start.10) | collective-permute-done | bytes 589856 | tf_op jit(solution)/shard_map/ppermute | solution.py:674
  68.5 1.2 %products_1.3.refs_7_ = bf16[8,96,384]{2,1,0:T(8,128)(2,1)S(1)} custom-call(s32[40]{0:T(128)S(1)} %concatenate.6.refs_0_, f32[64,384]{1,0:T(8,128)S(1)} %get-tuple-element.43.refs_1_, f32[64,384]{1,0:T(8,128)S(1)} %get-tuple-element.44.refs_2_, f32[96,128]{1,0:T(8,128)S(1)} %get-tuple-element.45.refs_3_, f32[64,96,384]{2,1,0:T(8,128)S(1)} %row_filter.5.refs_4_, ...), custom_call_target="tpu_custom_call" | custom-call | flops 2359296 | bytes 2359296 | tf_op jit(solution)/shard_map/products_1/pallas_call | solution.py:438
  69.7 0.3 collective-permute-done.9.refs_6_
  70.0 1.2 %products_3.3.refs_8_ = bf16[8,96,384]{2,1,0:T(8,128)(2,1)S(1)} custom-call(s32[40]{0:T(128)S(1)} %concatenate.6.refs_0_, f32[64,384]{1,0:T(8,128)S(1)} %get-tuple-element.43.refs_1_, f32[64,384]{1,0:T(8,128)S(1)} %get-tuple-element.44.refs_2_, f32[96,128]{1,0:T(8,128)S(1)} %get-tuple-element.45.refs_3_, f32[64,96,384]{2,1,0:T(8,128)S(1)} %row_filter.5.refs_4_, ...), custom_call_target="tpu_custom_call" | custom-call | flops 2359296 | bytes 2359296 | tf_op jit(solution)/shard_map/products_3/pallas_call | solution.py:438
  71.2 2.9 %collective-permute-start.12 = (bf16[8,96,384]{2,1,0:T(8,128)(2,1)S(1)}, bf16[8,96,384]{2,1,0:T(8,128)(2,1)S(1)}, u32[]{:S(2)}, u32[]{:S(2)}) collective-permute-start(bf16[8,96,384]{2,1,0:T(8,128)(2,1)S(1)} %products_3.3.refs_8_), channel_id=1, source_target_pairs={{0,96},{32,0},{64,32},{96,64},{1,97},{33,1},{65,33},{97,65},{2,98}... | collective-permute-start | bytes 1769480 | tf_op jit(solution)/shard_map/ppermute | solution.py:574
  74.1 0.0 collective-permute-start.11
  74.1 8.5 %collective-permute-done.7.refs_6_ = bf16[8,96,384]{2,1,0:T(8,128)(2,1)S(1)} collective-permute-done((bf16[8,96,384]{2,1,0:T(8,128)(2,1)S(1)}, bf16[8,96,384]{2,1,0:T(8,128)(2,1)S(1)}, u32[]{:S(2)}, u32[]{:S(2)}) %collective-permute-start.7) | collective-permute-done | bytes 589856 | tf_op jit(solution)/shard_map/ppermute | solution.py:680
  82.6 0.0 collective-permute-done.8.refs_7_
  82.6 1.7 %products_here.1 = f32[16,96,384]{2,1,0:T(8,128)S(1)} custom-call(s32[40]{0:T(128)S(1)} %concatenate.6.refs_0_, f32[64,384]{1,0:T(8,128)S(1)} %get-tuple-element.43.refs_1_, f32[64,384]{1,0:T(8,128)S(1)} %get-tuple-element.44.refs_2_, f32[96,128]{1,0:T(8,128)S(1)} %get-tuple-element.45.refs_3_, f32[64,96,384]{2,1,0:T(8,128)S(1)} %row_filter.5.refs_4_, ...), custom_call_target="tpu_custom_call" | custom-call | flops 4718592 | bytes 8257536 | tf_op jit(solution)/shard_map/products_here/pallas_call | solution.py:438
  84.3 7.3 %collective-permute-done.12 = bf16[8,96,384]{2,1,0:T(8,128)(2,1)S(1)} collective-permute-done((bf16[8,96,384]{2,1,0:T(8,128)(2,1)S(1)}, bf16[8,96,384]{2,1,0:T(8,128)(2,1)S(1)}, u32[]{:S(2)}, u32[]{:S(2)}) %collective-permute-start.12) | collective-permute-done | bytes 589856 | tf_op jit(solution)/shard_map/ppermute | solution.py:574
  91.6 0.0 collective-permute-done.11
  91.6 1.7 %add_multiply_fusion = f32[16,96,384]{2,1,0:T(8,128)} fusion(f32[16,96,384]{2,1,0:T(8,128)S(1)} %products_here.1, bf16[8,96,384]{2,1,0:T(8,128)(2,1)S(1)} %collective-permute-done.12, bf16[8,96,384]{2,1,0:T(8,128)(2,1)S(1)} %collective-permute-done.11), kind=kLoop, calls=%fused_computation | loop fusion | flops 2359296 | bytes 5898240 | tf_op jit(solution)/shard_map/mul | solution.py:591
  (5 shorter events, 0.0 us)
Async XLA Ops:
  1.4 0.9 copy-start
  2.3 11.9 %copy-start.1 = (f32[32,768]{1,0:T(8,128)S(1)}, f32[32,768]{1,0:T(8,128)}, u32[]{:S(2)}) copy-start(f32[32,768]{1,0:T(8,128)} %refs_1_.3) | copy-start | bytes 294916
  2.3 14.7 %copy-start.2 = (bf16[256,256]{1,0:T(8,128)(2,1)S(1)}, bf16[256,256]{1,0:T(8,128)(2,1)}, u32[]{:S(2)}) copy-start(bf16[256,256]{1,0:T(8,128)(2,1)} %constant.16.clone.refs_11_) | copy-start | bytes 393220
  10.7 6.3 %collective-permute-start = (f32[96,64]{1,0:T(8,128)S(1)}, f32[96,64]{1,0:T(8,128)S(1)}, u32[]{:S(2)}, u32[]{:S(2)}) collective-permute-start(f32[96,64]{1,0:T(8,128)S(1)} %get-tuple-element.30), channel_id=1, source_target_pairs={{0,8},{8,16},{16,24},{24,0},{1,9},{9,17},{17,25},{25,1},{2,10},{10... | collective-permute-start | bytes 73736 | tf_op jit(solution)/shard_map/ppermute | solution.py:507
  10.8 6.2 %collective-permute-start.1 = (f32[96,64]{1,0:T(8,128)S(1)}, f32[96,64]{1,0:T(8,128)S(1)}, u32[]{:S(2)}, u32[]{:S(2)}) collective-permute-start(f32[96,64]{1,0:T(8,128)S(1)} %get-tuple-element.31), channel_id=1, source_target_pairs={{0,16},{8,24},{16,0},{24,8},{1,17},{9,25},{17,1},{25,9},{2,18},{10... | collective-permute-start | bytes 73736 | tf_op jit(solution)/shard_map/ppermute | solution.py:507
  12.9 4.1 %collective-permute-start.2 = (f32[96,64]{1,0:T(8,128)S(1)}, f32[96,64]{1,0:T(8,128)S(1)}, u32[]{:S(2)}, u32[]{:S(2)}) collective-permute-start(f32[96,64]{1,0:T(8,128)S(1)} %get-tuple-element.32), channel_id=1, source_target_pairs={{0,24},{8,0},{16,8},{24,16},{1,25},{9,1},{17,9},{25,17},{2,26},{10... | collective-permute-start | bytes 73736 | tf_op jit(solution)/shard_map/ppermute | solution.py:507
  30.7 8.3 %collective-permute-start.3 = (f32[2,64,384]{2,1,0:T(8,128)S(1)}, f32[2,64,384]{2,1,0:T(8,128)S(1)}, u32[]{:S(2)}, u32[]{:S(2)}) collective-permute-start(f32[2,64,384]{2,1,0:T(8,128)S(1)} %get-tuple-element.36.refs_1_), channel_id=1, source_target_pairs={{0,1},{1,0},{2,3},{3,2},{4,5},{5,4},{6,7},{7,6},{8,9},{9,8},{10,11... | collective-permute-start | bytes 589832 | tf_op jit(solution)/shard_map/ppermute | solution.py:648
  39.6 7.5 %collective-permute-start.5 = (f32[64,384]{1,0:T(8,128)S(1)}, f32[64,384]{1,0:T(8,128)S(1)}, u32[]{:S(2)}, u32[]{:S(2)}) collective-permute-start(f32[64,384]{1,0:T(8,128)S(1)} %get-tuple-element.41), channel_id=1, source_target_pairs={{0,4},{1,5},{2,6},{3,7},{4,0},{5,1},{6,2},{7,3},{8,12},{9,13},{10,... | collective-permute-start | bytes 294920 | tf_op jit(solution)/shard_map/ppermute | solution.py:660
  42.7 4.6 %collective-permute-start.6 = (f32[64,384]{1,0:T(8,128)S(1)}, f32[64,384]{1,0:T(8,128)S(1)}, u32[]{:S(2)}, u32[]{:S(2)}) collective-permute-start(f32[64,384]{1,0:T(8,128)S(1)} %get-tuple-element.42), channel_id=1, source_target_pairs={{0,6},{1,7},{2,0},{3,1},{4,2},{5,3},{6,4},{7,5},{8,14},{9,15},{10,... | collective-permute-start | bytes 294920 | tf_op jit(solution)/shard_map/ppermute | solution.py:660
  43.8 5.8 %slice-start = ((s8[4718592]{0:T(1024)(128)(4,1)}), s8[4194304]{0:T(1024)(128)(4,1)S(1)}, s32[]{:S(2)}) async-start(s8[4718592]{0:T(1024)(128)(4,1)} %bitcast.3), calls=%async_computation | async-start | bytes 8388608
  43.8 5.8 %slice-start.1 = ((s8[4718592]{0:T(1024)(128)(4,1)}), s8[524288]{0:T(1024)(128)(4,1)S(1)}, s32[]{:S(2)}) async-start(s8[4718592]{0:T(1024)(128)(4,1)} %bitcast.3), calls=%async_computation.1 | async-start | bytes 1048576
  43.8 5.8 %collective-permute-start.4 = (f32[64,384]{1,0:T(8,128)S(1)}, f32[64,384]{1,0:T(8,128)S(1)}, u32[]{:S(2)}, u32[]{:S(2)}) collective-permute-start(f32[64,384]{1,0:T(8,128)S(1)} %get-tuple-element.40.refs_7_), channel_id=1, source_target_pairs={{0,2},{1,3},{2,4},{3,5},{4,6},{5,7},{6,0},{7,1},{8,10},{9,11},{10,... | collective-permute-start | bytes 294920 | tf_op jit(solution)/shard_map/ppermute | solution.py:660
  50.9 17.5 %collective-permute-start.10 = (bf16[8,96,384]{2,1,0:T(8,128)(2,1)S(1)}, bf16[8,96,384]{2,1,0:T(8,128)(2,1)S(1)}, u32[]{:S(2)}, u32[]{:S(2)}) collective-permute-start(bf16[8,96,384]{2,1,0:T(8,128)(2,1)S(1)} %get-tuple-element.46.refs_6_), channel_id=1, source_target_pairs={{0,32},{32,64},{64,96},{96,0},{1,33},{33,65},{65,97},{97,1},{2,34}... | collective-permute-start | bytes 1769480 | tf_op jit(solution)/shard_map/ppermute | solution.py:674
  53.7 16.3 %collective-permute-start.9 = (bf16[8,96,384]{2,1,0:T(8,128)(2,1)S(1)}, bf16[8,96,384]{2,1,0:T(8,128)(2,1)S(1)}, u32[]{:S(2)}, u32[]{:S(2)}) collective-permute-start(bf16[8,96,384]{2,1,0:T(8,128)(2,1)S(1)} %products_2.3.refs_6_), channel_id=1, source_target_pairs={{0,96},{32,0},{64,32},{96,64},{1,97},{33,1},{65,33},{97,65},{2,98}... | collective-permute-start | bytes 1769480 | tf_op jit(solution)/shard_map/ppermute | solution.py:676
  56.5 26.2 %collective-permute-start.8 = (bf16[8,96,384]{2,1,0:T(8,128)(2,1)S(1)}, bf16[8,96,384]{2,1,0:T(8,128)(2,1)S(1)}, u32[]{:S(2)}, u32[]{:S(2)}) collective-permute-start(bf16[8,96,384]{2,1,0:T(8,128)(2,1)S(1)} %products_1.2.refs_6_), channel_id=1, source_target_pairs={{0,32},{32,64},{64,96},{96,0},{1,33},{33,65},{65,97},{97,1},{2,34}... | collective-permute-start | bytes 1769480 | tf_op jit(solution)/shard_map/ppermute | solution.py:678
  58.2 24.5 %collective-permute-start.7 = (bf16[8,96,384]{2,1,0:T(8,128)(2,1)S(1)}, bf16[8,96,384]{2,1,0:T(8,128)(2,1)S(1)}, u32[]{:S(2)}, u32[]{:S(2)}) collective-permute-start(bf16[8,96,384]{2,1,0:T(8,128)(2,1)S(1)} %products_3.2.refs_7_), channel_id=1, source_target_pairs={{0,96},{32,0},{64,32},{96,64},{1,97},{33,1},{65,33},{97,65},{2,98}... | collective-permute-start | bytes 1769480 | tf_op jit(solution)/shard_map/ppermute | solution.py:680
  71.2 20.4 %collective-permute-start.12 = (bf16[8,96,384]{2,1,0:T(8,128)(2,1)S(1)}, bf16[8,96,384]{2,1,0:T(8,128)(2,1)S(1)}, u32[]{:S(2)}, u32[]{:S(2)}) collective-permute-start(bf16[8,96,384]{2,1,0:T(8,128)(2,1)S(1)} %products_3.3.refs_8_), channel_id=1, source_target_pairs={{0,96},{32,0},{64,32},{96,64},{1,97},{33,1},{65,33},{97,65},{2,98}... | collective-permute-start | bytes 1769480 | tf_op jit(solution)/shard_map/ppermute | solution.py:574
  74.1 17.5 %collective-permute-start.11 = (bf16[8,96,384]{2,1,0:T(8,128)(2,1)S(1)}, bf16[8,96,384]{2,1,0:T(8,128)(2,1)S(1)}, u32[]{:S(2)}, u32[]{:S(2)}) collective-permute-start(bf16[8,96,384]{2,1,0:T(8,128)(2,1)S(1)} %products_1.3.refs_7_), channel_id=1, source_target_pairs={{0,32},{32,64},{64,96},{96,0},{1,33},{33,65},{65,97},{97,1},{2,34}... | collective-permute-start | bytes 1769480 | tf_op jit(solution)/shard_map/ppermute | solution.py:572

commit v5 on v4

--- a/solution.py
+++ b/solution.py
@@ -229,7 +229,7 @@
 def field_kernel(
     sizes, where_ref, column_ref, decay_ref, gain_ref, end_ref, got1_ref, got2_ref, got3_ref,
     right_ref, right_sum_ref, chain_ref, triangle_ref,
-    fields, edge_ref, tables, powers, enters, scaled, sums,
+    fields, edge_ref, edge_send_ref, tables, powers, enters, scaled, sums,
 ):
     rows, cols, first_place, per_step, lat_count = sizes
     step = pl.program_id(0)
@@ -317,6 +317,10 @@
         edge_ref[0, pl.ds(row, 1), :] = end
         edge_ref[1, pl.ds(row, 1), :] = result[1:2] + result[3:4] + over_rows * echo * end
 
+    @pl.when(step == pl.num_programs(0) - 1)
+    def _():
+        edge_send_ref[...] = edge_ref[...].astype(BF16)
+
 
 def turn_block(scalars, number, quarters, blocks):
     turn = number // blocks
@@ -358,13 +362,13 @@
     chain = chain_ref[places, :]
     over, partner_over = chain[:, 32:33], chain[:, 34:35]
     end, returning = own_ref[0], own_ref[1]
-    got_end, got_returning = got_ref[0], got_ref[1]
+    got_end, got_returning = got_ref[0].astype(F32), got_ref[1].astype(F32)
     pair_end = jnp.where(second, end + over * got_end, got_end + partner_over * end)
     pair_returning = jnp.where(
         second, got_returning + partner_over * returning, returning + over * got_returning
     )
     for shift, ref in ((1, send1_ref), (2, send2_ref), (3, send3_ref)):
-        ref[...] = jnp.where(pair + shift < pairs, pair_end, pair_returning)
+        ref[...] = jnp.where(pair + shift < pairs, pair_end, pair_returning).astype(BF16)
 
 
 def first_send_kernel(
@@ -376,11 +380,12 @@
         second = jnp.bitwise_and(where_ref[2], 1) == 1
         chain = chain_ref[places, :]
         over, echo = chain[:, 32:33], chain[:, 33:34]
-        enter = jnp.where(second, got_ref[0], 0.0)
-        leave = jnp.where(second, 0.0, got_ref[1])
+        enter = jnp.where(second, got_ref[0].astype(F32), 0.0)
+        leave = jnp.where(second, 0.0, got_ref[1].astype(F32))
         for shift, ref in ((1, got1_ref), (2, got2_ref), (3, got3_ref)):
-            enter = enter + chain[:, shift : shift + 1] * ref[...]
-            leave = leave + chain[:, 64 + shift : 65 + shift] * ref[...]
+            got = ref[...].astype(F32)
+            enter = enter + chain[:, shift : shift + 1] * got
+            leave = leave + chain[:, 64 + shift : 65 + shift] * got
         enter_ref[...] = enter
         leave_ref[...] = over * (leave + echo * (own_ref[0] + over * enter))
         table_ref[...] = jnp.concatenate([left_ref[...], left_sum_ref[...]], axis=1)
@@ -398,7 +403,7 @@
     wide = lambda lane: jnp.concatenate([lane_of(table_ref[...], lane)] * (cols // LANES), axis=1)
     enter, leave = enter_ref[pl.ds(row, 1), :], leave_ref[pl.ds(row, 1), :]
     filtered = field_ref[u] + wide(place + half) * enter + wide(place) * leave
-    return spread_ref[0, u].astype(F32) * filtered.astype(BF16).astype(F32)
+    return spread_ref[0, u].astype(F32) * filtered
 
 
 def send_kernel(sizes, turn, start, where_ref, enter_ref, leave_ref, table_ref, field_ref, spread_ref, *refs):
@@ -599,15 +604,15 @@
         edge_row = sds((in_chunk, cols), F32)
         block = first_place // FIELD_STEP
         by_place = pl.BlockSpec((FIELD_STEP, LANES), lambda g, _, block=block: (block + g, 0))
-        fields, edge = call(
+        fields, edge, edge_send = call(
             functools.partial(field_kernel, (rows, cols, first_place, FIELD_STEP, lat_count)),
             "zonal_rows",
             (where, column, decay, gain, end, *got, right, right_sum, chain, triangle),
             [pl.BlockSpec((FIELD_STEP, rows, cols), lambda g, _, block=block: (block + g, 0, 0))]
             + [whole((rows, levels))] * 6
             + [by_place, by_place, by_place, whole(triangle.shape)],
-            (sds((in_chunk, 2 * LANES, cols), BF16), sds((2, in_chunk, cols), F32)),
-            (pl.BlockSpec((FIELD_STEP, 2 * LANES, cols), lambda g, _: (g, 0, 0)), edge_spec),
+            (sds((in_chunk, 2 * LANES, cols), BF16), sds((2, in_chunk, cols), F32), sds((2, in_chunk, cols), BF16)),
+            (pl.BlockSpec((FIELD_STEP, 2 * LANES, cols), lambda g, _: (g, 0, 0)), edge_spec, edge_spec),
             scratch=[
                 pltpu.VMEM((2, rows, 2 * levels), F32),
                 pltpu.VMEM((FIELD_STEP, 3, rows, LANES), F32),
@@ -645,18 +650,18 @@
                 aliases={6: 0} if extra else None,
             )
 
-        partner = lax.ppermute(edge, "lon", to_partner)
-        field = filter_rows(0, 4, None)
+        partner = lax.ppermute(edge_send, "lon", to_partner)
+        field = filter_rows(0, 2, None)
         pair_sends = call(
             functools.partial(pair_kernel, pairs=lon_count // 2, places=places),
             "pair_ends",
             (where, edge, partner, chain),
             [edge_spec, edge_spec, whole((levels, LANES))],
-            (edge_row,) * 3,
+            (sds((in_chunk, cols), BF16),) * 3,
             (row_spec,) * 3,
             after=(field,),
         )
-        field = filter_rows(4, 2, field, after=(pair_sends[0],))
+        field = filter_rows(2, 2, field, after=(pair_sends[0],))
         pair_got = [lax.ppermute(p, "lon", to_pair(k + 1)) for k, p in enumerate(pair_sends)]
         count = parts[0]
         two_up, enter, leave, lanes = call(
@@ -676,7 +681,9 @@
         two = two_up_moved, lax.ppermute(two_down, "mem", down)
         one_up = send(c, 1, 1, after=(two_down,))
         one_up_moved = lax.ppermute(one_up, "mem", up)
-        one_down = send(c, 3, 0, after=(one_up,))
+        field = filter_rows(4, 2, field, after=(one_up,))
+        states[c] = (field, enter, leave, lanes)
+        one_down = send(c, 3, 0)
         one = one_up_moved, lax.ppermute(one_down, "mem", down)
         field = filter_rows(6, 2, field, after=(one_down,))
         states[c] = (field, enter, leave, lanes)

time: 93.5 us -> 90.7 us (0.970)
  waiting for transfers between devices: 24.3 us -> 21.1 us
    ppermute x1, waiting for transfers between devices: 5.05 us -> 2.85 us  [per_device(): two_up_moved = lax.ppermute(two_up, 'mem', up)]
    pallas_call x14 -> x15, Pallas kernels: 42.7 us -> 42.9 us  [call(): pl.pallas_call(ordered, out_shape=outputs, grid_spec=pltpu.PrefetchScalar...]
  transfers between devices with their start and end apart: 13 -> 13, of which waited for: 7 -> 6; matrix products, arithmetic and copies ran while one was open for 0% -> 0% of each run, Pallas kernels for 20% -> 21%
where the time goes in v5:
time: 90.7 us; the launch traced here: 90.4 us
  Pallas kernels  42.9 us (47%)
  starting transfers between devices  22.2 us (24%)
  waiting for transfers between devices  21.1 us (23%)
  other arithmetic  1.72 us (2%)
  local copies, waits for them, and re-layouts  1.66 us (2%)
    pallas_call x15, Pallas kernels, call(): pl.pallas_call(ordered, out_shape=outputs, grid_spec=pltpu.PrefetchScalar...  42.9 us
    ppermute x1, waiting for transfers between devices, per_device(): one = (one_up_moved, lax.ppermute(one_down, 'mem', down))  8.6 us
    ppermute x1, waiting for transfers between devices, finish(): moved_down = lax.ppermute(sum_down, 'mem', down)  7.06 us
    ppermute x3, starting transfers between devices, per_device(): lax.ppermute(p, 'lon', to_pair(k + 1))  5.12 us
    ppermute x1, starting transfers between devices, per_device(): partner = lax.ppermute(edge_send, 'lon', to_partner)  3.66 us
    ppermute x3, starting transfers between devices, per_device(): lax.ppermute(s, 'lat', ring('lat', i + 1))  3.53 us
    ppermute x1, starting transfers between devices, finish(): moved_down = lax.ppermute(sum_down, 'mem', down)  2.94 us
    ppermute x1, starting transfers between devices, per_device(): one = (one_up_moved, lax.ppermute(one_down, 'mem', down))  2.93 us
  transfers between devices with their start and end apart: 13, of which 6 were waited for; matrix products, arithmetic and copies ran while one was open for 0% of the time, Pallas kernels for 21%

profile of v5, /device:TPU:0, one launch (start us, length us, event | category | flops | bytes accessed | tf_op | source)
XLA Modules:
  0.0 90.4 jit_solution(17260194237762828640)
XLA Ops:
  0.7 0.8 concatenate.6.refs_0_
  1.4 0.9 copy-done
  2.3 8.4 %vertical_columns.1 = (bf16[64,96,384]{2,1,0:T(8,128)(2,1)S(1)}, f32[96,64]{1,0:T(8,128)S(1)}, f32[96,64]{1,0:T(8,128)S(1)}, f32[96,64]{1,0:T(8,128)S(1)}, f32[9...) custom-call(s32[40]{0:T(128)S(1)} %concatenate.6.refs_0_, bf16[1,64,96,384]{3,2,1,0:T(8,128)(2,1)} %refs_1_.2, ...), custom_call_target="tpu_custom_call" | custom-call | flops 2415919104 | bytes 9437184 | tf_op jit(solution)/shard_map/vertical_columns/pallas_call | solution.py:443
  10.7 0.1 collective-permute-start
  10.8 2.1 %collective-permute-start.1 = (f32[96,64]{1,0:T(8,128)S(1)}, f32[96,64]{1,0:T(8,128)S(1)}, u32[]{:S(2)}, u32[]{:S(2)}) collective-permute-start(f32[96,64]{1,0:T(8,128)S(1)} %get-tuple-element.32), channel_id=1, source_target_pairs={{0,16},{8,24},{16,0},{24,8},{1,17},{9,25},{17,1},{25,9},{2,18},{10... | collective-permute-start | bytes 73736 | tf_op jit(solution)/shard_map/ppermute | solution.py:512
  12.9 1.4 %collective-permute-start.2 = (f32[96,64]{1,0:T(8,128)S(1)}, f32[96,64]{1,0:T(8,128)S(1)}, u32[]{:S(2)}, u32[]{:S(2)}) collective-permute-start(f32[96,64]{1,0:T(8,128)S(1)} %get-tuple-element.33), channel_id=1, source_target_pairs={{0,24},{8,0},{16,8},{24,16},{1,25},{9,1},{17,9},{25,17},{2,26},{10... | collective-permute-start | bytes 73736 | tf_op jit(solution)/shard_map/ppermute | solution.py:512
  14.2 0.0 copy-done.1
  14.2 2.7 %row_terms.1 = (f32[96,64]{1,0:T(8,128)S(1)}, f32[96,64]{1,0:T(8,128)S(1)}, f32[64,128]{1,0:T(8,128)S(1)}, f32[64,128]{1,0:T(8,128)S(1)}, f32[64,128]{1,0:T(8,128)S(1)}) custom-call(s32[40]{0:T(128)S(1)} %concatenate.6.refs_0_, f32[32,768]{1,0:T(8,128)S(1)} %copy-done.1), custom_call_target="tpu_custom_call" | custom-call | flops 452984832 | bytes 1048576 | tf_op jit(solution)/shard_map/row_terms/pallas_call | solution.py:443
  17.0 0.0 collective-permute-done.refs_5_
  17.0 0.0 collective-permute-done.1.refs_6_
  17.0 0.0 collective-permute-done.2.refs_7_
  17.0 0.0 copy-done.2
  17.0 13.7 %zonal_rows.1 = (bf16[64,256,384]{2,1,0:T(8,128)(2,1)S(1)}, f32[2,64,384]{2,1,0:T(8,128)S(1)}, bf16[2,64,384]{2,1,0:T(8,128)(2,1)S(1)}) custom-call(s32[40]{0:T(128)S(1)} %concatenate.6.refs_0_, bf16[64,96,384]{2,1,0:T(8,128)(2,1)S(1)} %get-tuple-element.27.refs_1_, f32[96,64]{1,0:T(8,128)S(1)} %get-tuple-element.28.refs_2_, ...), custom_call_target="tpu_custom_call" | custom-call | flops 14495514624 | bytes 14155776 | tf_op jit(solution)/shard_map/zonal_rows/pallas_call | solution.py:443
  30.7 3.7 %collective-permute-start.3 = (bf16[2,64,384]{2,1,0:T(8,128)(2,1)S(1)}, bf16[2,64,384]{2,1,0:T(8,128)(2,1)S(1)}, u32[]{:S(2)}, u32[]{:S(2)}) collective-permute-start(bf16[2,64,384]{2,1,0:T(8,128)(2,1)S(1)} %get-tuple-element.38), channel_id=1, source_target_pairs={{0,1},{1,0},{2,3},{3,2},{4,5},{5,4},{6,7},{7,6},{8,9},{9,8},{10,11... | collective-permute-start | bytes 294920 | tf_op jit(solution)/shard_map/ppermute | solution.py:653
  34.4 2.4 %row_filter.4.refs_4_.refs_6_ = f32[64,96,384]{2,1,0:T(8,128)S(1)} custom-call(s32[40]{0:T(128)S(1)} %concatenate.6.refs_0_, bf16[64,256,384]{2,1,0:T(8,128)(2,1)S(1)} %get-tuple-element.39.refs_1_, f32[96,64]{1,0:T(8,128)S(1)} %get-tuple-element.40.refs_2_.refs_7_, f32[96,64]{1,0:T(8,128)S(1)} %get-tuple-element.41.refs_3_.refs_8_, ...), custom_call_target="tpu_custom_call" | custom-call | flops 301989888 | bytes 4718592 | tf_op jit(solution)/shard_map/row_filter/pallas_call | solution.py:443
  36.7 0.2 collective-permute-done.3.refs_2_
  37.0 0.7 pair_ends.1
  37.6 3.1 %collective-permute-start.5 = (bf16[64,384]{1,0:T(8,128)(2,1)S(1)}, bf16[64,384]{1,0:T(8,128)(2,1)S(1)}, u32[]{:S(2)}, u32[]{:S(2)}) collective-permute-start(bf16[64,384]{1,0:T(8,128)(2,1)S(1)} %get-tuple-element.43), channel_id=1, source_target_pairs={{0,4},{1,5},{2,6},{3,7},{4,0},{5,1},{6,2},{7,3},{8,12},{9,13},{10,... | collective-permute-start | bytes 147464 | tf_op jit(solution)/shard_map/ppermute | solution.py:665
  40.7 1.1 %collective-permute-start.6 = (bf16[64,384]{1,0:T(8,128)(2,1)S(1)}, bf16[64,384]{1,0:T(8,128)(2,1)S(1)}, u32[]{:S(2)}, u32[]{:S(2)}) collective-permute-start(bf16[64,384]{1,0:T(8,128)(2,1)S(1)} %get-tuple-element.44), channel_id=1, source_target_pairs={{0,6},{1,7},{2,0},{3,1},{4,2},{5,3},{6,4},{7,5},{8,14},{9,15},{10,... | collective-permute-start | bytes 147464 | tf_op jit(solution)/shard_map/ppermute | solution.py:665
  41.9 0.9 collective-permute-start.4
  42.8 2.4 %row_filter.5.refs_9_.refs_4_.refs_6_ = f32[64,96,384]{2,1,0:T(8,128)S(1)} custom-call(s32[40]{0:T(128)S(1)} %concatenate.6.refs_0_, bf16[64,256,384]{2,1,0:T(8,128)(2,1)S(1)} %get-tuple-element.39.refs_1_, f32[96,64]{1,0:T(8,128)S(1)} %get-tuple-element.40.refs_2_.refs_7_, ...), custom_call_target="tpu_custom_call", output_to_operand_aliasing={{}: (6, {})} | custom-call | flops 301989888 | bytes 4718592 | tf_op jit(solution)/shard_map/row_filter/pallas_call | solution.py:443
  45.1 0.0 collective-permute-done.5.refs_4_
  45.1 0.0 collective-permute-done.6.refs_5_
  45.1 2.0 %collective-permute-done.4.refs_3_ = bf16[64,384]{1,0:T(8,128)(2,1)S(1)} collective-permute-done((bf16[64,384]{1,0:T(8,128)(2,1)S(1)}, bf16[64,384]{1,0:T(8,128)(2,1)S(1)}, u32[]{:S(2)}, u32[]{:S(2)}) %collective-permute-start.4) | collective-permute-done | bytes 49184 | tf_op jit(solution)/shard_map/ppermute | solution.py:665
  47.2 0.0 slice-done
  47.2 0.0 slice-done.1
  47.2 1.2 %products_2.2 = (bf16[8,96,384]{2,1,0:T(8,128)(2,1)S(1)}, f32[64,384]{1,0:T(8,128)S(1)}, f32[64,384]{1,0:T(8,128)S(1)}, f32[96,128]{1,0:T(8,128)S(1)}) custom-call(s32[40]{0:T(128)S(1)} %concatenate.6.refs_0_, f32[2,64,384]{2,1,0:T(8,128)S(1)} %get-tuple-element.37.refs_1_, bf16[2,64,384]{2,1,0:T(8,128)(2,1)S(1)} %collective-permute-done.3.refs_2_, ...), custom_call_target="tpu_custom_call" | custom-call | flops 2359296 | bytes 2359296 | tf_op jit(solution)/shard_map/products_2/pallas_call | solution.py:443
  48.4 1.6 %collective-permute-start.10 = (bf16[8,96,384]{2,1,0:T(8,128)(2,1)S(1)}, bf16[8,96,384]{2,1,0:T(8,128)(2,1)S(1)}, u32[]{:S(2)}, u32[]{:S(2)}) collective-permute-start(bf16[8,96,384]{2,1,0:T(8,128)(2,1)S(1)} %get-tuple-element.48.refs_6_), channel_id=1, source_target_pairs={{0,32},{32,64},{64,96},{96,0},{1,33},{33,65},{65,97},{97,1},{2,34}... | collective-permute-start | bytes 1769480 | tf_op jit(solution)/shard_map/ppermute | solution.py:679
  50.1 1.0 %products_2.3.refs_6_ = bf16[8,96,384]{2,1,0:T(8,128)(2,1)S(1)} custom-call(s32[40]{0:T(128)S(1)} %concatenate.6.refs_0_, f32[64,384]{1,0:T(8,128)S(1)} %get-tuple-element.45.refs_1_, f32[64,384]{1,0:T(8,128)S(1)} %get-tuple-element.46.refs_2_, f32[96,128]{1,0:T(8,128)S(1)} %get-tuple-element.47.refs_3_, ...), custom_call_target="tpu_custom_call" | custom-call | flops 2359296 | bytes 2359296 | tf_op jit(solution)/shard_map/products_2/pallas_call | solution.py:443
  51.1 1.7 %collective-permute-start.9 = (bf16[8,96,384]{2,1,0:T(8,128)(2,1)S(1)}, bf16[8,96,384]{2,1,0:T(8,128)(2,1)S(1)}, u32[]{:S(2)}, u32[]{:S(2)}) collective-permute-start(bf16[8,96,384]{2,1,0:T(8,128)(2,1)S(1)} %products_2.3.refs_6_), channel_id=1, source_target_pairs={{0,96},{32,0},{64,32},{96,64},{1,97},{33,1},{65,33},{97,65},{2,98}... | collective-permute-start | bytes 1769480 | tf_op jit(solution)/shard_map/ppermute | solution.py:681
  52.8 1.0 %products_1.2.refs_7_ = bf16[8,96,384]{2,1,0:T(8,128)(2,1)S(1)} custom-call(s32[40]{0:T(128)S(1)} %concatenate.6.refs_0_, f32[64,384]{1,0:T(8,128)S(1)} %get-tuple-element.45.refs_1_, f32[64,384]{1,0:T(8,128)S(1)} %get-tuple-element.46.refs_2_, f32[96,128]{1,0:T(8,128)S(1)} %get-tuple-element.47.refs_3_, ...), custom_call_target="tpu_custom_call" | custom-call | flops 2359296 | bytes 2359296 | tf_op jit(solution)/shard_map/products_1/pallas_call | solution.py:443
  53.8 0.6 collective-permute-start.8
  54.4 2.4 %row_filter.6.refs_4_.refs_6_ = f32[64,96,384]{2,1,0:T(8,128)S(1)} custom-call(s32[40]{0:T(128)S(1)} %concatenate.6.refs_0_, bf16[64,256,384]{2,1,0:T(8,128)(2,1)S(1)} %get-tuple-element.39.refs_1_, f32[96,64]{1,0:T(8,128)S(1)} %get-tuple-element.40.refs_2_.refs_7_, f32[96,64]{1,0:T(8,128)S(1)} %get-tuple-element.41.refs_3_.refs_8_, ...), custom_call_target="tpu_custom_call", output_to_operand_aliasing={{}: (6, {})} | custom-call | flops 301989888 | bytes 4718592 | tf_op jit(solution)/shard_map/row_filter/pallas_call | solution.py:443
  56.8 1.0 %products_3.2.refs_7_ = bf16[8,96,384]{2,1,0:T(8,128)(2,1)S(1)} custom-call(s32[40]{0:T(128)S(1)} %concatenate.6.refs_0_, f32[64,384]{1,0:T(8,128)S(1)} %get-tuple-element.45.refs_1_, f32[64,384]{1,0:T(8,128)S(1)} %get-tuple-element.46.refs_2_, f32[96,128]{1,0:T(8,128)S(1)} %get-tuple-element.47.refs_3_, f32[64,96,384]{2,1,0:T(8,128)S(1)} %row_filter.6.refs_4_.refs_6_, ...), custom_call_target="tpu_custom_call" | custom-call | flops 2359296 | bytes 2359296 | tf_op jit(solution)/shard_map/products_3/pallas_call | solution.py:443
  57.8 2.9 %collective-permute-start.7 = (bf16[8,96,384]{2,1,0:T(8,128)(2,1)S(1)}, bf16[8,96,384]{2,1,0:T(8,128)(2,1)S(1)}, u32[]{:S(2)}, u32[]{:S(2)}) collective-permute-start(bf16[8,96,384]{2,1,0:T(8,128)(2,1)S(1)} %products_3.2.refs_7_), channel_id=1, source_target_pairs={{0,96},{32,0},{64,32},{96,64},{1,97},{33,1},{65,33},{97,65},{2,98}... | collective-permute-start | bytes 1769480 | tf_op jit(solution)/shard_map/ppermute | solution.py:687
  60.8 2.4 %row_filter.7.refs_4_ = f32[64,96,384]{2,1,0:T(8,128)S(1)} custom-call(s32[40]{0:T(128)S(1)} %concatenate.6.refs_0_, bf16[64,256,384]{2,1,0:T(8,128)(2,1)S(1)} %get-tuple-element.39.refs_1_, f32[96,64]{1,0:T(8,128)S(1)} %get-tuple-element.40.refs_2_.refs_7_, f32[96,64]{1,0:T(8,128)S(1)} %get-tuple-element.41.refs_3_.refs_8_, ...), custom_call_target="tpu_custom_call", output_to_operand_aliasing={{}: (6, {})} | custom-call | flops 301989888 | bytes 4718592 | tf_op jit(solution)/shard_map/row_filter/pallas_call | solution.py:443
  63.1 2.8 %collective-permute-done.10.refs_6_ = bf16[8,96,384]{2,1,0:T(8,128)(2,1)S(1)} collective-permute-done((bf16[8,96,384]{2,1,0:T(8,128)(2,1)S(1)}, bf16[8,96,384]{2,1,0:T(8,128)(2,1)S(1)}, u32[]{:S(2)}, u32[]{:S(2)}) %collective-permute-start.10) | collective-permute-done | bytes 589856 | tf_op jit(solution)/shard_map/ppermute | solution.py:679
  66.0 1.1 %products_1.3.refs_7_ = bf16[8,96,384]{2,1,0:T(8,128)(2,1)S(1)} custom-call(s32[40]{0:T(128)S(1)} %concatenate.6.refs_0_, f32[64,384]{1,0:T(8,128)S(1)} %get-tuple-element.45.refs_1_, f32[64,384]{1,0:T(8,128)S(1)} %get-tuple-element.46.refs_2_, f32[96,128]{1,0:T(8,128)S(1)} %get-tuple-element.47.refs_3_, f32[64,96,384]{2,1,0:T(8,128)S(1)} %row_filter.7.refs_4_, ...), custom_call_target="tpu_custom_call" | custom-call | flops 2359296 | bytes 2359296 | tf_op jit(solution)/shard_map/products_1/pallas_call | solution.py:443
  67.1 0.3 collective-permute-done.9.refs_6_
  67.4 1.1 %products_3.3.refs_8_ = bf16[8,96,384]{2,1,0:T(8,128)(2,1)S(1)} custom-call(s32[40]{0:T(128)S(1)} %concatenate.6.refs_0_, f32[64,384]{1,0:T(8,128)S(1)} %get-tuple-element.45.refs_1_, f32[64,384]{1,0:T(8,128)S(1)} %get-tuple-element.46.refs_2_, f32[96,128]{1,0:T(8,128)S(1)} %get-tuple-element.47.refs_3_, f32[64,96,384]{2,1,0:T(8,128)S(1)} %row_filter.7.refs_4_, ...), custom_call_target="tpu_custom_call" | custom-call | flops 2359296 | bytes 2359296 | tf_op jit(solution)/shard_map/products_3/pallas_call | solution.py:443
  68.5 2.9 %collective-permute-start.12 = (bf16[8,96,384]{2,1,0:T(8,128)(2,1)S(1)}, bf16[8,96,384]{2,1,0:T(8,128)(2,1)S(1)}, u32[]{:S(2)}, u32[]{:S(2)}) collective-permute-start(bf16[8,96,384]{2,1,0:T(8,128)(2,1)S(1)} %products_3.3.refs_8_), channel_id=1, source_target_pairs={{0,96},{32,0},{64,32},{96,64},{1,97},{33,1},{65,33},{97,65},{2,98}... | collective-permute-start | bytes 1769480 | tf_op jit(solution)/shard_map/ppermute | solution.py:579
  71.5 0.0 collective-permute-start.11
  71.5 8.6 %collective-permute-done.7.refs_6_ = bf16[8,96,384]{2,1,0:T(8,128)(2,1)S(1)} collective-permute-done((bf16[8,96,384]{2,1,0:T(8,128)(2,1)S(1)}, bf16[8,96,384]{2,1,0:T(8,128)(2,1)S(1)}, u32[]{:S(2)}, u32[]{:S(2)}) %collective-permute-start.7) | collective-permute-done | bytes 589856 | tf_op jit(solution)/shard_map/ppermute | solution.py:687
  80.1 0.0 collective-permute-done.8.refs_7_
  80.1 1.6 %products_here.1 = f32[16,96,384]{2,1,0:T(8,128)S(1)} custom-call(s32[40]{0:T(128)S(1)} %concatenate.6.refs_0_, f32[64,384]{1,0:T(8,128)S(1)} %get-tuple-element.45.refs_1_, f32[64,384]{1,0:T(8,128)S(1)} %get-tuple-element.46.refs_2_, f32[96,128]{1,0:T(8,128)S(1)} %get-tuple-element.47.refs_3_, f32[64,96,384]{2,1,0:T(8,128)S(1)} %row_filter.7.refs_4_, ...), custom_call_target="tpu_custom_call" | custom-call | flops 4718592 | bytes 8257536 | tf_op jit(solution)/shard_map/products_here/pallas_call | solution.py:443
  81.6 7.1 %collective-permute-done.12 = bf16[8,96,384]{2,1,0:T(8,128)(2,1)S(1)} collective-permute-done((bf16[8,96,384]{2,1,0:T(8,128)(2,1)S(1)}, bf16[8,96,384]{2,1,0:T(8,128)(2,1)S(1)}, u32[]{:S(2)}, u32[]{:S(2)}) %collective-permute-start.12) | collective-permute-done | bytes 589856 | tf_op jit(solution)/shard_map/ppermute | solution.py:579
  88.7 0.0 collective-permute-done.11
  88.7 1.7 %add_multiply_fusion = f32[16,96,384]{2,1,0:T(8,128)} fusion(f32[16,96,384]{2,1,0:T(8,128)S(1)} %products_here.1, bf16[8,96,384]{2,1,0:T(8,128)(2,1)S(1)} %collective-permute-done.12, bf16[8,96,384]{2,1,0:T(8,128)(2,1)S(1)} %collective-permute-done.11), kind=kLoop, calls=%fused_computation | loop fusion | flops 2359296 | bytes 5898240 | tf_op jit(solution)/shard_map/mul | solution.py:596
  (6 shorter events, 0.0 us)
Async XLA Ops:
  1.4 0.9 copy-start
  2.3 11.9 %copy-start.1 = (f32[32,768]{1,0:T(8,128)S(1)}, f32[32,768]{1,0:T(8,128)}, u32[]{:S(2)}) copy-start(f32[32,768]{1,0:T(8,128)} %refs_1_.3) | copy-start | bytes 294916
  2.3 14.7 %copy-start.2 = (bf16[256,256]{1,0:T(8,128)(2,1)S(1)}, bf16[256,256]{1,0:T(8,128)(2,1)}, u32[]{:S(2)}) copy-start(bf16[256,256]{1,0:T(8,128)(2,1)} %constant.16.clone.refs_11_) | copy-start | bytes 393220
  10.7 6.3 %collective-permute-start = (f32[96,64]{1,0:T(8,128)S(1)}, f32[96,64]{1,0:T(8,128)S(1)}, u32[]{:S(2)}, u32[]{:S(2)}) collective-permute-start(f32[96,64]{1,0:T(8,128)S(1)} %get-tuple-element.31), channel_id=1, source_target_pairs={{0,8},{8,16},{16,24},{24,0},{1,9},{9,17},{17,25},{25,1},{2,10},{10... | collective-permute-start | bytes 73736 | tf_op jit(solution)/shard_map/ppermute | solution.py:512
  10.8 6.2 %collective-permute-start.1 = (f32[96,64]{1,0:T(8,128)S(1)}, f32[96,64]{1,0:T(8,128)S(1)}, u32[]{:S(2)}, u32[]{:S(2)}) collective-permute-start(f32[96,64]{1,0:T(8,128)S(1)} %get-tuple-element.32), channel_id=1, source_target_pairs={{0,16},{8,24},{16,0},{24,8},{1,17},{9,25},{17,1},{25,9},{2,18},{10... | collective-permute-start | bytes 73736 | tf_op jit(solution)/shard_map/ppermute | solution.py:512
  12.9 4.1 %collective-permute-start.2 = (f32[96,64]{1,0:T(8,128)S(1)}, f32[96,64]{1,0:T(8,128)S(1)}, u32[]{:S(2)}, u32[]{:S(2)}) collective-permute-start(f32[96,64]{1,0:T(8,128)S(1)} %get-tuple-element.33), channel_id=1, source_target_pairs={{0,24},{8,0},{16,8},{24,16},{1,25},{9,1},{17,9},{25,17},{2,26},{10... | collective-permute-start | bytes 73736 | tf_op jit(solution)/shard_map/ppermute | solution.py:512
  30.7 6.3 %collective-permute-start.3 = (bf16[2,64,384]{2,1,0:T(8,128)(2,1)S(1)}, bf16[2,64,384]{2,1,0:T(8,128)(2,1)S(1)}, u32[]{:S(2)}, u32[]{:S(2)}) collective-permute-start(bf16[2,64,384]{2,1,0:T(8,128)(2,1)S(1)} %get-tuple-element.38), channel_id=1, source_target_pairs={{0,1},{1,0},{2,3},{3,2},{4,5},{5,4},{6,7},{7,6},{8,9},{9,8},{10,11... | collective-permute-start | bytes 294920 | tf_op jit(solution)/shard_map/ppermute | solution.py:653
  37.6 7.5 %collective-permute-start.5 = (bf16[64,384]{1,0:T(8,128)(2,1)S(1)}, bf16[64,384]{1,0:T(8,128)(2,1)S(1)}, u32[]{:S(2)}, u32[]{:S(2)}) collective-permute-start(bf16[64,384]{1,0:T(8,128)(2,1)S(1)} %get-tuple-element.43), channel_id=1, source_target_pairs={{0,4},{1,5},{2,6},{3,7},{4,0},{5,1},{6,2},{7,3},{8,12},{9,13},{10,... | collective-permute-start | bytes 147464 | tf_op jit(solution)/shard_map/ppermute | solution.py:665
  40.7 4.4 %collective-permute-start.6 = (bf16[64,384]{1,0:T(8,128)(2,1)S(1)}, bf16[64,384]{1,0:T(8,128)(2,1)S(1)}, u32[]{:S(2)}, u32[]{:S(2)}) collective-permute-start(bf16[64,384]{1,0:T(8,128)(2,1)S(1)} %get-tuple-element.44), channel_id=1, source_target_pairs={{0,6},{1,7},{2,0},{3,1},{4,2},{5,3},{6,4},{7,5},{8,14},{9,15},{10,... | collective-permute-start | bytes 147464 | tf_op jit(solution)/shard_map/ppermute | solution.py:665
  41.9 5.3 %slice-start = ((s8[4718592]{0:T(1024)(128)(4,1)}), s8[4194304]{0:T(1024)(128)(4,1)S(1)}, s32[]{:S(2)}) async-start(s8[4718592]{0:T(1024)(128)(4,1)} %bitcast.3), calls=%async_computation | async-start | bytes 8388608
  41.9 5.3 %slice-start.1 = ((s8[4718592]{0:T(1024)(128)(4,1)}), s8[524288]{0:T(1024)(128)(4,1)S(1)}, s32[]{:S(2)}) async-start(s8[4718592]{0:T(1024)(128)(4,1)} %bitcast.3), calls=%async_computation.1 | async-start | bytes 1048576
  41.9 5.3 %collective-permute-start.4 = (bf16[64,384]{1,0:T(8,128)(2,1)S(1)}, bf16[64,384]{1,0:T(8,128)(2,1)S(1)}, u32[]{:S(2)}, u32[]{:S(2)}) collective-permute-start(bf16[64,384]{1,0:T(8,128)(2,1)S(1)} %get-tuple-element.42.refs_7_), channel_id=1, source_target_pairs={{0,2},{1,3},{2,4},{3,5},{4,6},{5,7},{6,0},{7,1},{8,10},{9,11},{10,... | collective-permute-start | bytes 147464 | tf_op jit(solution)/shard_map/ppermute | solution.py:665
  48.4 17.5 %collective-permute-start.10 = (bf16[8,96,384]{2,1,0:T(8,128)(2,1)S(1)}, bf16[8,96,384]{2,1,0:T(8,128)(2,1)S(1)}, u32[]{:S(2)}, u32[]{:S(2)}) collective-permute-start(bf16[8,96,384]{2,1,0:T(8,128)(2,1)S(1)} %get-tuple-element.48.refs_6_), channel_id=1, source_target_pairs={{0,32},{32,64},{64,96},{96,0},{1,33},{33,65},{65,97},{97,1},{2,34}... | collective-permute-start | bytes 1769480 | tf_op jit(solution)/shard_map/ppermute | solution.py:679
  51.1 16.3 %collective-permute-start.9 = (bf16[8,96,384]{2,1,0:T(8,128)(2,1)S(1)}, bf16[8,96,384]{2,1,0:T(8,128)(2,1)S(1)}, u32[]{:S(2)}, u32[]{:S(2)}) collective-permute-start(bf16[8,96,384]{2,1,0:T(8,128)(2,1)S(1)} %products_2.3.refs_6_), channel_id=1, source_target_pairs={{0,96},{32,0},{64,32},{96,64},{1,97},{33,1},{65,33},{97,65},{2,98}... | collective-permute-start | bytes 1769480 | tf_op jit(solution)/shard_map/ppermute | solution.py:681
  53.8 26.2 %collective-permute-start.8 = (bf16[8,96,384]{2,1,0:T(8,128)(2,1)S(1)}, bf16[8,96,384]{2,1,0:T(8,128)(2,1)S(1)}, u32[]{:S(2)}, u32[]{:S(2)}) collective-permute-start(bf16[8,96,384]{2,1,0:T(8,128)(2,1)S(1)} %products_1.2.refs_7_), channel_id=1, source_target_pairs={{0,32},{32,64},{64,96},{96,0},{1,33},{33,65},{65,97},{97,1},{2,34}... | collective-permute-start | bytes 1769480 | tf_op jit(solution)/shard_map/ppermute | solution.py:683
  57.8 22.2 %collective-permute-start.7 = (bf16[8,96,384]{2,1,0:T(8,128)(2,1)S(1)}, bf16[8,96,384]{2,1,0:T(8,128)(2,1)S(1)}, u32[]{:S(2)}, u32[]{:S(2)}) collective-permute-start(bf16[8,96,384]{2,1,0:T(8,128)(2,1)S(1)} %products_3.2.refs_7_), channel_id=1, source_target_pairs={{0,96},{32,0},{64,32},{96,64},{1,97},{33,1},{65,33},{97,65},{2,98}... | collective-permute-start | bytes 1769480 | tf_op jit(solution)/shard_map/ppermute | solution.py:687
  68.5 20.2 %collective-permute-start.12 = (bf16[8,96,384]{2,1,0:T(8,128)(2,1)S(1)}, bf16[8,96,384]{2,1,0:T(8,128)(2,1)S(1)}, u32[]{:S(2)}, u32[]{:S(2)}) collective-permute-start(bf16[8,96,384]{2,1,0:T(8,128)(2,1)S(1)} %products_3.3.refs_8_), channel_id=1, source_target_pairs={{0,96},{32,0},{64,32},{96,64},{1,97},{33,1},{65,33},{97,65},{2,98}... | collective-permute-start | bytes 1769480 | tf_op jit(solution)/shard_map/ppermute | solution.py:579
  71.5 17.3 %collective-permute-start.11 = (bf16[8,96,384]{2,1,0:T(8,128)(2,1)S(1)}, bf16[8,96,384]{2,1,0:T(8,128)(2,1)S(1)}, u32[]{:S(2)}, u32[]{:S(2)}) collective-permute-start(bf16[8,96,384]{2,1,0:T(8,128)(2,1)S(1)} %products_1.3.refs_7_), channel_id=1, source_target_pairs={{0,32},{32,64},{64,96},{96,0},{1,33},{33,65},{65,97},{97,1},{2,34}... | collective-permute-start | bytes 1769480 | tf_op jit(solution)/shard_map/ppermute | solution.py:577

commit v6 on v5

--- a/solution.py
+++ b/solution.py
@@ -373,7 +373,7 @@
 
 def first_send_kernel(
     sizes, turn, places, where_ref, own_ref, got_ref, got1_ref, got2_ref, got3_ref, chain_ref, left_ref, left_sum_ref,
-    field_ref, spread_ref, out_ref, enter_ref, leave_ref, table_ref,
+    field0_ref, spread0_ref, field1_ref, spread1_ref, out0_ref, out1_ref, enter_ref, leave_ref, table_ref,
 ):
     @pl.when(pl.program_id(0) == 0)
     def _():
@@ -390,7 +390,9 @@
         leave_ref[...] = over * (leave + echo * (own_ref[0] + over * enter))
         table_ref[...] = jnp.concatenate([left_ref[...], left_sum_ref[...]], axis=1)
 
-    send_kernel(sizes, turn, 0, where_ref, enter_ref, leave_ref, table_ref, field_ref, spread_ref, out_ref)
+    state = (where_ref, enter_ref, leave_ref, table_ref)
+    send_kernel(sizes, turn, 0, *state, field0_ref, spread0_ref, out0_ref)
+    send_kernel(sizes, turn, sizes[1] // 2, *state, field1_ref, spread1_ref, out1_ref)
 
 
 def one_product(where_ref, refs, sizes, turn, step, u):
@@ -664,20 +666,20 @@
         field = filter_rows(2, 2, field, after=(pair_sends[0],))
         pair_got = [lax.ppermute(p, "lon", to_pair(k + 1)) for k, p in enumerate(pair_sends)]
         count = parts[0]
-        two_up, enter, leave, lanes = call(
+        two_up, two_down, enter, leave, lanes = call(
             functools.partial(first_send_kernel, product_sizes(c), 2, places),
             "products_2",
-            (where, edge, partner, *pair_got, chain, left, left_sum, field, perturbation),
+            (where, edge, partner, *pair_got, chain, left, left_sum, *((field, perturbation) * 2)),
             [edge_spec, edge_spec, row_spec, row_spec, row_spec, whole((levels, LANES)), *table_specs]
-            + quarter_specs(c, 2, 0),
-            (sds((count, rows, cols), BF16), edge_row, edge_row, table_wide),
-            (by_step(0), row_spec, row_spec, whole(table_wide.shape)),
+            + quarter_specs(c, 2, 0)
+            + quarter_specs(c, 2, count),
+            (sds((count, rows, cols), BF16),) * 2 + (edge_row, edge_row, table_wide),
+            (by_step(0), by_step(0), row_spec, row_spec, whole(table_wide.shape)),
             grid=(count // PRODUCT_STEP,),
             cost=cost(count * plane * 8, count * plane * 8),
         )
         states.append((field, enter, leave, lanes))
         two_up_moved = lax.ppermute(two_up, "mem", up)
-        two_down = send(c, 2, 1, after=(two_up,))
         two = two_up_moved, lax.ppermute(two_down, "mem", down)
         one_up = send(c, 1, 1, after=(two_down,))
         one_up_moved = lax.ppermute(one_up, "mem", up)

time: 90.7 us -> 89.9 us (level)
    ppermute x1, waiting for transfers between devices: 0.01 us -> 7.03 us  [finish(): moved_up = lax.ppermute(sum_up, 'mem', up)]
    ppermute x1, waiting for transfers between devices: 7.06 us -> 0.03 us  [finish(): moved_down = lax.ppermute(sum_down, 'mem', down)]
    ppermute x1, waiting for transfers between devices: 8.6 us -> 7.42 us  [per_device(): one = (one_up_moved, lax.ppermute(one_down, 'mem', down))]
    ppermute x1, waiting for transfers between devices: 2.85 us -> 3.93 us  [per_device(): two_up_moved = lax.ppermute(two_up, 'mem', up)]
    pallas_call x15 -> x14, Pallas kernels: 42.9 us -> 42.2 us  [call(): pl.pallas_call(ordered, out_shape=outputs, grid_spec=pltpu.PrefetchScalar...]
  transfers between devices with their start and end apart: 13 -> 13, of which waited for: 6 -> 5; matrix products, arithmetic and copies ran while one was open for 0% -> 0% of each run, Pallas kernels for 21% -> 20%
where the time goes in v6:
time: 89.9 us; the launch traced here: 89.6 us
  Pallas kernels  42.2 us (47%)
  starting transfers between devices  22.5 us (25%)
  waiting for transfers between devices  20.7 us (23%)
  other arithmetic  1.72 us (2%)
  local copies, waits for them, and re-layouts  1.66 us (2%)
    pallas_call x14, Pallas kernels, call(): pl.pallas_call(ordered, out_shape=outputs, grid_spec=pltpu.PrefetchScalar...  42.2 us
    ppermute x1, waiting for transfers between devices, per_device(): one = (one_up_moved, lax.ppermute(one_down, 'mem', down))  7.42 us
    ppermute x1, waiting for transfers between devices, finish(): moved_up = lax.ppermute(sum_up, 'mem', up)  7.03 us
    ppermute x3, starting transfers between devices, per_device(): lax.ppermute(p, 'lon', to_pair(k + 1))  5.12 us
    ppermute x1, waiting for transfers between devices, per_device(): two_up_moved = lax.ppermute(two_up, 'mem', up)  3.93 us
    ppermute x1, starting transfers between devices, per_device(): partner = lax.ppermute(edge_send, 'lon', to_partner)  3.66 us
    ppermute x3, starting transfers between devices, per_device(): lax.ppermute(s, 'lat', ring('lat', i + 1))  3.53 us
    ppermute x1, starting transfers between devices, finish(): moved_down = lax.ppermute(sum_down, 'mem', down)  2.95 us
  transfers between devices with their start and end apart: 13, of which 5 were waited for; matrix products, arithmetic and copies ran while one was open for 0% of the time, Pallas kernels for 20%

profile of v6, /device:TPU:0, one launch (start us, length us, event | category | flops | bytes accessed | tf_op | source)
XLA Modules:
  0.0 89.6 jit_solution(1351655250995501844)
XLA Ops:
  0.7 0.8 concatenate.6.refs_0_
  1.4 0.0 copy-start
  1.4 0.9 copy-done
  2.3 8.4 %vertical_columns.1 = (bf16[64,96,384]{2,1,0:T(8,128)(2,1)S(1)}, f32[96,64]{1,0:T(8,128)S(1)}, f32[96,64]{1,0:T(8,128)S(1)}, f32[96,64]{1,0:T(8,128)S(1)}, f32[9...) custom-call(s32[40]{0:T(128)S(1)} %concatenate.6.refs_0_, bf16[1,64,96,384]{3,2,1,0:T(8,128)(2,1)} %refs_1_.2, ...), custom_call_target="tpu_custom_call" | custom-call | flops 2415919104 | bytes 9437184 | tf_op jit(solution)/shard_map/vertical_columns/pallas_call | solution.py:445
  10.7 0.1 collective-permute-start
  10.8 2.1 %collective-permute-start.1 = (f32[96,64]{1,0:T(8,128)S(1)}, f32[96,64]{1,0:T(8,128)S(1)}, u32[]{:S(2)}, u32[]{:S(2)}) collective-permute-start(f32[96,64]{1,0:T(8,128)S(1)} %get-tuple-element.33), channel_id=1, source_target_pairs={{0,16},{8,24},{16,0},{24,8},{1,17},{9,25},{17,1},{25,9},{2,18},{10... | collective-permute-start | bytes 73736 | tf_op jit(solution)/shard_map/ppermute | solution.py:514
  12.9 1.4 %collective-permute-start.2 = (f32[96,64]{1,0:T(8,128)S(1)}, f32[96,64]{1,0:T(8,128)S(1)}, u32[]{:S(2)}, u32[]{:S(2)}) collective-permute-start(f32[96,64]{1,0:T(8,128)S(1)} %get-tuple-element.34), channel_id=1, source_target_pairs={{0,24},{8,0},{16,8},{24,16},{1,25},{9,1},{17,9},{25,17},{2,26},{10... | collective-permute-start | bytes 73736 | tf_op jit(solution)/shard_map/ppermute | solution.py:514
  14.2 0.0 copy-done.1
  14.2 2.7 %row_terms.1 = (f32[96,64]{1,0:T(8,128)S(1)}, f32[96,64]{1,0:T(8,128)S(1)}, f32[64,128]{1,0:T(8,128)S(1)}, f32[64,128]{1,0:T(8,128)S(1)}, f32[64,128]{1,0:T(8,128)S(1)}) custom-call(s32[40]{0:T(128)S(1)} %concatenate.6.refs_0_, f32[32,768]{1,0:T(8,128)S(1)} %copy-done.1), custom_call_target="tpu_custom_call" | custom-call | flops 452984832 | bytes 1048576 | tf_op jit(solution)/shard_map/row_terms/pallas_call | solution.py:445
  17.0 0.0 collective-permute-done.refs_5_
  17.0 0.0 collective-permute-done.1.refs_6_
  17.0 0.0 collective-permute-done.2.refs_7_
  17.0 0.0 copy-done.2
  17.0 13.7 %zonal_rows.1 = (bf16[64,256,384]{2,1,0:T(8,128)(2,1)S(1)}, f32[2,64,384]{2,1,0:T(8,128)S(1)}, bf16[2,64,384]{2,1,0:T(8,128)(2,1)S(1)}) custom-call(s32[40]{0:T(128)S(1)} %concatenate.6.refs_0_, bf16[64,96,384]{2,1,0:T(8,128)(2,1)S(1)} %get-tuple-element.28.refs_1_, f32[96,64]{1,0:T(8,128)S(1)} %get-tuple-element.29.refs_2_, ...), custom_call_target="tpu_custom_call" | custom-call | flops 14495514624 | bytes 14155776 | tf_op jit(solution)/shard_map/zonal_rows/pallas_call | solution.py:445
  30.7 3.7 %collective-permute-start.3 = (bf16[2,64,384]{2,1,0:T(8,128)(2,1)S(1)}, bf16[2,64,384]{2,1,0:T(8,128)(2,1)S(1)}, u32[]{:S(2)}, u32[]{:S(2)}) collective-permute-start(bf16[2,64,384]{2,1,0:T(8,128)(2,1)S(1)} %get-tuple-element.39), channel_id=1, source_target_pairs={{0,1},{1,0},{2,3},{3,2},{4,5},{5,4},{6,7},{7,6},{8,9},{9,8},{10,11... | collective-permute-start | bytes 294920 | tf_op jit(solution)/shard_map/ppermute | solution.py:655
  34.4 2.4 %row_filter.4.refs_4_.refs_6_ = f32[64,96,384]{2,1,0:T(8,128)S(1)} custom-call(s32[40]{0:T(128)S(1)} %concatenate.6.refs_0_, bf16[64,256,384]{2,1,0:T(8,128)(2,1)S(1)} %get-tuple-element.40.refs_1_, f32[96,64]{1,0:T(8,128)S(1)} %get-tuple-element.41.refs_2_.refs_7_, f32[96,64]{1,0:T(8,128)S(1)} %get-tuple-element.42.refs_3_.refs_8_, ...), custom_call_target="tpu_custom_call" | custom-call | flops 301989888 | bytes 4718592 | tf_op jit(solution)/shard_map/row_filter/pallas_call | solution.py:445
  36.7 0.2 collective-permute-done.3.refs_2_
  37.0 0.7 pair_ends.1
  37.6 3.1 %collective-permute-start.5 = (bf16[64,384]{1,0:T(8,128)(2,1)S(1)}, bf16[64,384]{1,0:T(8,128)(2,1)S(1)}, u32[]{:S(2)}, u32[]{:S(2)}) collective-permute-start(bf16[64,384]{1,0:T(8,128)(2,1)S(1)} %get-tuple-element.44), channel_id=1, source_target_pairs={{0,4},{1,5},{2,6},{3,7},{4,0},{5,1},{6,2},{7,3},{8,12},{9,13},{10,... | collective-permute-start | bytes 147464 | tf_op jit(solution)/shard_map/ppermute | solution.py:667
  40.7 1.2 %collective-permute-start.6 = (bf16[64,384]{1,0:T(8,128)(2,1)S(1)}, bf16[64,384]{1,0:T(8,128)(2,1)S(1)}, u32[]{:S(2)}, u32[]{:S(2)}) collective-permute-start(bf16[64,384]{1,0:T(8,128)(2,1)S(1)} %get-tuple-element.45), channel_id=1, source_target_pairs={{0,6},{1,7},{2,0},{3,1},{4,2},{5,3},{6,4},{7,5},{8,14},{9,15},{10,... | collective-permute-start | bytes 147464 | tf_op jit(solution)/shard_map/ppermute | solution.py:667
  41.9 0.9 collective-permute-start.4
  42.8 2.4 %row_filter.5.refs_9_.refs_11_.refs_4_.refs_6_ = f32[64,96,384]{2,1,0:T(8,128)S(1)} custom-call(s32[40]{0:T(128)S(1)} %concatenate.6.refs_0_, bf16[64,256,384]{2,1,0:T(8,128)(2,1)S(1)} %get-tuple-element.40.refs_1_, f32[96,64]{1,0:T(8,128)S(1)} %get-tuple-element.41.refs_2_.refs_7_, ...), custom_call_target="tpu_custom_call", output_to_operand_aliasing={{}: (6, {})} | custom-call | flops 301989888 | bytes 4718592 | tf_op jit(solution)/shard_map/row_filter/pallas_call | solution.py:445
  45.1 0.0 collective-permute-done.5.refs_4_
  45.1 0.0 collective-permute-done.6.refs_5_
  45.1 2.0 %collective-permute-done.4.refs_3_ = bf16[64,384]{1,0:T(8,128)(2,1)S(1)} collective-permute-done((bf16[64,384]{1,0:T(8,128)(2,1)S(1)}, bf16[64,384]{1,0:T(8,128)(2,1)S(1)}, u32[]{:S(2)}, u32[]{:S(2)}) %collective-permute-start.4) | collective-permute-done | bytes 49184 | tf_op jit(solution)/shard_map/ppermute | solution.py:667
  47.2 0.0 slice-done
  47.2 0.0 slice-done.1
  47.2 1.5 %products_2.1 = (bf16[8,96,384]{2,1,0:T(8,128)(2,1)S(1)}, bf16[8,96,384]{2,1,0:T(8,128)(2,1)S(1)}, f32[64,384]{1,0:T(8,128)S(1)}, f32[64,384]{1,0:T(8,128)S(1)}, f32[96,128]{1,0:T(8,128)S(1)}) custom-call(s32[40]{0:T(128)S(1)} %concatenate.6.refs_0_, f32[2,64,384]{2,1,0:T(8,128)S(1)} %get-tuple-element.38.refs_1_, ...), custom_call_target="tpu_custom_call" | custom-call | flops 2359296 | bytes 2359296 | tf_op jit(solution)/shard_map/products_2/pallas_call | solution.py:445
  48.7 1.6 %collective-permute-start.10 = (bf16[8,96,384]{2,1,0:T(8,128)(2,1)S(1)}, bf16[8,96,384]{2,1,0:T(8,128)(2,1)S(1)}, u32[]{:S(2)}, u32[]{:S(2)}) collective-permute-start(bf16[8,96,384]{2,1,0:T(8,128)(2,1)S(1)} %get-tuple-element.50), channel_id=1, source_target_pairs={{0,32},{32,64},{64,96},{96,0},{1,33},{33,65},{65,97},{97,1},{2,34}... | collective-permute-start | bytes 1769480 | tf_op jit(solution)/shard_map/ppermute | solution.py:682
  50.3 1.7 %collective-permute-start.9 = (bf16[8,96,384]{2,1,0:T(8,128)(2,1)S(1)}, bf16[8,96,384]{2,1,0:T(8,128)(2,1)S(1)}, u32[]{:S(2)}, u32[]{:S(2)}) collective-permute-start(bf16[8,96,384]{2,1,0:T(8,128)(2,1)S(1)} %get-tuple-element.49.refs_6_), channel_id=1, source_target_pairs={{0,96},{32,0},{64,32},{96,64},{1,97},{33,1},{65,33},{97,65},{2,98}... | collective-permute-start | bytes 1769480 | tf_op jit(solution)/shard_map/ppermute | solution.py:683
  52.0 1.0 %products_1.2.refs_7_ = bf16[8,96,384]{2,1,0:T(8,128)(2,1)S(1)} custom-call(s32[40]{0:T(128)S(1)} %concatenate.6.refs_0_, f32[64,384]{1,0:T(8,128)S(1)} %get-tuple-element.46.refs_1_, f32[64,384]{1,0:T(8,128)S(1)} %get-tuple-element.47.refs_2_, f32[96,128]{1,0:T(8,128)S(1)} %get-tuple-element.48.refs_3_, ...), custom_call_target="tpu_custom_call" | custom-call | flops 2359296 | bytes 2359296 | tf_op jit(solution)/shard_map/products_1/pallas_call | solution.py:445
  53.0 0.6 collective-permute-start.8
  53.6 2.4 %row_filter.6.refs_4_.refs_6_ = f32[64,96,384]{2,1,0:T(8,128)S(1)} custom-call(s32[40]{0:T(128)S(1)} %concatenate.6.refs_0_, bf16[64,256,384]{2,1,0:T(8,128)(2,1)S(1)} %get-tuple-element.40.refs_1_, f32[96,64]{1,0:T(8,128)S(1)} %get-tuple-element.41.refs_2_.refs_7_, f32[96,64]{1,0:T(8,128)S(1)} %get-tuple-element.42.refs_3_.refs_8_, ...), custom_call_target="tpu_custom_call", output_to_operand_aliasing={{}: (6, {})} | custom-call | flops 301989888 | bytes 4718592 | tf_op jit(solution)/shard_map/row_filter/pallas_call | solution.py:445
  56.0 1.0 %products_3.2.refs_7_ = bf16[8,96,384]{2,1,0:T(8,128)(2,1)S(1)} custom-call(s32[40]{0:T(128)S(1)} %concatenate.6.refs_0_, f32[64,384]{1,0:T(8,128)S(1)} %get-tuple-element.46.refs_1_, f32[64,384]{1,0:T(8,128)S(1)} %get-tuple-element.47.refs_2_, f32[96,128]{1,0:T(8,128)S(1)} %get-tuple-element.48.refs_3_, f32[64,96,384]{2,1,0:T(8,128)S(1)} %row_filter.6.refs_4_.refs_6_, ...), custom_call_target="tpu_custom_call" | custom-call | flops 2359296 | bytes 2359296 | tf_op jit(solution)/shard_map/products_3/pallas_call | solution.py:445
  57.0 2.9 %collective-permute-start.7 = (bf16[8,96,384]{2,1,0:T(8,128)(2,1)S(1)}, bf16[8,96,384]{2,1,0:T(8,128)(2,1)S(1)}, u32[]{:S(2)}, u32[]{:S(2)}) collective-permute-start(bf16[8,96,384]{2,1,0:T(8,128)(2,1)S(1)} %products_3.2.refs_7_), channel_id=1, source_target_pairs={{0,96},{32,0},{64,32},{96,64},{1,97},{33,1},{65,33},{97,65},{2,98}... | collective-permute-start | bytes 1769480 | tf_op jit(solution)/shard_map/ppermute | solution.py:689
  60.0 2.4 %row_filter.7.refs_4_ = f32[64,96,384]{2,1,0:T(8,128)S(1)} custom-call(s32[40]{0:T(128)S(1)} %concatenate.6.refs_0_, bf16[64,256,384]{2,1,0:T(8,128)(2,1)S(1)} %get-tuple-element.40.refs_1_, f32[96,64]{1,0:T(8,128)S(1)} %get-tuple-element.41.refs_2_.refs_7_, f32[96,64]{1,0:T(8,128)S(1)} %get-tuple-element.42.refs_3_.refs_8_, ...), custom_call_target="tpu_custom_call", output_to_operand_aliasing={{}: (6, {})} | custom-call | flops 301989888 | bytes 4718592 | tf_op jit(solution)/shard_map/row_filter/pallas_call | solution.py:445
  62.3 3.9 %collective-permute-done.10.refs_6_ = bf16[8,96,384]{2,1,0:T(8,128)(2,1)S(1)} collective-permute-done((bf16[8,96,384]{2,1,0:T(8,128)(2,1)S(1)}, bf16[8,96,384]{2,1,0:T(8,128)(2,1)S(1)}, u32[]{:S(2)}, u32[]{:S(2)}) %collective-permute-start.10) | collective-permute-done | bytes 589856 | tf_op jit(solution)/shard_map/ppermute | solution.py:682
  66.3 1.1 %products_1.3.refs_7_ = bf16[8,96,384]{2,1,0:T(8,128)(2,1)S(1)} custom-call(s32[40]{0:T(128)S(1)} %concatenate.6.refs_0_, f32[64,384]{1,0:T(8,128)S(1)} %get-tuple-element.46.refs_1_, f32[64,384]{1,0:T(8,128)S(1)} %get-tuple-element.47.refs_2_, f32[96,128]{1,0:T(8,128)S(1)} %get-tuple-element.48.refs_3_, f32[64,96,384]{2,1,0:T(8,128)S(1)} %row_filter.7.refs_4_, ...), custom_call_target="tpu_custom_call" | custom-call | flops 2359296 | bytes 2359296 | tf_op jit(solution)/shard_map/products_1/pallas_call | solution.py:445
  67.4 0.4 collective-permute-start.11
  67.8 0.0 collective-permute-done.9.refs_6_
  67.8 1.1 %products_3.3.refs_8_ = bf16[8,96,384]{2,1,0:T(8,128)(2,1)S(1)} custom-call(s32[40]{0:T(128)S(1)} %concatenate.6.refs_0_, f32[64,384]{1,0:T(8,128)S(1)} %get-tuple-element.46.refs_1_, f32[64,384]{1,0:T(8,128)S(1)} %get-tuple-element.47.refs_2_, f32[96,128]{1,0:T(8,128)S(1)} %get-tuple-element.48.refs_3_, f32[64,96,384]{2,1,0:T(8,128)S(1)} %row_filter.7.refs_4_, ...), custom_call_target="tpu_custom_call" | custom-call | flops 2359296 | bytes 2359296 | tf_op jit(solution)/shard_map/products_3/pallas_call | solution.py:445
  68.9 2.9 %collective-permute-start.12 = (bf16[8,96,384]{2,1,0:T(8,128)(2,1)S(1)}, bf16[8,96,384]{2,1,0:T(8,128)(2,1)S(1)}, u32[]{:S(2)}, u32[]{:S(2)}) collective-permute-start(bf16[8,96,384]{2,1,0:T(8,128)(2,1)S(1)} %products_3.3.refs_8_), channel_id=1, source_target_pairs={{0,96},{32,0},{64,32},{96,64},{1,97},{33,1},{65,33},{97,65},{2,98}... | collective-permute-start | bytes 1769480 | tf_op jit(solution)/shard_map/ppermute | solution.py:581
  71.8 7.4 %collective-permute-done.7.refs_6_ = bf16[8,96,384]{2,1,0:T(8,128)(2,1)S(1)} collective-permute-done((bf16[8,96,384]{2,1,0:T(8,128)(2,1)S(1)}, bf16[8,96,384]{2,1,0:T(8,128)(2,1)S(1)}, u32[]{:S(2)}, u32[]{:S(2)}) %collective-permute-start.7) | collective-permute-done | bytes 589856 | tf_op jit(solution)/shard_map/ppermute | solution.py:689
  79.3 0.0 collective-permute-done.8.refs_7_
  79.3 1.6 %products_here.1 = f32[16,96,384]{2,1,0:T(8,128)S(1)} custom-call(s32[40]{0:T(128)S(1)} %concatenate.6.refs_0_, f32[64,384]{1,0:T(8,128)S(1)} %get-tuple-element.46.refs_1_, f32[64,384]{1,0:T(8,128)S(1)} %get-tuple-element.47.refs_2_, f32[96,128]{1,0:T(8,128)S(1)} %get-tuple-element.48.refs_3_, f32[64,96,384]{2,1,0:T(8,128)S(1)} %row_filter.7.refs_4_, ...), custom_call_target="tpu_custom_call" | custom-call | flops 4718592 | bytes 8257536 | tf_op jit(solution)/shard_map/products_here/pallas_call | solution.py:445
  80.9 7.0 %collective-permute-done.11 = bf16[8,96,384]{2,1,0:T(8,128)(2,1)S(1)} collective-permute-done((bf16[8,96,384]{2,1,0:T(8,128)(2,1)S(1)}, bf16[8,96,384]{2,1,0:T(8,128)(2,1)S(1)}, u32[]{:S(2)}, u32[]{:S(2)}) %collective-permute-start.11) | collective-permute-done | bytes 589856 | tf_op jit(solution)/shard_map/ppermute | solution.py:579
  87.9 0.0 collective-permute-done.12
  87.9 1.7 %add_multiply_fusion = f32[16,96,384]{2,1,0:T(8,128)} fusion(f32[16,96,384]{2,1,0:T(8,128)S(1)} %products_here.1, bf16[8,96,384]{2,1,0:T(8,128)(2,1)S(1)} %collective-permute-done.12, bf16[8,96,384]{2,1,0:T(8,128)(2,1)S(1)} %collective-permute-done.11), kind=kLoop, calls=%fused_computation | loop fusion | flops 2359296 | bytes 5898240 | tf_op jit(solution)/shard_map/mul | solution.py:598
  (5 shorter events, 0.0 us)
Async XLA Ops:
  1.4 0.9 copy-start
  2.3 11.9 %copy-start.1 = (f32[32,768]{1,0:T(8,128)S(1)}, f32[32,768]{1,0:T(8,128)}, u32[]{:S(2)}) copy-start(f32[32,768]{1,0:T(8,128)} %refs_1_.3) | copy-start | bytes 294916
  2.3 14.7 %copy-start.2 = (bf16[256,256]{1,0:T(8,128)(2,1)S(1)}, bf16[256,256]{1,0:T(8,128)(2,1)}, u32[]{:S(2)}) copy-start(bf16[256,256]{1,0:T(8,128)(2,1)} %constant.16.clone.refs_11_) | copy-start | bytes 393220
  10.7 6.3 %collective-permute-start = (f32[96,64]{1,0:T(8,128)S(1)}, f32[96,64]{1,0:T(8,128)S(1)}, u32[]{:S(2)}, u32[]{:S(2)}) collective-permute-start(f32[96,64]{1,0:T(8,128)S(1)} %get-tuple-element.32), channel_id=1, source_target_pairs={{0,8},{8,16},{16,24},{24,0},{1,9},{9,17},{17,25},{25,1},{2,10},{10... | collective-permute-start | bytes 73736 | tf_op jit(solution)/shard_map/ppermute | solution.py:514
  10.8 6.2 %collective-permute-start.1 = (f32[96,64]{1,0:T(8,128)S(1)}, f32[96,64]{1,0:T(8,128)S(1)}, u32[]{:S(2)}, u32[]{:S(2)}) collective-permute-start(f32[96,64]{1,0:T(8,128)S(1)} %get-tuple-element.33), channel_id=1, source_target_pairs={{0,16},{8,24},{16,0},{24,8},{1,17},{9,25},{17,1},{25,9},{2,18},{10... | collective-permute-start | bytes 73736 | tf_op jit(solution)/shard_map/ppermute | solution.py:514
  12.9 4.1 %collective-permute-start.2 = (f32[96,64]{1,0:T(8,128)S(1)}, f32[96,64]{1,0:T(8,128)S(1)}, u32[]{:S(2)}, u32[]{:S(2)}) collective-permute-start(f32[96,64]{1,0:T(8,128)S(1)} %get-tuple-element.34), channel_id=1, source_target_pairs={{0,24},{8,0},{16,8},{24,16},{1,25},{9,1},{17,9},{25,17},{2,26},{10... | collective-permute-start | bytes 73736 | tf_op jit(solution)/shard_map/ppermute | solution.py:514
  30.7 6.3 %collective-permute-start.3 = (bf16[2,64,384]{2,1,0:T(8,128)(2,1)S(1)}, bf16[2,64,384]{2,1,0:T(8,128)(2,1)S(1)}, u32[]{:S(2)}, u32[]{:S(2)}) collective-permute-start(bf16[2,64,384]{2,1,0:T(8,128)(2,1)S(1)} %get-tuple-element.39), channel_id=1, source_target_pairs={{0,1},{1,0},{2,3},{3,2},{4,5},{5,4},{6,7},{7,6},{8,9},{9,8},{10,11... | collective-permute-start | bytes 294920 | tf_op jit(solution)/shard_map/ppermute | solution.py:655
  37.6 7.5 %collective-permute-start.5 = (bf16[64,384]{1,0:T(8,128)(2,1)S(1)}, bf16[64,384]{1,0:T(8,128)(2,1)S(1)}, u32[]{:S(2)}, u32[]{:S(2)}) collective-permute-start(bf16[64,384]{1,0:T(8,128)(2,1)S(1)} %get-tuple-element.44), channel_id=1, source_target_pairs={{0,4},{1,5},{2,6},{3,7},{4,0},{5,1},{6,2},{7,3},{8,12},{9,13},{10,... | collective-permute-start | bytes 147464 | tf_op jit(solution)/shard_map/ppermute | solution.py:667
  40.7 4.4 %collective-permute-start.6 = (bf16[64,384]{1,0:T(8,128)(2,1)S(1)}, bf16[64,384]{1,0:T(8,128)(2,1)S(1)}, u32[]{:S(2)}, u32[]{:S(2)}) collective-permute-start(bf16[64,384]{1,0:T(8,128)(2,1)S(1)} %get-tuple-element.45), channel_id=1, source_target_pairs={{0,6},{1,7},{2,0},{3,1},{4,2},{5,3},{6,4},{7,5},{8,14},{9,15},{10,... | collective-permute-start | bytes 147464 | tf_op jit(solution)/shard_map/ppermute | solution.py:667
  41.9 5.3 %slice-start = ((s8[4718592]{0:T(1024)(128)(4,1)}), s8[4194304]{0:T(1024)(128)(4,1)S(1)}, s32[]{:S(2)}) async-start(s8[4718592]{0:T(1024)(128)(4,1)} %bitcast.3), calls=%async_computation | async-start | bytes 8388608
  41.9 5.3 %slice-start.1 = ((s8[4718592]{0:T(1024)(128)(4,1)}), s8[524288]{0:T(1024)(128)(4,1)S(1)}, s32[]{:S(2)}) async-start(s8[4718592]{0:T(1024)(128)(4,1)} %bitcast.3), calls=%async_computation.1 | async-start | bytes 1048576
  41.9 5.3 %collective-permute-start.4 = (bf16[64,384]{1,0:T(8,128)(2,1)S(1)}, bf16[64,384]{1,0:T(8,128)(2,1)S(1)}, u32[]{:S(2)}, u32[]{:S(2)}) collective-permute-start(bf16[64,384]{1,0:T(8,128)(2,1)S(1)} %get-tuple-element.43.refs_7_), channel_id=1, source_target_pairs={{0,2},{1,3},{2,4},{3,5},{4,6},{5,7},{6,0},{7,1},{8,10},{9,11},{10,... | collective-permute-start | bytes 147464 | tf_op jit(solution)/shard_map/ppermute | solution.py:667
  48.7 17.5 %collective-permute-start.10 = (bf16[8,96,384]{2,1,0:T(8,128)(2,1)S(1)}, bf16[8,96,384]{2,1,0:T(8,128)(2,1)S(1)}, u32[]{:S(2)}, u32[]{:S(2)}) collective-permute-start(bf16[8,96,384]{2,1,0:T(8,128)(2,1)S(1)} %get-tuple-element.50), channel_id=1, source_target_pairs={{0,32},{32,64},{64,96},{96,0},{1,33},{33,65},{65,97},{97,1},{2,34}... | collective-permute-start | bytes 1769480 | tf_op jit(solution)/shard_map/ppermute | solution.py:682
  50.3 17.4 %collective-permute-start.9 = (bf16[8,96,384]{2,1,0:T(8,128)(2,1)S(1)}, bf16[8,96,384]{2,1,0:T(8,128)(2,1)S(1)}, u32[]{:S(2)}, u32[]{:S(2)}) collective-permute-start(bf16[8,96,384]{2,1,0:T(8,128)(2,1)S(1)} %get-tuple-element.49.refs_6_), channel_id=1, source_target_pairs={{0,96},{32,0},{64,32},{96,64},{1,97},{33,1},{65,33},{97,65},{2,98}... | collective-permute-start | bytes 1769480 | tf_op jit(solution)/shard_map/ppermute | solution.py:683
  53.0 26.2 %collective-permute-start.8 = (bf16[8,96,384]{2,1,0:T(8,128)(2,1)S(1)}, bf16[8,96,384]{2,1,0:T(8,128)(2,1)S(1)}, u32[]{:S(2)}, u32[]{:S(2)}) collective-permute-start(bf16[8,96,384]{2,1,0:T(8,128)(2,1)S(1)} %products_1.2.refs_7_), channel_id=1, source_target_pairs={{0,32},{32,64},{64,96},{96,0},{1,33},{33,65},{65,97},{97,1},{2,34}... | collective-permute-start | bytes 1769480 | tf_op jit(solution)/shard_map/ppermute | solution.py:685
  57.0 22.2 %collective-permute-start.7 = (bf16[8,96,384]{2,1,0:T(8,128)(2,1)S(1)}, bf16[8,96,384]{2,1,0:T(8,128)(2,1)S(1)}, u32[]{:S(2)}, u32[]{:S(2)}) collective-permute-start(bf16[8,96,384]{2,1,0:T(8,128)(2,1)S(1)} %products_3.2.refs_7_), channel_id=1, source_target_pairs={{0,96},{32,0},{64,32},{96,64},{1,97},{33,1},{65,33},{97,65},{2,98}... | collective-permute-start | bytes 1769480 | tf_op jit(solution)/shard_map/ppermute | solution.py:689
  67.4 20.5 %collective-permute-start.11 = (bf16[8,96,384]{2,1,0:T(8,128)(2,1)S(1)}, bf16[8,96,384]{2,1,0:T(8,128)(2,1)S(1)}, u32[]{:S(2)}, u32[]{:S(2)}) collective-permute-start(bf16[8,96,384]{2,1,0:T(8,128)(2,1)S(1)} %products_1.3.refs_7_), channel_id=1, source_target_pairs={{0,32},{32,64},{64,96},{96,0},{1,33},{33,65},{65,97},{97,1},{2,34}... | collective-permute-start | bytes 1769480 | tf_op jit(solution)/shard_map/ppermute | solution.py:579
  68.9 19.0 %collective-permute-start.12 = (bf16[8,96,384]{2,1,0:T(8,128)(2,1)S(1)}, bf16[8,96,384]{2,1,0:T(8,128)(2,1)S(1)}, u32[]{:S(2)}, u32[]{:S(2)}) collective-permute-start(bf16[8,96,384]{2,1,0:T(8,128)(2,1)S(1)} %products_3.3.refs_8_), channel_id=1, source_target_pairs={{0,96},{32,0},{64,32},{96,64},{1,97},{33,1},{65,33},{97,65},{2,98}... | collective-permute-start | bytes 1769480 | tf_op jit(solution)/shard_map/ppermute | solution.py:581

commit v7 on v6

--- a/solution.py
+++ b/solution.py
@@ -16,8 +16,8 @@
 SLAB_AT = 8
 ROW_GROUP = 32
 FIELD_STEP = 8
-PRODUCT_STEP = 4
-VMEM_LIMIT = 8 * 1024 * 1024
+PRODUCT_STEP = 8
+VMEM_LIMIT = 12 * 1024 * 1024
 COLUMN_VMEM_LIMIT = 48 * 1024 * 1024
 FIELD_VMEM_LIMIT = 16 * 1024 * 1024
 

time: 89.9 us -> 94.3 us (1.049)
  local copies, waits for them, and re-layouts: 1.66 us -> 6.13 us
    unnamed x10 -> x14, local copies, waits for them, and re-layouts: 0.91 us -> 5.38 us
  transfers between devices with their start and end apart: 13 -> 13, of which waited for: 5 -> 5; matrix products, arithmetic and copies ran while one was open for 0% -> 0% of each run, Pallas kernels for 20% -> 18%
where the time goes in v7:
time: 94.3 us; the launch traced here: 93.8 us
  Pallas kernels  41.3 us (44%)
  starting transfers between devices  22.4 us (24%)
  waiting for transfers between devices  21.5 us (23%)
  local copies, waits for them, and re-layouts  6.13 us (7%)
  other arithmetic  1.72 us (2%)
    pallas_call x14, Pallas kernels, call(): pl.pallas_call(ordered, out_shape=outputs, grid_spec=pltpu.PrefetchScalar...  41.3 us
    ppermute x1, waiting for transfers between devices, per_device(): one = (one_up_moved, lax.ppermute(one_down, 'mem', down))  7.69 us
    ppermute x1, waiting for transfers between devices, finish(): moved_up = lax.ppermute(sum_up, 'mem', up)  7.2 us
    unnamed x14, local copies, waits for them, and re-layouts  5.38 us
    ppermute x3, starting transfers between devices, per_device(): lax.ppermute(p, 'lon', to_pair(k + 1))  5.12 us
    ppermute x1, waiting for transfers between devices, per_device(): two_up_moved = lax.ppermute(two_up, 'mem', up)  4.28 us
    ppermute x1, starting transfers between devices, per_device(): partner = lax.ppermute(edge_send, 'lon', to_partner)  3.66 us
    ppermute x3, starting transfers between devices, per_device(): lax.ppermute(s, 'lat', ring('lat', i + 1))  3.46 us
  transfers between devices with their start and end apart: 13, of which 5 were waited for; matrix products, arithmetic and copies ran while one was open for 0% of the time, Pallas kernels for 18%

profile of v7, /device:TPU:0, one launch (start us, length us, event | category | flops | bytes accessed | tf_op | source)
XLA Modules:
  0.0 93.8 jit_solution(3744772555399720972)
XLA Ops:
  0.7 0.8 concatenate.6.refs_0_
  1.4 0.9 copy-done
  2.3 8.4 %vertical_columns.1 = (bf16[64,96,384]{2,1,0:T(8,128)(2,1)S(1)}, f32[96,64]{1,0:T(8,128)S(1)}, f32[96,64]{1,0:T(8,128)S(1)}, f32[96,64]{1,0:T(8,128)S(1)}, f32[9...) custom-call(s32[40]{0:T(128)S(1)} %concatenate.6.refs_0_, bf16[1,64,96,384]{3,2,1,0:T(8,128)(2,1)} %refs_1_.2, ...), custom_call_target="tpu_custom_call" | custom-call | flops 2415919104 | bytes 9437184 | tf_op jit(solution)/shard_map/vertical_columns/pallas_call | solution.py:445
  10.7 0.0 copy-start.3
  10.7 2.1 %copy-done.3 = bf16[64,96,384]{2,1,0:T(8,128)(2,1)} copy-done((bf16[64,96,384]{2,1,0:T(8,128)(2,1)}, bf16[64,96,384]{2,1,0:T(8,128)(2,1)S(1)}, u32[]{:S(2)}) %copy-start.3) | copy-done | bytes 4718616
  12.8 0.0 collective-permute-start
  12.8 2.0 %collective-permute-start.1 = (f32[96,64]{1,0:T(8,128)S(1)}, f32[96,64]{1,0:T(8,128)S(1)}, u32[]{:S(2)}, u32[]{:S(2)}) collective-permute-start(f32[96,64]{1,0:T(8,128)S(1)} %get-tuple-element.33), channel_id=1, source_target_pairs={{0,16},{8,24},{16,0},{24,8},{1,17},{9,25},{17,1},{25,9},{2,18},{10... | collective-permute-start | bytes 73736 | tf_op jit(solution)/shard_map/ppermute | solution.py:514
  14.9 1.4 %collective-permute-start.2 = (f32[96,64]{1,0:T(8,128)S(1)}, f32[96,64]{1,0:T(8,128)S(1)}, u32[]{:S(2)}, u32[]{:S(2)}) collective-permute-start(f32[96,64]{1,0:T(8,128)S(1)} %get-tuple-element.34), channel_id=1, source_target_pairs={{0,24},{8,0},{16,8},{24,16},{1,25},{9,1},{17,9},{25,17},{2,26},{10... | collective-permute-start | bytes 73736 | tf_op jit(solution)/shard_map/ppermute | solution.py:514
  16.3 0.0 copy-done.1
  16.3 2.7 %row_terms.1 = (f32[96,64]{1,0:T(8,128)S(1)}, f32[96,64]{1,0:T(8,128)S(1)}, f32[64,128]{1,0:T(8,128)S(1)}, f32[64,128]{1,0:T(8,128)S(1)}, f32[64,128]{1,0:T(8,128)S(1)}) custom-call(s32[40]{0:T(128)S(1)} %concatenate.6.refs_0_, f32[32,768]{1,0:T(8,128)S(1)} %copy-done.1), custom_call_target="tpu_custom_call" | custom-call | flops 452984832 | bytes 1048576 | tf_op jit(solution)/shard_map/row_terms/pallas_call | solution.py:445
  19.0 0.0 collective-permute-done.refs_5_
  19.0 0.0 collective-permute-done.1.refs_6_
  19.0 0.0 collective-permute-done.2.refs_7_
  19.1 0.0 copy-done.2
  19.1 2.3 %copy-done.4 = bf16[64,96,384]{2,1,0:T(8,128)(2,1)S(1)} copy-done((bf16[64,96,384]{2,1,0:T(8,128)(2,1)S(1)}, bf16[64,96,384]{2,1,0:T(8,128)(2,1)}, u32[]{:S(2)}) %copy-start.4) | copy-done | bytes 4718616
  21.4 13.6 %zonal_rows.1 = (bf16[64,256,384]{2,1,0:T(8,128)(2,1)S(1)}, f32[2,64,384]{2,1,0:T(8,128)S(1)}, bf16[2,64,384]{2,1,0:T(8,128)(2,1)S(1)}) custom-call(s32[40]{0:T(128)S(1)} %concatenate.6.refs_0_, bf16[64,96,384]{2,1,0:T(8,128)(2,1)S(1)} %copy-done.4, f32[96,64]{1,0:T(8,128)S(1)} %get-tuple-element.29.refs_2_, f32[96,64]{1,0:T(8,128)S(1)} %get-tuple-element.30.refs_3_, ...), custom_call_target="tpu_custom_call" | custom-call | flops 14495514624 | bytes 14155776 | tf_op jit(solution)/shard_map/zonal_rows/pallas_call | solution.py:445
  35.0 3.7 %collective-permute-start.3 = (bf16[2,64,384]{2,1,0:T(8,128)(2,1)S(1)}, bf16[2,64,384]{2,1,0:T(8,128)(2,1)S(1)}, u32[]{:S(2)}, u32[]{:S(2)}) collective-permute-start(bf16[2,64,384]{2,1,0:T(8,128)(2,1)S(1)} %get-tuple-element.39), channel_id=1, source_target_pairs={{0,1},{1,0},{2,3},{3,2},{4,5},{5,4},{6,7},{7,6},{8,9},{9,8},{10,11... | collective-permute-start | bytes 294920 | tf_op jit(solution)/shard_map/ppermute | solution.py:655
  38.7 2.4 %row_filter.4.refs_4_.refs_6_ = f32[64,96,384]{2,1,0:T(8,128)S(1)} custom-call(s32[40]{0:T(128)S(1)} %concatenate.6.refs_0_, bf16[64,256,384]{2,1,0:T(8,128)(2,1)S(1)} %get-tuple-element.40.refs_1_, f32[96,64]{1,0:T(8,128)S(1)} %get-tuple-element.41.refs_2_.refs_7_, f32[96,64]{1,0:T(8,128)S(1)} %get-tuple-element.42.refs_3_.refs_8_, ...), custom_call_target="tpu_custom_call" | custom-call | flops 301989888 | bytes 4718592 | tf_op jit(solution)/shard_map/row_filter/pallas_call | solution.py:445
  41.1 0.2 collective-permute-done.3.refs_2_
  41.3 0.7 pair_ends.1
  42.0 3.1 %collective-permute-start.5 = (bf16[64,384]{1,0:T(8,128)(2,1)S(1)}, bf16[64,384]{1,0:T(8,128)(2,1)S(1)}, u32[]{:S(2)}, u32[]{:S(2)}) collective-permute-start(bf16[64,384]{1,0:T(8,128)(2,1)S(1)} %get-tuple-element.44), channel_id=1, source_target_pairs={{0,4},{1,5},{2,6},{3,7},{4,0},{5,1},{6,2},{7,3},{8,12},{9,13},{10,... | collective-permute-start | bytes 147464 | tf_op jit(solution)/shard_map/ppermute | solution.py:667
  45.1 1.1 %collective-permute-start.6 = (bf16[64,384]{1,0:T(8,128)(2,1)S(1)}, bf16[64,384]{1,0:T(8,128)(2,1)S(1)}, u32[]{:S(2)}, u32[]{:S(2)}) collective-permute-start(bf16[64,384]{1,0:T(8,128)(2,1)S(1)} %get-tuple-element.45), channel_id=1, source_target_pairs={{0,6},{1,7},{2,0},{3,1},{4,2},{5,3},{6,4},{7,5},{8,14},{9,15},{10,... | collective-permute-start | bytes 147464 | tf_op jit(solution)/shard_map/ppermute | solution.py:667
  46.2 0.9 collective-permute-start.4
  47.1 2.4 %row_filter.5.refs_9_.refs_11_.refs_4_.refs_6_ = f32[64,96,384]{2,1,0:T(8,128)S(1)} custom-call(s32[40]{0:T(128)S(1)} %concatenate.6.refs_0_, bf16[64,256,384]{2,1,0:T(8,128)(2,1)S(1)} %get-tuple-element.40.refs_1_, f32[96,64]{1,0:T(8,128)S(1)} %get-tuple-element.41.refs_2_.refs_7_, ...), custom_call_target="tpu_custom_call", output_to_operand_aliasing={{}: (6, {})} | custom-call | flops 301989888 | bytes 4718592 | tf_op jit(solution)/shard_map/row_filter/pallas_call | solution.py:445
  49.5 0.0 collective-permute-done.5.refs_4_
  49.5 0.0 collective-permute-done.6.refs_5_
  49.5 2.0 %collective-permute-done.4.refs_3_ = bf16[64,384]{1,0:T(8,128)(2,1)S(1)} collective-permute-done((bf16[64,384]{1,0:T(8,128)(2,1)S(1)}, bf16[64,384]{1,0:T(8,128)(2,1)S(1)}, u32[]{:S(2)}, u32[]{:S(2)}) %collective-permute-start.4) | collective-permute-done | bytes 49184 | tf_op jit(solution)/shard_map/ppermute | solution.py:667
  51.5 1.3 %products_2.1 = (bf16[8,96,384]{2,1,0:T(8,128)(2,1)S(1)}, bf16[8,96,384]{2,1,0:T(8,128)(2,1)S(1)}, f32[64,384]{1,0:T(8,128)S(1)}, f32[64,384]{1,0:T(8,128)S(1)}, f32[96,128]{1,0:T(8,128)S(1)}) custom-call(s32[40]{0:T(128)S(1)} %concatenate.6.refs_0_, f32[2,64,384]{2,1,0:T(8,128)S(1)} %get-tuple-element.38.refs_1_, ...), custom_call_target="tpu_custom_call" | custom-call | flops 2359296 | bytes 2359296 | tf_op jit(solution)/shard_map/products_2/pallas_call | solution.py:445
  52.9 1.7 %collective-permute-start.10 = (bf16[8,96,384]{2,1,0:T(8,128)(2,1)S(1)}, bf16[8,96,384]{2,1,0:T(8,128)(2,1)S(1)}, u32[]{:S(2)}, u32[]{:S(2)}) collective-permute-start(bf16[8,96,384]{2,1,0:T(8,128)(2,1)S(1)} %get-tuple-element.50), channel_id=1, source_target_pairs={{0,32},{32,64},{64,96},{96,0},{1,33},{33,65},{65,97},{97,1},{2,34}... | collective-permute-start | bytes 1769480 | tf_op jit(solution)/shard_map/ppermute | solution.py:682
  54.5 1.7 %collective-permute-start.9 = (bf16[8,96,384]{2,1,0:T(8,128)(2,1)S(1)}, bf16[8,96,384]{2,1,0:T(8,128)(2,1)S(1)}, u32[]{:S(2)}, u32[]{:S(2)}) collective-permute-start(bf16[8,96,384]{2,1,0:T(8,128)(2,1)S(1)} %get-tuple-element.49.refs_6_), channel_id=1, source_target_pairs={{0,96},{32,0},{64,32},{96,64},{1,97},{33,1},{65,33},{97,65},{2,98}... | collective-permute-start | bytes 1769480 | tf_op jit(solution)/shard_map/ppermute | solution.py:683
  56.2 0.9 products_1.2.refs_7_
  57.1 0.4 collective-permute-start.8
  57.5 2.4 %row_filter.6.refs_4_.refs_6_ = f32[64,96,384]{2,1,0:T(8,128)S(1)} custom-call(s32[40]{0:T(128)S(1)} %concatenate.6.refs_0_, bf16[64,256,384]{2,1,0:T(8,128)(2,1)S(1)} %get-tuple-element.40.refs_1_, f32[96,64]{1,0:T(8,128)S(1)} %get-tuple-element.41.refs_2_.refs_7_, f32[96,64]{1,0:T(8,128)S(1)} %get-tuple-element.42.refs_3_.refs_8_, ...), custom_call_target="tpu_custom_call", output_to_operand_aliasing={{}: (6, {})} | custom-call | flops 301989888 | bytes 4718592 | tf_op jit(solution)/shard_map/row_filter/pallas_call | solution.py:445
  59.9 0.9 products_3.2.refs_7_
  60.8 3.0 %collective-permute-start.7 = (bf16[8,96,384]{2,1,0:T(8,128)(2,1)S(1)}, bf16[8,96,384]{2,1,0:T(8,128)(2,1)S(1)}, u32[]{:S(2)}, u32[]{:S(2)}) collective-permute-start(bf16[8,96,384]{2,1,0:T(8,128)(2,1)S(1)} %products_3.2.refs_7_), channel_id=1, source_target_pairs={{0,96},{32,0},{64,32},{96,64},{1,97},{33,1},{65,33},{97,65},{2,98}... | collective-permute-start | bytes 1769480 | tf_op jit(solution)/shard_map/ppermute | solution.py:689
  63.8 2.4 %row_filter.7.refs_4_ = f32[64,96,384]{2,1,0:T(8,128)S(1)} custom-call(s32[40]{0:T(128)S(1)} %concatenate.6.refs_0_, bf16[64,256,384]{2,1,0:T(8,128)(2,1)S(1)} %get-tuple-element.40.refs_1_, f32[96,64]{1,0:T(8,128)S(1)} %get-tuple-element.41.refs_2_.refs_7_, f32[96,64]{1,0:T(8,128)S(1)} %get-tuple-element.42.refs_3_.refs_8_, ...), custom_call_target="tpu_custom_call", output_to_operand_aliasing={{}: (6, {})} | custom-call | flops 301989888 | bytes 4718592 | tf_op jit(solution)/shard_map/row_filter/pallas_call | solution.py:445
  66.1 4.3 %collective-permute-done.10.refs_6_ = bf16[8,96,384]{2,1,0:T(8,128)(2,1)S(1)} collective-permute-done((bf16[8,96,384]{2,1,0:T(8,128)(2,1)S(1)}, bf16[8,96,384]{2,1,0:T(8,128)(2,1)S(1)}, u32[]{:S(2)}, u32[]{:S(2)}) %collective-permute-start.10) | collective-permute-done | bytes 589856 | tf_op jit(solution)/shard_map/ppermute | solution.py:682
  70.4 1.0 %products_1.3.refs_7_ = bf16[8,96,384]{2,1,0:T(8,128)(2,1)S(1)} custom-call(s32[40]{0:T(128)S(1)} %concatenate.6.refs_0_, f32[64,384]{1,0:T(8,128)S(1)} %get-tuple-element.46.refs_1_, f32[64,384]{1,0:T(8,128)S(1)} %get-tuple-element.47.refs_2_, f32[96,128]{1,0:T(8,128)S(1)} %get-tuple-element.48.refs_3_, f32[64,96,384]{2,1,0:T(8,128)S(1)} %row_filter.7.refs_4_, ...), custom_call_target="tpu_custom_call" | custom-call | flops 2359296 | bytes 2359296 | tf_op jit(solution)/shard_map/products_1/pallas_call | solution.py:445
  71.4 0.4 collective-permute-start.11
  71.8 0.0 collective-permute-done.9.refs_6_
  71.8 1.0 %products_3.3.refs_8_ = bf16[8,96,384]{2,1,0:T(8,128)(2,1)S(1)} custom-call(s32[40]{0:T(128)S(1)} %concatenate.6.refs_0_, f32[64,384]{1,0:T(8,128)S(1)} %get-tuple-element.46.refs_1_, f32[64,384]{1,0:T(8,128)S(1)} %get-tuple-element.47.refs_2_, f32[96,128]{1,0:T(8,128)S(1)} %get-tuple-element.48.refs_3_, f32[64,96,384]{2,1,0:T(8,128)S(1)} %row_filter.7.refs_4_, ...), custom_call_target="tpu_custom_call" | custom-call | flops 2359296 | bytes 2359296 | tf_op jit(solution)/shard_map/products_3/pallas_call | solution.py:445
  72.8 2.9 %collective-permute-start.12 = (bf16[8,96,384]{2,1,0:T(8,128)(2,1)S(1)}, bf16[8,96,384]{2,1,0:T(8,128)(2,1)S(1)}, u32[]{:S(2)}, u32[]{:S(2)}) collective-permute-start(bf16[8,96,384]{2,1,0:T(8,128)(2,1)S(1)} %products_3.3.refs_8_), channel_id=1, source_target_pairs={{0,96},{32,0},{64,32},{96,64},{1,97},{33,1},{65,33},{97,65},{2,98}... | collective-permute-start | bytes 1769480 | tf_op jit(solution)/shard_map/ppermute | solution.py:581
  75.7 7.7 %collective-permute-done.7.refs_6_ = bf16[8,96,384]{2,1,0:T(8,128)(2,1)S(1)} collective-permute-done((bf16[8,96,384]{2,1,0:T(8,128)(2,1)S(1)}, bf16[8,96,384]{2,1,0:T(8,128)(2,1)S(1)}, u32[]{:S(2)}, u32[]{:S(2)}) %collective-permute-start.7) | collective-permute-done | bytes 589856 | tf_op jit(solution)/shard_map/ppermute | solution.py:689
  83.4 0.0 collective-permute-done.8.refs_7_
  83.4 1.4 %products_here.1 = f32[16,96,384]{2,1,0:T(8,128)S(1)} custom-call(s32[40]{0:T(128)S(1)} %concatenate.6.refs_0_, f32[64,384]{1,0:T(8,128)S(1)} %get-tuple-element.46.refs_1_, f32[64,384]{1,0:T(8,128)S(1)} %get-tuple-element.47.refs_2_, f32[96,128]{1,0:T(8,128)S(1)} %get-tuple-element.48.refs_3_, f32[64,96,384]{2,1,0:T(8,128)S(1)} %row_filter.7.refs_4_, ...), custom_call_target="tpu_custom_call" | custom-call | flops 4718592 | bytes 8257536 | tf_op jit(solution)/shard_map/products_here/pallas_call | solution.py:445
  84.9 7.2 %collective-permute-done.11 = bf16[8,96,384]{2,1,0:T(8,128)(2,1)S(1)} collective-permute-done((bf16[8,96,384]{2,1,0:T(8,128)(2,1)S(1)}, bf16[8,96,384]{2,1,0:T(8,128)(2,1)S(1)}, u32[]{:S(2)}, u32[]{:S(2)}) %collective-permute-start.11) | collective-permute-done | bytes 589856 | tf_op jit(solution)/shard_map/ppermute | solution.py:579
  92.1 0.0 collective-permute-done.12
  92.1 1.7 %add_multiply_fusion = f32[16,96,384]{2,1,0:T(8,128)} fusion(f32[16,96,384]{2,1,0:T(8,128)S(1)} %products_here.1, bf16[8,96,384]{2,1,0:T(8,128)(2,1)S(1)} %collective-permute-done.12, bf16[8,96,384]{2,1,0:T(8,128)(2,1)S(1)} %collective-permute-done.11), kind=kLoop, calls=%fused_computation | loop fusion | flops 2359296 | bytes 5898240 | tf_op jit(solution)/shard_map/mul | solution.py:598
  (9 shorter events, 0.0 us)
Async XLA Ops:
  1.4 0.9 copy-start
  2.3 14.0 %copy-start.1 = (f32[32,768]{1,0:T(8,128)S(1)}, f32[32,768]{1,0:T(8,128)}, u32[]{:S(2)}) copy-start(f32[32,768]{1,0:T(8,128)} %refs_1_.3) | copy-start | bytes 294916
  2.3 16.8 %copy-start.2 = (bf16[256,256]{1,0:T(8,128)(2,1)S(1)}, bf16[256,256]{1,0:T(8,128)(2,1)}, u32[]{:S(2)}) copy-start(bf16[256,256]{1,0:T(8,128)(2,1)} %constant.16.clone.refs_11_) | copy-start | bytes 393220
  10.7 2.1 %copy-start.3 = (bf16[64,96,384]{2,1,0:T(8,128)(2,1)}, bf16[64,96,384]{2,1,0:T(8,128)(2,1)S(1)}, u32[]{:S(2)}) copy-start(bf16[64,96,384]{2,1,0:T(8,128)(2,1)S(1)} %get-tuple-element.28.refs_1_) | copy-start | bytes 14155780
  12.8 6.2 %collective-permute-start = (f32[96,64]{1,0:T(8,128)S(1)}, f32[96,64]{1,0:T(8,128)S(1)}, u32[]{:S(2)}, u32[]{:S(2)}) collective-permute-start(f32[96,64]{1,0:T(8,128)S(1)} %get-tuple-element.32), channel_id=1, source_target_pairs={{0,8},{8,16},{16,24},{24,0},{1,9},{9,17},{17,25},{25,1},{2,10},{10... | collective-permute-start | bytes 73736 | tf_op jit(solution)/shard_map/ppermute | solution.py:514
  12.8 6.2 %collective-permute-start.1 = (f32[96,64]{1,0:T(8,128)S(1)}, f32[96,64]{1,0:T(8,128)S(1)}, u32[]{:S(2)}, u32[]{:S(2)}) collective-permute-start(f32[96,64]{1,0:T(8,128)S(1)} %get-tuple-element.33), channel_id=1, source_target_pairs={{0,16},{8,24},{16,0},{24,8},{1,17},{9,25},{17,1},{25,9},{2,18},{10... | collective-permute-start | bytes 73736 | tf_op jit(solution)/shard_map/ppermute | solution.py:514
  14.9 4.2 %collective-permute-start.2 = (f32[96,64]{1,0:T(8,128)S(1)}, f32[96,64]{1,0:T(8,128)S(1)}, u32[]{:S(2)}, u32[]{:S(2)}) collective-permute-start(f32[96,64]{1,0:T(8,128)S(1)} %get-tuple-element.34), channel_id=1, source_target_pairs={{0,24},{8,0},{16,8},{24,16},{1,25},{9,1},{17,9},{25,17},{2,26},{10... | collective-permute-start | bytes 73736 | tf_op jit(solution)/shard_map/ppermute | solution.py:514
  19.1 2.3 %copy-start.4 = (bf16[64,96,384]{2,1,0:T(8,128)(2,1)S(1)}, bf16[64,96,384]{2,1,0:T(8,128)(2,1)}, u32[]{:S(2)}) copy-start(bf16[64,96,384]{2,1,0:T(8,128)(2,1)} %copy-done.3) | copy-start | bytes 14155780
  35.0 6.3 %collective-permute-start.3 = (bf16[2,64,384]{2,1,0:T(8,128)(2,1)S(1)}, bf16[2,64,384]{2,1,0:T(8,128)(2,1)S(1)}, u32[]{:S(2)}, u32[]{:S(2)}) collective-permute-start(bf16[2,64,384]{2,1,0:T(8,128)(2,1)S(1)} %get-tuple-element.39), channel_id=1, source_target_pairs={{0,1},{1,0},{2,3},{3,2},{4,5},{5,4},{6,7},{7,6},{8,9},{9,8},{10,11... | collective-permute-start | bytes 294920 | tf_op jit(solution)/shard_map/ppermute | solution.py:655
  42.0 7.5 %collective-permute-start.5 = (bf16[64,384]{1,0:T(8,128)(2,1)S(1)}, bf16[64,384]{1,0:T(8,128)(2,1)S(1)}, u32[]{:S(2)}, u32[]{:S(2)}) collective-permute-start(bf16[64,384]{1,0:T(8,128)(2,1)S(1)} %get-tuple-element.44), channel_id=1, source_target_pairs={{0,4},{1,5},{2,6},{3,7},{4,0},{5,1},{6,2},{7,3},{8,12},{9,13},{10,... | collective-permute-start | bytes 147464 | tf_op jit(solution)/shard_map/ppermute | solution.py:667
  45.1 4.4 %collective-permute-start.6 = (bf16[64,384]{1,0:T(8,128)(2,1)S(1)}, bf16[64,384]{1,0:T(8,128)(2,1)S(1)}, u32[]{:S(2)}, u32[]{:S(2)}) collective-permute-start(bf16[64,384]{1,0:T(8,128)(2,1)S(1)} %get-tuple-element.45), channel_id=1, source_target_pairs={{0,6},{1,7},{2,0},{3,1},{4,2},{5,3},{6,4},{7,5},{8,14},{9,15},{10,... | collective-permute-start | bytes 147464 | tf_op jit(solution)/shard_map/ppermute | solution.py:667
  46.2 5.3 %slice-start = ((s8[4718592]{0:T(1024)(128)(4,1)}), s8[4194304]{0:T(1024)(128)(4,1)S(1)}, s32[]{:S(2)}) async-start(s8[4718592]{0:T(1024)(128)(4,1)} %bitcast.3), calls=%async_computation | async-start | bytes 8388608
  46.2 5.3 %slice-start.1 = ((s8[4718592]{0:T(1024)(128)(4,1)}), s8[524288]{0:T(1024)(128)(4,1)S(1)}, s32[]{:S(2)}) async-start(s8[4718592]{0:T(1024)(128)(4,1)} %bitcast.3), calls=%async_computation.1 | async-start | bytes 1048576
  46.2 5.3 %collective-permute-start.4 = (bf16[64,384]{1,0:T(8,128)(2,1)S(1)}, bf16[64,384]{1,0:T(8,128)(2,1)S(1)}, u32[]{:S(2)}, u32[]{:S(2)}) collective-permute-start(bf16[64,384]{1,0:T(8,128)(2,1)S(1)} %get-tuple-element.43.refs_7_), channel_id=1, source_target_pairs={{0,2},{1,3},{2,4},{3,5},{4,6},{5,7},{6,0},{7,1},{8,10},{9,11},{10,... | collective-permute-start | bytes 147464 | tf_op jit(solution)/shard_map/ppermute | solution.py:667
  52.9 17.5 %collective-permute-start.10 = (bf16[8,96,384]{2,1,0:T(8,128)(2,1)S(1)}, bf16[8,96,384]{2,1,0:T(8,128)(2,1)S(1)}, u32[]{:S(2)}, u32[]{:S(2)}) collective-permute-start(bf16[8,96,384]{2,1,0:T(8,128)(2,1)S(1)} %get-tuple-element.50), channel_id=1, source_target_pairs={{0,32},{32,64},{64,96},{96,0},{1,33},{33,65},{65,97},{97,1},{2,34}... | collective-permute-start | bytes 1769480 | tf_op jit(solution)/shard_map/ppermute | solution.py:682
  54.5 17.3 %collective-permute-start.9 = (bf16[8,96,384]{2,1,0:T(8,128)(2,1)S(1)}, bf16[8,96,384]{2,1,0:T(8,128)(2,1)S(1)}, u32[]{:S(2)}, u32[]{:S(2)}) collective-permute-start(bf16[8,96,384]{2,1,0:T(8,128)(2,1)S(1)} %get-tuple-element.49.refs_6_), channel_id=1, source_target_pairs={{0,96},{32,0},{64,32},{96,64},{1,97},{33,1},{65,33},{97,65},{2,98}... | collective-permute-start | bytes 1769480 | tf_op jit(solution)/shard_map/ppermute | solution.py:683
  57.1 26.3 %collective-permute-start.8 = (bf16[8,96,384]{2,1,0:T(8,128)(2,1)S(1)}, bf16[8,96,384]{2,1,0:T(8,128)(2,1)S(1)}, u32[]{:S(2)}, u32[]{:S(2)}) collective-permute-start(bf16[8,96,384]{2,1,0:T(8,128)(2,1)S(1)} %products_1.2.refs_7_), channel_id=1, source_target_pairs={{0,32},{32,64},{64,96},{96,0},{1,33},{33,65},{65,97},{97,1},{2,34}... | collective-permute-start | bytes 1769480 | tf_op jit(solution)/shard_map/ppermute | solution.py:685
  60.8 22.6 %collective-permute-start.7 = (bf16[8,96,384]{2,1,0:T(8,128)(2,1)S(1)}, bf16[8,96,384]{2,1,0:T(8,128)(2,1)S(1)}, u32[]{:S(2)}, u32[]{:S(2)}) collective-permute-start(bf16[8,96,384]{2,1,0:T(8,128)(2,1)S(1)} %products_3.2.refs_7_), channel_id=1, source_target_pairs={{0,96},{32,0},{64,32},{96,64},{1,97},{33,1},{65,33},{97,65},{2,98}... | collective-permute-start | bytes 1769480 | tf_op jit(solution)/shard_map/ppermute | solution.py:689
  71.4 20.7 %collective-permute-start.11 = (bf16[8,96,384]{2,1,0:T(8,128)(2,1)S(1)}, bf16[8,96,384]{2,1,0:T(8,128)(2,1)S(1)}, u32[]{:S(2)}, u32[]{:S(2)}) collective-permute-start(bf16[8,96,384]{2,1,0:T(8,128)(2,1)S(1)} %products_1.3.refs_7_), channel_id=1, source_target_pairs={{0,32},{32,64},{64,96},{96,0},{1,33},{33,65},{65,97},{97,1},{2,34}... | collective-permute-start | bytes 1769480 | tf_op jit(solution)/shard_map/ppermute | solution.py:579
  72.8 19.3 %collective-permute-start.12 = (bf16[8,96,384]{2,1,0:T(8,128)(2,1)S(1)}, bf16[8,96,384]{2,1,0:T(8,128)(2,1)S(1)}, u32[]{:S(2)}, u32[]{:S(2)}) collective-permute-start(bf16[8,96,384]{2,1,0:T(8,128)(2,1)S(1)} %products_3.3.refs_8_), channel_id=1, source_target_pairs={{0,96},{32,0},{64,32},{96,64},{1,97},{33,1},{65,33},{97,65},{2,98}... | collective-permute-start | bytes 1769480 | tf_op jit(solution)/shard_map/ppermute | solution.py:581

commit v8 on v6

--- a/solution.py
+++ b/solution.py
@@ -663,7 +663,7 @@
             (row_spec,) * 3,
             after=(field,),
         )
-        field = filter_rows(2, 2, field, after=(pair_sends[0],))
+        field = filter_rows(2, 4, field, after=(pair_sends[0],))
         pair_got = [lax.ppermute(p, "lon", to_pair(k + 1)) for k, p in enumerate(pair_sends)]
         count = parts[0]
         two_up, two_down, enter, leave, lanes = call(
@@ -683,9 +683,7 @@
         two = two_up_moved, lax.ppermute(two_down, "mem", down)
         one_up = send(c, 1, 1, after=(two_down,))
         one_up_moved = lax.ppermute(one_up, "mem", up)
-        field = filter_rows(4, 2, field, after=(one_up,))
-        states[c] = (field, enter, leave, lanes)
-        one_down = send(c, 3, 0)
+        one_down = send(c, 3, 0, after=(one_up,))
         one = one_up_moved, lax.ppermute(one_down, "mem", down)
         field = filter_rows(6, 2, field, after=(one_down,))
         states[c] = (field, enter, leave, lanes)

time: 89.9 us -> 90.5 us (level)
  waiting for transfers between devices: 20.7 us -> 21.9 us
    ppermute x1, waiting for transfers between devices: 3.93 us -> 6.29 us  [per_device(): two_up_moved = lax.ppermute(two_up, 'mem', up)]
    ppermute x3, waiting for transfers between devices: 2.04 us -> 0.33 us  [per_device(): lax.ppermute(p, 'lon', to_pair(k + 1))]
    pallas_call x14 -> x13, Pallas kernels: 42.2 us -> 41.5 us  [call(): pl.pallas_call(ordered, out_shape=outputs, grid_spec=pltpu.PrefetchScalar...]
  transfers between devices with their start and end apart: 13 -> 13, of which waited for: 5 -> 5; matrix products, arithmetic and copies ran while one was open for 0% -> 0% of each run, Pallas kernels for 20% -> 19%
where the time goes in v8:
time: 90.5 us; the launch traced here: 90.2 us
  Pallas kernels  41.5 us (46%)
  starting transfers between devices  22.5 us (25%)
  waiting for transfers between devices  21.9 us (24%)
  other arithmetic  1.72 us (2%)
  local copies, waits for them, and re-layouts  1.66 us (2%)
    pallas_call x13, Pallas kernels, call(): pl.pallas_call(ordered, out_shape=outputs, grid_spec=pltpu.PrefetchScalar...  41.5 us
    ppermute x1, waiting for transfers between devices, finish(): moved_up = lax.ppermute(sum_up, 'mem', up)  7.64 us
    ppermute x1, waiting for transfers between devices, per_device(): one = (one_up_moved, lax.ppermute(one_down, 'mem', down))  7.42 us
    ppermute x1, waiting for transfers between devices, per_device(): two_up_moved = lax.ppermute(two_up, 'mem', up)  6.29 us
    ppermute x3, starting transfers between devices, per_device(): lax.ppermute(p, 'lon', to_pair(k + 1))  5.12 us
    ppermute x1, starting transfers between devices, per_device(): partner = lax.ppermute(edge_send, 'lon', to_partner)  3.66 us
    ppermute x3, starting transfers between devices, per_device(): lax.ppermute(s, 'lat', ring('lat', i + 1))  3.53 us
    ppermute x1, starting transfers between devices, finish(): moved_down = lax.ppermute(sum_down, 'mem', down)  2.95 us
  transfers between devices with their start and end apart: 13, of which 5 were waited for; matrix products, arithmetic and copies ran while one was open for 0% of the time, Pallas kernels for 19%

profile of v8, /device:TPU:0, one launch (start us, length us, event | category | flops | bytes accessed | tf_op | source)
XLA Modules:
  0.0 90.2 jit_solution(13090371298945576960)
XLA Ops:
  0.7 0.8 concatenate.6.refs_0_
  1.4 0.0 copy-start
  1.4 0.9 copy-done
  2.3 0.0 copy-start.1
  2.3 8.4 %vertical_columns.1 = (bf16[64,96,384]{2,1,0:T(8,128)(2,1)S(1)}, f32[96,64]{1,0:T(8,128)S(1)}, f32[96,64]{1,0:T(8,128)S(1)}, f32[96,64]{1,0:T(8,128)S(1)}, f32[9...) custom-call(s32[40]{0:T(128)S(1)} %concatenate.6.refs_0_, bf16[1,64,96,384]{3,2,1,0:T(8,128)(2,1)} %refs_1_.2, ...), custom_call_target="tpu_custom_call" | custom-call | flops 2415919104 | bytes 9437184 | tf_op jit(solution)/shard_map/vertical_columns/pallas_call | solution.py:445
  10.7 0.1 collective-permute-start
  10.8 2.1 %collective-permute-start.1 = (f32[96,64]{1,0:T(8,128)S(1)}, f32[96,64]{1,0:T(8,128)S(1)}, u32[]{:S(2)}, u32[]{:S(2)}) collective-permute-start(f32[96,64]{1,0:T(8,128)S(1)} %get-tuple-element.33), channel_id=1, source_target_pairs={{0,16},{8,24},{16,0},{24,8},{1,17},{9,25},{17,1},{25,9},{2,18},{10... | collective-permute-start | bytes 73736 | tf_op jit(solution)/shard_map/ppermute | solution.py:514
  12.9 1.4 %collective-permute-start.2 = (f32[96,64]{1,0:T(8,128)S(1)}, f32[96,64]{1,0:T(8,128)S(1)}, u32[]{:S(2)}, u32[]{:S(2)}) collective-permute-start(f32[96,64]{1,0:T(8,128)S(1)} %get-tuple-element.34), channel_id=1, source_target_pairs={{0,24},{8,0},{16,8},{24,16},{1,25},{9,1},{17,9},{25,17},{2,26},{10... | collective-permute-start | bytes 73736 | tf_op jit(solution)/shard_map/ppermute | solution.py:514
  14.2 0.0 copy-done.1
  14.2 2.7 %row_terms.1 = (f32[96,64]{1,0:T(8,128)S(1)}, f32[96,64]{1,0:T(8,128)S(1)}, f32[64,128]{1,0:T(8,128)S(1)}, f32[64,128]{1,0:T(8,128)S(1)}, f32[64,128]{1,0:T(8,128)S(1)}) custom-call(s32[40]{0:T(128)S(1)} %concatenate.6.refs_0_, f32[32,768]{1,0:T(8,128)S(1)} %copy-done.1), custom_call_target="tpu_custom_call" | custom-call | flops 452984832 | bytes 1048576 | tf_op jit(solution)/shard_map/row_terms/pallas_call | solution.py:445
  17.0 0.0 collective-permute-done.refs_5_
  17.0 0.0 collective-permute-done.1.refs_6_
  17.0 0.0 collective-permute-done.2.refs_7_
  17.0 0.0 copy-done.2
  17.0 13.7 %zonal_rows.1 = (bf16[64,256,384]{2,1,0:T(8,128)(2,1)S(1)}, f32[2,64,384]{2,1,0:T(8,128)S(1)}, bf16[2,64,384]{2,1,0:T(8,128)(2,1)S(1)}) custom-call(s32[40]{0:T(128)S(1)} %concatenate.6.refs_0_, bf16[64,96,384]{2,1,0:T(8,128)(2,1)S(1)} %get-tuple-element.28.refs_1_, f32[96,64]{1,0:T(8,128)S(1)} %get-tuple-element.29.refs_2_, ...), custom_call_target="tpu_custom_call" | custom-call | flops 14495514624 | bytes 14155776 | tf_op jit(solution)/shard_map/zonal_rows/pallas_call | solution.py:445
  30.7 3.7 %collective-permute-start.3 = (bf16[2,64,384]{2,1,0:T(8,128)(2,1)S(1)}, bf16[2,64,384]{2,1,0:T(8,128)(2,1)S(1)}, u32[]{:S(2)}, u32[]{:S(2)}) collective-permute-start(bf16[2,64,384]{2,1,0:T(8,128)(2,1)S(1)} %get-tuple-element.39), channel_id=1, source_target_pairs={{0,1},{1,0},{2,3},{3,2},{4,5},{5,4},{6,7},{7,6},{8,9},{9,8},{10,11... | collective-permute-start | bytes 294920 | tf_op jit(solution)/shard_map/ppermute | solution.py:655
  34.4 2.4 %row_filter.3.refs_4_.refs_6_ = f32[64,96,384]{2,1,0:T(8,128)S(1)} custom-call(s32[40]{0:T(128)S(1)} %concatenate.6.refs_0_, bf16[64,256,384]{2,1,0:T(8,128)(2,1)S(1)} %get-tuple-element.40.refs_1_, f32[96,64]{1,0:T(8,128)S(1)} %get-tuple-element.41.refs_2_.refs_7_, f32[96,64]{1,0:T(8,128)S(1)} %get-tuple-element.42.refs_3_.refs_8_, ...), custom_call_target="tpu_custom_call" | custom-call | flops 301989888 | bytes 4718592 | tf_op jit(solution)/shard_map/row_filter/pallas_call | solution.py:445
  36.7 0.2 collective-permute-done.3.refs_2_
  37.0 0.7 pair_ends.1
  37.6 3.1 %collective-permute-start.5 = (bf16[64,384]{1,0:T(8,128)(2,1)S(1)}, bf16[64,384]{1,0:T(8,128)(2,1)S(1)}, u32[]{:S(2)}, u32[]{:S(2)}) collective-permute-start(bf16[64,384]{1,0:T(8,128)(2,1)S(1)} %get-tuple-element.44), channel_id=1, source_target_pairs={{0,4},{1,5},{2,6},{3,7},{4,0},{5,1},{6,2},{7,3},{8,12},{9,13},{10,... | collective-permute-start | bytes 147464 | tf_op jit(solution)/shard_map/ppermute | solution.py:667
  40.7 1.2 %collective-permute-start.6 = (bf16[64,384]{1,0:T(8,128)(2,1)S(1)}, bf16[64,384]{1,0:T(8,128)(2,1)S(1)}, u32[]{:S(2)}, u32[]{:S(2)}) collective-permute-start(bf16[64,384]{1,0:T(8,128)(2,1)S(1)} %get-tuple-element.45), channel_id=1, source_target_pairs={{0,6},{1,7},{2,0},{3,1},{4,2},{5,3},{6,4},{7,5},{8,14},{9,15},{10,... | collective-permute-start | bytes 147464 | tf_op jit(solution)/shard_map/ppermute | solution.py:667
  41.9 0.9 collective-permute-start.4
  42.8 4.1 %row_filter.4.refs_9_.refs_11_.refs_4_.refs_6_ = f32[64,96,384]{2,1,0:T(8,128)S(1)} custom-call(s32[40]{0:T(128)S(1)} %concatenate.6.refs_0_, bf16[64,256,384]{2,1,0:T(8,128)(2,1)S(1)} %get-tuple-element.40.refs_1_, f32[96,64]{1,0:T(8,128)S(1)} %get-tuple-element.41.refs_2_.refs_7_, ...), custom_call_target="tpu_custom_call", output_to_operand_aliasing={{}: (6, {})} | custom-call | flops 603979776 | bytes 9437184 | tf_op jit(solution)/shard_map/row_filter/pallas_call | solution.py:445
  46.8 0.0 collective-permute-done.5.refs_4_
  46.9 0.0 collective-permute-done.6.refs_5_
  46.9 0.3 collective-permute-done.4.refs_3_
  47.2 0.0 slice-done
  47.2 0.0 slice-done.1
  47.2 1.5 %products_2.1 = (bf16[8,96,384]{2,1,0:T(8,128)(2,1)S(1)}, bf16[8,96,384]{2,1,0:T(8,128)(2,1)S(1)}, f32[64,384]{1,0:T(8,128)S(1)}, f32[64,384]{1,0:T(8,128)S(1)}, f32[96,128]{1,0:T(8,128)S(1)}) custom-call(s32[40]{0:T(128)S(1)} %concatenate.6.refs_0_, f32[2,64,384]{2,1,0:T(8,128)S(1)} %get-tuple-element.38.refs_1_, ...), custom_call_target="tpu_custom_call" | custom-call | flops 2359296 | bytes 2359296 | tf_op jit(solution)/shard_map/products_2/pallas_call | solution.py:445
  48.7 1.6 %collective-permute-start.10 = (bf16[8,96,384]{2,1,0:T(8,128)(2,1)S(1)}, bf16[8,96,384]{2,1,0:T(8,128)(2,1)S(1)}, u32[]{:S(2)}, u32[]{:S(2)}) collective-permute-start(bf16[8,96,384]{2,1,0:T(8,128)(2,1)S(1)} %get-tuple-element.50), channel_id=1, source_target_pairs={{0,32},{32,64},{64,96},{96,0},{1,33},{33,65},{65,97},{97,1},{2,34}... | collective-permute-start | bytes 1769480 | tf_op jit(solution)/shard_map/ppermute | solution.py:682
  50.3 1.7 %collective-permute-start.9 = (bf16[8,96,384]{2,1,0:T(8,128)(2,1)S(1)}, bf16[8,96,384]{2,1,0:T(8,128)(2,1)S(1)}, u32[]{:S(2)}, u32[]{:S(2)}) collective-permute-start(bf16[8,96,384]{2,1,0:T(8,128)(2,1)S(1)} %get-tuple-element.49.refs_6_), channel_id=1, source_target_pairs={{0,96},{32,0},{64,32},{96,64},{1,97},{33,1},{65,33},{97,65},{2,98}... | collective-permute-start | bytes 1769480 | tf_op jit(solution)/shard_map/ppermute | solution.py:683
  52.0 1.0 %products_1.2.refs_6_ = bf16[8,96,384]{2,1,0:T(8,128)(2,1)S(1)} custom-call(s32[40]{0:T(128)S(1)} %concatenate.6.refs_0_, f32[64,384]{1,0:T(8,128)S(1)} %get-tuple-element.46.refs_1_, f32[64,384]{1,0:T(8,128)S(1)} %get-tuple-element.47.refs_2_, f32[96,128]{1,0:T(8,128)S(1)} %get-tuple-element.48.refs_3_, ...), custom_call_target="tpu_custom_call" | custom-call | flops 2359296 | bytes 2359296 | tf_op jit(solution)/shard_map/products_1/pallas_call | solution.py:445
  53.0 0.6 collective-permute-start.8
  53.6 1.0 %products_3.2.refs_7_ = bf16[8,96,384]{2,1,0:T(8,128)(2,1)S(1)} custom-call(s32[40]{0:T(128)S(1)} %concatenate.6.refs_0_, f32[64,384]{1,0:T(8,128)S(1)} %get-tuple-element.46.refs_1_, f32[64,384]{1,0:T(8,128)S(1)} %get-tuple-element.47.refs_2_, f32[96,128]{1,0:T(8,128)S(1)} %get-tuple-element.48.refs_3_, ...), custom_call_target="tpu_custom_call" | custom-call | flops 2359296 | bytes 2359296 | tf_op jit(solution)/shard_map/products_3/pallas_call | solution.py:445
  54.7 2.9 %collective-permute-start.7 = (bf16[8,96,384]{2,1,0:T(8,128)(2,1)S(1)}, bf16[8,96,384]{2,1,0:T(8,128)(2,1)S(1)}, u32[]{:S(2)}, u32[]{:S(2)}) collective-permute-start(bf16[8,96,384]{2,1,0:T(8,128)(2,1)S(1)} %products_3.2.refs_7_), channel_id=1, source_target_pairs={{0,96},{32,0},{64,32},{96,64},{1,97},{33,1},{65,33},{97,65},{2,98}... | collective-permute-start | bytes 1769480 | tf_op jit(solution)/shard_map/ppermute | solution.py:687
  57.6 2.4 %row_filter.5.refs_4_ = f32[64,96,384]{2,1,0:T(8,128)S(1)} custom-call(s32[40]{0:T(128)S(1)} %concatenate.6.refs_0_, bf16[64,256,384]{2,1,0:T(8,128)(2,1)S(1)} %get-tuple-element.40.refs_1_, f32[96,64]{1,0:T(8,128)S(1)} %get-tuple-element.41.refs_2_.refs_7_, f32[96,64]{1,0:T(8,128)S(1)} %get-tuple-element.42.refs_3_.refs_8_, ...), custom_call_target="tpu_custom_call", output_to_operand_aliasing={{}: (6, {})} | custom-call | flops 301989888 | bytes 4718592 | tf_op jit(solution)/shard_map/row_filter/pallas_call | solution.py:445
  60.0 6.3 %collective-permute-done.10.refs_6_ = bf16[8,96,384]{2,1,0:T(8,128)(2,1)S(1)} collective-permute-done((bf16[8,96,384]{2,1,0:T(8,128)(2,1)S(1)}, bf16[8,96,384]{2,1,0:T(8,128)(2,1)S(1)}, u32[]{:S(2)}, u32[]{:S(2)}) %collective-permute-start.10) | collective-permute-done | bytes 589856 | tf_op jit(solution)/shard_map/ppermute | solution.py:682
  66.2 1.1 %products_1.3.refs_7_ = bf16[8,96,384]{2,1,0:T(8,128)(2,1)S(1)} custom-call(s32[40]{0:T(128)S(1)} %concatenate.6.refs_0_, f32[64,384]{1,0:T(8,128)S(1)} %get-tuple-element.46.refs_1_, f32[64,384]{1,0:T(8,128)S(1)} %get-tuple-element.47.refs_2_, f32[96,128]{1,0:T(8,128)S(1)} %get-tuple-element.48.refs_3_, f32[64,96,384]{2,1,0:T(8,128)S(1)} %row_filter.5.refs_4_, ...), custom_call_target="tpu_custom_call" | custom-call | flops 2359296 | bytes 2359296 | tf_op jit(solution)/shard_map/products_1/pallas_call | solution.py:445
  67.4 0.4 collective-permute-start.11
  67.8 0.0 collective-permute-done.9.refs_6_
  67.8 1.1 %products_3.3.refs_8_ = bf16[8,96,384]{2,1,0:T(8,128)(2,1)S(1)} custom-call(s32[40]{0:T(128)S(1)} %concatenate.6.refs_0_, f32[64,384]{1,0:T(8,128)S(1)} %get-tuple-element.46.refs_1_, f32[64,384]{1,0:T(8,128)S(1)} %get-tuple-element.47.refs_2_, f32[96,128]{1,0:T(8,128)S(1)} %get-tuple-element.48.refs_3_, f32[64,96,384]{2,1,0:T(8,128)S(1)} %row_filter.5.refs_4_, ...), custom_call_target="tpu_custom_call" | custom-call | flops 2359296 | bytes 2359296 | tf_op jit(solution)/shard_map/products_3/pallas_call | solution.py:445
  68.9 3.0 %collective-permute-start.12 = (bf16[8,96,384]{2,1,0:T(8,128)(2,1)S(1)}, bf16[8,96,384]{2,1,0:T(8,128)(2,1)S(1)}, u32[]{:S(2)}, u32[]{:S(2)}) collective-permute-start(bf16[8,96,384]{2,1,0:T(8,128)(2,1)S(1)} %products_3.3.refs_8_), channel_id=1, source_target_pairs={{0,96},{32,0},{64,32},{96,64},{1,97},{33,1},{65,33},{97,65},{2,98}... | collective-permute-start | bytes 1769480 | tf_op jit(solution)/shard_map/ppermute | solution.py:581
  71.8 7.4 %collective-permute-done.7.refs_6_ = bf16[8,96,384]{2,1,0:T(8,128)(2,1)S(1)} collective-permute-done((bf16[8,96,384]{2,1,0:T(8,128)(2,1)S(1)}, bf16[8,96,384]{2,1,0:T(8,128)(2,1)S(1)}, u32[]{:S(2)}, u32[]{:S(2)}) %collective-permute-start.7) | collective-permute-done | bytes 589856 | tf_op jit(solution)/shard_map/ppermute | solution.py:687
  79.3 0.0 collective-permute-done.8.refs_7_
  79.3 1.6 %products_here.1 = f32[16,96,384]{2,1,0:T(8,128)S(1)} custom-call(s32[40]{0:T(128)S(1)} %concatenate.6.refs_0_, f32[64,384]{1,0:T(8,128)S(1)} %get-tuple-element.46.refs_1_, f32[64,384]{1,0:T(8,128)S(1)} %get-tuple-element.47.refs_2_, f32[96,128]{1,0:T(8,128)S(1)} %get-tuple-element.48.refs_3_, f32[64,96,384]{2,1,0:T(8,128)S(1)} %row_filter.5.refs_4_, ...), custom_call_target="tpu_custom_call" | custom-call | flops 4718592 | bytes 8257536 | tf_op jit(solution)/shard_map/products_here/pallas_call | solution.py:445
  80.8 7.6 %collective-permute-done.11 = bf16[8,96,384]{2,1,0:T(8,128)(2,1)S(1)} collective-permute-done((bf16[8,96,384]{2,1,0:T(8,128)(2,1)S(1)}, bf16[8,96,384]{2,1,0:T(8,128)(2,1)S(1)}, u32[]{:S(2)}, u32[]{:S(2)}) %collective-permute-start.11) | collective-permute-done | bytes 589856 | tf_op jit(solution)/shard_map/ppermute | solution.py:579
  88.5 0.0 collective-permute-done.12
  88.5 1.7 %add_multiply_fusion = f32[16,96,384]{2,1,0:T(8,128)} fusion(f32[16,96,384]{2,1,0:T(8,128)S(1)} %products_here.1, bf16[8,96,384]{2,1,0:T(8,128)(2,1)S(1)} %collective-permute-done.12, bf16[8,96,384]{2,1,0:T(8,128)(2,1)S(1)} %collective-permute-done.11), kind=kLoop, calls=%fused_computation | loop fusion | flops 2359296 | bytes 5898240 | tf_op jit(solution)/shard_map/mul | solution.py:598
  (4 shorter events, 0.0 us)
Async XLA Ops:
  1.4 0.9 copy-start
  2.3 11.9 %copy-start.1 = (f32[32,768]{1,0:T(8,128)S(1)}, f32[32,768]{1,0:T(8,128)}, u32[]{:S(2)}) copy-start(f32[32,768]{1,0:T(8,128)} %refs_1_.3) | copy-start | bytes 294916
  2.3 14.7 %copy-start.2 = (bf16[256,256]{1,0:T(8,128)(2,1)S(1)}, bf16[256,256]{1,0:T(8,128)(2,1)}, u32[]{:S(2)}) copy-start(bf16[256,256]{1,0:T(8,128)(2,1)} %constant.16.clone.refs_11_) | copy-start | bytes 393220
  10.7 6.3 %collective-permute-start = (f32[96,64]{1,0:T(8,128)S(1)}, f32[96,64]{1,0:T(8,128)S(1)}, u32[]{:S(2)}, u32[]{:S(2)}) collective-permute-start(f32[96,64]{1,0:T(8,128)S(1)} %get-tuple-element.32), channel_id=1, source_target_pairs={{0,8},{8,16},{16,24},{24,0},{1,9},{9,17},{17,25},{25,1},{2,10},{10... | collective-permute-start | bytes 73736 | tf_op jit(solution)/shard_map/ppermute | solution.py:514
  10.8 6.2 %collective-permute-start.1 = (f32[96,64]{1,0:T(8,128)S(1)}, f32[96,64]{1,0:T(8,128)S(1)}, u32[]{:S(2)}, u32[]{:S(2)}) collective-permute-start(f32[96,64]{1,0:T(8,128)S(1)} %get-tuple-element.33), channel_id=1, source_target_pairs={{0,16},{8,24},{16,0},{24,8},{1,17},{9,25},{17,1},{25,9},{2,18},{10... | collective-permute-start | bytes 73736 | tf_op jit(solution)/shard_map/ppermute | solution.py:514
  12.9 4.1 %collective-permute-start.2 = (f32[96,64]{1,0:T(8,128)S(1)}, f32[96,64]{1,0:T(8,128)S(1)}, u32[]{:S(2)}, u32[]{:S(2)}) collective-permute-start(f32[96,64]{1,0:T(8,128)S(1)} %get-tuple-element.34), channel_id=1, source_target_pairs={{0,24},{8,0},{16,8},{24,16},{1,25},{9,1},{17,9},{25,17},{2,26},{10... | collective-permute-start | bytes 73736 | tf_op jit(solution)/shard_map/ppermute | solution.py:514
  30.7 6.3 %collective-permute-start.3 = (bf16[2,64,384]{2,1,0:T(8,128)(2,1)S(1)}, bf16[2,64,384]{2,1,0:T(8,128)(2,1)S(1)}, u32[]{:S(2)}, u32[]{:S(2)}) collective-permute-start(bf16[2,64,384]{2,1,0:T(8,128)(2,1)S(1)} %get-tuple-element.39), channel_id=1, source_target_pairs={{0,1},{1,0},{2,3},{3,2},{4,5},{5,4},{6,7},{7,6},{8,9},{9,8},{10,11... | collective-permute-start | bytes 294920 | tf_op jit(solution)/shard_map/ppermute | solution.py:655
  37.6 9.2 %collective-permute-start.5 = (bf16[64,384]{1,0:T(8,128)(2,1)S(1)}, bf16[64,384]{1,0:T(8,128)(2,1)S(1)}, u32[]{:S(2)}, u32[]{:S(2)}) collective-permute-start(bf16[64,384]{1,0:T(8,128)(2,1)S(1)} %get-tuple-element.44), channel_id=1, source_target_pairs={{0,4},{1,5},{2,6},{3,7},{4,0},{5,1},{6,2},{7,3},{8,12},{9,13},{10,... | collective-permute-start | bytes 147464 | tf_op jit(solution)/shard_map/ppermute | solution.py:667
  40.7 6.1 %collective-permute-start.6 = (bf16[64,384]{1,0:T(8,128)(2,1)S(1)}, bf16[64,384]{1,0:T(8,128)(2,1)S(1)}, u32[]{:S(2)}, u32[]{:S(2)}) collective-permute-start(bf16[64,384]{1,0:T(8,128)(2,1)S(1)} %get-tuple-element.45), channel_id=1, source_target_pairs={{0,6},{1,7},{2,0},{3,1},{4,2},{5,3},{6,4},{7,5},{8,14},{9,15},{10,... | collective-permute-start | bytes 147464 | tf_op jit(solution)/shard_map/ppermute | solution.py:667
  41.9 5.3 %slice-start = ((s8[4718592]{0:T(1024)(128)(4,1)}), s8[4194304]{0:T(1024)(128)(4,1)S(1)}, s32[]{:S(2)}) async-start(s8[4718592]{0:T(1024)(128)(4,1)} %bitcast.3), calls=%async_computation | async-start | bytes 8388608
  41.9 5.3 %slice-start.1 = ((s8[4718592]{0:T(1024)(128)(4,1)}), s8[524288]{0:T(1024)(128)(4,1)S(1)}, s32[]{:S(2)}) async-start(s8[4718592]{0:T(1024)(128)(4,1)} %bitcast.3), calls=%async_computation.1 | async-start | bytes 1048576
  41.9 5.3 %collective-permute-start.4 = (bf16[64,384]{1,0:T(8,128)(2,1)S(1)}, bf16[64,384]{1,0:T(8,128)(2,1)S(1)}, u32[]{:S(2)}, u32[]{:S(2)}) collective-permute-start(bf16[64,384]{1,0:T(8,128)(2,1)S(1)} %get-tuple-element.43.refs_7_), channel_id=1, source_target_pairs={{0,2},{1,3},{2,4},{3,5},{4,6},{5,7},{6,0},{7,1},{8,10},{9,11},{10,... | collective-permute-start | bytes 147464 | tf_op jit(solution)/shard_map/ppermute | solution.py:667
  48.7 17.5 %collective-permute-start.10 = (bf16[8,96,384]{2,1,0:T(8,128)(2,1)S(1)}, bf16[8,96,384]{2,1,0:T(8,128)(2,1)S(1)}, u32[]{:S(2)}, u32[]{:S(2)}) collective-permute-start(bf16[8,96,384]{2,1,0:T(8,128)(2,1)S(1)} %get-tuple-element.50), channel_id=1, source_target_pairs={{0,32},{32,64},{64,96},{96,0},{1,33},{33,65},{65,97},{97,1},{2,34}... | collective-permute-start | bytes 1769480 | tf_op jit(solution)/shard_map/ppermute | solution.py:682
  50.3 17.4 %collective-permute-start.9 = (bf16[8,96,384]{2,1,0:T(8,128)(2,1)S(1)}, bf16[8,96,384]{2,1,0:T(8,128)(2,1)S(1)}, u32[]{:S(2)}, u32[]{:S(2)}) collective-permute-start(bf16[8,96,384]{2,1,0:T(8,128)(2,1)S(1)} %get-tuple-element.49.refs_6_), channel_id=1, source_target_pairs={{0,96},{32,0},{64,32},{96,64},{1,97},{33,1},{65,33},{97,65},{2,98}... | collective-permute-start | bytes 1769480 | tf_op jit(solution)/shard_map/ppermute | solution.py:683
  53.0 26.2 %collective-permute-start.8 = (bf16[8,96,384]{2,1,0:T(8,128)(2,1)S(1)}, bf16[8,96,384]{2,1,0:T(8,128)(2,1)S(1)}, u32[]{:S(2)}, u32[]{:S(2)}) collective-permute-start(bf16[8,96,384]{2,1,0:T(8,128)(2,1)S(1)} %products_1.2.refs_6_), channel_id=1, source_target_pairs={{0,32},{32,64},{64,96},{96,0},{1,33},{33,65},{65,97},{97,1},{2,34}... | collective-permute-start | bytes 1769480 | tf_op jit(solution)/shard_map/ppermute | solution.py:685
  54.7 24.6 %collective-permute-start.7 = (bf16[8,96,384]{2,1,0:T(8,128)(2,1)S(1)}, bf16[8,96,384]{2,1,0:T(8,128)(2,1)S(1)}, u32[]{:S(2)}, u32[]{:S(2)}) collective-permute-start(bf16[8,96,384]{2,1,0:T(8,128)(2,1)S(1)} %products_3.2.refs_7_), channel_id=1, source_target_pairs={{0,96},{32,0},{64,32},{96,64},{1,97},{33,1},{65,33},{97,65},{2,98}... | collective-permute-start | bytes 1769480 | tf_op jit(solution)/shard_map/ppermute | solution.py:687
  67.4 21.1 %collective-permute-start.11 = (bf16[8,96,384]{2,1,0:T(8,128)(2,1)S(1)}, bf16[8,96,384]{2,1,0:T(8,128)(2,1)S(1)}, u32[]{:S(2)}, u32[]{:S(2)}) collective-permute-start(bf16[8,96,384]{2,1,0:T(8,128)(2,1)S(1)} %products_1.3.refs_7_), channel_id=1, source_target_pairs={{0,32},{32,64},{64,96},{96,0},{1,33},{33,65},{65,97},{97,1},{2,34}... | collective-permute-start | bytes 1769480 | tf_op jit(solution)/shard_map/ppermute | solution.py:579
  68.9 19.6 %collective-permute-start.12 = (bf16[8,96,384]{2,1,0:T(8,128)(2,1)S(1)}, bf16[8,96,384]{2,1,0:T(8,128)(2,1)S(1)}, u32[]{:S(2)}, u32[]{:S(2)}) collective-permute-start(bf16[8,96,384]{2,1,0:T(8,128)(2,1)S(1)} %products_3.3.refs_8_), channel_id=1, source_target_pairs={{0,96},{32,0},{64,32},{96,64},{1,97},{33,1},{65,33},{97,65},{2,98}... | collective-permute-start | bytes 1769480 | tf_op jit(solution)/shard_map/ppermute | solution.py:581
